TPU v7x, 32 devices: a whole 2x2x4 slice. The times are simulated.
32 devices in a mesh: slab: 4 (over z), filt: 8 (over y, x, core).
Axes of the slice: x: 2, y: 2, z: 4, core: 2. Of those that a mesh axis runs over, the one named last changes fastest.
Arguments:
- features: bfloat16 [16, 256, 64, 128], P('slab', 'filt'), may hold values from -6 to 6
- kernel: bfloat16 [3, 3, 3, 256, 256], P(None, None, None, 'filt'), may hold values from -0.078125 to 0.078125
- bias_vector: float32 [256], replicated, may hold values from -0.6 to 0.6
Outputs:
- activated: bfloat16 [16, 256, 64, 128], P('slab', 'filt')
All inputs are finite; a program needn't handle non-finite values.
Results may differ from a plain program's by a relative error of at most 0.005.
Values may be sent and summed in bfloat16 or wider, within the bound.
No kernel may reach another device: no remote copies, remote signals or barrier semaphores. Data moves between devices by JAX's collectives and lax.ppermute only.
A program may use at most 256 MiB of HBM per device.

v0:
```python
import functools

import jax
import jax.numpy as jnp
from jax import lax
from jax.experimental import pallas as pl
from jax.experimental.pallas import tpu as pltpu
from jax.sharding import PartitionSpec as P

slope = 0.3
PAIR = 2


def neighbour_planes(first, last, axis):
    devices = lax.axis_size(axis)
    up = [(i, i + 1) for i in range(devices - 1)]
    down = [(j, i) for i, j in up]
    return lax.ppermute(last, axis, up), lax.ppermute(first, axis, down)


def conv_kernel(vol_in, before_in, after_in, taps_in, bias_ref, out_ref, vol, taps, vol_sem, edge_sem, taps_sem):
    sources, planes, rows_in, chan, cols = vol_in.shape
    out_sources, out_chan = taps_in.shape[0], taps_in.shape[4]
    rows = rows_in - 2
    total_out = out_sources * out_chan
    copies = []
    for s in range(sources):
        part = pl.ds(s * chan, chan)
        copies.append(pltpu.make_async_copy(vol_in.at[s], vol.at[pl.ds(1, planes), :, part, :], vol_sem.at[s]))
        copies.append(pltpu.make_async_copy(before_in.at[s], vol.at[0, :, part, :], edge_sem.at[0, s]))
        copies.append(pltpu.make_async_copy(after_in.at[s], vol.at[planes + 1, :, part, :], edge_sem.at[1, s]))
    for s in range(out_sources):
        part = pl.ds(s * out_chan, out_chan)
        copies.append(pltpu.make_async_copy(taps_in.at[s], taps.at[:, :, :, part, :], taps_sem.at[s]))
    for copy in copies:
        copy.start()
    for copy in copies:
        copy.wait()

    lane = lax.broadcasted_iota(jnp.int32, (total_out, cols), 1)

    def tile(step, carry):
        plane = step // (rows // PAIR)
        row = (step % (rows // PAIR)) * PAIR
        total = jnp.zeros((3 * total_out, PAIR * cols), jnp.float32)
        for a in range(3):
            for b in range(3):
                piece = jnp.concatenate([vol[plane + a, row + b + r] for r in range(PAIR)], axis=1)
                total = total + jnp.dot(
                    taps[a, b].reshape(3 * total_out, -1), piece, preferred_element_type=jnp.float32
                )
        for r in range(PAIR):
            part = total[:, r * cols : (r + 1) * cols].reshape(3, total_out, cols)
            left = jnp.where(lane == 0, 0.0, pltpu.roll(part[0], 1, 1))
            right = jnp.where(lane == cols - 1, 0.0, pltpu.roll(part[2], cols - 1, 1))
            shifted = part[1] + left + right + bias_ref[...]
            done = jnp.where(shifted > 0, shifted, slope * shifted).astype(jnp.bfloat16)
            out_ref[:, plane, row + r] = done.reshape(out_sources, out_chan, cols)
        return carry

    lax.fori_loop(0, planes * (rows // PAIR), tile, 0)


def convolve(volume, before, after, taps, bias):
    sources, planes, rows_in, chan, cols = volume.shape
    out_sources, out_chan, in_chan = taps.shape[0], taps.shape[4], taps.shape[5]
    total_out = out_sources * out_chan
    rows = rows_in - 2
    wide_bias = jnp.broadcast_to(bias[:, None], (total_out, cols))
    macs = 27 * total_out * in_chan * planes * rows * cols
    any_space = pl.BlockSpec(memory_space=pl.ANY)
    in_vmem = pl.BlockSpec(memory_space=pltpu.VMEM)
    return pl.pallas_call(
        conv_kernel,
        out_shape=jax.ShapeDtypeStruct((out_sources, planes, rows, out_chan, cols), jnp.bfloat16),
        in_specs=[any_space] * 4 + [in_vmem],
        out_specs=in_vmem,
        scratch_shapes=[
            pltpu.VMEM((planes + 2, rows_in, sources * chan, cols), jnp.bfloat16),
            pltpu.VMEM((3, 3, 3, total_out, in_chan), jnp.bfloat16),
            pltpu.SemaphoreType.DMA((sources,)),
            pltpu.SemaphoreType.DMA((2, sources)),
            pltpu.SemaphoreType.DMA((out_sources,)),
        ],
        cost_estimate=pl.CostEstimate(flops=2 * macs, bytes_accessed=10_000_000, transcendentals=0),
        compiler_params=pltpu.CompilerParams(vmem_limit_bytes=48 * 2**20),
    )(volume, before, after, taps, wide_bias)


def body(features, kernel, bias_vector):
    planes, chan, y_cells, cols = features.shape
    out_chan = kernel.shape[3]
    parts = lax.axis_size("filt")
    me = lax.axis_index("filt")
    rows = y_cells // parts
    taps = lax.all_gather(kernel, "filt", axis=0)
    by_row = jnp.pad(features.transpose(0, 2, 1, 3), ((0, 0), (1, 1), (0, 0), (0, 0)))
    blocks = jnp.stack([by_row[:, j * rows : (j + 1) * rows + 2] for j in range(parts)])
    volume = lax.all_to_all(blocks, "filt", 0, 0)
    before, after = neighbour_planes(volume[:, 0], volume[:, -1], "slab")
    if chan % 16:
        volume = volume.transpose(1, 2, 0, 3, 4).reshape(1, planes, rows + 2, parts * chan, cols)
        before = before.transpose(1, 0, 2, 3).reshape(1, rows + 2, parts * chan, cols)
        after = after.transpose(1, 0, 2, 3).reshape(1, rows + 2, parts * chan, cols)
    if out_chan % 16:
        taps = taps.transpose(1, 2, 3, 0, 4, 5).reshape(1, 3, 3, 3, parts * out_chan, -1)
    result = convolve(volume, before, after, taps, bias_vector)
    if out_chan % 16:
        result = result.reshape(planes, rows, parts, out_chan, cols).transpose(2, 0, 1, 3, 4)
    final = jnp.zeros((planes, y_cells, out_chan, cols), jnp.bfloat16)
    for k in range(parts):
        other = me ^ k
        block = lax.dynamic_index_in_dim(result, other, 0, keepdims=False)
        if k:
            block = lax.ppermute(block, "filt", [(i, i ^ k) for i in range(parts)])
        final = lax.dynamic_update_slice_in_dim(final, block, other * rows, 1)
    return final.transpose(0, 2, 1, 3)


def solution(mesh):
    placed = (P("slab", "filt", None, None), P(None, None, None, "filt", None), P())
    return jax.shard_map(
        body, mesh=mesh, in_specs=placed, out_specs=P("slab", "filt", None, None), check_vma=False
    )
```

profile of v0, /device:TPU:0, one launch (start us, length us, event | category | flops | bytes accessed | tf_op | source)
XLA Modules:
  0.0 138.7 jit_solution(1431991412672500617)
XLA Ops:
  6.5 0.7 all-gather.3.cloned.1.call-update
  7.3 2.9 %copy.52 = bf16[4,32,64,128]{3,1,2,0:T(8,128)(2,1)S(1)} copy(bf16[4,32,64,128]{3,2,1,0:T(8,128)(2,1)} %param.3) | data formatting | bytes 4194304 | tf_op args[0]
  10.6 49.3 %all_to_all.5.vol_in = bf16[8,4,10,32,128]{4,3,2,1,0:T(8,128)(2,1)S(1)} all-to-all(bf16[8,4,10,32,128]{4,3,2,1,0:T(8,128)(2,1)S(1)} %fusion.3), channel_id=1, replica_groups=mesh['slab'=4,'filt'=8] {'filt'}, dimensions={0} | all-to-all | bytes 5242880 | tf_op jit(solution)/shard_map/all_to_all | solution.py:99
  60.0 1.3 slice_bitcast_fusion
  61.3 3.6 %collective-permute-start = (bf16[8,10,32,128]{3,2,1,0:T(8,128)(2,1)}, bf16[8,10,32,128]{3,2,1,0:T(8,128)(2,1)S(1)}, u32[]{:S(2)}, u32[]{:S(2)}) collective-permute-start(bf16[8,10,32,128]{3,2,1,0:T(8,128)(2,1)} %get-tuple-element.6), channel_id=1, source_target_pairs={{0,8},{8,16},{16,24},{1,9},{9,17},{17,25},{2,10},{10,18},{18,26},{... | collective-permute-start | bytes 1966088 | tf_op jit(solution)/shard_map/ppermute | solution.py:18
  64.9 1.3 collective-permute-start.1
  66.3 10.8 %collective-permute-done.before_in = bf16[8,10,32,128]{3,2,1,0:T(8,128)(2,1)S(1)} collective-permute-done((bf16[8,10,32,128]{3,2,1,0:T(8,128)(2,1)}, bf16[8,10,32,128]{3,2,1,0:T(8,128)(2,1)S(1)}, u32[]{:S(2)}, u32[]{:S(2)}) %collective-permute-start) | collective-permute-done | bytes 655392 | tf_op jit(solution)/shard_map/ppermute | solution.py:18
  77.1 4.2 %collective-permute-done.1.after_in = bf16[8,10,32,128]{3,2,1,0:T(8,128)(2,1)} collective-permute-done((bf16[8,10,32,128]{3,2,1,0:T(8,128)(2,1)}, bf16[8,10,32,128]{3,2,1,0:T(8,128)(2,1)}, u32[]{:S(2)}, u32[]{:S(2)}) %collective-permute-start.1) | collective-permute-done | bytes 655392 | tf_op jit(solution)/shard_map/ppermute | solution.py:18
  81.3 21.2 %shard_map.37 = bf16[8,4,8,32,128]{4,3,2,1,0:T(8,128)(2,1)S(1)} custom-call(bf16[8,4,10,32,128]{4,3,2,1,0:T(8,128)(2,1)S(1)} %all_to_all.5.vol_in, bf16[8,10,32,128]{3,2,1,0:T(8,128)(2,1)S(1)} %collective-permute-done.before_in, bf16[8,10,32,128]{3,2,1,0:T(8,128)(2,1)} %collective-permute-done.1.after_in, bf16[8,3,3,3,32,256]{5,4,3,2,1,0:T(8,128)(2,1)} %bitcast.69, ...), custom_call_target="tpu_custom_call" | custom-call | flops 14495514624 | bytes 10000000 | tf_op jit(solution)/shard_map/pallas_call | solution.py:73
  102.6 0.4 dynamic-slice_bitcast_fusion
  103.2 1.7 %collective-permute-start.4 = (bf16[4,8,32,128]{3,2,1,0:T(8,128)(2,1)S(1)}, bf16[4,8,32,128]{3,2,1,0:T(8,128)(2,1)S(1)}, u32[]{:S(2)}, u32[]{:S(2)}) collective-permute-start(bf16[4,8,32,128]{3,2,1,0:T(8,128)(2,1)S(1)} %get-tuple-element.11), channel_id=1, source_target_pairs={{0,3},{1,2},{2,1},{3,0},{4,7},{5,6},{6,5},{7,4},{8,11},{9,10},{10,... | collective-permute-start | bytes 786440 | tf_op jit(solution)/shard_map/ppermute | solution.py:115
  104.9 0.6 collective-permute-start.5
  105.5 1.2 collective-permute-start.6
  106.7 0.5 broadcast_in_dim.4
  107.2 0.2 copy_dynamic-update-slice_fusion.7
  107.4 0.7 collective-permute-start.7
  108.1 0.2 copy_dynamic-update-slice_fusion.6
  108.3 4.0 %collective-permute-done.3 = bf16[4,8,32,128]{3,2,1,0:T(8,128)(2,1)S(1)} collective-permute-done((bf16[4,8,32,128]{3,2,1,0:T(8,128)(2,1)S(1)}, bf16[4,8,32,128]{3,2,1,0:T(8,128)(2,1)S(1)}, u32[]{:S(2)}, u32[]{:S(2)}) %collective-permute-start.3) | collective-permute-done | bytes 262176 | tf_op jit(solution)/shard_map/ppermute | solution.py:115
  112.5 4.3 %collective-permute-done.4 = bf16[4,8,32,128]{3,2,1,0:T(8,128)(2,1)S(1)} collective-permute-done((bf16[4,8,32,128]{3,2,1,0:T(8,128)(2,1)S(1)}, bf16[4,8,32,128]{3,2,1,0:T(8,128)(2,1)S(1)}, u32[]{:S(2)}, u32[]{:S(2)}) %collective-permute-start.4) | collective-permute-done | bytes 262176 | tf_op jit(solution)/shard_map/ppermute | solution.py:115
  117.0 0.2 copy_dynamic-update-slice_fusion.3
  117.2 12.8 %collective-permute-done.6 = bf16[4,8,32,128]{3,2,1,0:T(8,128)(2,1)S(1)} collective-permute-done((bf16[4,8,32,128]{3,2,1,0:T(8,128)(2,1)S(1)}, bf16[4,8,32,128]{3,2,1,0:T(8,128)(2,1)S(1)}, u32[]{:S(2)}, u32[]{:S(2)}) %collective-permute-start.6) | collective-permute-done | bytes 262176 | tf_op jit(solution)/shard_map/ppermute | solution.py:115
  130.1 0.2 copy_dynamic-update-slice_fusion.1
  130.3 0.2 copy_dynamic-update-slice_fusion
  130.5 1.3 copy-done
  (24 shorter events, 1.1 us)
Async XLA Ops:
  6.5 74.7 %all-gather.3.cloned.1.call-start = ((), (), s32[]{:S(2)}) async-start(), calls=%async_computation.1 | async-start | bytes 3981312 | tf_op jit(solution)/shard_map/all_gather | solution.py:96
  60.0 21.3 %copy-start.1 = (f32[256]{0:T(256)S(1)}, f32[256]{0:T(256)}, u32[]{:S(2)}) copy-start(f32[256]{0:T(256)} %param.5) | copy-start | bytes 3076
  61.3 15.8 %collective-permute-start = (bf16[8,10,32,128]{3,2,1,0:T(8,128)(2,1)}, bf16[8,10,32,128]{3,2,1,0:T(8,128)(2,1)S(1)}, u32[]{:S(2)}, u32[]{:S(2)}) collective-permute-start(bf16[8,10,32,128]{3,2,1,0:T(8,128)(2,1)} %get-tuple-element.6), channel_id=1, source_target_pairs={{0,8},{8,16},{16,24},{1,9},{9,17},{17,25},{2,10},{10,18},{18,26},{... | collective-permute-start | bytes 1966088 | tf_op jit(solution)/shard_map/ppermute | solution.py:18
  64.9 16.3 %collective-permute-start.1 = (bf16[8,10,32,128]{3,2,1,0:T(8,128)(2,1)}, bf16[8,10,32,128]{3,2,1,0:T(8,128)(2,1)}, u32[]{:S(2)}, u32[]{:S(2)}) collective-permute-start(bf16[8,10,32,128]{3,2,1,0:T(8,128)(2,1)} %get-tuple-element.5), channel_id=1, source_target_pairs={{8,0},{16,8},{24,16},{9,1},{17,9},{25,17},{10,2},{18,10},{26,18},{... | collective-permute-start | bytes 1966088 | tf_op jit(solution)/shard_map/ppermute | solution.py:18
  103.0 4.4 %collective-permute-start.2 = (bf16[4,8,32,128]{3,2,1,0:T(8,128)(2,1)S(1)}, bf16[4,8,32,128]{3,2,1,0:T(8,128)(2,1)S(1)}, u32[]{:S(2)}, u32[]{:S(2)}) collective-permute-start(bf16[4,8,32,128]{3,2,1,0:T(8,128)(2,1)S(1)} %get-tuple-element.13), channel_id=1, source_target_pairs={{0,1},{1,0},{2,3},{3,2},{4,5},{5,4},{6,7},{7,6},{8,9},{9,8},{10,11... | collective-permute-start | bytes 786440 | tf_op jit(solution)/shard_map/ppermute | solution.py:115
  103.1 9.2 %collective-permute-start.3 = (bf16[4,8,32,128]{3,2,1,0:T(8,128)(2,1)S(1)}, bf16[4,8,32,128]{3,2,1,0:T(8,128)(2,1)S(1)}, u32[]{:S(2)}, u32[]{:S(2)}) collective-permute-start(bf16[4,8,32,128]{3,2,1,0:T(8,128)(2,1)S(1)} %get-tuple-element.12), channel_id=1, source_target_pairs={{0,2},{1,3},{2,0},{3,1},{4,6},{5,7},{6,4},{7,5},{8,10},{9,11},{10,... | collective-permute-start | bytes 786440 | tf_op jit(solution)/shard_map/ppermute | solution.py:115
  103.2 13.6 %collective-permute-start.4 = (bf16[4,8,32,128]{3,2,1,0:T(8,128)(2,1)S(1)}, bf16[4,8,32,128]{3,2,1,0:T(8,128)(2,1)S(1)}, u32[]{:S(2)}, u32[]{:S(2)}) collective-permute-start(bf16[4,8,32,128]{3,2,1,0:T(8,128)(2,1)S(1)} %get-tuple-element.11), channel_id=1, source_target_pairs={{0,3},{1,2},{2,1},{3,0},{4,7},{5,6},{6,5},{7,4},{8,11},{9,10},{10,... | collective-permute-start | bytes 786440 | tf_op jit(solution)/shard_map/ppermute | solution.py:115
  104.9 12.1 %collective-permute-start.5 = (bf16[4,8,32,128]{3,2,1,0:T(8,128)(2,1)S(1)}, bf16[4,8,32,128]{3,2,1,0:T(8,128)(2,1)S(1)}, u32[]{:S(2)}, u32[]{:S(2)}) collective-permute-start(bf16[4,8,32,128]{3,2,1,0:T(8,128)(2,1)S(1)} %get-tuple-element.10), channel_id=1, source_target_pairs={{0,4},{1,5},{2,6},{3,7},{4,0},{5,1},{6,2},{7,3},{8,12},{9,13},{10,... | collective-permute-start | bytes 786440 | tf_op jit(solution)/shard_map/ppermute | solution.py:115
  105.5 24.5 %collective-permute-start.6 = (bf16[4,8,32,128]{3,2,1,0:T(8,128)(2,1)S(1)}, bf16[4,8,32,128]{3,2,1,0:T(8,128)(2,1)S(1)}, u32[]{:S(2)}, u32[]{:S(2)}) collective-permute-start(bf16[4,8,32,128]{3,2,1,0:T(8,128)(2,1)S(1)} %get-tuple-element.9), channel_id=1, source_target_pairs={{0,5},{1,4},{2,7},{3,6},{4,1},{5,0},{6,3},{7,2},{8,13},{9,12},{10,... | collective-permute-start | bytes 786440 | tf_op jit(solution)/shard_map/ppermute | solution.py:115
  107.4 22.7 %collective-permute-start.7 = (bf16[4,8,32,128]{3,2,1,0:T(8,128)(2,1)S(1)}, bf16[4,8,32,128]{3,2,1,0:T(8,128)(2,1)S(1)}, u32[]{:S(2)}, u32[]{:S(2)}) collective-permute-start(bf16[4,8,32,128]{3,2,1,0:T(8,128)(2,1)S(1)} %get-tuple-element.8), channel_id=1, source_target_pairs={{0,6},{1,7},{2,4},{3,5},{4,2},{5,3},{6,0},{7,1},{8,14},{9,15},{10,... | collective-permute-start | bytes 786440 | tf_op jit(solution)/shard_map/ppermute | solution.py:115
  112.3 18.0 %collective-permute-start.8 = (bf16[4,8,32,128]{3,2,1,0:T(8,128)(2,1)S(1)}, bf16[4,8,32,128]{3,2,1,0:T(8,128)(2,1)S(1)}, u32[]{:S(2)}, u32[]{:S(2)}) collective-permute-start(bf16[4,8,32,128]{3,2,1,0:T(8,128)(2,1)S(1)} %get-tuple-element.7), channel_id=1, source_target_pairs={{0,7},{1,6},{2,5},{3,4},{4,3},{5,2},{6,1},{7,0},{8,15},{9,14},{10,... | collective-permute-start | bytes 786440 | tf_op jit(solution)/shard_map/ppermute | solution.py:115
  130.5 1.3 copy-start
Sparse Core Ops, SparseCore 0:
  9.2 53.5 all-gather.2
where the time goes:
time: 139 us
  blocking collectives  49.3 us (35%)
  waiting for transfers between devices  36.8 us (26%)
  Pallas kernels  21.2 us (15%)
  between operations  13.7 us (10%)
  starting transfers between devices  9.28 us (7%)
  local copies, waits for them, and re-layouts  8.28 us (6%)
    all_to_all x1, blocking collectives, body(): volume = lax.all_to_all(blocks, 'filt', 0, 0)  49.3 us
    pallas_call x1, Pallas kernels, convolve(): pl.pallas_call(conv_kernel, out_shape=jax.ShapeDtypeStruct((out_sources,...  21.2 us
    ppermute x7, waiting for transfers between devices, body(): block = lax.ppermute(block, 'filt', [(i, i ^ k) for i in range(parts)])  21.1 us
    ppermute x2, waiting for transfers between devices, neighbour_planes(): return (lax.ppermute(last, axis, up), lax.ppermute(first, axis, down))  15 us
    ppermute x2, starting transfers between devices, neighbour_planes(): return (lax.ppermute(last, axis, up), lax.ppermute(first, axis, down))  4.9 us
    unnamed x12, local copies, waits for them, and re-layouts  4.57 us
    ppermute x7, starting transfers between devices, body(): block = lax.ppermute(block, 'filt', [(i, i ^ k) for i in range(parts)])  4.38 us
  transfers between devices with their start and end apart: 10, of which 5 were waited for; matrix products, arithmetic and copies ran while one was open for 5% of the time, Pallas kernels for 0%

commit v1 on v0

v1 whole, which is shorter than its diff:
```python
import functools

import jax
import jax.numpy as jnp
from jax import lax
from jax.experimental import pallas as pl
from jax.experimental.pallas import tpu as pltpu
from jax.sharding import PartitionSpec as P

slope = 0.3
PAIR = 2


def conv_kernel(out_planes, planes, chips, middle_planes, with_edges, *refs):
    refs = list(refs)
    chip_ref = refs.pop(0)
    outer = [refs.pop(0) for _ in range(chips)]
    inner = [refs.pop(0) for _ in range(chips)]
    edges = [refs.pop(0) for _ in range(2)] if with_edges else []
    taps_in, bias_ref, out_ref, vol, taps, vol_sem, edge_sem, taps_sem = refs
    rows_in, chan, cols = outer[0].shape[1:]
    halves, blocks, out_chan = taps_in.shape[0], taps_in.shape[1], taps_in.shape[5]
    total_out = halves * blocks * out_chan
    rows = rows_in - 2
    chip = chip_ref[0]
    copies = []
    for s in range(halves):
        for g in range(blocks):
            part = pl.ds((g * halves + s) * out_chan, out_chan)
            copies.append(pltpu.make_async_copy(taps_in.at[s, g], taps.at[:, :, :, part, :], taps_sem.at[s, g]))
    for k in range(chips):
        part = pl.ds(pl.multiple_of((chip ^ k) * chan, chan), chan)
        copies.append(pltpu.make_async_copy(outer[k].at[0], vol.at[1, :, part, :], vol_sem.at[0, k]))
        copies.append(pltpu.make_async_copy(outer[k].at[1], vol.at[planes, :, part, :], vol_sem.at[1, k]))
        copies.append(pltpu.make_async_copy(inner[k], vol.at[pl.ds(2, middle_planes), :, part, :], vol_sem.at[2, k]))
        for side, edge in enumerate(edges):
            place = (planes + 1) * side
            copies.append(pltpu.make_async_copy(edge.at[k], vol.at[place, :, part, :], edge_sem.at[side, k]))
    for copy in copies:
        copy.start()
    for copy in copies:
        copy.wait()

    lane = lax.broadcasted_iota(jnp.int32, (total_out, cols), 1)
    per_plane = rows // PAIR
    first, stride = out_planes[0], (out_planes[1] - out_planes[0] if len(out_planes) > 1 else 0)

    def tile(step, carry):
        slot = step // per_plane
        plane = first + slot * stride
        row = (step % per_plane) * PAIR
        total = jnp.zeros((3 * total_out, PAIR * cols), jnp.float32)
        for a in range(3):
            for b in range(3):
                piece = jnp.concatenate([vol[plane + a, row + b + r] for r in range(PAIR)], axis=1)
                total = total + jnp.dot(
                    taps[a, b].reshape(3 * total_out, -1), piece, preferred_element_type=jnp.float32
                )
        for r in range(PAIR):
            part = total[:, r * cols : (r + 1) * cols].reshape(3, total_out, cols)
            left = jnp.where(lane == 0, 0.0, pltpu.roll(part[0], 1, 1))
            right = jnp.where(lane == cols - 1, 0.0, pltpu.roll(part[2], cols - 1, 1))
            shifted = part[1] + left + right + bias_ref[...]
            done = jnp.where(shifted > 0, shifted, slope * shifted).astype(jnp.bfloat16)
            out_ref[:, slot, row + r] = done.reshape(out_ref.shape[0], out_ref.shape[3], cols)
        return carry

    lax.fori_loop(0, len(out_planes) * per_plane, tile, 0)


def convolve(out_planes, planes, chip, outer, inner, edges, taps, bias):
    chips = len(outer)
    middle_planes, rows_in, chan, cols = inner[0].shape
    halves, blocks, out_chan, in_chan = taps.shape[0], taps.shape[1], taps.shape[5], taps.shape[6]
    total_out = halves * blocks * out_chan
    rows = rows_in - 2
    wide_bias = jnp.broadcast_to(bias[:, None], (total_out, cols))
    macs = 27 * total_out * in_chan * len(out_planes) * rows * cols
    any_space = pl.BlockSpec(memory_space=pl.ANY)
    in_vmem = pl.BlockSpec(memory_space=pltpu.VMEM)
    in_smem = pl.BlockSpec(memory_space=pltpu.SMEM)
    arrays = [*outer, *inner, *edges, taps]
    return pl.pallas_call(
        functools.partial(conv_kernel, out_planes, planes, chips, middle_planes, bool(edges)),
        out_shape=jax.ShapeDtypeStruct((chips, len(out_planes), rows, total_out // chips, cols), jnp.bfloat16),
        in_specs=[in_smem] + [any_space] * len(arrays) + [in_vmem],
        out_specs=in_vmem,
        scratch_shapes=[
            pltpu.VMEM((planes + 2, rows_in, chips * chan, cols), jnp.bfloat16),
            pltpu.VMEM((3, 3, 3, total_out, in_chan), jnp.bfloat16),
            pltpu.SemaphoreType.DMA((3, chips)),
            pltpu.SemaphoreType.DMA((2, chips)),
            pltpu.SemaphoreType.DMA((halves, blocks)),
        ],
        cost_estimate=pl.CostEstimate(flops=2 * macs, bytes_accessed=10_000_000, transcendentals=0),
        compiler_params=pltpu.CompilerParams(vmem_limit_bytes=48 * 2**20),
    )(chip, *arrays, wide_bias)


def body(features, kernel, bias_vector):
    planes, chan, y_cells, cols = features.shape
    out_chan = kernel.shape[3]
    parts = lax.axis_size("filt")
    slabs = lax.axis_size("slab")
    me = lax.axis_index("filt")
    chips = parts // 2
    chip, core = me // 2, me % 2
    rows = y_cells // parts

    def swap(array, k):
        return lax.ppermute(array, "filt", [(i, i ^ k) for i in range(parts)])

    same_core = [[2 * g + c for g in range(chips)] for c in range(2)]
    pairs = [[2 * g, 2 * g + 1] for g in range(chips)]
    taps = lax.all_gather(kernel, "filt", axis=0, axis_index_groups=same_core)
    taps = lax.all_gather(taps, "filt", axis=0, axis_index_groups=pairs)
    if out_chan % 16:
        taps = taps.transpose(2, 3, 4, 1, 0, 5, 6).reshape(1, 1, 3, 3, 3, parts * out_chan, -1)

    def exchange(piece):
        count = piece.shape[0]
        by_row = jnp.pad(piece.transpose(0, 2, 1, 3), ((0, 0), (1, 1), (0, 0), (0, 0)))
        span = (parts - 2) * rows + rows + 2

        def windows(which):
            cut = lax.dynamic_slice_in_dim(by_row, which * rows, span, 1)
            return jnp.stack([cut[:, 2 * h * rows : 2 * h * rows + rows + 2] for h in range(chips)])

        mine = windows(core)
        theirs = swap(windows(1 - core), 1)
        both = jnp.concatenate(
            [jnp.where(core == 0, mine, theirs), jnp.where(core == 0, theirs, mine)], axis=3
        )
        blocks = [lax.dynamic_index_in_dim(both, chip ^ k, 0, keepdims=False) for k in range(chips)]
        return [block if k == 0 else swap(block, 2 * k) for k, block in enumerate(blocks)]

    outer = exchange(jnp.concatenate([features[:1], features[-1:]]))
    inner = exchange(features[1:-1])
    up = [(i, i + 1) for i in range(slabs - 1)]
    down = [(i + 1, i) for i in range(slabs - 1)]
    before = lax.ppermute(jnp.stack([block[1] for block in outer]), "slab", up)
    after = lax.ppermute(jnp.stack([block[0] for block in outer]), "slab", down)

    chip_array = jnp.full((1,), chip, jnp.int32)
    middle = tuple(range(1, planes - 1))
    ends = (0, planes - 1)

    def send_back(result):
        count = result.shape[1]
        result = result.reshape(chips, count, rows, 2, out_chan, cols)
        final = jnp.zeros((count, y_cells, out_chan, cols), jnp.bfloat16)
        for k in range(parts):
            other = me ^ k
            block = lax.dynamic_slice(
                result, (other // 2, 0, 0, other % 2, 0, 0), (1, count, rows, 1, out_chan, cols)
            ).reshape(count, rows, out_chan, cols)
            if k:
                block = swap(block, k)
            final = lax.dynamic_update_slice_in_dim(final, block, other * rows, 1)
        return final.transpose(0, 2, 1, 3)

    inside = send_back(convolve(middle, planes, chip_array, outer, inner, [], taps, bias_vector))
    outside = send_back(convolve(ends, planes, chip_array, outer, inner, [before, after], taps, bias_vector))
    return jnp.concatenate([outside[:1], inside, outside[1:]])


def solution(mesh):
    placed = (P("slab", "filt", None, None), P(None, None, None, "filt", None), P())
    return jax.shard_map(
        body, mesh=mesh, in_specs=placed, out_specs=P("slab", "filt", None, None), check_vma=False
    )
```

time: 139 us -> 163 us (1.17)
  blocking collectives: 49.3 us -> 0 us
  waiting for transfers between devices: 36.8 us -> 81.5 us
  starting transfers between devices: 9.28 us -> 29.8 us
  other arithmetic: 0 us -> 5.3 us
  Pallas kernels: 21.2 us -> 23 us
    all_to_all x1 -> x0, blocking collectives: 49.3 us -> none  [body(): volume = lax.all_to_all(blocks, 'filt', 0, 0)]
    all_gather x1 -> x2, waiting for transfers between devices: 0.01 us -> 37.2 us  [the longest x1 37.2 us: body(): taps = lax.all_gather(kernel, 'filt', axis=0, axis_index_groups=same_core)]
    ppermute x9 -> x24, starting transfers between devices: 9.28 us -> 29.8 us  [the longest x22 23.9 us: swap(): return lax.ppermute(array, 'filt', [(i, i ^ k) for i in range(parts)])]
    ppermute x9 -> x24, waiting for transfers between devices: 36.1 us -> 43.5 us  [the longest x22 43.5 us: swap(): return lax.ppermute(array, 'filt', [(i, i ^ k) for i in range(parts)])]
    another operation x0 -> x4, other arithmetic: none -> 2.04 us  [the longest x1 0.95 us: body(): after = lax.ppermute(jnp.stack([block[0] for block in outer]), 'slab', down)]
    pallas_call x1 -> x2, Pallas kernels: 21.2 us -> 23 us  [convolve(): pl.pallas_call(functools.partial(conv_kernel, out_planes, planes, chips,...]
    squeeze x2 -> x0, local copies, waits for them, and re-layouts: 1.71 us -> none  [the longest x1 1.31 us: body(): before, after = neighbour_planes(volume[:, 0], volume[:, -1], 'slab')]
    unnamed x12 -> x15, local copies, waits for them, and re-layouts: 4.57 us -> 4.79 us
  transfers between devices with their start and end apart: 10 -> 26, of which waited for: 5 -> 10; matrix products, arithmetic and copies ran while one was open for 5% -> 5% of each run, Pallas kernels for 0% -> 14%
where the time goes in v1:
time: 163 us
  waiting for transfers between devices  81.5 us (50%)
  starting transfers between devices  29.8 us (18%)
  Pallas kernels  23 us (14%)
  between operations  14.4 us (9%)
  local copies, waits for them, and re-layouts  9.09 us (6%)
  other arithmetic  5.3 us (3%)
    ppermute x22, waiting for transfers between devices, swap(): return lax.ppermute(array, 'filt', [(i, i ^ k) for i in range(parts)])  43.5 us
    all_gather x1, waiting for transfers between devices, body(): taps = lax.all_gather(kernel, 'filt', axis=0, axis_index_groups=same_core)  37.2 us
    ppermute x22, starting transfers between devices, swap(): return lax.ppermute(array, 'filt', [(i, i ^ k) for i in range(parts)])  23.9 us
    pallas_call x2, Pallas kernels, convolve(): pl.pallas_call(functools.partial(conv_kernel, out_planes, planes, chips,...  23 us
    unnamed x15, local copies, waits for them, and re-layouts  4.79 us
    ppermute x1, starting transfers between devices, body(): before = lax.ppermute(jnp.stack([block[1] for block in outer]), 'slab', up)  4.57 us
  transfers between devices with their start and end apart: 26, of which 10 were waited for; matrix products, arithmetic and copies ran while one was open for 5% of the time, Pallas kernels for 14%

profile of v1, /device:TPU:0, one launch (start us, length us, event | category | flops | bytes accessed | tf_op | source)
XLA Modules:
  0.0 163.1 jit_solution(12282178874165458795)
XLA Ops:
  7.3 37.2 %all-gather.5.cloned.1.call-done = bf16[12,3,3,32,256]{4,3,2,1,0:T(8,128)(2,1)} async-done(((bf16[3,3,3,32,256]{4,3,2,1,0:T(8,128)(2,1)}), bf16[12,3,3,32,256]{4,3,2,1,0:T(8,128)(2,1)}) %all-gather.5.cloned.1.call-update) | async-done | bytes 1769488 | tf_op jit(solution)/shard_map/all_gather | solution.py:115
  48.8 1.7 %collective-permute-done.4 = bf16[4,2,10,32,128]{4,3,2,1,0:T(8,128)(2,1)S(1)} collective-permute-done((bf16[4,2,10,32,128]{4,3,2,1,0:T(8,128)(2,1)S(1)}, bf16[4,2,10,32,128]{4,3,2,1,0:T(8,128)(2,1)S(1)}, u32[]{:S(2)}, u32[]{:S(2)}) %collective-permute-start.4) | collective-permute-done | bytes 655392 | tf_op jit(solution)/shard_map/ppermute | solution.py:111
  51.9 1.5 collective-permute-start.1
  54.2 1.5 collective-permute-start.6
  55.7 1.5 collective-permute-start.7
  57.7 4.8 %collective-permute-done.1.refs_2_ = bf16[2,10,64,128]{3,2,1,0:T(8,128)(2,1)S(1)} collective-permute-done((bf16[2,10,64,128]{3,2,1,0:T(8,128)(2,1)S(1)}, bf16[2,10,64,128]{3,2,1,0:T(8,128)(2,1)S(1)}, u32[]{:S(2)}, u32[]{:S(2)}) %collective-permute-start.1) | collective-permute-done | bytes 327712 | tf_op jit(solution)/shard_map/ppermute | solution.py:111
  62.5 1.5 collective-permute-start.3
  64.0 20.4 %collective-permute-done.2.refs_3_ = bf16[2,10,64,128]{3,2,1,0:T(8,128)(2,1)S(1)} collective-permute-done((bf16[2,10,64,128]{3,2,1,0:T(8,128)(2,1)S(1)}, bf16[2,10,64,128]{3,2,1,0:T(8,128)(2,1)S(1)}, u32[]{:S(2)}, u32[]{:S(2)}) %collective-permute-start.2) | collective-permute-done | bytes 327712 | tf_op jit(solution)/shard_map/ppermute | solution.py:111
  87.7 4.6 %collective-permute-start.8 = (bf16[4,10,64,128]{3,2,1,0:T(8,128)(2,1)}, bf16[4,10,64,128]{3,2,1,0:T(8,128)(2,1)S(1)}, u32[]{:S(2)}, u32[]{:S(2)}) collective-permute-start(bf16[4,10,64,128]{3,2,1,0:T(8,128)(2,1)} %pad_maximum_fusion.5), channel_id=1, source_target_pairs={{0,8},{8,16},{16,24},{1,9},{9,17},{17,25},{2,10},{10,18},{18,26},{... | collective-permute-start | bytes 1966088 | tf_op jit(solution)/shard_map/ppermute | solution.py:141
  95.8 11.5 %shard_map.38 = bf16[4,2,8,64,128]{4,3,2,1,0:T(8,128)(2,1)S(1)} custom-call(s32[1]{0:T(128)} %bitcast.refs_0_, bf16[2,10,64,128]{3,2,1,0:T(8,128)(2,1)S(1)} %bitcast.109, bf16[2,10,64,128]{3,2,1,0:T(8,128)(2,1)S(1)} %collective-permute-done.1.refs_2_, bf16[2,10,64,128]{3,2,1,0:T(8,128)(2,1)S(1)} %collective-permute-done.2.refs_3_, ...), custom_call_target="tpu_custom_call" | custom-call | flops 7247757312 | bytes 10000000 | tf_op jit(solution)/shard_map/pallas_call | solution.py:83
  107.7 1.5 collective-permute-start.18
  109.7 11.5 %shard_map.37 = bf16[4,2,8,64,128]{4,3,2,1,0:T(8,128)(2,1)S(1)} custom-call(s32[1]{0:T(128)} %bitcast.refs_0_, bf16[2,10,64,128]{3,2,1,0:T(8,128)(2,1)S(1)} %bitcast.110, bf16[2,10,64,128]{3,2,1,0:T(8,128)(2,1)S(1)} %collective-permute-done.1.refs_2_, bf16[2,10,64,128]{3,2,1,0:T(8,128)(2,1)S(1)} %collective-permute-done.2.refs_3_, ...), custom_call_target="tpu_custom_call" | custom-call | flops 7247757312 | bytes 10000000 | tf_op jit(solution)/shard_map/pallas_call | solution.py:83
  121.8 1.5 collective-permute-start.11
  124.8 2.7 %collective-permute-done.11 = bf16[2,8,32,128]{3,1,2,0:T(8,128)(2,1)S(1)} collective-permute-done((bf16[2,8,32,128]{3,1,2,0:T(8,128)(2,1)S(1)}, bf16[2,8,32,128]{3,1,2,0:T(8,128)(2,1)S(1)}, u32[]{:S(2)}, u32[]{:S(2)}) %collective-permute-start.11) | collective-permute-done | bytes 131104 | tf_op jit(solution)/shard_map/ppermute | solution.py:111
  127.5 2.2 %collective-permute-start.13 = (bf16[2,8,32,128]{3,1,2,0:T(8,128)(2,1)S(1)}, bf16[2,8,32,128]{3,1,2,0:T(8,128)(2,1)S(1)}, u32[]{:S(2)}, u32[]{:S(2)}) collective-permute-start(bf16[2,8,32,128]{3,1,2,0:T(8,128)(2,1)S(1)} %bitcast.129), channel_id=1, source_target_pairs={{0,4},{1,5},{2,6},{3,7},{4,0},{5,1},{6,2},{7,3},{8,12},{9,13},{10,... | collective-permute-start | bytes 393224 | tf_op jit(solution)/shard_map/ppermute | solution.py:111
  131.3 1.6 collective-permute-done.13
  132.8 1.4 collective-permute-start.15
  134.3 3.0 %collective-permute-done.14 = bf16[2,8,32,128]{3,1,2,0:T(8,128)(2,1)S(1)} collective-permute-done((bf16[2,8,32,128]{3,1,2,0:T(8,128)(2,1)S(1)}, bf16[2,8,32,128]{3,1,2,0:T(8,128)(2,1)S(1)}, u32[]{:S(2)}, u32[]{:S(2)}) %collective-permute-start.14) | collective-permute-done | bytes 131104 | tf_op jit(solution)/shard_map/ppermute | solution.py:111
  137.3 2.6 %collective-permute-start.16 = (bf16[2,8,32,128]{3,1,2,0:T(8,128)(2,1)S(1)}, bf16[2,8,32,128]{3,1,2,0:T(8,128)(2,1)S(1)}, u32[]{:S(2)}, u32[]{:S(2)}) collective-permute-start(bf16[2,8,32,128]{3,1,2,0:T(8,128)(2,1)S(1)} %bitcast.124), channel_id=1, source_target_pairs={{0,7},{1,6},{2,5},{3,4},{4,3},{5,2},{6,1},{7,0},{8,15},{9,14},{10,... | collective-permute-start | bytes 393224 | tf_op jit(solution)/shard_map/ppermute | solution.py:111
  141.2 1.5 collective-permute-done.16
  142.7 1.8 %collective-permute-start.21 = (bf16[2,8,32,128]{3,1,2,0:T(8,128)(2,1)S(1)}, bf16[2,8,32,128]{3,1,2,0:T(8,128)(2,1)S(1)}, u32[]{:S(2)}, u32[]{:S(2)}) collective-permute-start(bf16[2,8,32,128]{3,1,2,0:T(8,128)(2,1)S(1)} %bitcast.122), channel_id=1, source_target_pairs={{0,5},{1,4},{2,7},{3,6},{4,1},{5,0},{6,3},{7,2},{8,13},{9,12},{10,... | collective-permute-start | bytes 393224 | tf_op jit(solution)/shard_map/ppermute | solution.py:111
  144.6 1.8 %collective-permute-start.22 = (bf16[2,8,32,128]{3,1,2,0:T(8,128)(2,1)S(1)}, bf16[2,8,32,128]{3,1,2,0:T(8,128)(2,1)S(1)}, u32[]{:S(2)}, u32[]{:S(2)}) collective-permute-start(bf16[2,8,32,128]{3,1,2,0:T(8,128)(2,1)S(1)} %bitcast.121), channel_id=1, source_target_pairs={{0,6},{1,7},{2,4},{3,5},{4,2},{5,3},{6,0},{7,1},{8,14},{9,15},{10,... | collective-permute-start | bytes 393224 | tf_op jit(solution)/shard_map/ppermute | solution.py:111
  147.3 7.2 %collective-permute-done.21 = bf16[2,8,32,128]{3,1,2,0:T(8,128)(2,1)S(1)} collective-permute-done((bf16[2,8,32,128]{3,1,2,0:T(8,128)(2,1)S(1)}, bf16[2,8,32,128]{3,1,2,0:T(8,128)(2,1)S(1)}, u32[]{:S(2)}, u32[]{:S(2)}) %collective-permute-start.21) | collective-permute-done | bytes 131104 | tf_op jit(solution)/shard_map/ppermute | solution.py:111
  154.7 1.6 pad_maximum_fusion
  (101 shorter events, 20.6 us)
Async XLA Ops:
  6.5 38.0 %all-gather.5.cloned.1.call-start = ((), (), s32[]{:S(2)}) async-start(), calls=%async_computation | async-start | bytes 2211840 | tf_op jit(solution)/shard_map/all_gather | solution.py:115
  7.3 86.5 %all-gather.7.cloned.1.call-start = ((), (), s32[]{:S(2)}) async-start(), calls=%async_computation.1 | async-start | bytes 5308416 | tf_op jit(solution)/shard_map/all_gather | solution.py:116
  51.9 10.6 %collective-permute-start.1 = (bf16[2,10,64,128]{3,2,1,0:T(8,128)(2,1)S(1)}, bf16[2,10,64,128]{3,2,1,0:T(8,128)(2,1)S(1)}, u32[]{:S(2)}, u32[]{:S(2)}) collective-permute-start(bf16[2,10,64,128]{3,2,1,0:T(8,128)(2,1)S(1)} %get-tuple-element.15), channel_id=1, source_target_pairs={{0,2},{1,3},{2,0},{3,1},{4,6},{5,7},{6,4},{7,5},{8,10},{9,11},{10,... | collective-permute-start | bytes 983048 | tf_op jit(solution)/shard_map/ppermute | solution.py:111
  53.6 38.7 %collective-permute-start.5 = (bf16[2,10,64,128]{3,2,1,0:T(8,128)(2,1)S(1)}, bf16[2,10,64,128]{3,2,1,0:T(8,128)(2,1)S(1)}, u32[]{:S(2)}, u32[]{:S(2)}) collective-permute-start(bf16[2,10,64,128]{3,2,1,0:T(8,128)(2,1)S(1)} %get-tuple-element.9), channel_id=1, source_target_pairs={{0,2},{1,3},{2,0},{3,1},{4,6},{5,7},{6,4},{7,5},{8,10},{9,11},{10,... | collective-permute-start | bytes 983048 | tf_op jit(solution)/shard_map/ppermute | solution.py:111
  54.2 38.1 %collective-permute-start.6 = (bf16[2,10,64,128]{3,2,1,0:T(8,128)(2,1)S(1)}, bf16[2,10,64,128]{3,2,1,0:T(8,128)(2,1)S(1)}, u32[]{:S(2)}, u32[]{:S(2)}) collective-permute-start(bf16[2,10,64,128]{3,2,1,0:T(8,128)(2,1)S(1)} %get-tuple-element.10), channel_id=1, source_target_pairs={{0,4},{1,5},{2,6},{3,7},{4,0},{5,1},{6,2},{7,3},{8,12},{9,13},{10,... | collective-permute-start | bytes 983048 | tf_op jit(solution)/shard_map/ppermute | solution.py:111
  55.7 37.4 %collective-permute-start.7 = (bf16[2,10,64,128]{3,2,1,0:T(8,128)(2,1)S(1)}, bf16[2,10,64,128]{3,2,1,0:T(8,128)(2,1)S(1)}, u32[]{:S(2)}, u32[]{:S(2)}) collective-permute-start(bf16[2,10,64,128]{3,2,1,0:T(8,128)(2,1)S(1)} %get-tuple-element.7), channel_id=1, source_target_pairs={{0,6},{1,7},{2,4},{3,5},{4,2},{5,3},{6,0},{7,1},{8,14},{9,15},{10,... | collective-permute-start | bytes 983048 | tf_op jit(solution)/shard_map/ppermute | solution.py:111
  57.1 27.3 %collective-permute-start.2 = (bf16[2,10,64,128]{3,2,1,0:T(8,128)(2,1)S(1)}, bf16[2,10,64,128]{3,2,1,0:T(8,128)(2,1)S(1)}, u32[]{:S(2)}, u32[]{:S(2)}) collective-permute-start(bf16[2,10,64,128]{3,2,1,0:T(8,128)(2,1)S(1)} %get-tuple-element.16), channel_id=1, source_target_pairs={{0,4},{1,5},{2,6},{3,7},{4,0},{5,1},{6,2},{7,3},{8,12},{9,13},{10,... | collective-permute-start | bytes 983048 | tf_op jit(solution)/shard_map/ppermute | solution.py:111
  62.5 22.0 %collective-permute-start.3 = (bf16[2,10,64,128]{3,2,1,0:T(8,128)(2,1)S(1)}, bf16[2,10,64,128]{3,2,1,0:T(8,128)(2,1)S(1)}, u32[]{:S(2)}, u32[]{:S(2)}) collective-permute-start(bf16[2,10,64,128]{3,2,1,0:T(8,128)(2,1)S(1)} %get-tuple-element.13), channel_id=1, source_target_pairs={{0,6},{1,7},{2,4},{3,5},{4,2},{5,3},{6,0},{7,1},{8,14},{9,15},{10,... | collective-permute-start | bytes 983048 | tf_op jit(solution)/shard_map/ppermute | solution.py:111
  85.5 24.2 %collective-permute-start.9 = (bf16[4,10,64,128]{3,2,1,0:T(8,128)(2,1)}, bf16[4,10,64,128]{3,2,1,0:T(8,128)(2,1)S(1)}, u32[]{:S(2)}, u32[]{:S(2)}) collective-permute-start(bf16[4,10,64,128]{3,2,1,0:T(8,128)(2,1)} %pad_maximum_fusion.6), channel_id=1, source_target_pairs={{8,0},{16,8},{24,16},{9,1},{17,9},{25,17},{10,2},{18,10},{26,18},{... | collective-permute-start | bytes 1966088 | tf_op jit(solution)/shard_map/ppermute | solution.py:142
  87.7 22.0 %collective-permute-start.8 = (bf16[4,10,64,128]{3,2,1,0:T(8,128)(2,1)}, bf16[4,10,64,128]{3,2,1,0:T(8,128)(2,1)S(1)}, u32[]{:S(2)}, u32[]{:S(2)}) collective-permute-start(bf16[4,10,64,128]{3,2,1,0:T(8,128)(2,1)} %pad_maximum_fusion.5), channel_id=1, source_target_pairs={{0,8},{8,16},{16,24},{1,9},{9,17},{17,25},{2,10},{10,18},{18,26},{... | collective-permute-start | bytes 1966088 | tf_op jit(solution)/shard_map/ppermute | solution.py:141
  107.5 37.1 %collective-permute-start.17 = (bf16[2,8,32,128]{3,1,2,0:T(8,128)(2,1)S(1)}, bf16[2,8,32,128]{3,1,2,0:T(8,128)(2,1)S(1)}, u32[]{:S(2)}, u32[]{:S(2)}) collective-permute-start(bf16[2,8,32,128]{3,1,2,0:T(8,128)(2,1)S(1)} %bitcast.119), channel_id=1, source_target_pairs={{0,1},{1,0},{2,3},{3,2},{4,5},{5,4},{6,7},{7,6},{8,9},{9,8},{10,11... | collective-permute-start | bytes 393224 | tf_op jit(solution)/shard_map/ppermute | solution.py:111
  107.7 38.8 %collective-permute-start.18 = (bf16[2,8,32,128]{3,1,2,0:T(8,128)(2,1)S(1)}, bf16[2,8,32,128]{3,1,2,0:T(8,128)(2,1)S(1)}, u32[]{:S(2)}, u32[]{:S(2)}) collective-permute-start(bf16[2,8,32,128]{3,1,2,0:T(8,128)(2,1)S(1)} %bitcast.118), channel_id=1, source_target_pairs={{0,2},{1,3},{2,0},{3,1},{4,6},{5,7},{6,4},{7,5},{8,10},{9,11},{10,... | collective-permute-start | bytes 393224 | tf_op jit(solution)/shard_map/ppermute | solution.py:111
  109.3 37.9 %collective-permute-start.19 = (bf16[2,8,32,128]{3,1,2,0:T(8,128)(2,1)S(1)}, bf16[2,8,32,128]{3,1,2,0:T(8,128)(2,1)S(1)}, u32[]{:S(2)}, u32[]{:S(2)}) collective-permute-start(bf16[2,8,32,128]{3,1,2,0:T(8,128)(2,1)S(1)} %bitcast.117), channel_id=1, source_target_pairs={{0,3},{1,2},{2,1},{3,0},{4,7},{5,6},{6,5},{7,4},{8,11},{9,10},{10,... | collective-permute-start | bytes 393224 | tf_op jit(solution)/shard_map/ppermute | solution.py:111
  121.4 3.2 %collective-permute-start.10 = (bf16[2,8,32,128]{3,1,2,0:T(8,128)(2,1)S(1)}, bf16[2,8,32,128]{3,1,2,0:T(8,128)(2,1)S(1)}, u32[]{:S(2)}, u32[]{:S(2)}) collective-permute-start(bf16[2,8,32,128]{3,1,2,0:T(8,128)(2,1)S(1)} %bitcast.128), channel_id=1, source_target_pairs={{0,1},{1,0},{2,3},{3,2},{4,5},{5,4},{6,7},{7,6},{8,9},{9,8},{10,11... | collective-permute-start | bytes 393224 | tf_op jit(solution)/shard_map/ppermute | solution.py:111
  121.8 5.7 %collective-permute-start.11 = (bf16[2,8,32,128]{3,1,2,0:T(8,128)(2,1)S(1)}, bf16[2,8,32,128]{3,1,2,0:T(8,128)(2,1)S(1)}, u32[]{:S(2)}, u32[]{:S(2)}) collective-permute-start(bf16[2,8,32,128]{3,1,2,0:T(8,128)(2,1)S(1)} %bitcast.127), channel_id=1, source_target_pairs={{0,2},{1,3},{2,0},{3,1},{4,6},{5,7},{6,4},{7,5},{8,10},{9,11},{10,... | collective-permute-start | bytes 393224 | tf_op jit(solution)/shard_map/ppermute | solution.py:111
  124.6 5.7 %collective-permute-start.12 = (bf16[2,8,32,128]{3,1,2,0:T(8,128)(2,1)S(1)}, bf16[2,8,32,128]{3,1,2,0:T(8,128)(2,1)S(1)}, u32[]{:S(2)}, u32[]{:S(2)}) collective-permute-start(bf16[2,8,32,128]{3,1,2,0:T(8,128)(2,1)S(1)} %bitcast.130), channel_id=1, source_target_pairs={{0,3},{1,2},{2,1},{3,0},{4,7},{5,6},{6,5},{7,4},{8,11},{9,10},{10,... | collective-permute-start | bytes 393224 | tf_op jit(solution)/shard_map/ppermute | solution.py:111
  127.5 5.3 %collective-permute-start.13 = (bf16[2,8,32,128]{3,1,2,0:T(8,128)(2,1)S(1)}, bf16[2,8,32,128]{3,1,2,0:T(8,128)(2,1)S(1)}, u32[]{:S(2)}, u32[]{:S(2)}) collective-permute-start(bf16[2,8,32,128]{3,1,2,0:T(8,128)(2,1)S(1)} %bitcast.129), channel_id=1, source_target_pairs={{0,4},{1,5},{2,6},{3,7},{4,0},{5,1},{6,2},{7,3},{8,12},{9,13},{10,... | collective-permute-start | bytes 393224 | tf_op jit(solution)/shard_map/ppermute | solution.py:111
  130.4 6.9 %collective-permute-start.14 = (bf16[2,8,32,128]{3,1,2,0:T(8,128)(2,1)S(1)}, bf16[2,8,32,128]{3,1,2,0:T(8,128)(2,1)S(1)}, u32[]{:S(2)}, u32[]{:S(2)}) collective-permute-start(bf16[2,8,32,128]{3,1,2,0:T(8,128)(2,1)S(1)} %bitcast.126), channel_id=1, source_target_pairs={{0,5},{1,4},{2,7},{3,6},{4,1},{5,0},{6,3},{7,2},{8,13},{9,12},{10,... | collective-permute-start | bytes 393224 | tf_op jit(solution)/shard_map/ppermute | solution.py:111
  132.8 7.1 %collective-permute-start.15 = (bf16[2,8,32,128]{3,1,2,0:T(8,128)(2,1)S(1)}, bf16[2,8,32,128]{3,1,2,0:T(8,128)(2,1)S(1)}, u32[]{:S(2)}, u32[]{:S(2)}) collective-permute-start(bf16[2,8,32,128]{3,1,2,0:T(8,128)(2,1)S(1)} %bitcast.125), channel_id=1, source_target_pairs={{0,6},{1,7},{2,4},{3,5},{4,2},{5,3},{6,0},{7,1},{8,14},{9,15},{10,... | collective-permute-start | bytes 393224 | tf_op jit(solution)/shard_map/ppermute | solution.py:111
  137.3 5.4 %collective-permute-start.16 = (bf16[2,8,32,128]{3,1,2,0:T(8,128)(2,1)S(1)}, bf16[2,8,32,128]{3,1,2,0:T(8,128)(2,1)S(1)}, u32[]{:S(2)}, u32[]{:S(2)}) collective-permute-start(bf16[2,8,32,128]{3,1,2,0:T(8,128)(2,1)S(1)} %bitcast.124), channel_id=1, source_target_pairs={{0,7},{1,6},{2,5},{3,4},{4,3},{5,2},{6,1},{7,0},{8,15},{9,14},{10,... | collective-permute-start | bytes 393224 | tf_op jit(solution)/shard_map/ppermute | solution.py:111
  140.0 7.3 %collective-permute-start.20 = (bf16[2,8,32,128]{3,1,2,0:T(8,128)(2,1)S(1)}, bf16[2,8,32,128]{3,1,2,0:T(8,128)(2,1)S(1)}, u32[]{:S(2)}, u32[]{:S(2)}) collective-permute-start(bf16[2,8,32,128]{3,1,2,0:T(8,128)(2,1)S(1)} %bitcast.123), channel_id=1, source_target_pairs={{0,4},{1,5},{2,6},{3,7},{4,0},{5,1},{6,2},{7,3},{8,12},{9,13},{10,... | collective-permute-start | bytes 393224 | tf_op jit(solution)/shard_map/ppermute | solution.py:111
  142.7 11.9 %collective-permute-start.21 = (bf16[2,8,32,128]{3,1,2,0:T(8,128)(2,1)S(1)}, bf16[2,8,32,128]{3,1,2,0:T(8,128)(2,1)S(1)}, u32[]{:S(2)}, u32[]{:S(2)}) collective-permute-start(bf16[2,8,32,128]{3,1,2,0:T(8,128)(2,1)S(1)} %bitcast.122), channel_id=1, source_target_pairs={{0,5},{1,4},{2,7},{3,6},{4,1},{5,0},{6,3},{7,2},{8,13},{9,12},{10,... | collective-permute-start | bytes 393224 | tf_op jit(solution)/shard_map/ppermute | solution.py:111
  144.6 10.0 %collective-permute-start.22 = (bf16[2,8,32,128]{3,1,2,0:T(8,128)(2,1)S(1)}, bf16[2,8,32,128]{3,1,2,0:T(8,128)(2,1)S(1)}, u32[]{:S(2)}, u32[]{:S(2)}) collective-permute-start(bf16[2,8,32,128]{3,1,2,0:T(8,128)(2,1)S(1)} %bitcast.121), channel_id=1, source_target_pairs={{0,6},{1,7},{2,4},{3,5},{4,2},{5,3},{6,0},{7,1},{8,14},{9,15},{10,... | collective-permute-start | bytes 393224 | tf_op jit(solution)/shard_map/ppermute | solution.py:111
  146.5 8.2 %collective-permute-start.23 = (bf16[2,8,32,128]{3,1,2,0:T(8,128)(2,1)S(1)}, bf16[2,8,32,128]{3,1,2,0:T(8,128)(2,1)S(1)}, u32[]{:S(2)}, u32[]{:S(2)}) collective-permute-start(bf16[2,8,32,128]{3,1,2,0:T(8,128)(2,1)S(1)} %bitcast.120), channel_id=1, source_target_pairs={{0,7},{1,6},{2,5},{3,4},{4,3},{5,2},{6,1},{7,0},{8,15},{9,14},{10,... | collective-permute-start | bytes 393224 | tf_op jit(solution)/shard_map/ppermute | solution.py:111
  (9 other events, 57.0 us)
Sparse Core Ops, SparseCore 0:
  9.2 35.2 all-gather.4
  46.1 12.6 all-gather.6

commit v2 on v0

v2 whole, which is shorter than its diff:
```python
import functools

import jax
import jax.numpy as jnp
from jax import lax
from jax.experimental import pallas as pl
from jax.experimental.pallas import tpu as pltpu
from jax.sharding import PartitionSpec as P

slope = 0.3
PAIR = 2


def conv_kernel(first, stride, count, plan, tap_count, *refs):
    refs = list(refs)
    pieces = [refs.pop(0) for _ in plan]
    tap_parts = [refs.pop(0) for _ in range(tap_count)]
    bias_ref = refs.pop(0)
    outs = refs[:-4]
    vol, taps, vol_sem, taps_sem = refs[-4:]
    rows_in, total_in, cols = vol.shape[1:]
    total_out = taps.shape[3]
    rows = rows_in - 2
    copies = []
    start = 0
    for n, part in enumerate(tap_parts):
        size = part.shape[3]
        copies.append(pltpu.make_async_copy(part, taps.at[:, :, :, pl.ds(start, size), :], taps_sem.at[n]))
        start += size
    for n, (piece, (slot, plane_count)) in enumerate(zip(pieces, plan)):
        chan = piece.shape[3]
        for s in range(piece.shape[0]):
            copies.append(
                pltpu.make_async_copy(
                    piece.at[s], vol.at[pl.ds(slot, plane_count), :, pl.ds(s * chan, chan), :], vol_sem.at[n, s]
                )
            )
    for copy in copies:
        copy.start()
    for copy in copies:
        copy.wait()

    lane = lax.broadcasted_iota(jnp.int32, (total_out, cols), 1)
    per_plane = rows // PAIR
    block = total_out // len(outs)

    def tile(step, carry):
        slot = step // per_plane
        plane = first + slot * stride
        row = (step % per_plane) * PAIR
        total = jnp.zeros((3 * total_out, PAIR * cols), jnp.float32)
        for a in range(3):
            for b in range(3):
                piece = jnp.concatenate([vol[plane + a, row + b + r] for r in range(PAIR)], axis=1)
                total = total + jnp.dot(
                    taps[a, b].reshape(3 * total_out, -1), piece, preferred_element_type=jnp.float32
                )
        for r in range(PAIR):
            part = total[:, r * cols : (r + 1) * cols].reshape(3, total_out, cols)
            left = jnp.where(lane == 0, 0.0, pltpu.roll(part[0], 1, 1))
            right = jnp.where(lane == cols - 1, 0.0, pltpu.roll(part[2], cols - 1, 1))
            shifted = part[1] + left + right + bias_ref[...]
            done = jnp.where(shifted > 0, shifted, slope * shifted).astype(jnp.bfloat16)
            for n, out_ref in enumerate(outs):
                out_ref[slot, row + r] = done[n * block : (n + 1) * block]
        return carry

    lax.fori_loop(0, count * per_plane, tile, 0)


def convolve(first, stride, count, pieces, plan, tap_parts, bias, blocks):
    sources, _, rows_in, chan, cols = pieces[0].shape
    in_chan = tap_parts[0].shape[4]
    total_out = sum(part.shape[3] for part in tap_parts)
    rows = rows_in - 2
    depth = max(slot + n for slot, n in plan)
    wide_bias = jnp.broadcast_to(bias[:, None], (total_out, cols))
    macs = 27 * total_out * in_chan * count * rows * cols
    any_space = pl.BlockSpec(memory_space=pl.ANY)
    in_vmem = pl.BlockSpec(memory_space=pltpu.VMEM)
    return pl.pallas_call(
        functools.partial(conv_kernel, first, stride, count, plan, len(tap_parts)),
        out_shape=[jax.ShapeDtypeStruct((count, rows, total_out // blocks, cols), jnp.bfloat16)] * blocks,
        in_specs=[any_space] * (len(pieces) + len(tap_parts)) + [in_vmem],
        out_specs=[in_vmem] * blocks,
        scratch_shapes=[
            pltpu.VMEM((depth, rows_in, sources * chan, cols), jnp.bfloat16),
            pltpu.VMEM((3, 3, 3, total_out, in_chan), jnp.bfloat16),
            pltpu.SemaphoreType.DMA((len(pieces), sources)),
            pltpu.SemaphoreType.DMA((len(tap_parts),)),
        ],
        cost_estimate=pl.CostEstimate(flops=2 * macs, bytes_accessed=10_000_000, transcendentals=0),
        compiler_params=pltpu.CompilerParams(vmem_limit_bytes=32 * 2**20),
    )(*pieces, *tap_parts, wide_bias)


def body(features, kernel, bias_vector):
    planes, chan, y_cells, cols = features.shape
    out_chan = kernel.shape[3]
    parts = lax.axis_size("filt")
    slabs = lax.axis_size("slab")
    me = lax.axis_index("filt")
    rows = y_cells // parts
    aligned = chan % 16 == 0 and out_chan % 16 == 0
    across = list(range(0, parts, 2))

    def swap(array, k):
        if k == 0:
            return array
        return lax.ppermute(array, "filt", [(i, i ^ k) for i in range(parts)])

    same = [swap(kernel, k) for k in across]
    other = swap(jnp.concatenate(same, axis=0), 1)
    tap_parts = []
    for n, part in enumerate(same):
        tap_parts += [part, other[3 * n : 3 * n + 3]]
    if not aligned:
        tap_parts = [jnp.concatenate(tap_parts, axis=3)]
    order = jnp.stack([me ^ k ^ c for k in across for c in range(2)])
    bias = jnp.take(bias_vector.reshape(parts, out_chan), order, axis=0).reshape(-1)

    def gather_rows(piece):
        by_row = jnp.pad(piece.transpose(0, 2, 1, 3), ((0, 0), (1, 1), (0, 0), (0, 0)))
        blocks = jnp.stack([by_row[:, j * rows : (j + 1) * rows + 2] for j in range(parts)])
        got = lax.all_to_all(blocks, "filt", 0, 0)
        if not aligned:
            got = got.transpose(1, 2, 0, 3, 4).reshape(1, piece.shape[0], rows + 2, parts * chan, cols)
        return got

    def send_back(results):
        count = results[0].shape[0]
        got = [swap(result, k) for result, k in zip(results, across)]
        mine = [block[:, :, :out_chan] for block in got]
        theirs = swap(jnp.stack([block[:, :, out_chan:] for block in got]), 1)
        final = jnp.zeros((count, y_cells, out_chan, cols), jnp.bfloat16)
        for n, k in enumerate(across):
            final = lax.dynamic_update_slice_in_dim(final, mine[n], (me ^ k) * rows, 1)
            final = lax.dynamic_update_slice_in_dim(final, theirs[n], (me ^ k ^ 1) * rows, 1)
        return final.transpose(0, 2, 1, 3)

    up = [(i, i + 1) for i in range(slabs - 1)]
    down = [(i + 1, i) for i in range(slabs - 1)]
    outer = gather_rows(jnp.concatenate([features[:1], features[-1:]]))
    first, last = outer[:, :1], outer[:, 1:]
    after = lax.ppermute(first, "slab", down)
    before = lax.ppermute(last, "slab", up)
    inner = gather_rows(features[1:-1])

    conv = functools.partial(convolve, tap_parts=tap_parts, bias=bias, blocks=len(across))
    middle = conv(0, 1, planes - 2, [first, inner, last], ((0, 1), (1, planes - 2), (planes - 1, 1)))
    inside = send_back(middle)
    ends = conv(
        0, planes - 1, 2, [first, inner, last, before, after],
        ((1, 1), (2, planes - 2), (planes, 1), (0, 1), (planes + 1, 1)),
    )
    outside = send_back(ends)
    return jnp.concatenate([outside[:1], inside, outside[1:]])


def solution(mesh):
    placed = (P("slab", "filt", None, None), P(None, None, None, "filt", None), P())
    return jax.shard_map(
        body, mesh=mesh, in_specs=placed, out_specs=P("slab", "filt", None, None), check_vma=False
    )
```

time: 139 us -> 118 us (0.85)
  blocking collectives: 49.3 us -> 0 us
  local copies, waits for them, and re-layouts: 8.28 us -> 28.1 us
  starting transfers between devices: 9.28 us -> 25.2 us
  between operations: 13.7 us -> 0.49 us
  other arithmetic: 0 us -> 3.32 us
  waiting for transfers between devices: 36.8 us -> 38.2 us
    all_to_all x1 -> x0, blocking collectives: 49.3 us -> none  [body(): volume = lax.all_to_all(blocks, 'filt', 0, 0)]
    all_to_all x0 -> x2, waiting for transfers between devices: none -> 16.4 us  [gather_rows(): got = lax.all_to_all(blocks, 'filt', 0, 0)]
    ppermute x9 -> x14, waiting for transfers between devices: 36.1 us -> 21.8 us  [the longest x12 14.6 us: swap(): return lax.ppermute(array, 'filt', [(i, i ^ k) for i in range(parts)])]
    unnamed x12 -> x37, local copies, waits for them, and re-layouts: 4.57 us -> 17 us
    ppermute x9 -> x14, starting transfers between devices: 9.28 us -> 17.4 us  [the longest x12 11.8 us: swap(): return lax.ppermute(array, 'filt', [(i, i ^ k) for i in range(parts)])]
    all_to_all x0 -> x2, starting transfers between devices: none -> 7.83 us  [gather_rows(): got = lax.all_to_all(blocks, 'filt', 0, 0)]
    slice x0 -> x12, local copies, waits for them, and re-layouts: none -> 6.81 us  [the longest x1 2.63 us: body(): tap_parts += [part, other[3 * n:3 * n + 3]]]
    concatenate x0 -> x2, other arithmetic: none -> 2.99 us  [the longest x1 1.56 us: body(): return jnp.concatenate([outside[:1], inside, outside[1:]])]
  transfers between devices with their start and end apart: 10 -> 16, of which waited for: 5 -> 9; matrix products, arithmetic and copies ran while one was open for 5% -> 18% of each run, Pallas kernels for 0% -> 9%
where the time goes in v2:
time: 118 us; the launch traced here: 117 us
  waiting for transfers between devices  38.2 us (32%)
  local copies, waits for them, and re-layouts  28.1 us (24%)
  starting transfers between devices  25.2 us (21%)
  Pallas kernels  22 us (19%)
  other arithmetic  3.32 us (3%)
    pallas_call x2, Pallas kernels, convolve(): pl.pallas_call(functools.partial(conv_kernel, first, stride, count, plan,...  22 us
    unnamed x37, local copies, waits for them, and re-layouts  17 us
    all_to_all x2, waiting for transfers between devices, gather_rows(): got = lax.all_to_all(blocks, 'filt', 0, 0)  16.4 us
    ppermute x12, waiting for transfers between devices, swap(): return lax.ppermute(array, 'filt', [(i, i ^ k) for i in range(parts)])  14.6 us
    ppermute x12, starting transfers between devices, swap(): return lax.ppermute(array, 'filt', [(i, i ^ k) for i in range(parts)])  11.8 us
    all_to_all x2, starting transfers between devices, gather_rows(): got = lax.all_to_all(blocks, 'filt', 0, 0)  7.83 us
    ppermute x1, waiting for transfers between devices, body(): after = lax.ppermute(first, 'slab', down)  5.05 us
    ppermute x1, starting transfers between devices, body(): before = lax.ppermute(last, 'slab', up)  4.33 us
  transfers between devices with their start and end apart: 16, of which 9 were waited for; matrix products, arithmetic and copies ran while one was open for 18% of the time, Pallas kernels for 9%

profile of v2, /device:TPU:0, one launch (start us, length us, event | category | flops | bytes accessed | tf_op | source)
XLA Modules:
  0.0 117.4 jit_solution(11769902048650836301)
XLA Ops:
  0.0 2.9 %collective-permute-start.2 = (bf16[3,3,3,32,256]{4,3,2,1,0:T(8,128)(2,1)}, bf16[3,3,3,32,256]{4,3,2,1,0:T(8,128)(2,1)S(1)}, u32[]{:S(2)}, u32[]{:S(2)}) collective-permute-start(bf16[3,3,3,32,256]{4,3,2,1,0:T(8,128)(2,1)} %refs_3_.1), channel_id=1, source_target_pairs={{0,2},{1,3},{2,0},{3,1},{4,6},{5,7},{6,4},{7,5},{8,10},{9,11},{10,... | collective-permute-start | bytes 1327112 | tf_op jit(solution)/shard_map/ppermute | solution.py:110
  2.9 1.5 %collective-permute-start.3 = (bf16[3,3,3,32,256]{4,3,2,1,0:T(8,128)(2,1)}, bf16[3,3,3,32,256]{4,3,2,1,0:T(8,128)(2,1)S(1)}, u32[]{:S(2)}, u32[]{:S(2)}) collective-permute-start(bf16[3,3,3,32,256]{4,3,2,1,0:T(8,128)(2,1)} %refs_3_.1), channel_id=1, source_target_pairs={{0,4},{1,5},{2,6},{3,7},{4,0},{5,1},{6,2},{7,3},{8,12},{9,13},{10,... | collective-permute-start | bytes 1327112 | tf_op jit(solution)/shard_map/ppermute | solution.py:110
  4.5 1.3 %fusion.21 = (bf16[1,32,64,128]{3,2,1,0:T(8,128)(2,1)S(1)}, bf16[1,32,64,128]{3,2,1,0:T(8,128)(2,1)S(1)}) fusion(bf16[4,32,64,128]{3,2,1,0:T(8,128)(2,1)} %param.3), kind=kLoop, calls=%fused_computation.81 | loop fusion | bytes 2097152 | tf_op jit(solution)/shard_map/slice | solution.py:143
  12.0 4.3 %all-to-all-start = ((bf16[8,2,10,32,128]{4,3,2,1,0:T(8,128)(2,1)}), bf16[8,2,10,32,128]{4,3,2,1,0:T(8,128)(2,1)}, u32[]{:S(2)}, u32[]{:S(2)}) async-start(bf16[8,2,10,32,128]{4,3,2,1,0:T(8,128)(2,1)} %fusion.3), calls=%async_computation | async-start | bytes 2621440 | tf_op jit(solution)/shard_map/all_to_all | solution.py:125
  16.3 1.2 %slice-done = bf16[2,32,64,128]{3,2,1,0:T(8,128)(2,1)S(1)} async-done(((bf16[4,32,64,128]{3,2,1,0:T(8,128)(2,1)}), bf16[2,32,64,128]{3,2,1,0:T(8,128)(2,1)S(1)}, s32[]{:S(2)}) %slice-start) | async-done | bytes 1048600 | tf_op jit(solution)/shard_map/slice | solution.py:147
  21.0 3.8 %collective-permute-done.3.refs_9_.refs_7_ = bf16[3,3,3,32,256]{4,3,2,1,0:T(8,128)(2,1)S(1)} collective-permute-done((bf16[3,3,3,32,256]{4,3,2,1,0:T(8,128)(2,1)}, bf16[3,3,3,32,256]{4,3,2,1,0:T(8,128)(2,1)S(1)}, u32[]{:S(2)}, u32[]{:S(2)}) %collective-permute-start.3) | collective-permute-done | bytes 442400 | tf_op jit(solution)/shard_map/ppermute | solution.py:110
  25.2 1.4 %pad_maximum_fusion.1 = bf16[12,3,3,32,256]{4,3,2,1,0:T(8,128)(2,1)} fusion(bf16[3,3,3,32,256]{4,3,2,1,0:T(8,128)(2,1)S(1)} %collective-permute-done.4.refs_11_.refs_9_, bf16[3,3,3,32,256]{4,3,2,1,0:T(8,128)(2,1)S(1)} %collective-permute-done.3.refs_9_.refs_7_, bf16[3,3,3,32,256]{4,3,2,1,0:T(8,128)(2,1)S(1)} %collective-permute-done.2.refs_7_.refs_5_, ...), kind=kLoop, calls=%fused_computation.2 | loop fusion | flops 2654208 | bytes 3538944 | tf_op jit(solution)/shard_map/concatenate | solution.py:113
  29.4 9.0 %all-to-all-done = bf16[8,2,10,32,128]{4,3,2,1,0:T(8,128)(2,1)} async-done(((bf16[8,2,10,32,128]{4,3,2,1,0:T(8,128)(2,1)}), bf16[8,2,10,32,128]{4,3,2,1,0:T(8,128)(2,1)}, u32[]{:S(2)}, u32[]{:S(2)}) %all-to-all-start) | async-done | bytes 1310752 | tf_op jit(solution)/shard_map/all_to_all | solution.py:125
  38.4 3.6 %all-to-all-start.1 = ((bf16[8,2,10,32,128]{4,3,2,1,0:T(8,128)(2,1)}), bf16[8,2,10,32,128]{4,3,2,1,0:T(8,128)(2,1)S(1)}, u32[]{:S(2)}, u32[]{:S(2)}) async-start(bf16[8,2,10,32,128]{4,3,2,1,0:T(8,128)(2,1)} %fusion.7), calls=%async_computation.1 | async-start | bytes 2621440 | tf_op jit(solution)/shard_map/all_to_all | solution.py:125
  42.8 1.5 %fusion.23 = (bf16[8,1,10,32,128]{4,3,2,1,0:T(8,128)(2,1)S(1)}, bf16[8,1,10,32,128]{4,3,2,1,0:T(8,128)(2,1)S(1)}) fusion(bf16[8,2,10,32,128]{4,3,2,1,0:T(8,128)(2,1)} %all-to-all-done), kind=kLoop, calls=%fused_computation.83 | loop fusion | bytes 2621440 | tf_op jit(solution)/shard_map/slice | solution.py:144
  44.3 4.3 %collective-permute-start = (bf16[8,1,10,32,128]{4,3,2,1,0:T(8,128)(2,1)S(1)}, bf16[8,1,10,32,128]{4,3,2,1,0:T(8,128)(2,1)}, u32[]{:S(2)}, u32[]{:S(2)}) collective-permute-start(bf16[8,1,10,32,128]{4,3,2,1,0:T(8,128)(2,1)S(1)} %get-tuple-element.27.refs_2_), channel_id=1, source_target_pairs={{0,8},{8,16},{16,24},{1,9},{9,17},{17,25},{2,10},{10,18},{18,26},{... | collective-permute-start | bytes 1966088 | tf_op jit(solution)/shard_map/ppermute | solution.py:146
  48.7 1.3 %collective-permute-start.1 = (bf16[8,1,10,32,128]{4,3,2,1,0:T(8,128)(2,1)S(1)}, bf16[8,1,10,32,128]{4,3,2,1,0:T(8,128)(2,1)}, u32[]{:S(2)}, u32[]{:S(2)}) collective-permute-start(bf16[8,1,10,32,128]{4,3,2,1,0:T(8,128)(2,1)S(1)} %get-tuple-element.28.refs_0_), channel_id=1, source_target_pairs={{8,0},{16,8},{24,16},{9,1},{17,9},{25,17},{10,2},{18,10},{26,18},{... | collective-permute-start | bytes 1966088 | tf_op jit(solution)/shard_map/ppermute | solution.py:145
  50.1 2.6 %fusion.22 = (bf16[3,3,3,32,256]{4,3,2,1,0:T(8,128)(2,1)}, bf16[3,3,3,32,256]{4,3,2,1,0:T(8,128)(2,1)}, bf16[3,3,3,32,256]{4,3,2,1,0:T(8,128)(2,1)}, bf16[3,3,3,32,256]{4,3,2,1,0:T(8,128)(2,1)}) fusion(bf16[12,3,3,32,256]{4,3,2,1,0:T(8,128)(2,1)} %collective-permute-done.5), kind=kLoop, calls=%fused_computation.82 | loop fusion | bytes 3538944 | tf_op jit(solution)/shard_map/slice | solution.py:116
  52.7 7.4 %all-to-all-done.1.refs_1_ = bf16[8,2,10,32,128]{4,3,2,1,0:T(8,128)(2,1)S(1)} async-done(((bf16[8,2,10,32,128]{4,3,2,1,0:T(8,128)(2,1)}), bf16[8,2,10,32,128]{4,3,2,1,0:T(8,128)(2,1)S(1)}, u32[]{:S(2)}, u32[]{:S(2)}) %all-to-all-start.1) | async-done | bytes 1310752 | tf_op jit(solution)/shard_map/all_to_all | solution.py:125
  60.1 2.2 %collective-permute-done.refs_3_ = bf16[8,1,10,32,128]{4,3,2,1,0:T(8,128)(2,1)} collective-permute-done((bf16[8,1,10,32,128]{4,3,2,1,0:T(8,128)(2,1)S(1)}, bf16[8,1,10,32,128]{4,3,2,1,0:T(8,128)(2,1)}, u32[]{:S(2)}, u32[]{:S(2)}) %collective-permute-start) | collective-permute-done | bytes 655392 | tf_op jit(solution)/shard_map/ppermute | solution.py:146
  62.3 5.0 %collective-permute-done.1.refs_4_ = bf16[8,1,10,32,128]{4,3,2,1,0:T(8,128)(2,1)} collective-permute-done((bf16[8,1,10,32,128]{4,3,2,1,0:T(8,128)(2,1)S(1)}, bf16[8,1,10,32,128]{4,3,2,1,0:T(8,128)(2,1)}, u32[]{:S(2)}, u32[]{:S(2)}) %collective-permute-start.1) | collective-permute-done | bytes 655392 | tf_op jit(solution)/shard_map/ppermute | solution.py:145
  73.5 11.8 %shard_map.37 = (bf16[2,8,64,128]{3,2,1,0:T(8,128)(2,1)S(1)}, bf16[2,8,64,128]{3,2,1,0:T(8,128)(2,1)S(1)}, bf16[2,8,64,128]{3,2,1,0:T(8,128)(2,1)S(1)}, bf16[2,8,64,128]{3,2,1,0:T(8,128)(2,1)S(1)}) custom-call(bf16[8,1,10,32,128]{4,3,2,1,0:T(8,128)(2,1)S(1)} %get-tuple-element.28.refs_0_, bf16[8,2,10,32,128]{4,3,2,1,0:T(8,128)(2,1)S(1)} %all-to-all-done.1.refs_1_, ...), custom_call_target="tpu_custom_call" | custom-call | flops 7247757312 | bytes 10000000 | tf_op jit(solution)/shard_map/pallas_call | solution.py:81
  85.3 2.7 %collective-permute-start.8 = (bf16[2,8,64,128]{3,2,1,0:T(8,128)(2,1)S(1)}, bf16[2,8,64,128]{3,2,1,0:T(8,128)(2,1)S(1)}, u32[]{:S(2)}, u32[]{:S(2)}) collective-permute-start(bf16[2,8,64,128]{3,2,1,0:T(8,128)(2,1)S(1)} %get-tuple-element.16), channel_id=1, source_target_pairs={{0,6},{1,7},{2,4},{3,5},{4,2},{5,3},{6,0},{7,1},{8,14},{9,15},{10,... | collective-permute-start | bytes 786440 | tf_op jit(solution)/shard_map/ppermute | solution.py:110
  88.8 10.3 %shard_map.38 = (bf16[2,8,64,128]{3,2,1,0:T(8,128)(2,1)S(1)}, bf16[2,8,64,128]{3,2,1,0:T(8,128)(2,1)S(1)}, bf16[2,8,64,128]{3,2,1,0:T(8,128)(2,1)S(1)}, bf16[2,8,64,128]{3,2,1,0:T(8,128)(2,1)S(1)}) custom-call(bf16[8,1,10,32,128]{4,3,2,1,0:T(8,128)(2,1)S(1)} %get-tuple-element.28.refs_0_, bf16[8,2,10,32,128]{4,3,2,1,0:T(8,128)(2,1)S(1)} %all-to-all-done.1.refs_1_, ...), custom_call_target="tpu_custom_call" | custom-call | flops 7247757312 | bytes 10000000 | tf_op jit(solution)/shard_map/pallas_call | solution.py:81
  99.1 2.7 %collective-permute-start.12 = (bf16[2,8,64,128]{3,2,1,0:T(8,128)(2,1)S(1)}, bf16[2,8,64,128]{3,2,1,0:T(8,128)(2,1)S(1)}, u32[]{:S(2)}, u32[]{:S(2)}) collective-permute-start(bf16[2,8,64,128]{3,2,1,0:T(8,128)(2,1)S(1)} %get-tuple-element.20), channel_id=1, source_target_pairs={{0,6},{1,7},{2,4},{3,5},{4,2},{5,3},{6,0},{7,1},{8,14},{9,15},{10,... | collective-permute-start | bytes 786440 | tf_op jit(solution)/shard_map/ppermute | solution.py:110
  103.0 6.3 %collective-permute-done.12 = bf16[2,8,64,128]{3,2,1,0:T(8,128)(2,1)S(1)} collective-permute-done((bf16[2,8,64,128]{3,2,1,0:T(8,128)(2,1)S(1)}, bf16[2,8,64,128]{3,2,1,0:T(8,128)(2,1)S(1)}, u32[]{:S(2)}, u32[]{:S(2)}) %collective-permute-start.12) | collective-permute-done | bytes 262176 | tf_op jit(solution)/shard_map/ppermute | solution.py:110
  109.4 2.9 %collective-permute-done.11 = bf16[2,8,64,128]{3,2,1,0:T(8,128)(2,1)S(1)} collective-permute-done((bf16[2,8,64,128]{3,2,1,0:T(8,128)(2,1)S(1)}, bf16[2,8,64,128]{3,2,1,0:T(8,128)(2,1)S(1)}, u32[]{:S(2)}, u32[]{:S(2)}) %collective-permute-start.11) | collective-permute-done | bytes 262176 | tf_op jit(solution)/shard_map/ppermute | solution.py:110
  113.3 1.2 collective-permute-done.13
  115.8 1.6 %pad_maximum_fusion = bf16[4,32,64,128]{3,2,1,0:T(8,128)(2,1)} fusion(bf16[1,32,64,128]{3,2,1,0:T(8,128)(2,1)S(1)} %get-tuple-element.30, bf16[2,32,64,128]{3,2,1,0:T(8,128)(2,1)S(1)} %bitcast.130, bf16[1,32,64,128]{3,2,1,0:T(8,128)(2,1)S(1)} %get-tuple-element.29), kind=kLoop, calls=%fused_computation.1 | loop fusion | flops 2097152 | bytes 4194304 | tf_op jit(solution)/shard_map/concatenate | solution.py:157
  (97 shorter events, 24.2 us)
Async XLA Ops:
  0.0 21.0 %collective-permute-start.2 = (bf16[3,3,3,32,256]{4,3,2,1,0:T(8,128)(2,1)}, bf16[3,3,3,32,256]{4,3,2,1,0:T(8,128)(2,1)S(1)}, u32[]{:S(2)}, u32[]{:S(2)}) collective-permute-start(bf16[3,3,3,32,256]{4,3,2,1,0:T(8,128)(2,1)} %refs_3_.1), channel_id=1, source_target_pairs={{0,2},{1,3},{2,0},{3,1},{4,6},{5,7},{6,4},{7,5},{8,10},{9,11},{10,... | collective-permute-start | bytes 1327112 | tf_op jit(solution)/shard_map/ppermute | solution.py:110
  2.9 21.9 %collective-permute-start.3 = (bf16[3,3,3,32,256]{4,3,2,1,0:T(8,128)(2,1)}, bf16[3,3,3,32,256]{4,3,2,1,0:T(8,128)(2,1)S(1)}, u32[]{:S(2)}, u32[]{:S(2)}) collective-permute-start(bf16[3,3,3,32,256]{4,3,2,1,0:T(8,128)(2,1)} %refs_3_.1), channel_id=1, source_target_pairs={{0,4},{1,5},{2,6},{3,7},{4,0},{5,1},{6,2},{7,3},{8,12},{9,13},{10,... | collective-permute-start | bytes 1327112 | tf_op jit(solution)/shard_map/ppermute | solution.py:110
  4.5 20.7 %collective-permute-start.4 = (bf16[3,3,3,32,256]{4,3,2,1,0:T(8,128)(2,1)}, bf16[3,3,3,32,256]{4,3,2,1,0:T(8,128)(2,1)S(1)}, u32[]{:S(2)}, u32[]{:S(2)}) collective-permute-start(bf16[3,3,3,32,256]{4,3,2,1,0:T(8,128)(2,1)} %refs_3_.1), channel_id=1, source_target_pairs={{0,6},{1,7},{2,4},{3,5},{4,2},{5,3},{6,0},{7,1},{8,14},{9,15},{10,... | collective-permute-start | bytes 1327112 | tf_op jit(solution)/shard_map/ppermute | solution.py:110
  12.0 26.4 %all-to-all-start = ((bf16[8,2,10,32,128]{4,3,2,1,0:T(8,128)(2,1)}), bf16[8,2,10,32,128]{4,3,2,1,0:T(8,128)(2,1)}, u32[]{:S(2)}, u32[]{:S(2)}) async-start(bf16[8,2,10,32,128]{4,3,2,1,0:T(8,128)(2,1)} %fusion.3), calls=%async_computation | async-start | bytes 2621440 | tf_op jit(solution)/shard_map/all_to_all | solution.py:125
  16.2 1.2 %slice-start = ((bf16[4,32,64,128]{3,2,1,0:T(8,128)(2,1)}), bf16[2,32,64,128]{3,2,1,0:T(8,128)(2,1)S(1)}, s32[]{:S(2)}) async-start(bf16[4,32,64,128]{3,2,1,0:T(8,128)(2,1)} %param.3), calls=%async_computation.2 | async-start | bytes 2097152 | tf_op jit(solution)/shard_map/slice | solution.py:147
  18.2 7.0 %copy-start = (bf16[3,3,3,32,256]{4,3,2,1,0:T(8,128)(2,1)S(1)}, bf16[3,3,3,32,256]{4,3,2,1,0:T(8,128)(2,1)}, u32[]{:S(2)}) copy-start(bf16[3,3,3,32,256]{4,3,2,1,0:T(8,128)(2,1)} %refs_3_.1) | copy-start | bytes 1327108
  24.8 1.8 %copy-start.1 = (bf16[3,3,3,32,256]{4,3,2,1,0:T(8,128)(2,1)}, bf16[3,3,3,32,256]{4,3,2,1,0:T(8,128)(2,1)S(1)}, u32[]{:S(2)}) copy-start(bf16[3,3,3,32,256]{4,3,2,1,0:T(8,128)(2,1)S(1)} %collective-permute-done.3.refs_9_.refs_7_) | copy-start | bytes 1327108
  25.2 1.4 %copy-start.3 = (bf16[3,3,3,32,256]{4,3,2,1,0:T(8,128)(2,1)}, bf16[3,3,3,32,256]{4,3,2,1,0:T(8,128)(2,1)S(1)}, u32[]{:S(2)}) copy-start(bf16[3,3,3,32,256]{4,3,2,1,0:T(8,128)(2,1)S(1)} %collective-permute-done.4.refs_11_.refs_9_) | copy-start | bytes 1327108
  26.6 23.5 %collective-permute-start.5 = (bf16[12,3,3,32,256]{4,3,2,1,0:T(8,128)(2,1)}, bf16[12,3,3,32,256]{4,3,2,1,0:T(8,128)(2,1)}, u32[]{:S(2)}, u32[]{:S(2)}) collective-permute-start(bf16[12,3,3,32,256]{4,3,2,1,0:T(8,128)(2,1)} %pad_maximum_fusion.1), channel_id=1, source_target_pairs={{0,1},{1,0},{2,3},{3,2},{4,5},{5,4},{6,7},{7,6},{8,9},{9,8},{10,11... | collective-permute-start | bytes 5308424 | tf_op jit(solution)/shard_map/ppermute | solution.py:110
  29.4 12.7 %copy-start.9 = (f32[256]{0:T(256)S(1)}, f32[256]{0:T(256)}, u32[]{:S(2)}) copy-start(f32[256]{0:T(256)} %param.5) | copy-start | bytes 3076
  38.4 21.7 %all-to-all-start.1 = ((bf16[8,2,10,32,128]{4,3,2,1,0:T(8,128)(2,1)}), bf16[8,2,10,32,128]{4,3,2,1,0:T(8,128)(2,1)S(1)}, u32[]{:S(2)}, u32[]{:S(2)}) async-start(bf16[8,2,10,32,128]{4,3,2,1,0:T(8,128)(2,1)} %fusion.7), calls=%async_computation.1 | async-start | bytes 2621440 | tf_op jit(solution)/shard_map/all_to_all | solution.py:125
  44.3 18.0 %collective-permute-start = (bf16[8,1,10,32,128]{4,3,2,1,0:T(8,128)(2,1)S(1)}, bf16[8,1,10,32,128]{4,3,2,1,0:T(8,128)(2,1)}, u32[]{:S(2)}, u32[]{:S(2)}) collective-permute-start(bf16[8,1,10,32,128]{4,3,2,1,0:T(8,128)(2,1)S(1)} %get-tuple-element.27.refs_2_), channel_id=1, source_target_pairs={{0,8},{8,16},{16,24},{1,9},{9,17},{17,25},{2,10},{10,18},{18,26},{... | collective-permute-start | bytes 1966088 | tf_op jit(solution)/shard_map/ppermute | solution.py:146
  48.7 18.7 %collective-permute-start.1 = (bf16[8,1,10,32,128]{4,3,2,1,0:T(8,128)(2,1)S(1)}, bf16[8,1,10,32,128]{4,3,2,1,0:T(8,128)(2,1)}, u32[]{:S(2)}, u32[]{:S(2)}) collective-permute-start(bf16[8,1,10,32,128]{4,3,2,1,0:T(8,128)(2,1)S(1)} %get-tuple-element.28.refs_0_), channel_id=1, source_target_pairs={{8,0},{16,8},{24,16},{9,1},{17,9},{25,17},{10,2},{18,10},{26,18},{... | collective-permute-start | bytes 1966088 | tf_op jit(solution)/shard_map/ppermute | solution.py:145
  67.4 1.0 copy-start.2
  68.5 1.0 copy-start.4
  69.5 1.0 copy-start.5
  85.3 17.1 %collective-permute-start.8 = (bf16[2,8,64,128]{3,2,1,0:T(8,128)(2,1)S(1)}, bf16[2,8,64,128]{3,2,1,0:T(8,128)(2,1)S(1)}, u32[]{:S(2)}, u32[]{:S(2)}) collective-permute-start(bf16[2,8,64,128]{3,2,1,0:T(8,128)(2,1)S(1)} %get-tuple-element.16), channel_id=1, source_target_pairs={{0,6},{1,7},{2,4},{3,5},{4,2},{5,3},{6,0},{7,1},{8,14},{9,15},{10,... | collective-permute-start | bytes 786440 | tf_op jit(solution)/shard_map/ppermute | solution.py:110
  87.9 14.9 %collective-permute-start.7 = (bf16[2,8,64,128]{3,2,1,0:T(8,128)(2,1)S(1)}, bf16[2,8,64,128]{3,2,1,0:T(8,128)(2,1)S(1)}, u32[]{:S(2)}, u32[]{:S(2)}) collective-permute-start(bf16[2,8,64,128]{3,2,1,0:T(8,128)(2,1)S(1)} %get-tuple-element.15), channel_id=1, source_target_pairs={{0,4},{1,5},{2,6},{3,7},{4,0},{5,1},{6,2},{7,3},{8,12},{9,13},{10,... | collective-permute-start | bytes 786440 | tf_op jit(solution)/shard_map/ppermute | solution.py:110
  88.5 14.4 %collective-permute-start.6 = (bf16[2,8,64,128]{3,2,1,0:T(8,128)(2,1)S(1)}, bf16[2,8,64,128]{3,2,1,0:T(8,128)(2,1)S(1)}, u32[]{:S(2)}, u32[]{:S(2)}) collective-permute-start(bf16[2,8,64,128]{3,2,1,0:T(8,128)(2,1)S(1)} %get-tuple-element.14), channel_id=1, source_target_pairs={{0,2},{1,3},{2,0},{3,1},{4,6},{5,7},{6,4},{7,5},{8,10},{9,11},{10,... | collective-permute-start | bytes 786440 | tf_op jit(solution)/shard_map/ppermute | solution.py:110
  99.1 10.2 %collective-permute-start.12 = (bf16[2,8,64,128]{3,2,1,0:T(8,128)(2,1)S(1)}, bf16[2,8,64,128]{3,2,1,0:T(8,128)(2,1)S(1)}, u32[]{:S(2)}, u32[]{:S(2)}) collective-permute-start(bf16[2,8,64,128]{3,2,1,0:T(8,128)(2,1)S(1)} %get-tuple-element.20), channel_id=1, source_target_pairs={{0,6},{1,7},{2,4},{3,5},{4,2},{5,3},{6,0},{7,1},{8,14},{9,15},{10,... | collective-permute-start | bytes 786440 | tf_op jit(solution)/shard_map/ppermute | solution.py:110
  101.8 10.5 %collective-permute-start.11 = (bf16[2,8,64,128]{3,2,1,0:T(8,128)(2,1)S(1)}, bf16[2,8,64,128]{3,2,1,0:T(8,128)(2,1)S(1)}, u32[]{:S(2)}, u32[]{:S(2)}) collective-permute-start(bf16[2,8,64,128]{3,2,1,0:T(8,128)(2,1)S(1)} %get-tuple-element.19), channel_id=1, source_target_pairs={{0,4},{1,5},{2,6},{3,7},{4,0},{5,1},{6,2},{7,3},{8,12},{9,13},{10,... | collective-permute-start | bytes 786440 | tf_op jit(solution)/shard_map/ppermute | solution.py:110
  102.4 10.0 %collective-permute-start.10 = (bf16[2,8,64,128]{3,2,1,0:T(8,128)(2,1)S(1)}, bf16[2,8,64,128]{3,2,1,0:T(8,128)(2,1)S(1)}, u32[]{:S(2)}, u32[]{:S(2)}) collective-permute-start(bf16[2,8,64,128]{3,2,1,0:T(8,128)(2,1)S(1)} %get-tuple-element.18), channel_id=1, source_target_pairs={{0,2},{1,3},{2,0},{3,1},{4,6},{5,7},{6,4},{7,5},{8,10},{9,11},{10,... | collective-permute-start | bytes 786440 | tf_op jit(solution)/shard_map/ppermute | solution.py:110
  103.0 10.3 %collective-permute-start.9 = (bf16[4,2,8,32,128]{4,3,2,1,0:T(8,128)(2,1)S(1)}, bf16[4,2,8,32,128]{4,3,2,1,0:T(8,128)(2,1)S(1)}, u32[]{:S(2)}, u32[]{:S(2)}) collective-permute-start(bf16[4,2,8,32,128]{4,3,2,1,0:T(8,128)(2,1)S(1)} %pad_maximum_fusion.2), channel_id=1, source_target_pairs={{0,1},{1,0},{2,3},{3,2},{4,5},{5,4},{6,7},{7,6},{8,9},{9,8},{10,11... | collective-permute-start | bytes 1572872 | tf_op jit(solution)/shard_map/ppermute | solution.py:110
  112.5 2.0 %collective-permute-start.13 = (bf16[4,2,8,32,128]{4,3,2,1,0:T(8,128)(2,1)S(1)}, bf16[4,2,8,32,128]{4,3,2,1,0:T(8,128)(2,1)S(1)}, u32[]{:S(2)}, u32[]{:S(2)}) collective-permute-start(bf16[4,2,8,32,128]{4,3,2,1,0:T(8,128)(2,1)S(1)} %pad_maximum_fusion.3), channel_id=1, source_target_pairs={{0,1},{1,0},{2,3},{3,2},{4,5},{5,4},{6,7},{7,6},{8,9},{9,8},{10,11... | collective-permute-start | bytes 1572872 | tf_op jit(solution)/shard_map/ppermute | solution.py:110
  (3 other events, 3.0 us)

commit v3 on v2

--- a/solution.py
+++ b/solution.py
@@ -11,9 +11,9 @@
 PAIR = 2
 
 
-def conv_kernel(first, stride, count, plan, tap_count, *refs):
+def conv_kernel(first, stride, count, plan, piece_count, tap_count, *refs):
     refs = list(refs)
-    pieces = [refs.pop(0) for _ in plan]
+    pieces = [refs.pop(0) for _ in range(piece_count)]
     tap_parts = [refs.pop(0) for _ in range(tap_count)]
     bias_ref = refs.pop(0)
     outs = refs[:-4]
@@ -22,17 +22,20 @@
     total_out = taps.shape[3]
     rows = rows_in - 2
     copies = []
-    start = 0
     for n, part in enumerate(tap_parts):
-        size = part.shape[3]
-        copies.append(pltpu.make_async_copy(part, taps.at[:, :, :, pl.ds(start, size), :], taps_sem.at[n]))
-        start += size
-    for n, (piece, (slot, plane_count)) in enumerate(zip(pieces, plan)):
+        groups, size = part.shape[0], part.shape[4]
+        for g in range(groups):
+            where = pl.ds((g * tap_count + n) * size, size)
+            copies.append(pltpu.make_async_copy(part.at[g], taps.at[:, :, :, where, :], taps_sem.at[n, g]))
+    for n, (source, begin, slot, plane_count) in enumerate(plan):
+        piece = pieces[source]
         chan = piece.shape[3]
         for s in range(piece.shape[0]):
             copies.append(
                 pltpu.make_async_copy(
-                    piece.at[s], vol.at[pl.ds(slot, plane_count), :, pl.ds(s * chan, chan), :], vol_sem.at[n, s]
+                    piece.at[s, pl.ds(begin, plane_count)],
+                    vol.at[pl.ds(slot, plane_count), :, pl.ds(s * chan, chan), :],
+                    vol_sem.at[n, s],
                 )
             )
     for copy in copies:
@@ -70,27 +73,27 @@
 
 def convolve(first, stride, count, pieces, plan, tap_parts, bias, blocks):
     sources, _, rows_in, chan, cols = pieces[0].shape
-    in_chan = tap_parts[0].shape[4]
-    total_out = sum(part.shape[3] for part in tap_parts)
+    groups, in_chan = tap_parts[0].shape[0], tap_parts[0].shape[5]
+    total_out = bias.shape[0]
     rows = rows_in - 2
-    depth = max(slot + n for slot, n in plan)
+    depth = max(slot + n for _, _, slot, n in plan)
     wide_bias = jnp.broadcast_to(bias[:, None], (total_out, cols))
     macs = 27 * total_out * in_chan * count * rows * cols
     any_space = pl.BlockSpec(memory_space=pl.ANY)
     in_vmem = pl.BlockSpec(memory_space=pltpu.VMEM)
     return pl.pallas_call(
-        functools.partial(conv_kernel, first, stride, count, plan, len(tap_parts)),
+        functools.partial(conv_kernel, first, stride, count, plan, len(pieces), len(tap_parts)),
         out_shape=[jax.ShapeDtypeStruct((count, rows, total_out // blocks, cols), jnp.bfloat16)] * blocks,
         in_specs=[any_space] * (len(pieces) + len(tap_parts)) + [in_vmem],
         out_specs=[in_vmem] * blocks,
         scratch_shapes=[
             pltpu.VMEM((depth, rows_in, sources * chan, cols), jnp.bfloat16),
             pltpu.VMEM((3, 3, 3, total_out, in_chan), jnp.bfloat16),
-            pltpu.SemaphoreType.DMA((len(pieces), sources)),
-            pltpu.SemaphoreType.DMA((len(tap_parts),)),
+            pltpu.SemaphoreType.DMA((len(plan), sources)),
+            pltpu.SemaphoreType.DMA((len(tap_parts), groups)),
         ],
         cost_estimate=pl.CostEstimate(flops=2 * macs, bytes_accessed=10_000_000, transcendentals=0),
-        compiler_params=pltpu.CompilerParams(vmem_limit_bytes=32 * 2**20),
+        compiler_params=pltpu.CompilerParams(vmem_limit_bytes=16 * 2**20),
     )(*pieces, *tap_parts, wide_bias)
 
 
@@ -104,27 +107,35 @@
     aligned = chan % 16 == 0 and out_chan % 16 == 0
     across = list(range(0, parts, 2))
 
-    def swap(array, k):
+    def swap(array, k, axis="filt"):
         if k == 0:
             return array
-        return lax.ppermute(array, "filt", [(i, i ^ k) for i in range(parts)])
+        return lax.ppermute(array, axis, [(i, i ^ k) for i in range(lax.axis_size(axis))])
 
-    same = [swap(kernel, k) for k in across]
-    other = swap(jnp.concatenate(same, axis=0), 1)
-    tap_parts = []
-    for n, part in enumerate(same):
-        tap_parts += [part, other[3 * n : 3 * n + 3]]
+    half = out_chan // 2
+    odd = lax.axis_index("slab") % 2
+    mine = lax.dynamic_slice_in_dim(kernel, odd * half, half, 3)
+    mine = jnp.stack([swap(mine, k) for k in across[1:]])
+    theirs = swap(mine, 1, "slab")
+    rest = jnp.concatenate([jnp.where(odd == 0, mine, theirs), jnp.where(odd == 0, theirs, mine)], axis=4)
+    same = jnp.concatenate([kernel[None], rest])
+    other = swap(same, 1)
+    tap_parts = [same, other]
     if not aligned:
-        tap_parts = [jnp.concatenate(tap_parts, axis=3)]
+        joined = jnp.stack(tap_parts, axis=1).transpose(2, 3, 4, 0, 1, 5, 6)
+        tap_parts = [joined.reshape(1, 3, 3, 3, parts * out_chan, -1)]
     order = jnp.stack([me ^ k ^ c for k in across for c in range(2)])
     bias = jnp.take(bias_vector.reshape(parts, out_chan), order, axis=0).reshape(-1)
 
     def gather_rows(piece):
-        by_row = jnp.pad(piece.transpose(0, 2, 1, 3), ((0, 0), (1, 1), (0, 0), (0, 0)))
-        blocks = jnp.stack([by_row[:, j * rows : (j + 1) * rows + 2] for j in range(parts)])
-        got = lax.all_to_all(blocks, "filt", 0, 0)
+        count = piece.shape[0]
+        by_row = piece.transpose(0, 2, 1, 3).reshape(count, parts, rows, chan, cols).transpose(1, 0, 2, 3, 4)
+        nothing = jnp.zeros((1, count, 1, chan, cols), piece.dtype)
+        above = jnp.concatenate([nothing, by_row[:-1, :, -1:]])
+        below = jnp.concatenate([by_row[1:, :, :1], nothing])
+        got = lax.all_to_all(jnp.concatenate([above, by_row, below], axis=2), "filt", 0, 0)
         if not aligned:
-            got = got.transpose(1, 2, 0, 3, 4).reshape(1, piece.shape[0], rows + 2, parts * chan, cols)
+            got = got.transpose(1, 2, 0, 3, 4).reshape(1, count, rows + 2, parts * chan, cols)
         return got
 
     def send_back(results):
@@ -141,17 +152,17 @@
     up = [(i, i + 1) for i in range(slabs - 1)]
     down = [(i + 1, i) for i in range(slabs - 1)]
     outer = gather_rows(jnp.concatenate([features[:1], features[-1:]]))
-    first, last = outer[:, :1], outer[:, 1:]
-    after = lax.ppermute(first, "slab", down)
-    before = lax.ppermute(last, "slab", up)
     inner = gather_rows(features[1:-1])
 
+    after = lax.ppermute(outer[:, :1], "slab", down)
+    before = lax.ppermute(outer[:, 1:], "slab", up)
+
     conv = functools.partial(convolve, tap_parts=tap_parts, bias=bias, blocks=len(across))
-    middle = conv(0, 1, planes - 2, [first, inner, last], ((0, 1), (1, planes - 2), (planes - 1, 1)))
+    middle = conv(0, 1, planes - 2, [outer, inner], ((0, 0, 0, 1), (1, 0, 1, planes - 2), (0, 1, planes - 1, 1)))
     inside = send_back(middle)
     ends = conv(
-        0, planes - 1, 2, [first, inner, last, before, after],
-        ((1, 1), (2, planes - 2), (planes, 1), (0, 1), (planes + 1, 1)),
+        0, planes - 1, 2, [outer, inner, before, after],
+        ((0, 0, 1, 1), (1, 0, 2, planes - 2), (0, 1, planes, 1), (2, 0, 0, 1), (3, 0, planes + 1, 1)),
     )
     outside = send_back(ends)
     return jnp.concatenate([outside[:1], inside, outside[1:]])

time: 118 us -> 117 us (level)
  local copies, waits for them, and re-layouts: 28.1 us -> 9.46 us
  waiting for transfers between devices: 38.2 us -> 50.7 us
  other arithmetic: 3.32 us -> 5.96 us
  Pallas kernels: 22 us -> 23.7 us
    unnamed x37 -> x8, local copies, waits for them, and re-layouts: 17 us -> 1.97 us
    ppermute x14 -> x15, waiting for transfers between devices: 21.8 us -> 33 us  [the longest x13 27.6 us: swap(): lax.ppermute(array, axis, [(i, i ^ k) for i in range(lax.axis_size(axis))])]
    slice x4 -> x3, local copies, waits for them, and re-layouts: 5.37 us -> 1.35 us  [the longest x1 1.31 us: body(): after = lax.ppermute(outer[:, :1], 'slab', down)]
    pallas_call x2, Pallas kernels: 22 us -> 23.7 us  [convolve(): pl.pallas_call(functools.partial(conv_kernel, first, stride, count, plan,...]
    concatenate x1 -> x4, other arithmetic: 1.43 us -> 2.89 us  [the longest x2 2.58 us: gather_rows(): jnp.concatenate([above, by_row, below], axis=2)]
    another operation x4 -> x2, local copies, waits for them, and re-layouts: 1.85 us -> 0.49 us  [the longest x2 1.36 us: gather_rows(): jnp.stack([by_row[:, j * rows:(j + 1) * rows + 2] for j in range(parts)])]
    all_to_all x2, waiting for transfers between devices: 16.4 us -> 17.7 us  [gather_rows(): lax.all_to_all(jnp.concatenate([above, by_row, below], axis=2), 'filt', 0...]
    select_n x0 -> x1, other arithmetic: none -> 1.2 us  [body(): jnp.where(odd == 0, mine, theirs)]
  transfers between devices with their start and end apart: 16 -> 17, of which waited for: 9 -> 10; matrix products, arithmetic and copies ran while one was open for 18% -> 9% of each run, Pallas kernels for 9% -> 10%
where the time goes in v3:
time: 117 us; the launch traced here: 116 us
  waiting for transfers between devices  50.7 us (43%)
  starting transfers between devices  26 us (22%)
  Pallas kernels  23.7 us (20%)
  local copies, waits for them, and re-layouts  9.46 us (8%)
  other arithmetic  5.96 us (5%)
    ppermute x13, waiting for transfers between devices, swap(): lax.ppermute(array, axis, [(i, i ^ k) for i in range(lax.axis_size(axis))])  27.6 us
    pallas_call x2, Pallas kernels, convolve(): pl.pallas_call(functools.partial(conv_kernel, first, stride, count, plan,...  23.7 us
    all_to_all x2, waiting for transfers between devices, gather_rows(): lax.all_to_all(jnp.concatenate([above, by_row, below], axis=2), 'filt', 0...  17.7 us
    ppermute x13, starting transfers between devices, swap(): lax.ppermute(array, axis, [(i, i ^ k) for i in range(lax.axis_size(axis))])  13.6 us
    all_to_all x2, starting transfers between devices, gather_rows(): lax.all_to_all(jnp.concatenate([above, by_row, below], axis=2), 'filt', 0...  7.98 us
    ppermute x1, waiting for transfers between devices, body(): after = lax.ppermute(outer[:, :1], 'slab', down)  5.09 us
    ppermute x1, starting transfers between devices, body(): before = lax.ppermute(outer[:, 1:], 'slab', up)  3.22 us
    concatenate x2, other arithmetic, gather_rows(): jnp.concatenate([above, by_row, below], axis=2)  2.58 us
  transfers between devices with their start and end apart: 17, of which 10 were waited for; matrix products, arithmetic and copies ran while one was open for 9% of the time, Pallas kernels for 10%

profile of v3, /device:TPU:0, one launch (start us, length us, event | category | flops | bytes accessed | tf_op | source)
XLA Modules:
  0.0 116.4 jit_solution(15360409866621123441)
XLA Ops:
  1.0 3.0 %collective-permute-start.2 = (bf16[3,3,3,16,256]{4,3,2,1,0:T(8,128)(2,1)S(1)}, bf16[3,3,3,16,256]{4,3,2,1,0:T(8,128)(2,1)S(1)}, u32[]{:S(2)}, u32[]{:S(2)}) collective-permute-start(bf16[3,3,3,16,256]{4,3,2,1,0:T(8,128)(2,1)S(1)} %constant_dynamic-slice_fusion), channel_id=1, source_target_pairs={{0,2},{1,3},{2,0},{3,1},{4,6},{5,7},{6,4},{7,5},{8,10},{9,11},{10,... | collective-permute-start | bytes 663560 | tf_op jit(solution)/shard_map/ppermute | solution.py:113
  4.0 1.5 %collective-permute-start.3 = (bf16[3,3,3,16,256]{4,3,2,1,0:T(8,128)(2,1)S(1)}, bf16[3,3,3,16,256]{4,3,2,1,0:T(8,128)(2,1)S(1)}, u32[]{:S(2)}, u32[]{:S(2)}) collective-permute-start(bf16[3,3,3,16,256]{4,3,2,1,0:T(8,128)(2,1)S(1)} %constant_dynamic-slice_fusion), channel_id=1, source_target_pairs={{0,4},{1,5},{2,6},{3,7},{4,0},{5,1},{6,2},{7,3},{8,12},{9,13},{10,... | collective-permute-start | bytes 663560 | tf_op jit(solution)/shard_map/ppermute | solution.py:113
  5.5 4.7 %collective-permute-done.2 = bf16[3,3,3,16,256]{4,3,2,1,0:T(8,128)(2,1)S(1)} collective-permute-done((bf16[3,3,3,16,256]{4,3,2,1,0:T(8,128)(2,1)S(1)}, bf16[3,3,3,16,256]{4,3,2,1,0:T(8,128)(2,1)S(1)}, u32[]{:S(2)}, u32[]{:S(2)}) %collective-permute-start.2) | collective-permute-done | bytes 221216 | tf_op jit(solution)/shard_map/ppermute | solution.py:113
  10.2 5.4 %collective-permute-done.3 = bf16[3,3,3,16,256]{4,3,2,1,0:T(8,128)(2,1)S(1)} collective-permute-done((bf16[3,3,3,16,256]{4,3,2,1,0:T(8,128)(2,1)S(1)}, bf16[3,3,3,16,256]{4,3,2,1,0:T(8,128)(2,1)S(1)}, u32[]{:S(2)}, u32[]{:S(2)}) %collective-permute-start.3) | collective-permute-done | bytes 221216 | tf_op jit(solution)/shard_map/ppermute | solution.py:113
  15.7 1.6 %collective-permute-start.5 = (bf16[3,3,3,3,16,256]{5,4,3,2,1,0:T(8,128)(2,1)S(1)}, bf16[3,3,3,3,16,256]{5,4,3,2,1,0:T(8,128)(2,1)}, u32[]{:S(2)}, u32[]{:S(2)}) collective-permute-start(bf16[3,3,3,3,16,256]{5,4,3,2,1,0:T(8,128)(2,1)S(1)} %pad_maximum_fusion.2), channel_id=1, source_target_pairs={{0,8},{8,0},{16,24},{24,16},{1,9},{9,1},{17,25},{25,17},{2,10},{10... | collective-permute-start | bytes 1990664 | tf_op jit(solution)/shard_map/ppermute | solution.py:113
  19.5 1.3 %fusion.5 = bf16[8,2,10,32,128]{4,3,2,1,0:T(8,128)(2,1)} fusion(bf16[7,2,1,32,128]{4,3,2,1,0:T(8,128)(2,1)S(1)} %get-tuple-element.32, bf16[7,2,1,32,128]{4,3,2,1,0:T(8,128)(2,1)S(1)} %get-tuple-element.31, bf16[8,2,8,32,128]{4,3,2,1,0:T(8,128)(2,1)S(1)} %bitcast.71), kind=kLoop, calls=%fused_computation.10 | loop fusion | flops 6553600 | bytes 2588672 | tf_op jit(solution)/shard_map/concatenate | solution.py:136
  20.8 3.7 %all-to-all-start = ((bf16[8,2,10,32,128]{4,3,2,1,0:T(8,128)(2,1)}), bf16[8,2,10,32,128]{4,3,2,1,0:T(8,128)(2,1)S(1)}, u32[]{:S(2)}, u32[]{:S(2)}) async-start(bf16[8,2,10,32,128]{4,3,2,1,0:T(8,128)(2,1)} %fusion.5), calls=%async_computation | async-start | bytes 2621440 | tf_op jit(solution)/shard_map/all_to_all | solution.py:136
  24.5 6.9 %collective-permute-done.5 = bf16[3,3,3,3,16,256]{5,4,3,2,1,0:T(8,128)(2,1)} collective-permute-done((bf16[3,3,3,3,16,256]{5,4,3,2,1,0:T(8,128)(2,1)S(1)}, bf16[3,3,3,3,16,256]{5,4,3,2,1,0:T(8,128)(2,1)}, u32[]{:S(2)}, u32[]{:S(2)}) %collective-permute-start.5) | collective-permute-done | bytes 663584 | tf_op jit(solution)/shard_map/ppermute | solution.py:113
  32.9 1.3 %copy-done = bf16[4,32,64,128]{3,2,1,0:T(8,128)(2,1)S(1)} copy-done((bf16[4,32,64,128]{3,2,1,0:T(8,128)(2,1)S(1)}, bf16[4,32,64,128]{3,2,1,0:T(8,128)(2,1)}, u32[]{:S(2)}) %copy-start) | copy-done | bytes 2097176
  35.0 1.3 %fusion.7 = bf16[8,2,10,32,128]{4,3,2,1,0:T(8,128)(2,1)} fusion(bf16[7,2,1,32,128]{4,3,2,1,0:T(8,128)(2,1)S(1)} %get-tuple-element.30, bf16[7,2,1,32,128]{4,3,2,1,0:T(8,128)(2,1)S(1)} %get-tuple-element.29, bf16[8,2,8,32,128]{4,3,2,1,0:T(8,128)(2,1)S(1)} %bitcast.73), kind=kLoop, calls=%fused_computation.12 | loop fusion | flops 6553600 | bytes 2588672 | tf_op jit(solution)/shard_map/concatenate | solution.py:136
  36.3 6.4 %all-to-all-done.refs_0_ = bf16[8,2,10,32,128]{4,3,2,1,0:T(8,128)(2,1)S(1)} async-done(((bf16[8,2,10,32,128]{4,3,2,1,0:T(8,128)(2,1)}), bf16[8,2,10,32,128]{4,3,2,1,0:T(8,128)(2,1)S(1)}, u32[]{:S(2)}, u32[]{:S(2)}) %all-to-all-start) | async-done | bytes 1310752 | tf_op jit(solution)/shard_map/all_to_all | solution.py:136
  42.6 4.3 %all-to-all-start.1 = ((bf16[8,2,10,32,128]{4,3,2,1,0:T(8,128)(2,1)}), bf16[8,2,10,32,128]{4,3,2,1,0:T(8,128)(2,1)}, u32[]{:S(2)}, u32[]{:S(2)}) async-start(bf16[8,2,10,32,128]{4,3,2,1,0:T(8,128)(2,1)} %fusion.7), calls=%async_computation.1 | async-start | bytes 2621440 | tf_op jit(solution)/shard_map/all_to_all | solution.py:136
  47.0 1.3 %fusion.10 = (bf16[8,1,10,32,128]{4,3,2,1,0:T(8,128)(2,1)}, bf16[8,1,10,32,128]{4,3,2,1,0:T(8,128)(2,1)}) fusion(bf16[8,2,10,32,128]{4,3,2,1,0:T(8,128)(2,1)S(1)} %all-to-all-done.refs_0_), kind=kLoop, calls=%fused_computation.62 | loop fusion | bytes 2621440 | tf_op jit(solution)/shard_map/slice | solution.py:157
  48.4 3.2 %collective-permute-start = (bf16[8,1,10,32,128]{4,3,2,1,0:T(8,128)(2,1)}, bf16[8,1,10,32,128]{4,3,2,1,0:T(8,128)(2,1)}, u32[]{:S(2)}, u32[]{:S(2)}) collective-permute-start(bf16[8,1,10,32,128]{4,3,2,1,0:T(8,128)(2,1)} %get-tuple-element.26), channel_id=1, source_target_pairs={{0,8},{8,16},{16,24},{1,9},{9,17},{17,25},{2,10},{10,18},{18,26},{... | collective-permute-start | bytes 1966088 | tf_op jit(solution)/shard_map/ppermute | solution.py:158
  51.6 1.3 %collective-permute-start.1 = (bf16[8,1,10,32,128]{4,3,2,1,0:T(8,128)(2,1)}, bf16[8,1,10,32,128]{4,3,2,1,0:T(8,128)(2,1)}, u32[]{:S(2)}, u32[]{:S(2)}) collective-permute-start(bf16[8,1,10,32,128]{4,3,2,1,0:T(8,128)(2,1)} %get-tuple-element.25), channel_id=1, source_target_pairs={{8,0},{16,8},{24,16},{9,1},{17,9},{25,17},{10,2},{18,10},{26,18},{... | collective-permute-start | bytes 1966088 | tf_op jit(solution)/shard_map/ppermute | solution.py:157
  53.8 11.3 %all-to-all-done.1.refs_1_ = bf16[8,2,10,32,128]{4,3,2,1,0:T(8,128)(2,1)} async-done(((bf16[8,2,10,32,128]{4,3,2,1,0:T(8,128)(2,1)}), bf16[8,2,10,32,128]{4,3,2,1,0:T(8,128)(2,1)}, u32[]{:S(2)}, u32[]{:S(2)}) %all-to-all-start.1) | async-done | bytes 1310752 | tf_op jit(solution)/shard_map/all_to_all | solution.py:136
  65.5 5.1 %collective-permute-done.1.refs_3_ = bf16[8,1,10,32,128]{4,3,2,1,0:T(8,128)(2,1)} collective-permute-done((bf16[8,1,10,32,128]{4,3,2,1,0:T(8,128)(2,1)}, bf16[8,1,10,32,128]{4,3,2,1,0:T(8,128)(2,1)}, u32[]{:S(2)}, u32[]{:S(2)}) %collective-permute-start.1) | collective-permute-done | bytes 655392 | tf_op jit(solution)/shard_map/ppermute | solution.py:157
  70.7 12.1 %shard_map.37 = (bf16[2,8,64,128]{3,2,1,0:T(8,128)(2,1)S(1)}, bf16[2,8,64,128]{3,2,1,0:T(8,128)(2,1)S(1)}, bf16[2,8,64,128]{3,2,1,0:T(8,128)(2,1)S(1)}, bf16[2,8,64,128]{3,2,1,0:T(8,128)(2,1)S(1)}) custom-call(bf16[8,2,10,32,128]{4,3,2,1,0:T(8,128)(2,1)S(1)} %all-to-all-done.refs_0_, bf16[8,2,10,32,128]{4,3,2,1,0:T(8,128)(2,1)} %all-to-all-done.1.refs_1_, ...), custom_call_target="tpu_custom_call" | custom-call | flops 7247757312 | bytes 10000000 | tf_op jit(solution)/shard_map/pallas_call | solution.py:84
  82.8 2.7 %collective-permute-start.9 = (bf16[2,8,64,128]{3,2,1,0:T(8,128)(2,1)S(1)}, bf16[2,8,64,128]{3,2,1,0:T(8,128)(2,1)S(1)}, u32[]{:S(2)}, u32[]{:S(2)}) collective-permute-start(bf16[2,8,64,128]{3,2,1,0:T(8,128)(2,1)S(1)} %get-tuple-element.16), channel_id=1, source_target_pairs={{0,6},{1,7},{2,4},{3,5},{4,2},{5,3},{6,0},{7,1},{8,14},{9,15},{10,... | collective-permute-start | bytes 786440 | tf_op jit(solution)/shard_map/ppermute | solution.py:113
  86.4 11.6 %shard_map.38 = (bf16[2,8,64,128]{3,2,1,0:T(8,128)(2,1)S(1)}, bf16[2,8,64,128]{3,2,1,0:T(8,128)(2,1)S(1)}, bf16[2,8,64,128]{3,2,1,0:T(8,128)(2,1)S(1)}, bf16[2,8,64,128]{3,2,1,0:T(8,128)(2,1)S(1)}) custom-call(bf16[8,2,10,32,128]{4,3,2,1,0:T(8,128)(2,1)S(1)} %all-to-all-done.refs_0_, bf16[8,2,10,32,128]{4,3,2,1,0:T(8,128)(2,1)} %all-to-all-done.1.refs_1_, ...), custom_call_target="tpu_custom_call" | custom-call | flops 7247757312 | bytes 10000000 | tf_op jit(solution)/shard_map/pallas_call | solution.py:84
  98.0 2.7 %collective-permute-start.13 = (bf16[2,8,64,128]{3,2,1,0:T(8,128)(2,1)S(1)}, bf16[2,8,64,128]{3,2,1,0:T(8,128)(2,1)S(1)}, u32[]{:S(2)}, u32[]{:S(2)}) collective-permute-start(bf16[2,8,64,128]{3,2,1,0:T(8,128)(2,1)S(1)} %get-tuple-element.20), channel_id=1, source_target_pairs={{0,6},{1,7},{2,4},{3,5},{4,2},{5,3},{6,0},{7,1},{8,14},{9,15},{10,... | collective-permute-start | bytes 786440 | tf_op jit(solution)/shard_map/ppermute | solution.py:113
  101.9 6.3 %collective-permute-done.13 = bf16[2,8,64,128]{3,2,1,0:T(8,128)(2,1)S(1)} collective-permute-done((bf16[2,8,64,128]{3,2,1,0:T(8,128)(2,1)S(1)}, bf16[2,8,64,128]{3,2,1,0:T(8,128)(2,1)S(1)}, u32[]{:S(2)}, u32[]{:S(2)}) %collective-permute-start.13) | collective-permute-done | bytes 262176 | tf_op jit(solution)/shard_map/ppermute | solution.py:113
  108.3 3.1 %collective-permute-done.12 = bf16[2,8,64,128]{3,2,1,0:T(8,128)(2,1)S(1)} collective-permute-done((bf16[2,8,64,128]{3,2,1,0:T(8,128)(2,1)S(1)}, bf16[2,8,64,128]{3,2,1,0:T(8,128)(2,1)S(1)}, u32[]{:S(2)}, u32[]{:S(2)}) %collective-permute-start.12) | collective-permute-done | bytes 262176 | tf_op jit(solution)/shard_map/ppermute | solution.py:113
  114.8 1.6 %pad_maximum_fusion = bf16[4,32,64,128]{3,2,1,0:T(8,128)(2,1)} fusion(bf16[1,32,64,128]{3,2,1,0:T(8,128)(2,1)S(1)} %get-tuple-element.28, bf16[2,32,64,128]{3,2,1,0:T(8,128)(2,1)S(1)} %bitcast.76, bf16[1,32,64,128]{3,2,1,0:T(8,128)(2,1)S(1)} %get-tuple-element.27), kind=kLoop, calls=%fused_computation.7 | loop fusion | flops 2097152 | bytes 4194304 | tf_op jit(solution)/shard_map/concatenate | solution.py:168
  (75 shorter events, 12.3 us)
Async XLA Ops:
  1.0 9.3 %collective-permute-start.2 = (bf16[3,3,3,16,256]{4,3,2,1,0:T(8,128)(2,1)S(1)}, bf16[3,3,3,16,256]{4,3,2,1,0:T(8,128)(2,1)S(1)}, u32[]{:S(2)}, u32[]{:S(2)}) collective-permute-start(bf16[3,3,3,16,256]{4,3,2,1,0:T(8,128)(2,1)S(1)} %constant_dynamic-slice_fusion), channel_id=1, source_target_pairs={{0,2},{1,3},{2,0},{3,1},{4,6},{5,7},{6,4},{7,5},{8,10},{9,11},{10,... | collective-permute-start | bytes 663560 | tf_op jit(solution)/shard_map/ppermute | solution.py:113
  4.0 11.6 %collective-permute-start.3 = (bf16[3,3,3,16,256]{4,3,2,1,0:T(8,128)(2,1)S(1)}, bf16[3,3,3,16,256]{4,3,2,1,0:T(8,128)(2,1)S(1)}, u32[]{:S(2)}, u32[]{:S(2)}) collective-permute-start(bf16[3,3,3,16,256]{4,3,2,1,0:T(8,128)(2,1)S(1)} %constant_dynamic-slice_fusion), channel_id=1, source_target_pairs={{0,4},{1,5},{2,6},{3,7},{4,0},{5,1},{6,2},{7,3},{8,12},{9,13},{10,... | collective-permute-start | bytes 663560 | tf_op jit(solution)/shard_map/ppermute | solution.py:113
  5.5 10.1 %collective-permute-start.4 = (bf16[3,3,3,16,256]{4,3,2,1,0:T(8,128)(2,1)S(1)}, bf16[3,3,3,16,256]{4,3,2,1,0:T(8,128)(2,1)S(1)}, u32[]{:S(2)}, u32[]{:S(2)}) collective-permute-start(bf16[3,3,3,16,256]{4,3,2,1,0:T(8,128)(2,1)S(1)} %constant_dynamic-slice_fusion), channel_id=1, source_target_pairs={{0,6},{1,7},{2,4},{3,5},{4,2},{5,3},{6,0},{7,1},{8,14},{9,15},{10,... | collective-permute-start | bytes 663560 | tf_op jit(solution)/shard_map/ppermute | solution.py:113
  15.7 15.7 %collective-permute-start.5 = (bf16[3,3,3,3,16,256]{5,4,3,2,1,0:T(8,128)(2,1)S(1)}, bf16[3,3,3,3,16,256]{5,4,3,2,1,0:T(8,128)(2,1)}, u32[]{:S(2)}, u32[]{:S(2)}) collective-permute-start(bf16[3,3,3,3,16,256]{5,4,3,2,1,0:T(8,128)(2,1)S(1)} %pad_maximum_fusion.2), channel_id=1, source_target_pairs={{0,8},{8,0},{16,24},{24,16},{1,9},{9,1},{17,25},{25,17},{2,10},{10... | collective-permute-start | bytes 1990664 | tf_op jit(solution)/shard_map/ppermute | solution.py:113
  20.8 11.8 %copy-start.1 = (bf16[3,3,3,32,256]{4,3,2,1,0:T(8,128)(2,1)S(1)}, bf16[3,3,3,32,256]{4,3,2,1,0:T(8,128)(2,1)}, u32[]{:S(2)}) copy-start(bf16[3,3,3,32,256]{4,3,2,1,0:T(8,128)(2,1)} %param.4) | copy-start | bytes 1327108
  20.8 21.9 %all-to-all-start = ((bf16[8,2,10,32,128]{4,3,2,1,0:T(8,128)(2,1)}), bf16[8,2,10,32,128]{4,3,2,1,0:T(8,128)(2,1)S(1)}, u32[]{:S(2)}, u32[]{:S(2)}) async-start(bf16[8,2,10,32,128]{4,3,2,1,0:T(8,128)(2,1)} %fusion.5), calls=%async_computation | async-start | bytes 2621440 | tf_op jit(solution)/shard_map/all_to_all | solution.py:136
  32.6 1.6 %copy-start = (bf16[4,32,64,128]{3,2,1,0:T(8,128)(2,1)S(1)}, bf16[4,32,64,128]{3,2,1,0:T(8,128)(2,1)}, u32[]{:S(2)}) copy-start(bf16[4,32,64,128]{3,2,1,0:T(8,128)(2,1)} %param.3) | copy-start | bytes 6291460
  32.9 37.8 %collective-permute-start.6 = (bf16[4,3,3,3,32,256]{5,4,3,2,1,0:T(8,128)(2,1)S(1)}, bf16[4,3,3,3,32,256]{5,4,3,2,1,0:T(8,128)(2,1)}, u32[]{:S(2)}, u32[]{:S(2)}) collective-permute-start(bf16[4,3,3,3,32,256]{5,4,3,2,1,0:T(8,128)(2,1)S(1)} %maximum_maximum_fusion.refs_4_.refs_2_), channel_id=1, source_target_pairs={{0,1},{1,0},{2,3},{3,2},{4,5},{5,4},{6,7},{7,6},{8,9},{9,8},{10,11... | collective-permute-start | bytes 5308424 | tf_op jit(solution)/shard_map/ppermute | solution.py:113
  36.3 16.6 %copy-start.2 = (f32[256]{0:T(256)S(1)}, f32[256]{0:T(256)}, u32[]{:S(2)}) copy-start(f32[256]{0:T(256)} %param.5) | copy-start | bytes 3076
  42.6 22.5 %all-to-all-start.1 = ((bf16[8,2,10,32,128]{4,3,2,1,0:T(8,128)(2,1)}), bf16[8,2,10,32,128]{4,3,2,1,0:T(8,128)(2,1)}, u32[]{:S(2)}, u32[]{:S(2)}) async-start(bf16[8,2,10,32,128]{4,3,2,1,0:T(8,128)(2,1)} %fusion.7), calls=%async_computation.1 | async-start | bytes 2621440 | tf_op jit(solution)/shard_map/all_to_all | solution.py:136
  48.4 17.2 %collective-permute-start = (bf16[8,1,10,32,128]{4,3,2,1,0:T(8,128)(2,1)}, bf16[8,1,10,32,128]{4,3,2,1,0:T(8,128)(2,1)}, u32[]{:S(2)}, u32[]{:S(2)}) collective-permute-start(bf16[8,1,10,32,128]{4,3,2,1,0:T(8,128)(2,1)} %get-tuple-element.26), channel_id=1, source_target_pairs={{0,8},{8,16},{16,24},{1,9},{9,17},{17,25},{2,10},{10,18},{18,26},{... | collective-permute-start | bytes 1966088 | tf_op jit(solution)/shard_map/ppermute | solution.py:158
  51.6 19.0 %collective-permute-start.1 = (bf16[8,1,10,32,128]{4,3,2,1,0:T(8,128)(2,1)}, bf16[8,1,10,32,128]{4,3,2,1,0:T(8,128)(2,1)}, u32[]{:S(2)}, u32[]{:S(2)}) collective-permute-start(bf16[8,1,10,32,128]{4,3,2,1,0:T(8,128)(2,1)} %get-tuple-element.25), channel_id=1, source_target_pairs={{8,0},{16,8},{24,16},{9,1},{17,9},{25,17},{10,2},{18,10},{26,18},{... | collective-permute-start | bytes 1966088 | tf_op jit(solution)/shard_map/ppermute | solution.py:157
  82.8 18.4 %collective-permute-start.9 = (bf16[2,8,64,128]{3,2,1,0:T(8,128)(2,1)S(1)}, bf16[2,8,64,128]{3,2,1,0:T(8,128)(2,1)S(1)}, u32[]{:S(2)}, u32[]{:S(2)}) collective-permute-start(bf16[2,8,64,128]{3,2,1,0:T(8,128)(2,1)S(1)} %get-tuple-element.16), channel_id=1, source_target_pairs={{0,6},{1,7},{2,4},{3,5},{4,2},{5,3},{6,0},{7,1},{8,14},{9,15},{10,... | collective-permute-start | bytes 786440 | tf_op jit(solution)/shard_map/ppermute | solution.py:113
  85.5 16.2 %collective-permute-start.8 = (bf16[2,8,64,128]{3,2,1,0:T(8,128)(2,1)S(1)}, bf16[2,8,64,128]{3,2,1,0:T(8,128)(2,1)S(1)}, u32[]{:S(2)}, u32[]{:S(2)}) collective-permute-start(bf16[2,8,64,128]{3,2,1,0:T(8,128)(2,1)S(1)} %get-tuple-element.15), channel_id=1, source_target_pairs={{0,4},{1,5},{2,6},{3,7},{4,0},{5,1},{6,2},{7,3},{8,12},{9,13},{10,... | collective-permute-start | bytes 786440 | tf_op jit(solution)/shard_map/ppermute | solution.py:113
  86.0 15.7 %collective-permute-start.7 = (bf16[2,8,64,128]{3,2,1,0:T(8,128)(2,1)S(1)}, bf16[2,8,64,128]{3,2,1,0:T(8,128)(2,1)S(1)}, u32[]{:S(2)}, u32[]{:S(2)}) collective-permute-start(bf16[2,8,64,128]{3,2,1,0:T(8,128)(2,1)S(1)} %get-tuple-element.14), channel_id=1, source_target_pairs={{0,2},{1,3},{2,0},{3,1},{4,6},{5,7},{6,4},{7,5},{8,10},{9,11},{10,... | collective-permute-start | bytes 786440 | tf_op jit(solution)/shard_map/ppermute | solution.py:113
  98.0 10.3 %collective-permute-start.13 = (bf16[2,8,64,128]{3,2,1,0:T(8,128)(2,1)S(1)}, bf16[2,8,64,128]{3,2,1,0:T(8,128)(2,1)S(1)}, u32[]{:S(2)}, u32[]{:S(2)}) collective-permute-start(bf16[2,8,64,128]{3,2,1,0:T(8,128)(2,1)S(1)} %get-tuple-element.20), channel_id=1, source_target_pairs={{0,6},{1,7},{2,4},{3,5},{4,2},{5,3},{6,0},{7,1},{8,14},{9,15},{10,... | collective-permute-start | bytes 786440 | tf_op jit(solution)/shard_map/ppermute | solution.py:113
  100.6 10.7 %collective-permute-start.12 = (bf16[2,8,64,128]{3,2,1,0:T(8,128)(2,1)S(1)}, bf16[2,8,64,128]{3,2,1,0:T(8,128)(2,1)S(1)}, u32[]{:S(2)}, u32[]{:S(2)}) collective-permute-start(bf16[2,8,64,128]{3,2,1,0:T(8,128)(2,1)S(1)} %get-tuple-element.19), channel_id=1, source_target_pairs={{0,4},{1,5},{2,6},{3,7},{4,0},{5,1},{6,2},{7,3},{8,12},{9,13},{10,... | collective-permute-start | bytes 786440 | tf_op jit(solution)/shard_map/ppermute | solution.py:113
  101.2 10.1 %collective-permute-start.11 = (bf16[2,8,64,128]{3,2,1,0:T(8,128)(2,1)S(1)}, bf16[2,8,64,128]{3,2,1,0:T(8,128)(2,1)S(1)}, u32[]{:S(2)}, u32[]{:S(2)}) collective-permute-start(bf16[2,8,64,128]{3,2,1,0:T(8,128)(2,1)S(1)} %get-tuple-element.18), channel_id=1, source_target_pairs={{0,2},{1,3},{2,0},{3,1},{4,6},{5,7},{6,4},{7,5},{8,10},{9,11},{10,... | collective-permute-start | bytes 786440 | tf_op jit(solution)/shard_map/ppermute | solution.py:113
  101.8 10.4 %collective-permute-start.10 = (bf16[4,2,8,32,128]{4,3,2,1,0:T(8,128)(2,1)S(1)}, bf16[4,2,8,32,128]{4,3,2,1,0:T(8,128)(2,1)S(1)}, u32[]{:S(2)}, u32[]{:S(2)}) collective-permute-start(bf16[4,2,8,32,128]{4,3,2,1,0:T(8,128)(2,1)S(1)} %pad_maximum_fusion.3), channel_id=1, source_target_pairs={{0,1},{1,0},{2,3},{3,2},{4,5},{5,4},{6,7},{7,6},{8,9},{9,8},{10,11... | collective-permute-start | bytes 1572872 | tf_op jit(solution)/shard_map/ppermute | solution.py:113
  111.4 2.0 %collective-permute-start.14 = (bf16[4,2,8,32,128]{4,3,2,1,0:T(8,128)(2,1)S(1)}, bf16[4,2,8,32,128]{4,3,2,1,0:T(8,128)(2,1)S(1)}, u32[]{:S(2)}, u32[]{:S(2)}) collective-permute-start(bf16[4,2,8,32,128]{4,3,2,1,0:T(8,128)(2,1)S(1)} %pad_maximum_fusion.4), channel_id=1, source_target_pairs={{0,1},{1,0},{2,3},{3,2},{4,5},{5,4},{6,7},{7,6},{8,9},{9,8},{10,11... | collective-permute-start | bytes 1572872 | tf_op jit(solution)/shard_map/ppermute | solution.py:113

commit v4 on v3

v4 whole, which is shorter than its diff:
```python
import functools

import jax
import jax.numpy as jnp
from jax import lax
from jax.experimental import pallas as pl
from jax.experimental.pallas import tpu as pltpu
from jax.sharding import PartitionSpec as P

slope = 0.3
PAIR = 2


def conv_kernel(first, stride, count, plan, piece_count, *refs):
    refs = list(refs)
    place_ref = refs.pop(0)
    pieces = [refs.pop(0) for _ in range(piece_count)]
    taps = refs.pop(0)
    bias_ref = refs.pop(0)
    outs = refs[:-2]
    vol, vol_sem = refs[-2:]
    rows_in, total_in, cols = vol.shape[1:]
    total_out = bias_ref.shape[0]
    rows = rows_in - 2
    copies = []
    for n, (source, begin, slot, plane_count) in enumerate(plan):
        piece = pieces[source]
        chan = piece.shape[3]
        for s in range(piece.shape[0]):
            part = pl.ds(s * chan, chan)
            copies.append(
                pltpu.make_async_copy(
                    piece.at[s, pl.ds(begin, plane_count)],
                    vol.at[pl.ds(slot, plane_count), :, part, :],
                    vol_sem.at[n, s],
                )
            )
    for copy in copies:
        copy.start()
    for copy in copies:
        copy.wait()

    lane = lax.broadcasted_iota(jnp.int32, (total_out, cols), 1)
    per_plane = rows // PAIR
    block = total_out // len(outs)
    groups, size = taps.shape[0], taps.shape[4]
    places = [place_ref[g] for g in range(groups)]

    def tile(step, carry):
        slot = step // per_plane
        plane = first + slot * stride
        row = (step % per_plane) * PAIR
        cells = []
        weights = []
        for a in range(3):
            for b in range(3):
                cells.append(jnp.concatenate([vol[plane + a, row + b + r] for r in range(PAIR)], axis=1))
                weights.append(
                    jnp.concatenate(
                        [taps[place, a, b].reshape(3 * size, -1) for place in places], axis=0
                    )
                )
        total = jnp.dot(
            jnp.concatenate(weights, axis=1), jnp.concatenate(cells, axis=0), preferred_element_type=jnp.float32
        )
        for r in range(PAIR):
            part = total[:, r * cols : (r + 1) * cols].reshape(groups, 3, size, cols)
            side = [part[:, c].reshape(total_out, cols) for c in range(3)]
            left = jnp.where(lane == 0, 0.0, pltpu.roll(side[0], 1, 1))
            right = jnp.where(lane == cols - 1, 0.0, pltpu.roll(side[2], cols - 1, 1))
            shifted = side[1] + left + right + bias_ref[...]
            done = jnp.where(shifted > 0, shifted, slope * shifted).astype(jnp.bfloat16)
            for n, out_ref in enumerate(outs):
                out_ref[slot, row + r] = done[n * block : (n + 1) * block]
        return carry

    lax.fori_loop(0, count * per_plane, tile, 0)


def convolve(first, stride, count, places, pieces, plan, taps, bias, blocks):
    rows_in, cols = pieces[0].shape[2], pieces[0].shape[4]
    in_chan = taps.shape[5]
    total_out = bias.shape[0]
    rows = rows_in - 2
    depth = max(slot + n for _, _, slot, n in plan)
    wide_bias = jnp.broadcast_to(bias[:, None], (total_out, cols))
    macs = 27 * total_out * in_chan * count * rows * cols
    any_space = pl.BlockSpec(memory_space=pl.ANY)
    in_vmem = pl.BlockSpec(memory_space=pltpu.VMEM)
    in_smem = pl.BlockSpec(memory_space=pltpu.SMEM)
    return pl.pallas_call(
        functools.partial(conv_kernel, first, stride, count, plan, len(pieces)),
        out_shape=[jax.ShapeDtypeStruct((count, rows, total_out // blocks, cols), jnp.bfloat16)] * blocks,
        in_specs=[in_smem] + [any_space] * len(pieces) + [in_vmem] * 2,
        out_specs=[in_vmem] * blocks,
        scratch_shapes=[
            pltpu.VMEM((depth, rows_in, in_chan, cols), jnp.bfloat16),
            pltpu.SemaphoreType.DMA((len(plan), max(piece.shape[0] for piece in pieces))),
        ],
        cost_estimate=pl.CostEstimate(flops=2 * macs, bytes_accessed=10_000_000, transcendentals=0),
        compiler_params=pltpu.CompilerParams(vmem_limit_bytes=20 * 2**20),
    )(places, *pieces, taps, wide_bias)


def body(features, kernel, bias_vector):
    planes, chan, y_cells, cols = features.shape
    out_chan = kernel.shape[3]
    parts = lax.axis_size("filt")
    slabs = lax.axis_size("slab")
    me = lax.axis_index("filt")
    rows = y_cells // parts
    aligned = chan % 16 == 0 and out_chan % 16 == 0
    across = list(range(0, parts, 2))

    def swap(array, k):
        if k == 0:
            return array
        return lax.ppermute(array, "filt", [(i, i ^ k) for i in range(parts)])

    taps = lax.all_gather(kernel, "filt", axis=0)
    order = jnp.stack([me ^ k ^ c for k in across for c in range(2)])
    bias = jnp.take(bias_vector.reshape(parts, out_chan), order, axis=0).reshape(-1)
    if not aligned:
        taps = jnp.take(taps, order, axis=0).transpose(1, 2, 3, 0, 4, 5)
        taps = taps.reshape(1, 3, 3, 3, parts * out_chan, -1)
        order = jnp.zeros((1,), jnp.int32)

    def gather_rows(piece):
        count = piece.shape[0]
        by_row = piece.transpose(0, 2, 1, 3).reshape(count, parts, rows, chan, cols).transpose(1, 0, 2, 3, 4)
        nothing = jnp.zeros((1, count, 1, chan, cols), piece.dtype)
        above = jnp.concatenate([nothing, by_row[:-1, :, -1:]])
        below = jnp.concatenate([by_row[1:, :, :1], nothing])
        got = lax.all_to_all(jnp.concatenate([above, by_row, below], axis=2), "filt", 0, 0)
        if not aligned:
            got = got.transpose(1, 2, 0, 3, 4).reshape(1, count, rows + 2, parts * chan, cols)
        return got

    def send_back(results):
        count = results[0].shape[0]
        got = [swap(result, k) for result, k in zip(results, across)]
        mine = [block[:, :, :out_chan] for block in got]
        theirs = swap(jnp.stack([block[:, :, out_chan:] for block in got]), 1)
        final = jnp.zeros((count, y_cells, out_chan, cols), jnp.bfloat16)
        for n, k in enumerate(across):
            final = lax.dynamic_update_slice_in_dim(final, mine[n], (me ^ k) * rows, 1)
            final = lax.dynamic_update_slice_in_dim(final, theirs[n], (me ^ k ^ 1) * rows, 1)
        return final.transpose(0, 2, 1, 3)

    up = [(i, i + 1) for i in range(slabs - 1)]
    down = [(i + 1, i) for i in range(slabs - 1)]
    outer = gather_rows(jnp.concatenate([features[:1], features[-1:]]))
    inner = gather_rows(features[1:-1])
    after = lax.ppermute(outer[:, :1], "slab", down)
    before = lax.ppermute(outer[:, 1:], "slab", up)

    def conv(first, stride, count, edges, shift):
        plan = [(0, 0, shift, 1), (1, 0, 1 + shift, planes - 2), (0, 1, planes - 1 + shift, 1)]
        plan += [(2 + n, 0, n * (planes + 1), 1) for n in range(len(edges))]
        return convolve(first, stride, count, order, [outer, inner, *edges], tuple(plan), taps, bias, len(across))

    inside = send_back(conv(0, 1, planes - 2, [], 0))
    outside = send_back(conv(0, planes - 1, 2, [before, after], 1))
    return jnp.concatenate([outside[:1], inside, outside[1:]])


def solution(mesh):
    placed = (P("slab", "filt", None, None), P(None, None, None, "filt", None), P())
    return jax.shard_map(
        body, mesh=mesh, in_specs=placed, out_specs=P("slab", "filt", None, None), check_vma=False
    )
```

time: 117 us -> 123 us (1.051)
  between operations: 0.53 us -> 13.9 us
  starting transfers between devices: 26 us -> 21.1 us
  Pallas kernels: 23.7 us -> 22.2 us
  other arithmetic: 5.96 us -> 4.46 us
    all_to_all x2, waiting for transfers between devices: 17.7 us -> 39.3 us  [gather_rows(): lax.all_to_all(jnp.concatenate([above, by_row, below], axis=2), 'filt', 0...]
    ppermute x13 -> x8, waiting for transfers between devices: 27.6 us -> 11.7 us  [swap(): return lax.ppermute(array, 'filt', [(i, i ^ k) for i in range(parts)])]
    ppermute x13 -> x8, starting transfers between devices: 13.6 us -> 7.51 us  [swap(): return lax.ppermute(array, 'filt', [(i, i ^ k) for i in range(parts)])]
    ppermute x1, waiting for transfers between devices: 5.09 us -> 0.01 us  [body(): after = lax.ppermute(outer[:, :1], 'slab', down)]
    pallas_call x2, Pallas kernels: 23.7 us -> 22.2 us  [convolve(): pl.pallas_call(functools.partial(conv_kernel, first, stride, count, plan,...]
  transfers between devices with their start and end apart: 17 -> 13, of which waited for: 10 -> 5; matrix products, arithmetic and copies ran while one was open for 9% -> 7% of each run, Pallas kernels for 10% -> 8%
where the time goes in v4:
time: 123 us
  waiting for transfers between devices  51.7 us (42%)
  Pallas kernels  22.2 us (18%)
  starting transfers between devices  21.1 us (17%)
  between operations  13.9 us (11%)
  local copies, waits for them, and re-layouts  9.23 us (8%)
  other arithmetic  4.46 us (4%)
    all_to_all x2, waiting for transfers between devices, gather_rows(): lax.all_to_all(jnp.concatenate([above, by_row, below], axis=2), 'filt', 0...  39.3 us
    pallas_call x2, Pallas kernels, convolve(): pl.pallas_call(functools.partial(conv_kernel, first, stride, count, plan,...  22.2 us
    ppermute x8, waiting for transfers between devices, swap(): return lax.ppermute(array, 'filt', [(i, i ^ k) for i in range(parts)])  11.7 us
    all_to_all x2, starting transfers between devices, gather_rows(): lax.all_to_all(jnp.concatenate([above, by_row, below], axis=2), 'filt', 0...  8.77 us
    ppermute x8, starting transfers between devices, swap(): return lax.ppermute(array, 'filt', [(i, i ^ k) for i in range(parts)])  7.51 us
    ppermute x1, starting transfers between devices, body(): before = lax.ppermute(outer[:, 1:], 'slab', up)  3.51 us
    unnamed x8, local copies, waits for them, and re-layouts  2.7 us
    concatenate x2, other arithmetic, gather_rows(): jnp.concatenate([above, by_row, below], axis=2)  2.56 us
  transfers between devices with their start and end apart: 13, of which 5 were waited for; matrix products, arithmetic and copies ran while one was open for 7% of the time, Pallas kernels for 8%

profile of v4, /device:TPU:0, one launch (start us, length us, event | category | flops | bytes accessed | tf_op | source)
XLA Modules:
  0.0 122.6 jit_solution(1905107871752428416)
XLA Ops:
  6.5 0.7 all-gather.3.cloned.1.call-update
  7.3 1.3 %fusion.9 = (bf16[1,32,64,128]{3,2,1,0:T(8,128)(2,1)S(1)}, bf16[1,32,64,128]{3,2,1,0:T(8,128)(2,1)S(1)}) fusion(bf16[4,32,64,128]{3,2,1,0:T(8,128)(2,1)} %param.3), kind=kLoop, calls=%fused_computation.56 | loop fusion | bytes 2097152 | tf_op jit(solution)/shard_map/slice | solution.py:152
  9.5 1.3 %fusion.5 = bf16[8,2,10,32,128]{4,3,2,1,0:T(8,128)(2,1)} fusion(bf16[7,2,1,32,128]{4,3,2,1,0:T(8,128)(2,1)S(1)} %get-tuple-element.30, bf16[7,2,1,32,128]{4,3,2,1,0:T(8,128)(2,1)S(1)} %get-tuple-element.29, bf16[8,2,8,32,128]{4,3,2,1,0:T(8,128)(2,1)S(1)} %bitcast.70), kind=kLoop, calls=%fused_computation.9 | loop fusion | flops 6553600 | bytes 2588672 | tf_op jit(solution)/shard_map/concatenate | solution.py:134
  10.7 5.2 %all-to-all-start = ((bf16[8,2,10,32,128]{4,3,2,1,0:T(8,128)(2,1)}), bf16[8,2,10,32,128]{4,3,2,1,0:T(8,128)(2,1)S(1)}, u32[]{:S(2)}, u32[]{:S(2)}) async-start(bf16[8,2,10,32,128]{4,3,2,1,0:T(8,128)(2,1)} %fusion.5), calls=%async_computation | async-start | bytes 2621440 | tf_op jit(solution)/shard_map/all_to_all | solution.py:134
  16.0 0.7 copy.84
  16.7 1.3 %fusion.7 = bf16[8,2,10,32,128]{4,3,2,1,0:T(8,128)(2,1)} fusion(bf16[7,2,1,32,128]{4,3,2,1,0:T(8,128)(2,1)S(1)} %get-tuple-element.28, bf16[7,2,1,32,128]{4,3,2,1,0:T(8,128)(2,1)S(1)} %get-tuple-element.27, bf16[8,2,8,32,128]{4,3,2,1,0:T(8,128)(2,1)S(1)} %bitcast.72), kind=kLoop, calls=%fused_computation.11 | loop fusion | flops 6553600 | bytes 2588672 | tf_op jit(solution)/shard_map/concatenate | solution.py:134
  18.0 20.8 %all-to-all-done.refs_1_ = bf16[8,2,10,32,128]{4,3,2,1,0:T(8,128)(2,1)S(1)} async-done(((bf16[8,2,10,32,128]{4,3,2,1,0:T(8,128)(2,1)}), bf16[8,2,10,32,128]{4,3,2,1,0:T(8,128)(2,1)S(1)}, u32[]{:S(2)}, u32[]{:S(2)}) %all-to-all-start) | async-done | bytes 1310752 | tf_op jit(solution)/shard_map/all_to_all | solution.py:134
  38.8 3.6 %all-to-all-start.1 = ((bf16[8,2,10,32,128]{4,3,2,1,0:T(8,128)(2,1)}), bf16[8,2,10,32,128]{4,3,2,1,0:T(8,128)(2,1)S(1)}, u32[]{:S(2)}, u32[]{:S(2)}) async-start(bf16[8,2,10,32,128]{4,3,2,1,0:T(8,128)(2,1)} %fusion.7), calls=%async_computation.1 | async-start | bytes 2621440 | tf_op jit(solution)/shard_map/all_to_all | solution.py:134
  42.5 1.3 %fusion.10 = (bf16[8,1,10,32,128]{4,3,2,1,0:T(8,128)(2,1)}, bf16[8,1,10,32,128]{4,3,2,1,0:T(8,128)(2,1)}) fusion(bf16[8,2,10,32,128]{4,3,2,1,0:T(8,128)(2,1)S(1)} %all-to-all-done.refs_1_), kind=kLoop, calls=%fused_computation.57 | loop fusion | bytes 2621440 | tf_op jit(solution)/shard_map/slice | solution.py:154
  43.8 3.5 %collective-permute-start = (bf16[8,1,10,32,128]{4,3,2,1,0:T(8,128)(2,1)}, bf16[8,1,10,32,128]{4,3,2,1,0:T(8,128)(2,1)S(1)}, u32[]{:S(2)}, u32[]{:S(2)}) collective-permute-start(bf16[8,1,10,32,128]{4,3,2,1,0:T(8,128)(2,1)} %get-tuple-element.24), channel_id=1, source_target_pairs={{0,8},{8,16},{16,24},{1,9},{9,17},{17,25},{2,10},{10,18},{18,26},{... | collective-permute-start | bytes 1966088 | tf_op jit(solution)/shard_map/ppermute | solution.py:155
  47.4 1.3 %collective-permute-start.1 = (bf16[8,1,10,32,128]{4,3,2,1,0:T(8,128)(2,1)}, bf16[8,1,10,32,128]{4,3,2,1,0:T(8,128)(2,1)}, u32[]{:S(2)}, u32[]{:S(2)}) collective-permute-start(bf16[8,1,10,32,128]{4,3,2,1,0:T(8,128)(2,1)} %get-tuple-element.23), channel_id=1, source_target_pairs={{8,0},{16,8},{24,16},{9,1},{17,9},{25,17},{10,2},{18,10},{26,18},{... | collective-permute-start | bytes 1966088 | tf_op jit(solution)/shard_map/ppermute | solution.py:154
  48.8 0.6 gather_fusion
  49.6 18.5 %all-to-all-done.1.refs_2_ = bf16[8,2,10,32,128]{4,3,2,1,0:T(8,128)(2,1)S(1)} async-done(((bf16[8,2,10,32,128]{4,3,2,1,0:T(8,128)(2,1)}), bf16[8,2,10,32,128]{4,3,2,1,0:T(8,128)(2,1)S(1)}, u32[]{:S(2)}, u32[]{:S(2)}) %all-to-all-start.1) | async-done | bytes 1310752 | tf_op jit(solution)/shard_map/all_to_all | solution.py:134
  68.2 2.0 %copy-done = bf16[24,3,3,32,256]{4,3,2,1,0:T(8,128)(2,1)S(1)} copy-done((bf16[24,3,3,32,256]{4,3,2,1,0:T(8,128)(2,1)S(1)}, bf16[24,3,3,32,256]{4,3,2,1,0:T(8,128)(2,1)}, u32[]{:S(2)}) %copy-start) | copy-done | bytes 3538968
  70.2 11.8 %shard_map.37 = (bf16[2,8,64,128]{3,2,1,0:T(8,128)(2,1)S(1)}, bf16[2,8,64,128]{3,2,1,0:T(8,128)(2,1)S(1)}, bf16[2,8,64,128]{3,2,1,0:T(8,128)(2,1)S(1)}, bf16[2,8,64,128]{3,2,1,0:T(8,128)(2,1)S(1)}) custom-call(s32[8]{0:T(128)S(1)} %stack.83.refs_0_, bf16[8,2,10,32,128]{4,3,2,1,0:T(8,128)(2,1)S(1)} %all-to-all-done.refs_1_, ...), custom_call_target="tpu_custom_call" | custom-call | flops 7247757312 | bytes 10000000 | tf_op jit(solution)/shard_map/pallas_call | solution.py:91
  82.0 2.3 %collective-permute-start.4 = (bf16[2,8,64,128]{3,2,1,0:T(8,128)(2,1)S(1)}, bf16[2,8,64,128]{3,2,1,0:T(8,128)(2,1)S(1)}, u32[]{:S(2)}, u32[]{:S(2)}) collective-permute-start(bf16[2,8,64,128]{3,2,1,0:T(8,128)(2,1)S(1)} %get-tuple-element.16), channel_id=1, source_target_pairs={{0,6},{1,7},{2,4},{3,5},{4,2},{5,3},{6,0},{7,1},{8,14},{9,15},{10,... | collective-permute-start | bytes 786440 | tf_op jit(solution)/shard_map/ppermute | solution.py:118
  84.3 1.5 %collective-permute-start.3 = (bf16[2,8,64,128]{3,2,1,0:T(8,128)(2,1)S(1)}, bf16[2,8,64,128]{3,2,1,0:T(8,128)(2,1)S(1)}, u32[]{:S(2)}, u32[]{:S(2)}) collective-permute-start(bf16[2,8,64,128]{3,2,1,0:T(8,128)(2,1)S(1)} %get-tuple-element.15), channel_id=1, source_target_pairs={{0,4},{1,5},{2,6},{3,7},{4,0},{5,1},{6,2},{7,3},{8,12},{9,13},{10,... | collective-permute-start | bytes 786440 | tf_op jit(solution)/shard_map/ppermute | solution.py:118
  85.7 10.4 %shard_map.38 = (bf16[2,8,64,128]{3,2,1,0:T(8,128)(2,1)S(1)}, bf16[2,8,64,128]{3,2,1,0:T(8,128)(2,1)S(1)}, bf16[2,8,64,128]{3,2,1,0:T(8,128)(2,1)S(1)}, bf16[2,8,64,128]{3,2,1,0:T(8,128)(2,1)S(1)}) custom-call(s32[8]{0:T(128)S(1)} %stack.83.refs_0_, bf16[8,2,10,32,128]{4,3,2,1,0:T(8,128)(2,1)S(1)} %all-to-all-done.refs_1_, ...), custom_call_target="tpu_custom_call" | custom-call | flops 7247757312 | bytes 10000000 | tf_op jit(solution)/shard_map/pallas_call | solution.py:91
  96.2 2.1 %collective-permute-start.8 = (bf16[2,8,64,128]{3,2,1,0:T(8,128)(2,1)S(1)}, bf16[2,8,64,128]{3,2,1,0:T(8,128)(2,1)S(1)}, u32[]{:S(2)}, u32[]{:S(2)}) collective-permute-start(bf16[2,8,64,128]{3,2,1,0:T(8,128)(2,1)S(1)} %get-tuple-element.20), channel_id=1, source_target_pairs={{0,6},{1,7},{2,4},{3,5},{4,2},{5,3},{6,0},{7,1},{8,14},{9,15},{10,... | collective-permute-start | bytes 786440 | tf_op jit(solution)/shard_map/ppermute | solution.py:118
  98.3 1.5 %collective-permute-start.7 = (bf16[2,8,64,128]{3,2,1,0:T(8,128)(2,1)S(1)}, bf16[2,8,64,128]{3,2,1,0:T(8,128)(2,1)S(1)}, u32[]{:S(2)}, u32[]{:S(2)}) collective-permute-start(bf16[2,8,64,128]{3,2,1,0:T(8,128)(2,1)S(1)} %get-tuple-element.19), channel_id=1, source_target_pairs={{0,4},{1,5},{2,6},{3,7},{4,0},{5,1},{6,2},{7,3},{8,12},{9,13},{10,... | collective-permute-start | bytes 786440 | tf_op jit(solution)/shard_map/ppermute | solution.py:118
  100.1 6.3 %collective-permute-done.8 = bf16[2,8,64,128]{3,2,1,0:T(8,128)(2,1)S(1)} collective-permute-done((bf16[2,8,64,128]{3,2,1,0:T(8,128)(2,1)S(1)}, bf16[2,8,64,128]{3,2,1,0:T(8,128)(2,1)S(1)}, u32[]{:S(2)}, u32[]{:S(2)}) %collective-permute-start.8) | collective-permute-done | bytes 262176 | tf_op jit(solution)/shard_map/ppermute | solution.py:118
  106.4 4.2 %collective-permute-done.7 = bf16[2,8,64,128]{3,2,1,0:T(8,128)(2,1)S(1)} collective-permute-done((bf16[2,8,64,128]{3,2,1,0:T(8,128)(2,1)S(1)}, bf16[2,8,64,128]{3,2,1,0:T(8,128)(2,1)S(1)}, u32[]{:S(2)}, u32[]{:S(2)}) %collective-permute-start.7) | collective-permute-done | bytes 262176 | tf_op jit(solution)/shard_map/ppermute | solution.py:118
  111.6 1.2 collective-permute-done.9
  114.2 1.6 %pad_maximum_fusion = bf16[4,32,64,128]{3,2,1,0:T(8,128)(2,1)} fusion(bf16[1,32,64,128]{3,2,1,0:T(8,128)(2,1)S(1)} %get-tuple-element.26, bf16[2,32,64,128]{3,2,1,0:T(8,128)(2,1)S(1)} %bitcast.75, bf16[1,32,64,128]{3,2,1,0:T(8,128)(2,1)S(1)} %get-tuple-element.25), kind=kLoop, calls=%fused_computation.7 | loop fusion | flops 2097152 | bytes 4194304 | tf_op jit(solution)/shard_map/concatenate | solution.py:164
  (64 shorter events, 4.0 us)
Async XLA Ops:
  6.5 61.6 %all-gather.3.cloned.1.call-start = ((), (), s32[]{:S(2)}) async-start(), calls=%async_computation.2 | async-start | bytes 3981312 | tf_op jit(solution)/shard_map/all_gather | solution.py:120
  9.4 6.5 %copy-start.1 = (bf16[4,32,64,128]{3,2,1,0:T(8,128)(2,1)S(1)}, bf16[4,32,64,128]{3,2,1,0:T(8,128)(2,1)}, u32[]{:S(2)}) copy-start(bf16[4,32,64,128]{3,2,1,0:T(8,128)(2,1)} %param.3) | copy-start | bytes 6291460
  10.7 28.1 %all-to-all-start = ((bf16[8,2,10,32,128]{4,3,2,1,0:T(8,128)(2,1)}), bf16[8,2,10,32,128]{4,3,2,1,0:T(8,128)(2,1)S(1)}, u32[]{:S(2)}, u32[]{:S(2)}) async-start(bf16[8,2,10,32,128]{4,3,2,1,0:T(8,128)(2,1)} %fusion.5), calls=%async_computation | async-start | bytes 2621440 | tf_op jit(solution)/shard_map/all_to_all | solution.py:134
  18.0 30.7 %copy-start.2 = (f32[256]{0:T(256)S(1)}, f32[256]{0:T(256)}, u32[]{:S(2)}) copy-start(f32[256]{0:T(256)} %param.5) | copy-start | bytes 3076
  38.8 29.3 %all-to-all-start.1 = ((bf16[8,2,10,32,128]{4,3,2,1,0:T(8,128)(2,1)}), bf16[8,2,10,32,128]{4,3,2,1,0:T(8,128)(2,1)S(1)}, u32[]{:S(2)}, u32[]{:S(2)}) async-start(bf16[8,2,10,32,128]{4,3,2,1,0:T(8,128)(2,1)} %fusion.7), calls=%async_computation.1 | async-start | bytes 2621440 | tf_op jit(solution)/shard_map/all_to_all | solution.py:134
  43.8 24.3 %collective-permute-start = (bf16[8,1,10,32,128]{4,3,2,1,0:T(8,128)(2,1)}, bf16[8,1,10,32,128]{4,3,2,1,0:T(8,128)(2,1)S(1)}, u32[]{:S(2)}, u32[]{:S(2)}) collective-permute-start(bf16[8,1,10,32,128]{4,3,2,1,0:T(8,128)(2,1)} %get-tuple-element.24), channel_id=1, source_target_pairs={{0,8},{8,16},{16,24},{1,9},{9,17},{17,25},{2,10},{10,18},{18,26},{... | collective-permute-start | bytes 1966088 | tf_op jit(solution)/shard_map/ppermute | solution.py:155
  47.4 20.7 %collective-permute-start.1 = (bf16[8,1,10,32,128]{4,3,2,1,0:T(8,128)(2,1)}, bf16[8,1,10,32,128]{4,3,2,1,0:T(8,128)(2,1)}, u32[]{:S(2)}, u32[]{:S(2)}) collective-permute-start(bf16[8,1,10,32,128]{4,3,2,1,0:T(8,128)(2,1)} %get-tuple-element.23), channel_id=1, source_target_pairs={{8,0},{16,8},{24,16},{9,1},{17,9},{25,17},{10,2},{18,10},{26,18},{... | collective-permute-start | bytes 1966088 | tf_op jit(solution)/shard_map/ppermute | solution.py:154
  68.2 2.0 %copy-start = (bf16[24,3,3,32,256]{4,3,2,1,0:T(8,128)(2,1)S(1)}, bf16[24,3,3,32,256]{4,3,2,1,0:T(8,128)(2,1)}, u32[]{:S(2)}) copy-start(bf16[24,3,3,32,256]{4,3,2,1,0:T(8,128)(2,1)} %all-gather.3.cloned.1.call-done) | copy-start | bytes 10616836
  82.0 17.8 %collective-permute-start.4 = (bf16[2,8,64,128]{3,2,1,0:T(8,128)(2,1)S(1)}, bf16[2,8,64,128]{3,2,1,0:T(8,128)(2,1)S(1)}, u32[]{:S(2)}, u32[]{:S(2)}) collective-permute-start(bf16[2,8,64,128]{3,2,1,0:T(8,128)(2,1)S(1)} %get-tuple-element.16), channel_id=1, source_target_pairs={{0,6},{1,7},{2,4},{3,5},{4,2},{5,3},{6,0},{7,1},{8,14},{9,15},{10,... | collective-permute-start | bytes 786440 | tf_op jit(solution)/shard_map/ppermute | solution.py:118
  84.3 15.6 %collective-permute-start.3 = (bf16[2,8,64,128]{3,2,1,0:T(8,128)(2,1)S(1)}, bf16[2,8,64,128]{3,2,1,0:T(8,128)(2,1)S(1)}, u32[]{:S(2)}, u32[]{:S(2)}) collective-permute-start(bf16[2,8,64,128]{3,2,1,0:T(8,128)(2,1)S(1)} %get-tuple-element.15), channel_id=1, source_target_pairs={{0,4},{1,5},{2,6},{3,7},{4,0},{5,1},{6,2},{7,3},{8,12},{9,13},{10,... | collective-permute-start | bytes 786440 | tf_op jit(solution)/shard_map/ppermute | solution.py:118
  85.7 14.2 %collective-permute-start.2 = (bf16[2,8,64,128]{3,2,1,0:T(8,128)(2,1)S(1)}, bf16[2,8,64,128]{3,2,1,0:T(8,128)(2,1)S(1)}, u32[]{:S(2)}, u32[]{:S(2)}) collective-permute-start(bf16[2,8,64,128]{3,2,1,0:T(8,128)(2,1)S(1)} %get-tuple-element.14), channel_id=1, source_target_pairs={{0,2},{1,3},{2,0},{3,1},{4,6},{5,7},{6,4},{7,5},{8,10},{9,11},{10,... | collective-permute-start | bytes 786440 | tf_op jit(solution)/shard_map/ppermute | solution.py:118
  96.2 10.2 %collective-permute-start.8 = (bf16[2,8,64,128]{3,2,1,0:T(8,128)(2,1)S(1)}, bf16[2,8,64,128]{3,2,1,0:T(8,128)(2,1)S(1)}, u32[]{:S(2)}, u32[]{:S(2)}) collective-permute-start(bf16[2,8,64,128]{3,2,1,0:T(8,128)(2,1)S(1)} %get-tuple-element.20), channel_id=1, source_target_pairs={{0,6},{1,7},{2,4},{3,5},{4,2},{5,3},{6,0},{7,1},{8,14},{9,15},{10,... | collective-permute-start | bytes 786440 | tf_op jit(solution)/shard_map/ppermute | solution.py:118
  98.3 12.4 %collective-permute-start.7 = (bf16[2,8,64,128]{3,2,1,0:T(8,128)(2,1)S(1)}, bf16[2,8,64,128]{3,2,1,0:T(8,128)(2,1)S(1)}, u32[]{:S(2)}, u32[]{:S(2)}) collective-permute-start(bf16[2,8,64,128]{3,2,1,0:T(8,128)(2,1)S(1)} %get-tuple-element.19), channel_id=1, source_target_pairs={{0,4},{1,5},{2,6},{3,7},{4,0},{5,1},{6,2},{7,3},{8,12},{9,13},{10,... | collective-permute-start | bytes 786440 | tf_op jit(solution)/shard_map/ppermute | solution.py:118
  99.8 10.9 %collective-permute-start.6 = (bf16[2,8,64,128]{3,2,1,0:T(8,128)(2,1)S(1)}, bf16[2,8,64,128]{3,2,1,0:T(8,128)(2,1)S(1)}, u32[]{:S(2)}, u32[]{:S(2)}) collective-permute-start(bf16[2,8,64,128]{3,2,1,0:T(8,128)(2,1)S(1)} %get-tuple-element.18), channel_id=1, source_target_pairs={{0,2},{1,3},{2,0},{3,1},{4,6},{5,7},{6,4},{7,5},{8,10},{9,11},{10,... | collective-permute-start | bytes 786440 | tf_op jit(solution)/shard_map/ppermute | solution.py:118
  100.0 11.6 %collective-permute-start.5 = (bf16[4,2,8,32,128]{4,3,2,1,0:T(8,128)(2,1)S(1)}, bf16[4,2,8,32,128]{4,3,2,1,0:T(8,128)(2,1)S(1)}, u32[]{:S(2)}, u32[]{:S(2)}) collective-permute-start(bf16[4,2,8,32,128]{4,3,2,1,0:T(8,128)(2,1)S(1)} %pad_maximum_fusion.2), channel_id=1, source_target_pairs={{0,1},{1,0},{2,3},{3,2},{4,5},{5,4},{6,7},{7,6},{8,9},{9,8},{10,11... | collective-permute-start | bytes 1572872 | tf_op jit(solution)/shard_map/ppermute | solution.py:118
  110.8 2.0 %collective-permute-start.9 = (bf16[4,2,8,32,128]{4,3,2,1,0:T(8,128)(2,1)S(1)}, bf16[4,2,8,32,128]{4,3,2,1,0:T(8,128)(2,1)S(1)}, u32[]{:S(2)}, u32[]{:S(2)}) collective-permute-start(bf16[4,2,8,32,128]{4,3,2,1,0:T(8,128)(2,1)S(1)} %pad_maximum_fusion.3), channel_id=1, source_target_pairs={{0,1},{1,0},{2,3},{3,2},{4,5},{5,4},{6,7},{7,6},{8,9},{9,8},{10,11... | collective-permute-start | bytes 1572872 | tf_op jit(solution)/shard_map/ppermute | solution.py:118
Sparse Core Ops, SparseCore 0:
  9.2 56.0 all-gather.2

commit v5 on v4

v5 whole, which is shorter than its diff:
```python
import functools

import jax
import jax.numpy as jnp
from jax import lax
from jax.experimental import pallas as pl
from jax.experimental.pallas import tpu as pltpu
from jax.sharding import PartitionSpec as P

slope = 0.3
PAIR = 2


def conv_kernel(first, stride, count, plan, piece_count, tap_count, *refs):
    refs = list(refs)
    chip_ref = refs.pop(0)
    pieces = [refs.pop(0) for _ in range(piece_count)]
    tap_parts = [refs.pop(0) for _ in range(tap_count)]
    bias_ref = refs.pop(0)
    outs = refs[:-2]
    vol, vol_sem = refs[-2:]
    rows_in, total_in, cols = vol.shape[1:]
    total_out = bias_ref.shape[0]
    rows = rows_in - 2
    copies = []
    for n, (source, index, begin, slot, plane_count) in enumerate(plan):
        piece = pieces[source]
        chan = piece.shape[3]
        for s in range(piece.shape[0]):
            place = s if index is None else chip_ref[0] ^ index
            part = pl.ds(pl.multiple_of(place * chan, chan), chan)
            copies.append(
                pltpu.make_async_copy(
                    piece.at[s, pl.ds(begin, plane_count)],
                    vol.at[pl.ds(slot, plane_count), :, part, :],
                    vol_sem.at[n, s],
                )
            )
    for copy in copies:
        copy.start()
    for copy in copies:
        copy.wait()

    lane = lax.broadcasted_iota(jnp.int32, (total_out, cols), 1)
    per_plane = rows // PAIR
    block = total_out // len(outs)
    groups, size = tap_parts[0].shape[0], tap_parts[0].shape[4]

    def tile(step, carry):
        slot = step // per_plane
        plane = first + slot * stride
        row = (step % per_plane) * PAIR
        cells = []
        weights = []
        for a in range(3):
            for b in range(3):
                cells.append(jnp.concatenate([vol[plane + a, row + b + r] for r in range(PAIR)], axis=1))
                weights.append(
                    jnp.concatenate(
                        [part[g, a, b].reshape(3 * size, -1) for g in range(groups) for part in tap_parts], axis=0
                    )
                )
        total = jnp.dot(
            jnp.concatenate(weights, axis=1), jnp.concatenate(cells, axis=0), preferred_element_type=jnp.float32
        )
        for r in range(PAIR):
            part = total[:, r * cols : (r + 1) * cols].reshape(groups * tap_count, 3, size, cols)
            side = [part[:, c].reshape(total_out, cols) for c in range(3)]
            left = jnp.where(lane == 0, 0.0, pltpu.roll(side[0], 1, 1))
            right = jnp.where(lane == cols - 1, 0.0, pltpu.roll(side[2], cols - 1, 1))
            shifted = side[1] + left + right + bias_ref[...]
            done = jnp.where(shifted > 0, shifted, slope * shifted).astype(jnp.bfloat16)
            for n, out_ref in enumerate(outs):
                out_ref[slot, row + r] = done[n * block : (n + 1) * block]
        return carry

    lax.fori_loop(0, count * per_plane, tile, 0)


def convolve(first, stride, count, chip, pieces, plan, tap_parts, bias, blocks):
    rows_in, cols = pieces[0].shape[2], pieces[0].shape[4]
    in_chan = tap_parts[0].shape[5]
    total_out = bias.shape[0]
    rows = rows_in - 2
    depth = max(slot + n for _, _, _, slot, n in plan)
    wide_bias = jnp.broadcast_to(bias[:, None], (total_out, cols))
    macs = 27 * total_out * in_chan * count * rows * cols
    any_space = pl.BlockSpec(memory_space=pl.ANY)
    in_vmem = pl.BlockSpec(memory_space=pltpu.VMEM)
    in_smem = pl.BlockSpec(memory_space=pltpu.SMEM)
    return pl.pallas_call(
        functools.partial(conv_kernel, first, stride, count, plan, len(pieces), len(tap_parts)),
        out_shape=[jax.ShapeDtypeStruct((count, rows, total_out // blocks, cols), jnp.bfloat16)] * blocks,
        in_specs=[in_smem] + [any_space] * len(pieces) + [in_vmem] * (len(tap_parts) + 1),
        out_specs=[in_vmem] * blocks,
        scratch_shapes=[
            pltpu.VMEM((depth, rows_in, in_chan, cols), jnp.bfloat16),
            pltpu.SemaphoreType.DMA((len(plan), max(piece.shape[0] for piece in pieces))),
        ],
        cost_estimate=pl.CostEstimate(flops=2 * macs, bytes_accessed=10_000_000, transcendentals=0),
        compiler_params=pltpu.CompilerParams(vmem_limit_bytes=20 * 2**20),
    )(chip, *pieces, *tap_parts, wide_bias)


def body(features, kernel, bias_vector):
    planes, chan, y_cells, cols = features.shape
    out_chan = kernel.shape[3]
    parts = lax.axis_size("filt")
    slabs = lax.axis_size("slab")
    me = lax.axis_index("filt")
    core = me % 2
    rows = y_cells // parts
    chips = parts // 2
    aligned = chan % 16 == 0 and out_chan % 16 == 0
    across = list(range(0, parts, 2))

    def swap(array, k, axis="filt"):
        if k == 0:
            return array
        return lax.ppermute(array, axis, [(i, i ^ k) for i in range(lax.axis_size(axis))])

    def pack(piece):
        count = piece.shape[0]
        by_row = piece.transpose(0, 2, 1, 3).reshape(count, parts, rows, chan, cols).transpose(1, 0, 2, 3, 4)
        nothing = jnp.zeros((1, count, 1, chan, cols), piece.dtype)
        above = jnp.concatenate([nothing, by_row[:-1, :, -1:]])
        below = jnp.concatenate([by_row[1:, :, :1], nothing])
        return jnp.concatenate([above, by_row, below], axis=2)

    outer_rows = pack(jnp.concatenate([features[:1], features[-1:]]))
    inner_rows = pack(features[1:-1]).reshape(chips, 2, planes - 2, rows + 2, chan, cols)

    fetched = [swap(kernel, k) for k in across]
    outer_rows, inner_rows = lax.optimization_barrier((outer_rows, inner_rows))
    outer = lax.all_to_all(outer_rows, "filt", 0, 0)
    if not aligned:
        outer = outer.transpose(1, 2, 0, 3, 4).reshape(1, 2, rows + 2, parts * chan, cols)

    kept = lax.dynamic_index_in_dim(inner_rows, core, 1, keepdims=False)
    given = swap(lax.dynamic_index_in_dim(inner_rows, 1 - core, 1, keepdims=False), 1)
    both = jnp.concatenate([jnp.where(core == 0, kept, given), jnp.where(core == 0, given, kept)], axis=3)
    outer, both, fetched = lax.optimization_barrier((outer, both, fetched))
    inner = [swap(lax.dynamic_slice_in_dim(both, (me ^ k) // 2, 1, 0), k) for k in across]

    same = jnp.stack(fetched)
    tap_parts = [same, swap(same, 1)]
    if not aligned:
        joined = jnp.stack(tap_parts, axis=1).transpose(2, 3, 4, 0, 1, 5, 6)
        tap_parts = [joined.reshape(1, 3, 3, 3, parts * out_chan, -1)]
    order = jnp.stack([me ^ k ^ c for k in across for c in range(2)])
    bias = jnp.take(bias_vector.reshape(parts, out_chan), order, axis=0).reshape(-1)

    def send_back(results):
        count = results[0].shape[0]
        got = [swap(result, k) for result, k in zip(results, across)]
        mine = [block[:, :, :out_chan] for block in got]
        theirs = swap(jnp.stack([block[:, :, out_chan:] for block in got]), 1)
        final = jnp.zeros((count, y_cells, out_chan, cols), jnp.bfloat16)
        for n, k in enumerate(across):
            final = lax.dynamic_update_slice_in_dim(final, mine[n], (me ^ k) * rows, 1)
            final = lax.dynamic_update_slice_in_dim(final, theirs[n], (me ^ k ^ 1) * rows, 1)
        return final.transpose(0, 2, 1, 3)

    up = [(i, i + 1) for i in range(slabs - 1)]
    down = [(i + 1, i) for i in range(slabs - 1)]
    after = lax.ppermute(outer[:, :1], "slab", down)
    before = lax.ppermute(outer[:, 1:], "slab", up)

    chip = jnp.full((1,), me // 2, jnp.int32)

    def conv(first, stride, count, edges, shift):
        pieces = [outer, *inner, *edges]
        plan = [(0, None, 0, shift, 1), (0, None, 1, planes - 1 + shift, 1)]
        plan += [(1 + k, k, 0, 1 + shift, planes - 2) for k in range(chips)]
        plan += [(1 + chips + n, None, 0, n * (planes + 1), 1) for n in range(len(edges))]
        return convolve(first, stride, count, chip, pieces, tuple(plan), tap_parts, bias, chips)

    inside = send_back(conv(0, 1, planes - 2, [], 0))
    outside = send_back(conv(0, planes - 1, 2, [before, after], 1))
    return jnp.concatenate([outside[:1], inside, outside[1:]])


def solution(mesh):
    placed = (P("slab", "filt", None, None), P(None, None, None, "filt", None), P())
    return jax.shard_map(
        body, mesh=mesh, in_specs=placed, out_specs=P("slab", "filt", None, None), check_vma=False
    )
```

time: 123 us -> 125 us (1.016)
  between operations: 13.9 us -> 0.55 us
  waiting for transfers between devices: 51.7 us -> 57.4 us
  Pallas kernels: 22.2 us -> 25.6 us
  other arithmetic: 4.46 us -> 7.36 us
  starting transfers between devices: 21.1 us -> 23.7 us
    ppermute x8 -> x16, waiting for transfers between devices: 11.7 us -> 57.3 us  [swap(): lax.ppermute(array, axis, [(i, i ^ k) for i in range(lax.axis_size(axis))])]
    all_to_all x2 -> x1, waiting for transfers between devices: 39.3 us -> 0.01 us  [body(): outer = lax.all_to_all(outer_rows, 'filt', 0, 0)]
    ppermute x8 -> x16, starting transfers between devices: 7.51 us -> 12.8 us  [swap(): lax.ppermute(array, axis, [(i, i ^ k) for i in range(lax.axis_size(axis))])]
    all_to_all x2 -> x1, starting transfers between devices: 8.77 us -> 5.17 us  [body(): outer = lax.all_to_all(outer_rows, 'filt', 0, 0)]
    pallas_call x2, Pallas kernels: 22.2 us -> 25.6 us  [convolve(): pl.pallas_call(functools.partial(conv_kernel, first, stride, count, plan,...]
    another operation x0 -> x1, other arithmetic: none -> 1.5 us  [body(): same = jnp.stack(fetched)]
    unnamed x8 -> x9, local copies, waits for them, and re-layouts: 2.7 us -> 1.38 us
    concatenate x3 -> x4, other arithmetic: 2.66 us -> 2.89 us  [the longest x2 1.56 us: pack(): return jnp.concatenate([above, by_row, below], axis=2)]
  transfers between devices with their start and end apart: 13 -> 19, of which waited for: 5 -> 7; matrix products, arithmetic and copies ran while one was open for 7% -> 5% of each run, Pallas kernels for 8% -> 10%
where the time goes in v5:
time: 125 us; the launch traced here: 124 us
  waiting for transfers between devices  57.4 us (46%)
  Pallas kernels  25.6 us (20%)
  starting transfers between devices  23.7 us (19%)
  local copies, waits for them, and re-layouts  9.55 us (8%)
  other arithmetic  7.36 us (6%)
    ppermute x16, waiting for transfers between devices, swap(): lax.ppermute(array, axis, [(i, i ^ k) for i in range(lax.axis_size(axis))])  57.3 us
    pallas_call x2, Pallas kernels, convolve(): pl.pallas_call(functools.partial(conv_kernel, first, stride, count, plan,...  25.6 us
    ppermute x16, starting transfers between devices, swap(): lax.ppermute(array, axis, [(i, i ^ k) for i in range(lax.axis_size(axis))])  12.8 us
    all_to_all x1, starting transfers between devices, body(): outer = lax.all_to_all(outer_rows, 'filt', 0, 0)  5.17 us
    ppermute x1, starting transfers between devices, body(): before = lax.ppermute(outer[:, 1:], 'slab', up)  4.48 us
  transfers between devices with their start and end apart: 19, of which 7 were waited for; matrix products, arithmetic and copies ran while one was open for 5% of the time, Pallas kernels for 10%

profile of v5, /device:TPU:0, one launch (start us, length us, event | category | flops | bytes accessed | tf_op | source)
XLA Modules:
  0.0 124.2 jit_solution(5889200823981039753)
XLA Ops:
  0.0 1.3 %fusion.9 = (bf16[1,32,64,128]{3,2,1,0:T(8,128)(2,1)S(1)}, bf16[1,32,64,128]{3,2,1,0:T(8,128)(2,1)S(1)}) fusion(bf16[4,32,64,128]{3,2,1,0:T(8,128)(2,1)} %param.3), kind=kLoop, calls=%fused_computation.65 | loop fusion | bytes 2097152 | tf_op jit(solution)/shard_map/slice | solution.py:130
  4.5 1.3 %fusion.6 = bf16[8,2,10,32,128]{4,3,2,1,0:T(8,128)(2,1)} fusion(bf16[7,2,1,32,128]{4,3,2,1,0:T(8,128)(2,1)S(1)} %get-tuple-element.52, bf16[7,2,1,32,128]{4,3,2,1,0:T(8,128)(2,1)S(1)} %get-tuple-element.51, bf16[8,2,8,32,128]{4,3,2,1,0:T(8,128)(2,1)S(1)} %bitcast.77), kind=kLoop, calls=%fused_computation.13 | loop fusion | flops 6553600 | bytes 2588672 | tf_op jit(solution)/shard_map/concatenate | solution.py:128
  5.8 5.2 %all-to-all-start = ((bf16[8,2,10,32,128]{4,3,2,1,0:T(8,128)(2,1)}), bf16[8,2,10,32,128]{4,3,2,1,0:T(8,128)(2,1)S(1)}, u32[]{:S(2)}, u32[]{:S(2)}) async-start(bf16[8,2,10,32,128]{4,3,2,1,0:T(8,128)(2,1)} %fusion.6), calls=%async_computation | async-start | bytes 2621440 | tf_op jit(solution)/shard_map/all_to_all | solution.py:135
  11.6 1.7 %collective-permute-start.1 = (bf16[3,3,3,32,256]{4,3,2,1,0:T(8,128)(2,1)}, bf16[3,3,3,32,256]{4,3,2,1,0:T(8,128)(2,1)}, u32[]{:S(2)}, u32[]{:S(2)}) collective-permute-start(bf16[3,3,3,32,256]{4,3,2,1,0:T(8,128)(2,1)} %param.4), channel_id=1, source_target_pairs={{0,2},{1,3},{2,0},{3,1},{4,6},{5,7},{6,4},{7,5},{8,10},{9,11},{10,... | collective-permute-start | bytes 1327112 | tf_op jit(solution)/shard_map/ppermute | solution.py:120
  13.3 1.5 %collective-permute-start.2 = (bf16[3,3,3,32,256]{4,3,2,1,0:T(8,128)(2,1)}, bf16[3,3,3,32,256]{4,3,2,1,0:T(8,128)(2,1)}, u32[]{:S(2)}, u32[]{:S(2)}) collective-permute-start(bf16[3,3,3,32,256]{4,3,2,1,0:T(8,128)(2,1)} %param.4), channel_id=1, source_target_pairs={{0,4},{1,5},{2,6},{3,7},{4,0},{5,1},{6,2},{7,3},{8,12},{9,13},{10,... | collective-permute-start | bytes 1327112 | tf_op jit(solution)/shard_map/ppermute | solution.py:120
  15.1 1.2 bitcast_select_fusion.1
  16.3 1.2 pad_maximum_fusion.2
  17.5 20.9 %collective-permute-done.1 = bf16[3,3,3,32,256]{4,3,2,1,0:T(8,128)(2,1)} collective-permute-done((bf16[3,3,3,32,256]{4,3,2,1,0:T(8,128)(2,1)}, bf16[3,3,3,32,256]{4,3,2,1,0:T(8,128)(2,1)}, u32[]{:S(2)}, u32[]{:S(2)}) %collective-permute-start.1) | collective-permute-done | bytes 442400 | tf_op jit(solution)/shard_map/ppermute | solution.py:120
  38.4 9.9 %collective-permute-done.3 = bf16[3,3,3,32,256]{4,3,2,1,0:T(8,128)(2,1)} collective-permute-done((bf16[3,3,3,32,256]{4,3,2,1,0:T(8,128)(2,1)}, bf16[3,3,3,32,256]{4,3,2,1,0:T(8,128)(2,1)}, u32[]{:S(2)}, u32[]{:S(2)}) %collective-permute-start.3) | collective-permute-done | bytes 442400 | tf_op jit(solution)/shard_map/ppermute | solution.py:120
  48.3 1.5 %pad_maximum_fusion.1.refs_8_.refs_6_ = bf16[4,3,3,3,32,256]{5,4,3,2,1,0:T(8,128)(2,1)S(1)} fusion(bf16[1,3,3,3,32,256]{5,4,3,2,1,0:T(8,128)(2,1)} %bitcast.15, bf16[1,3,3,3,32,256]{5,4,3,2,1,0:T(8,128)(2,1)} %bitcast.14, bf16[1,3,3,3,32,256]{5,4,3,2,1,0:T(8,128)(2,1)} %bitcast.13, bf16[1,3,3,3,32,256]{5,4,3,2,1,0:T(8,128)(2,1)S(1)} %bitcast.83), kind=kLoop, calls=%fused_computation.10 | loop fusion | flops 2654208 | bytes 3538944 | tf_op jit(solution)/shard_map/stack | solution.py:145
  50.1 1.3 %fusion.10 = (bf16[8,1,10,32,128]{4,3,2,1,0:T(8,128)(2,1)}, bf16[8,1,10,32,128]{4,3,2,1,0:T(8,128)(2,1)}) fusion(bf16[8,2,10,32,128]{4,3,2,1,0:T(8,128)(2,1)S(1)} %all-to-all-done.refs_1_), kind=kLoop, calls=%fused_computation.66 | loop fusion | bytes 2621440 | tf_op jit(solution)/shard_map/slice | solution.py:166
  51.4 4.5 %collective-permute-start.7 = (bf16[8,1,10,32,128]{4,3,2,1,0:T(8,128)(2,1)}, bf16[8,1,10,32,128]{4,3,2,1,0:T(8,128)(2,1)}, u32[]{:S(2)}, u32[]{:S(2)}) collective-permute-start(bf16[8,1,10,32,128]{4,3,2,1,0:T(8,128)(2,1)} %get-tuple-element.42), channel_id=1, source_target_pairs={{0,8},{8,16},{16,24},{1,9},{9,17},{17,25},{2,10},{10,18},{18,26},{... | collective-permute-start | bytes 1966088 | tf_op jit(solution)/shard_map/ppermute | solution.py:167
  55.9 1.3 %collective-permute-start.8 = (bf16[8,1,10,32,128]{4,3,2,1,0:T(8,128)(2,1)}, bf16[8,1,10,32,128]{4,3,2,1,0:T(8,128)(2,1)}, u32[]{:S(2)}, u32[]{:S(2)}) collective-permute-start(bf16[8,1,10,32,128]{4,3,2,1,0:T(8,128)(2,1)} %get-tuple-element.41), channel_id=1, source_target_pairs={{8,0},{16,8},{24,16},{9,1},{17,9},{25,17},{10,2},{18,10},{26,18},{... | collective-permute-start | bytes 1966088 | tf_op jit(solution)/shard_map/ppermute | solution.py:166
  59.4 8.9 %collective-permute-done.4.refs_3_ = bf16[1,2,10,64,128]{4,3,2,1,0:T(8,128)(2,1)} collective-permute-done((bf16[1,2,10,64,128]{4,3,2,1,0:T(8,128)(2,1)}, bf16[1,2,10,64,128]{4,3,2,1,0:T(8,128)(2,1)}, u32[]{:S(2)}, u32[]{:S(2)}) %collective-permute-start.4) | collective-permute-done | bytes 327712 | tf_op jit(solution)/shard_map/ppermute | solution.py:120
  69.3 9.0 %collective-permute-done.6.refs_5_ = bf16[1,2,10,64,128]{4,3,2,1,0:T(8,128)(2,1)} collective-permute-done((bf16[1,2,10,64,128]{4,3,2,1,0:T(8,128)(2,1)}, bf16[1,2,10,64,128]{4,3,2,1,0:T(8,128)(2,1)}, u32[]{:S(2)}, u32[]{:S(2)}) %collective-permute-start.6) | collective-permute-done | bytes 327712 | tf_op jit(solution)/shard_map/ppermute | solution.py:120
  78.4 13.1 %shard_map.37 = (bf16[2,8,64,128]{3,2,1,0:T(8,128)(2,1)S(1)}, bf16[2,8,64,128]{3,2,1,0:T(8,128)(2,1)S(1)}, bf16[2,8,64,128]{3,2,1,0:T(8,128)(2,1)S(1)}, bf16[2,8,64,128]{3,2,1,0:T(8,128)(2,1)S(1)}) custom-call(s32[1]{0:T(128)} %bitcast.refs_0_, bf16[8,2,10,32,128]{4,3,2,1,0:T(8,128)(2,1)S(1)} %all-to-all-done.refs_1_, ...), custom_call_target="tpu_custom_call" | custom-call | flops 7247757312 | bytes 10000000 | tf_op jit(solution)/shard_map/pallas_call | solution.py:91
  91.9 1.7 %collective-permute-start.11 = (bf16[2,8,64,128]{3,2,1,0:T(8,128)(2,1)S(1)}, bf16[2,8,64,128]{3,2,1,0:T(8,128)(2,1)S(1)}, u32[]{:S(2)}, u32[]{:S(2)}) collective-permute-start(bf16[2,8,64,128]{3,2,1,0:T(8,128)(2,1)S(1)} %get-tuple-element.31), channel_id=1, source_target_pairs={{0,4},{1,5},{2,6},{3,7},{4,0},{5,1},{6,2},{7,3},{8,12},{9,13},{10,... | collective-permute-start | bytes 786440 | tf_op jit(solution)/shard_map/ppermute | solution.py:120
  93.6 1.5 %collective-permute-start.10 = (bf16[2,8,64,128]{3,2,1,0:T(8,128)(2,1)S(1)}, bf16[2,8,64,128]{3,2,1,0:T(8,128)(2,1)S(1)}, u32[]{:S(2)}, u32[]{:S(2)}) collective-permute-start(bf16[2,8,64,128]{3,2,1,0:T(8,128)(2,1)S(1)} %get-tuple-element.30), channel_id=1, source_target_pairs={{0,2},{1,3},{2,0},{3,1},{4,6},{5,7},{6,4},{7,5},{8,10},{9,11},{10,... | collective-permute-start | bytes 786440 | tf_op jit(solution)/shard_map/ppermute | solution.py:120
  95.0 12.6 %shard_map.38 = (bf16[2,8,64,128]{3,2,1,0:T(8,128)(2,1)S(1)}, bf16[2,8,64,128]{3,2,1,0:T(8,128)(2,1)S(1)}, bf16[2,8,64,128]{3,2,1,0:T(8,128)(2,1)S(1)}, bf16[2,8,64,128]{3,2,1,0:T(8,128)(2,1)S(1)}) custom-call(s32[1]{0:T(128)} %bitcast.refs_0_, bf16[8,2,10,32,128]{4,3,2,1,0:T(8,128)(2,1)S(1)} %all-to-all-done.refs_1_, ...), custom_call_target="tpu_custom_call" | custom-call | flops 7247757312 | bytes 10000000 | tf_op jit(solution)/shard_map/pallas_call | solution.py:91
  108.1 1.7 %collective-permute-start.15 = (bf16[2,8,64,128]{3,2,1,0:T(8,128)(2,1)S(1)}, bf16[2,8,64,128]{3,2,1,0:T(8,128)(2,1)S(1)}, u32[]{:S(2)}, u32[]{:S(2)}) collective-permute-start(bf16[2,8,64,128]{3,2,1,0:T(8,128)(2,1)S(1)} %get-tuple-element.35), channel_id=1, source_target_pairs={{0,4},{1,5},{2,6},{3,7},{4,0},{5,1},{6,2},{7,3},{8,12},{9,13},{10,... | collective-permute-start | bytes 786440 | tf_op jit(solution)/shard_map/ppermute | solution.py:120
  109.8 1.5 %collective-permute-start.14 = (bf16[2,8,64,128]{3,2,1,0:T(8,128)(2,1)S(1)}, bf16[2,8,64,128]{3,2,1,0:T(8,128)(2,1)S(1)}, u32[]{:S(2)}, u32[]{:S(2)}) collective-permute-start(bf16[2,8,64,128]{3,2,1,0:T(8,128)(2,1)S(1)} %get-tuple-element.34), channel_id=1, source_target_pairs={{0,2},{1,3},{2,0},{3,1},{4,6},{5,7},{6,4},{7,5},{8,10},{9,11},{10,... | collective-permute-start | bytes 786440 | tf_op jit(solution)/shard_map/ppermute | solution.py:120
  111.5 5.7 %collective-permute-done.16 = bf16[2,8,64,128]{3,2,1,0:T(8,128)(2,1)S(1)} collective-permute-done((bf16[2,8,64,128]{3,2,1,0:T(8,128)(2,1)S(1)}, bf16[2,8,64,128]{3,2,1,0:T(8,128)(2,1)S(1)}, u32[]{:S(2)}, u32[]{:S(2)}) %collective-permute-start.16) | collective-permute-done | bytes 262176 | tf_op jit(solution)/shard_map/ppermute | solution.py:120
  117.3 1.8 %collective-permute-done.15 = bf16[2,8,64,128]{3,2,1,0:T(8,128)(2,1)S(1)} collective-permute-done((bf16[2,8,64,128]{3,2,1,0:T(8,128)(2,1)S(1)}, bf16[2,8,64,128]{3,2,1,0:T(8,128)(2,1)S(1)}, u32[]{:S(2)}, u32[]{:S(2)}) %collective-permute-start.15) | collective-permute-done | bytes 262176 | tf_op jit(solution)/shard_map/ppermute | solution.py:120
  122.6 1.6 %pad_maximum_fusion = bf16[4,32,64,128]{3,2,1,0:T(8,128)(2,1)} fusion(bf16[1,32,64,128]{3,2,1,0:T(8,128)(2,1)S(1)} %get-tuple-element.48, bf16[2,32,64,128]{3,2,1,0:T(8,128)(2,1)S(1)} %bitcast.82, bf16[1,32,64,128]{3,2,1,0:T(8,128)(2,1)S(1)} %get-tuple-element.47), kind=kLoop, calls=%fused_computation.9 | loop fusion | flops 2097152 | bytes 4194304 | tf_op jit(solution)/shard_map/concatenate | solution.py:180
  (82 shorter events, 12.1 us)
Async XLA Ops:
  2.1 1.2 slice-start
  5.8 42.5 %all-to-all-start = ((bf16[8,2,10,32,128]{4,3,2,1,0:T(8,128)(2,1)}), bf16[8,2,10,32,128]{4,3,2,1,0:T(8,128)(2,1)S(1)}, u32[]{:S(2)}, u32[]{:S(2)}) async-start(bf16[8,2,10,32,128]{4,3,2,1,0:T(8,128)(2,1)} %fusion.6), calls=%async_computation | async-start | bytes 2621440 | tf_op jit(solution)/shard_map/all_to_all | solution.py:135
  11.0 4.1 %collective-permute-start = (bf16[4,2,10,32,128]{4,3,2,1,0:T(8,128)(2,1)S(1)}, bf16[4,2,10,32,128]{4,3,2,1,0:T(8,128)(2,1)}, u32[]{:S(2)}, u32[]{:S(2)}) collective-permute-start(bf16[4,2,10,32,128]{4,3,2,1,0:T(8,128)(2,1)S(1)} %dynamic-slice_bitcast_fusion), channel_id=1, source_target_pairs={{0,1},{1,0},{2,3},{3,2},{4,5},{5,4},{6,7},{7,6},{8,9},{9,8},{10,11... | collective-permute-start | bytes 1966088 | tf_op jit(solution)/shard_map/ppermute | solution.py:120
  11.6 26.8 %collective-permute-start.1 = (bf16[3,3,3,32,256]{4,3,2,1,0:T(8,128)(2,1)}, bf16[3,3,3,32,256]{4,3,2,1,0:T(8,128)(2,1)}, u32[]{:S(2)}, u32[]{:S(2)}) collective-permute-start(bf16[3,3,3,32,256]{4,3,2,1,0:T(8,128)(2,1)} %param.4), channel_id=1, source_target_pairs={{0,2},{1,3},{2,0},{3,1},{4,6},{5,7},{6,4},{7,5},{8,10},{9,11},{10,... | collective-permute-start | bytes 1327112 | tf_op jit(solution)/shard_map/ppermute | solution.py:120
  13.3 25.1 %collective-permute-start.2 = (bf16[3,3,3,32,256]{4,3,2,1,0:T(8,128)(2,1)}, bf16[3,3,3,32,256]{4,3,2,1,0:T(8,128)(2,1)}, u32[]{:S(2)}, u32[]{:S(2)}) collective-permute-start(bf16[3,3,3,32,256]{4,3,2,1,0:T(8,128)(2,1)} %param.4), channel_id=1, source_target_pairs={{0,4},{1,5},{2,6},{3,7},{4,0},{5,1},{6,2},{7,3},{8,12},{9,13},{10,... | collective-permute-start | bytes 1327112 | tf_op jit(solution)/shard_map/ppermute | solution.py:120
  14.8 33.6 %collective-permute-start.3 = (bf16[3,3,3,32,256]{4,3,2,1,0:T(8,128)(2,1)}, bf16[3,3,3,32,256]{4,3,2,1,0:T(8,128)(2,1)}, u32[]{:S(2)}, u32[]{:S(2)}) collective-permute-start(bf16[3,3,3,32,256]{4,3,2,1,0:T(8,128)(2,1)} %param.4), channel_id=1, source_target_pairs={{0,6},{1,7},{2,4},{3,5},{4,2},{5,3},{6,0},{7,1},{8,14},{9,15},{10,... | collective-permute-start | bytes 1327112 | tf_op jit(solution)/shard_map/ppermute | solution.py:120
  16.3 32.0 %copy-start.1 = (bf16[3,3,3,32,256]{4,3,2,1,0:T(8,128)(2,1)S(1)}, bf16[3,3,3,32,256]{4,3,2,1,0:T(8,128)(2,1)}, u32[]{:S(2)}) copy-start(bf16[3,3,3,32,256]{4,3,2,1,0:T(8,128)(2,1)} %param.4) | copy-start | bytes 1327108
  49.8 28.5 %collective-permute-start.9 = (bf16[4,3,3,3,32,256]{5,4,3,2,1,0:T(8,128)(2,1)S(1)}, bf16[4,3,3,3,32,256]{5,4,3,2,1,0:T(8,128)(2,1)}, u32[]{:S(2)}, u32[]{:S(2)}) collective-permute-start(bf16[4,3,3,3,32,256]{5,4,3,2,1,0:T(8,128)(2,1)S(1)} %pad_maximum_fusion.1.refs_8_.refs_6_), channel_id=1, source_target_pairs={{0,1},{1,0},{2,3},{3,2},{4,5},{5,4},{6,7},{7,6},{8,9},{9,8},{10,11... | collective-permute-start | bytes 5308424 | tf_op jit(solution)/shard_map/ppermute | solution.py:120
  50.1 7.1 %copy-start = (bf16[4,2,10,64,128]{4,3,2,1,0:T(8,128)(2,1)S(1)}, bf16[4,2,10,64,128]{4,3,2,1,0:T(8,128)(2,1)}, u32[]{:S(2)}) copy-start(bf16[4,2,10,64,128]{4,3,2,1,0:T(8,128)(2,1)} %pad_maximum_fusion.2) | copy-start | bytes 3932164
  51.4 7.3 %copy-start.2 = (f32[256]{0:T(256)S(1)}, f32[256]{0:T(256)}, u32[]{:S(2)}) copy-start(f32[256]{0:T(256)} %param.5) | copy-start | bytes 3076
  51.4 26.9 %collective-permute-start.7 = (bf16[8,1,10,32,128]{4,3,2,1,0:T(8,128)(2,1)}, bf16[8,1,10,32,128]{4,3,2,1,0:T(8,128)(2,1)}, u32[]{:S(2)}, u32[]{:S(2)}) collective-permute-start(bf16[8,1,10,32,128]{4,3,2,1,0:T(8,128)(2,1)} %get-tuple-element.42), channel_id=1, source_target_pairs={{0,8},{8,16},{16,24},{1,9},{9,17},{17,25},{2,10},{10,18},{18,26},{... | collective-permute-start | bytes 1966088 | tf_op jit(solution)/shard_map/ppermute | solution.py:167
  55.9 22.4 %collective-permute-start.8 = (bf16[8,1,10,32,128]{4,3,2,1,0:T(8,128)(2,1)}, bf16[8,1,10,32,128]{4,3,2,1,0:T(8,128)(2,1)}, u32[]{:S(2)}, u32[]{:S(2)}) collective-permute-start(bf16[8,1,10,32,128]{4,3,2,1,0:T(8,128)(2,1)} %get-tuple-element.41), channel_id=1, source_target_pairs={{8,0},{16,8},{24,16},{9,1},{17,9},{25,17},{10,2},{18,10},{26,18},{... | collective-permute-start | bytes 1966088 | tf_op jit(solution)/shard_map/ppermute | solution.py:166
  58.2 10.0 %collective-permute-start.4 = (bf16[1,2,10,64,128]{4,3,2,1,0:T(8,128)(2,1)}, bf16[1,2,10,64,128]{4,3,2,1,0:T(8,128)(2,1)}, u32[]{:S(2)}, u32[]{:S(2)}) collective-permute-start(bf16[1,2,10,64,128]{4,3,2,1,0:T(8,128)(2,1)} %get-tuple-element.45), channel_id=1, source_target_pairs={{0,2},{1,3},{2,0},{3,1},{4,6},{5,7},{6,4},{7,5},{8,10},{9,11},{10,... | collective-permute-start | bytes 983048 | tf_op jit(solution)/shard_map/ppermute | solution.py:120
  58.9 10.4 %collective-permute-start.5 = (bf16[1,2,10,64,128]{4,3,2,1,0:T(8,128)(2,1)}, bf16[1,2,10,64,128]{4,3,2,1,0:T(8,128)(2,1)}, u32[]{:S(2)}, u32[]{:S(2)}) collective-permute-start(bf16[1,2,10,64,128]{4,3,2,1,0:T(8,128)(2,1)} %get-tuple-element.44), channel_id=1, source_target_pairs={{0,4},{1,5},{2,6},{3,7},{4,0},{5,1},{6,2},{7,3},{8,12},{9,13},{10,... | collective-permute-start | bytes 983048 | tf_op jit(solution)/shard_map/ppermute | solution.py:120
  68.2 10.1 %collective-permute-start.6 = (bf16[1,2,10,64,128]{4,3,2,1,0:T(8,128)(2,1)}, bf16[1,2,10,64,128]{4,3,2,1,0:T(8,128)(2,1)}, u32[]{:S(2)}, u32[]{:S(2)}) collective-permute-start(bf16[1,2,10,64,128]{4,3,2,1,0:T(8,128)(2,1)} %get-tuple-element.43), channel_id=1, source_target_pairs={{0,6},{1,7},{2,4},{3,5},{4,2},{5,3},{6,0},{7,1},{8,14},{9,15},{10,... | collective-permute-start | bytes 983048 | tf_op jit(solution)/shard_map/ppermute | solution.py:120
  91.5 18.3 %collective-permute-start.12 = (bf16[2,8,64,128]{3,2,1,0:T(8,128)(2,1)S(1)}, bf16[2,8,64,128]{3,2,1,0:T(8,128)(2,1)S(1)}, u32[]{:S(2)}, u32[]{:S(2)}) collective-permute-start(bf16[2,8,64,128]{3,2,1,0:T(8,128)(2,1)S(1)} %get-tuple-element.32), channel_id=1, source_target_pairs={{0,6},{1,7},{2,4},{3,5},{4,2},{5,3},{6,0},{7,1},{8,14},{9,15},{10,... | collective-permute-start | bytes 786440 | tf_op jit(solution)/shard_map/ppermute | solution.py:120
  91.9 19.4 %collective-permute-start.11 = (bf16[2,8,64,128]{3,2,1,0:T(8,128)(2,1)S(1)}, bf16[2,8,64,128]{3,2,1,0:T(8,128)(2,1)S(1)}, u32[]{:S(2)}, u32[]{:S(2)}) collective-permute-start(bf16[2,8,64,128]{3,2,1,0:T(8,128)(2,1)S(1)} %get-tuple-element.31), channel_id=1, source_target_pairs={{0,4},{1,5},{2,6},{3,7},{4,0},{5,1},{6,2},{7,3},{8,12},{9,13},{10,... | collective-permute-start | bytes 786440 | tf_op jit(solution)/shard_map/ppermute | solution.py:120
  93.6 17.8 %collective-permute-start.10 = (bf16[2,8,64,128]{3,2,1,0:T(8,128)(2,1)S(1)}, bf16[2,8,64,128]{3,2,1,0:T(8,128)(2,1)S(1)}, u32[]{:S(2)}, u32[]{:S(2)}) collective-permute-start(bf16[2,8,64,128]{3,2,1,0:T(8,128)(2,1)S(1)} %get-tuple-element.30), channel_id=1, source_target_pairs={{0,2},{1,3},{2,0},{3,1},{4,6},{5,7},{6,4},{7,5},{8,10},{9,11},{10,... | collective-permute-start | bytes 786440 | tf_op jit(solution)/shard_map/ppermute | solution.py:120
  107.6 9.6 %collective-permute-start.16 = (bf16[2,8,64,128]{3,2,1,0:T(8,128)(2,1)S(1)}, bf16[2,8,64,128]{3,2,1,0:T(8,128)(2,1)S(1)}, u32[]{:S(2)}, u32[]{:S(2)}) collective-permute-start(bf16[2,8,64,128]{3,2,1,0:T(8,128)(2,1)S(1)} %get-tuple-element.36), channel_id=1, source_target_pairs={{0,6},{1,7},{2,4},{3,5},{4,2},{5,3},{6,0},{7,1},{8,14},{9,15},{10,... | collective-permute-start | bytes 786440 | tf_op jit(solution)/shard_map/ppermute | solution.py:120
  108.1 11.0 %collective-permute-start.15 = (bf16[2,8,64,128]{3,2,1,0:T(8,128)(2,1)S(1)}, bf16[2,8,64,128]{3,2,1,0:T(8,128)(2,1)S(1)}, u32[]{:S(2)}, u32[]{:S(2)}) collective-permute-start(bf16[2,8,64,128]{3,2,1,0:T(8,128)(2,1)S(1)} %get-tuple-element.35), channel_id=1, source_target_pairs={{0,4},{1,5},{2,6},{3,7},{4,0},{5,1},{6,2},{7,3},{8,12},{9,13},{10,... | collective-permute-start | bytes 786440 | tf_op jit(solution)/shard_map/ppermute | solution.py:120
  109.8 9.4 %collective-permute-start.14 = (bf16[2,8,64,128]{3,2,1,0:T(8,128)(2,1)S(1)}, bf16[2,8,64,128]{3,2,1,0:T(8,128)(2,1)S(1)}, u32[]{:S(2)}, u32[]{:S(2)}) collective-permute-start(bf16[2,8,64,128]{3,2,1,0:T(8,128)(2,1)S(1)} %get-tuple-element.34), channel_id=1, source_target_pairs={{0,2},{1,3},{2,0},{3,1},{4,6},{5,7},{6,4},{7,5},{8,10},{9,11},{10,... | collective-permute-start | bytes 786440 | tf_op jit(solution)/shard_map/ppermute | solution.py:120
  111.5 8.5 %collective-permute-start.13 = (bf16[4,2,8,32,128]{4,3,2,1,0:T(8,128)(2,1)S(1)}, bf16[4,2,8,32,128]{4,3,2,1,0:T(8,128)(2,1)S(1)}, u32[]{:S(2)}, u32[]{:S(2)}) collective-permute-start(bf16[4,2,8,32,128]{4,3,2,1,0:T(8,128)(2,1)S(1)} %pad_maximum_fusion.4), channel_id=1, source_target_pairs={{0,1},{1,0},{2,3},{3,2},{4,5},{5,4},{6,7},{7,6},{8,9},{9,8},{10,11... | collective-permute-start | bytes 1572872 | tf_op jit(solution)/shard_map/ppermute | solution.py:120
  119.2 2.0 %collective-permute-start.17 = (bf16[4,2,8,32,128]{4,3,2,1,0:T(8,128)(2,1)S(1)}, bf16[4,2,8,32,128]{4,3,2,1,0:T(8,128)(2,1)S(1)}, u32[]{:S(2)}, u32[]{:S(2)}) collective-permute-start(bf16[4,2,8,32,128]{4,3,2,1,0:T(8,128)(2,1)S(1)} %pad_maximum_fusion.5), channel_id=1, source_target_pairs={{0,1},{1,0},{2,3},{3,2},{4,5},{5,4},{6,7},{7,6},{8,9},{9,8},{10,11... | collective-permute-start | bytes 1572872 | tf_op jit(solution)/shard_map/ppermute | solution.py:120

commit v6 on v5

--- a/solution.py
+++ b/solution.py
@@ -11,9 +11,63 @@
 PAIR = 2
 
 
+def cut_kernel(rows, me_ref, vol_ref, nothing_ref, *refs):
+    outs, sems = refs[:-2], refs[-2:]
+    planes, y_cells = vol_ref.shape[:2]
+    parts = y_cells // rows
+    main, edge = sems
+    me = me_ref[0]
+
+    def moves(out, n, block, source):
+        top = block * rows
+        return [
+            (None, vol_ref.at[source, pl.ds(top, rows)], out.at[:, pl.ds(1, rows)], main.at[n]),
+            (block > 0, vol_ref.at[source, pl.ds(jnp.maximum(top - 1, 0), 1)], out.at[:, pl.ds(0, 1)], edge.at[n, 0]),
+            (block == 0, nothing_ref, out.at[:, pl.ds(0, 1)], edge.at[n, 0]),
+            (
+                block < parts - 1,
+                vol_ref.at[source, pl.ds(jnp.minimum(top + rows, y_cells - 1), 1)],
+                out.at[:, pl.ds(rows + 1, 1)],
+                edge.at[n, 1],
+            ),
+            (block == parts - 1, nothing_ref, out.at[:, pl.ds(rows + 1, 1)], edge.at[n, 1]),
+        ]
+
+    work = []
+    n = 0
+    for source, (kept, given) in ((pl.ds(0, 2), outs[:2]), (pl.ds(2, planes - 2), outs[2:])):
+        for k in range(parts // 2):
+            for core, out in enumerate((kept, given)):
+                work += moves(out.at[k], n, me ^ (2 * k + core), source)
+                n += 1
+    for act in ("start", "wait"):
+        for condition, src, dst, sem in work:
+            copy = pltpu.make_async_copy(src, dst, sem)
+            if condition is None:
+                getattr(copy, act)()
+            else:
+                pl.when(condition)(getattr(copy, act))
+
+
+def cut(me, volume, parts):
+    planes, y_cells, chan, cols = volume.shape
+    rows = y_cells // parts
+    count = planes - 2
+    any_space = pl.BlockSpec(memory_space=pl.ANY)
+    assert count == 2
+    shape = jax.ShapeDtypeStruct((parts // 2, 2, rows + 2, chan, cols), volume.dtype)
+    return pl.pallas_call(
+        functools.partial(cut_kernel, rows),
+        out_shape=[shape] * 4,
+        in_specs=[pl.BlockSpec(memory_space=pltpu.SMEM), any_space, any_space],
+        out_specs=[any_space] * 4,
+        scratch_shapes=[pltpu.SemaphoreType.DMA((2 * parts,)), pltpu.SemaphoreType.DMA((2 * parts, 2))],
+    )(jnp.full((1,), me, jnp.int32), volume, jnp.zeros((2, 1, chan, cols), volume.dtype))
+
+
 def conv_kernel(first, stride, count, plan, piece_count, tap_count, *refs):
     refs = list(refs)
-    chip_ref = refs.pop(0)
+    place_ref = refs.pop(0)
     pieces = [refs.pop(0) for _ in range(piece_count)]
     tap_parts = [refs.pop(0) for _ in range(tap_count)]
     bias_ref = refs.pop(0)
@@ -24,17 +78,14 @@
     rows = rows_in - 2
     copies = []
     for n, (source, index, begin, slot, plane_count) in enumerate(plan):
-        piece = pieces[source]
-        chan = piece.shape[3]
-        for s in range(piece.shape[0]):
-            place = s if index is None else chip_ref[0] ^ index
+        piece = pieces[source].at[pl.ds(begin, plane_count)]
+        into = vol.at[pl.ds(slot, plane_count)]
+        chan = piece.shape[2] // (1 if index is None else 2)
+        for c in range(piece.shape[2] // chan):
+            place = 0 if index is None else place_ref[2 * index + c]
             part = pl.ds(pl.multiple_of(place * chan, chan), chan)
             copies.append(
-                pltpu.make_async_copy(
-                    piece.at[s, pl.ds(begin, plane_count)],
-                    vol.at[pl.ds(slot, plane_count), :, part, :],
-                    vol_sem.at[n, s],
-                )
+                pltpu.make_async_copy(piece.at[:, :, pl.ds(c * chan, chan)], into.at[:, :, part], vol_sem.at[n, c])
             )
     for copy in copies:
         copy.start()
@@ -77,8 +128,8 @@
     lax.fori_loop(0, count * per_plane, tile, 0)
 
 
-def convolve(first, stride, count, chip, pieces, plan, tap_parts, bias, blocks):
-    rows_in, cols = pieces[0].shape[2], pieces[0].shape[4]
+def convolve(first, stride, count, places, pieces, plan, tap_parts, bias, blocks):
+    rows_in, cols = pieces[0].shape[1], pieces[0].shape[3]
     in_chan = tap_parts[0].shape[5]
     total_out = bias.shape[0]
     rows = rows_in - 2
@@ -95,11 +146,15 @@
         out_specs=[in_vmem] * blocks,
         scratch_shapes=[
             pltpu.VMEM((depth, rows_in, in_chan, cols), jnp.bfloat16),
-            pltpu.SemaphoreType.DMA((len(plan), max(piece.shape[0] for piece in pieces))),
+            pltpu.SemaphoreType.DMA((len(plan), 2)),
         ],
         cost_estimate=pl.CostEstimate(flops=2 * macs, bytes_accessed=10_000_000, transcendentals=0),
         compiler_params=pltpu.CompilerParams(vmem_limit_bytes=20 * 2**20),
-    )(chip, *pieces, *tap_parts, wide_bias)
+    )(places, *pieces, *tap_parts, wide_bias)
+
+
+def tie(value, *others):
+    return lax.optimization_barrier((value, others))[0]
 
 
 def body(features, kernel, bias_vector):
@@ -108,9 +163,7 @@
     parts = lax.axis_size("filt")
     slabs = lax.axis_size("slab")
     me = lax.axis_index("filt")
-    core = me % 2
     rows = y_cells // parts
-    chips = parts // 2
     aligned = chan % 16 == 0 and out_chan % 16 == 0
     across = list(range(0, parts, 2))
 
@@ -119,36 +172,47 @@
             return array
         return lax.ppermute(array, axis, [(i, i ^ k) for i in range(lax.axis_size(axis))])
 
-    def pack(piece):
-        count = piece.shape[0]
-        by_row = piece.transpose(0, 2, 1, 3).reshape(count, parts, rows, chan, cols).transpose(1, 0, 2, 3, 4)
-        nothing = jnp.zeros((1, count, 1, chan, cols), piece.dtype)
-        above = jnp.concatenate([nothing, by_row[:-1, :, -1:]])
-        below = jnp.concatenate([by_row[1:, :, :1], nothing])
-        return jnp.concatenate([above, by_row, below], axis=2)
-
-    outer_rows = pack(jnp.concatenate([features[:1], features[-1:]]))
-    inner_rows = pack(features[1:-1]).reshape(chips, 2, planes - 2, rows + 2, chan, cols)
-
-    fetched = [swap(kernel, k) for k in across]
-    outer_rows, inner_rows = lax.optimization_barrier((outer_rows, inner_rows))
-    outer = lax.all_to_all(outer_rows, "filt", 0, 0)
-    if not aligned:
-        outer = outer.transpose(1, 2, 0, 3, 4).reshape(1, 2, rows + 2, parts * chan, cols)
-
-    kept = lax.dynamic_index_in_dim(inner_rows, core, 1, keepdims=False)
-    given = swap(lax.dynamic_index_in_dim(inner_rows, 1 - core, 1, keepdims=False), 1)
-    both = jnp.concatenate([jnp.where(core == 0, kept, given), jnp.where(core == 0, given, kept)], axis=3)
-    outer, both, fetched = lax.optimization_barrier((outer, both, fetched))
-    inner = [swap(lax.dynamic_slice_in_dim(both, (me ^ k) // 2, 1, 0), k) for k in across]
-
-    same = jnp.stack(fetched)
-    tap_parts = [same, swap(same, 1)]
+    half = out_chan // 2
+    odd = lax.axis_index("slab") % 2
+    mine = lax.dynamic_slice_in_dim(kernel, odd * half, half, 3)
+    mine = [swap(mine, k) for k in across[1:]]
+
+    ordered = jnp.concatenate([features[:1], features[-1:], features[1:-1]])
+    outer_kept, outer_given, inner_kept, inner_given = cut(me, ordered.transpose(0, 2, 1, 3), parts)
+    outer_given = swap(outer_given, 1)
+    outer_out = [jnp.concatenate([outer_kept[n], outer_given[n]], axis=2) for n in range(len(across))]
+    inner_given = swap(tie(inner_given, outer_given), 1)
+    inner_out = [jnp.concatenate([inner_kept[n], inner_given[n]], axis=2) for n in range(len(across))]
+
+    mine = jnp.stack(tie(mine, outer_out))
+    theirs = swap(mine, 1, "slab")
+    rest = jnp.concatenate([jnp.where(odd == 0, mine, theirs), jnp.where(odd == 0, theirs, mine)], axis=4)
+    same = jnp.concatenate([kernel[None], rest])
+    other = swap(same, 1)
+    tap_parts = [same, other]
+
+    outer = [swap(block, k) for block, k in zip(outer_out, across)]
+    inner = [swap(tie(block, got) if k else block, k) for block, got, k in zip(inner_out, outer, across)]
+    up = [(i, i + 1) for i in range(slabs - 1)]
+    down = [(i + 1, i) for i in range(slabs - 1)]
+    after = lax.ppermute(jnp.stack([block[:1] for block in outer]), "slab", down)
+    before = lax.ppermute(jnp.stack([block[1:] for block in outer]), "slab", up)
+    after = [after[n] for n in range(len(across))]
+    before = [before[n] for n in range(len(across))]
+
+    order = jnp.stack([me ^ k ^ c for k in across for c in range(2)])
+    bias = jnp.take(bias_vector.reshape(parts, out_chan), order, axis=0).reshape(-1)
     if not aligned:
         joined = jnp.stack(tap_parts, axis=1).transpose(2, 3, 4, 0, 1, 5, 6)
         tap_parts = [joined.reshape(1, 3, 3, 3, parts * out_chan, -1)]
-    order = jnp.stack([me ^ k ^ c for k in across for c in range(2)])
-    bias = jnp.take(bias_vector.reshape(parts, out_chan), order, axis=0).reshape(-1)
+
+        def settle(blocks):
+            count = blocks[0].shape[0]
+            found = jnp.stack(blocks).reshape(-1, count, rows + 2, 2, chan, cols).transpose(0, 3, 1, 2, 4, 5)
+            found = jnp.take(found.reshape(parts, count, rows + 2, chan, cols), me ^ jnp.arange(parts), axis=0)
+            return [found.transpose(1, 2, 0, 3, 4).reshape(count, rows + 2, parts * chan, cols)]
+
+        outer, inner, before, after = settle(outer), settle(inner), settle(before), settle(after)
 
     def send_back(results):
         count = results[0].shape[0]
@@ -161,19 +225,15 @@
             final = lax.dynamic_update_slice_in_dim(final, theirs[n], (me ^ k ^ 1) * rows, 1)
         return final.transpose(0, 2, 1, 3)
 
-    up = [(i, i + 1) for i in range(slabs - 1)]
-    down = [(i + 1, i) for i in range(slabs - 1)]
-    after = lax.ppermute(outer[:, :1], "slab", down)
-    before = lax.ppermute(outer[:, 1:], "slab", up)
-
-    chip = jnp.full((1,), me // 2, jnp.int32)
-
     def conv(first, stride, count, edges, shift):
-        pieces = [outer, *inner, *edges]
-        plan = [(0, None, 0, shift, 1), (0, None, 1, planes - 1 + shift, 1)]
-        plan += [(1 + k, k, 0, 1 + shift, planes - 2) for k in range(chips)]
-        plan += [(1 + chips + n, None, 0, n * (planes + 1), 1) for n in range(len(edges))]
-        return convolve(first, stride, count, chip, pieces, tuple(plan), tap_parts, bias, chips)
+        pieces, plan = [], []
+        for blocks, moves in [(outer, ((0, shift, 1), (1, planes - 1 + shift, 1))), (inner, ((0, 1 + shift, planes - 2),))] + [
+            (edge, ((0, n * (planes + 1), 1),)) for n, edge in enumerate(edges)
+        ]:
+            for n, block in enumerate(blocks):
+                plan += [(len(pieces), n if aligned else None, *move) for move in moves]
+                pieces.append(block)
+        return convolve(first, stride, count, order, pieces, tuple(plan), tap_parts, bias, len(across))
 
     inside = send_back(conv(0, 1, planes - 2, [], 0))
     outside = send_back(conv(0, planes - 1, 2, [before, after], 1))

time: 125 us -> 188 us (1.50)
  Pallas kernels: 25.6 us -> 102 us
  waiting for transfers between devices: 57.4 us -> 39.8 us
  starting transfers between devices: 23.7 us -> 28.1 us
    pallas_call x0 -> x1, Pallas kernels: none -> 80.9 us  [cut(): pl.pallas_call(functools.partial(cut_kernel, rows), out_shape=[shape] * 4...]
    ppermute x16 -> x21, waiting for transfers between devices: 57.3 us -> 30.6 us  [swap(): lax.ppermute(array, axis, [(i, i ^ k) for i in range(lax.axis_size(axis))])]
    ppermute x16 -> x21, starting transfers between devices: 12.8 us -> 22.2 us  [swap(): lax.ppermute(array, axis, [(i, i ^ k) for i in range(lax.axis_size(axis))])]
    ppermute x2, waiting for transfers between devices: 0.01 us -> 9.21 us  [the longest x1 9.2 us: body(): lax.ppermute(jnp.stack([block[:1] for block in outer]), 'slab', down)]
    all_to_all x1 -> x0, starting transfers between devices: 5.17 us -> none  [body(): outer = lax.all_to_all(outer_rows, 'filt', 0, 0)]
    pallas_call x2, Pallas kernels: 25.6 us -> 21.5 us  [convolve(): pl.pallas_call(functools.partial(conv_kernel, first, stride, count, plan,...]
    slice x6 -> x3, local copies, waits for them, and re-layouts: 3.73 us -> 1.78 us  [body(): ordered = jnp.concatenate([features[:1], features[-1:], features[1:-1]])]
  transfers between devices with their start and end apart: 19 -> 23, of which waited for: 7 -> 12; matrix products, arithmetic and copies ran while one was open for 5% -> 6% of each run, Pallas kernels for 10% -> 49%
where the time goes in v6:
time: 188 us; the launch traced here: 187 us
  Pallas kernels  102 us (54%)
  waiting for transfers between devices  39.8 us (21%)
  starting transfers between devices  28.1 us (15%)
  local copies, waits for them, and re-layouts  10 us (5%)
  other arithmetic  6.36 us (3%)
    pallas_call x1, Pallas kernels, cut(): pl.pallas_call(functools.partial(cut_kernel, rows), out_shape=[shape] * 4...  80.9 us
    ppermute x21, waiting for transfers between devices, swap(): lax.ppermute(array, axis, [(i, i ^ k) for i in range(lax.axis_size(axis))])  30.6 us
    ppermute x21, starting transfers between devices, swap(): lax.ppermute(array, axis, [(i, i ^ k) for i in range(lax.axis_size(axis))])  22.2 us
    pallas_call x2, Pallas kernels, convolve(): pl.pallas_call(functools.partial(conv_kernel, first, stride, count, plan,...  21.5 us
    ppermute x1, waiting for transfers between devices, body(): lax.ppermute(jnp.stack([block[:1] for block in outer]), 'slab', down)  9.2 us
    ppermute x1, starting transfers between devices, body(): before = lax.ppermute(jnp.stack([block[1:] for block in outer]), 'slab', up)  4.59 us
  transfers between devices with their start and end apart: 23, of which 12 were waited for; matrix products, arithmetic and copies ran while one was open for 6% of the time, Pallas kernels for 49%

profile of v6, /device:TPU:0, one launch (start us, length us, event | category | flops | bytes accessed | tf_op | source)
XLA Modules:
  0.0 187.3 jit_solution(9985981156642383774)
XLA Ops:
  0.0 1.6 constant_dynamic-slice_fusion
  1.6 2.9 %collective-permute-start.10 = (bf16[3,3,3,16,256]{4,3,2,1,0:T(8,128)(2,1)}, bf16[3,3,3,16,256]{4,3,2,1,0:T(8,128)(2,1)S(1)}, u32[]{:S(2)}, u32[]{:S(2)}) collective-permute-start(bf16[3,3,3,16,256]{4,3,2,1,0:T(8,128)(2,1)} %constant_dynamic-slice_fusion), channel_id=1, source_target_pairs={{0,2},{1,3},{2,0},{3,1},{4,6},{5,7},{6,4},{7,5},{8,10},{9,11},{10,... | collective-permute-start | bytes 663560 | tf_op jit(solution)/shard_map/ppermute | solution.py:173
  4.6 1.5 collective-permute-start.11
  9.3 1.5 maximum_bitcast_fusion.vol_ref
  11.4 80.9 %shard_map.37 = (bf16[4,2,10,32,128]{4,3,2,1,0:T(8,128)(2,1)}, bf16[4,2,10,32,128]{4,3,2,1,0:T(8,128)(2,1)}, bf16[4,2,10,32,128]{4,3,2,1,0:T(8,128)(2,1)}, bf16[4,2,10,32,128]{4,3,2,1,0:T(8,128)(2,1)}) custom-call(s32[1]{0:T(128)} %bitcast.me_ref, bf16[4,64,32,128]{3,2,1,0:T(8,128)(2,1)} %maximum_bitcast_fusion.vol_ref, ...), custom_call_target="tpu_custom_call" | custom-call | tf_op jit(solution)/shard_map/pallas_call | solution.py:59
  97.2 2.1 %collective-permute-start.13 = (bf16[3,3,3,3,16,256]{5,4,3,2,1,0:T(8,128)(2,1)S(1)}, bf16[3,3,3,3,16,256]{5,4,3,2,1,0:T(8,128)(2,1)S(1)}, u32[]{:S(2)}, u32[]{:S(2)}) collective-permute-start(bf16[3,3,3,3,16,256]{5,4,3,2,1,0:T(8,128)(2,1)S(1)} %pad_maximum_fusion.1), channel_id=1, source_target_pairs={{0,8},{8,0},{16,24},{24,16},{1,9},{9,1},{17,25},{25,17},{2,10},{10... | collective-permute-start | bytes 1990664 | tf_op jit(solution)/shard_map/ppermute | solution.py:173
  99.5 2.5 %collective-permute-start.3 = (bf16[2,10,64,128]{3,2,1,0:T(8,128)(2,1)}, bf16[2,10,64,128]{3,2,1,0:T(8,128)(2,1)S(1)}, u32[]{:S(2)}, u32[]{:S(2)}) collective-permute-start(bf16[2,10,64,128]{3,2,1,0:T(8,128)(2,1)} %pad_maximum_fusion.9), channel_id=1, source_target_pairs={{0,6},{1,7},{2,4},{3,5},{4,2},{5,3},{6,0},{7,1},{8,14},{9,15},{10,... | collective-permute-start | bytes 983048 | tf_op jit(solution)/shard_map/ppermute | solution.py:173
  103.2 8.1 %collective-permute-done.3.refs_4_ = bf16[2,10,64,128]{3,2,1,0:T(8,128)(2,1)S(1)} collective-permute-done((bf16[2,10,64,128]{3,2,1,0:T(8,128)(2,1)}, bf16[2,10,64,128]{3,2,1,0:T(8,128)(2,1)S(1)}, u32[]{:S(2)}, u32[]{:S(2)}) %collective-permute-start.3) | collective-permute-done | bytes 327712 | tf_op jit(solution)/shard_map/ppermute | solution.py:173
  111.3 3.4 %collective-permute-done.13 = bf16[3,3,3,3,16,256]{5,4,3,2,1,0:T(8,128)(2,1)S(1)} collective-permute-done((bf16[3,3,3,3,16,256]{5,4,3,2,1,0:T(8,128)(2,1)S(1)}, bf16[3,3,3,3,16,256]{5,4,3,2,1,0:T(8,128)(2,1)S(1)}, u32[]{:S(2)}, u32[]{:S(2)}) %collective-permute-start.13) | collective-permute-done | bytes 663584 | tf_op jit(solution)/shard_map/ppermute | solution.py:173
  115.1 2.1 %collective-permute-done.2.refs_3_ = bf16[2,10,64,128]{3,2,1,0:T(8,128)(2,1)S(1)} collective-permute-done((bf16[2,10,64,128]{3,2,1,0:T(8,128)(2,1)}, bf16[2,10,64,128]{3,2,1,0:T(8,128)(2,1)S(1)}, u32[]{:S(2)}, u32[]{:S(2)}) %collective-permute-start.2) | collective-permute-done | bytes 327712 | tf_op jit(solution)/shard_map/ppermute | solution.py:173
  118.9 4.6 %collective-permute-start.8 = (bf16[4,1,10,64,128]{4,3,2,1,0:T(8,128)(2,1)S(1)}, bf16[4,1,10,64,128]{4,3,2,1,0:T(8,128)(2,1)S(1)}, u32[]{:S(2)}, u32[]{:S(2)}) collective-permute-start(bf16[4,1,10,64,128]{4,3,2,1,0:T(8,128)(2,1)S(1)} %pad_maximum_fusion.2), channel_id=1, source_target_pairs={{0,8},{8,16},{16,24},{1,9},{9,17},{17,25},{2,10},{10,18},{18,26},{... | collective-permute-start | bytes 1966088 | tf_op jit(solution)/shard_map/ppermute | solution.py:199
  123.6 1.9 %collective-permute-start.7 = (bf16[2,10,64,128]{3,2,1,0:T(8,128)(2,1)S(1)}, bf16[2,10,64,128]{3,2,1,0:T(8,128)(2,1)S(1)}, u32[]{:S(2)}, u32[]{:S(2)}) collective-permute-start(bf16[2,10,64,128]{3,2,1,0:T(8,128)(2,1)S(1)} %pad_maximum_fusion.13), channel_id=1, source_target_pairs={{0,6},{1,7},{2,4},{3,5},{4,2},{5,3},{6,0},{7,1},{8,14},{9,15},{10,... | collective-permute-start | bytes 983048 | tf_op jit(solution)/shard_map/ppermute | solution.py:173
  126.8 9.2 %collective-permute-done.9 = bf16[4,1,10,64,128]{4,3,2,1,0:T(8,128)(2,1)S(1)} collective-permute-done((bf16[4,1,10,64,128]{4,3,2,1,0:T(8,128)(2,1)S(1)}, bf16[4,1,10,64,128]{4,3,2,1,0:T(8,128)(2,1)S(1)}, u32[]{:S(2)}, u32[]{:S(2)}) %collective-permute-start.9) | collective-permute-done | bytes 655392 | tf_op jit(solution)/shard_map/ppermute | solution.py:198
  136.0 1.5 collective-permute-start.5
  137.6 3.0 %collective-permute-done.6.refs_7_ = bf16[2,10,64,128]{3,2,1,0:T(8,128)(2,1)S(1)} collective-permute-done((bf16[2,10,64,128]{3,2,1,0:T(8,128)(2,1)S(1)}, bf16[2,10,64,128]{3,2,1,0:T(8,128)(2,1)S(1)}, u32[]{:S(2)}, u32[]{:S(2)}) %collective-permute-start.6) | collective-permute-done | bytes 327712 | tf_op jit(solution)/shard_map/ppermute | solution.py:173
  140.6 4.1 %collective-permute-done.5.refs_6_ = bf16[2,10,64,128]{3,2,1,0:T(8,128)(2,1)S(1)} collective-permute-done((bf16[2,10,64,128]{3,2,1,0:T(8,128)(2,1)S(1)}, bf16[2,10,64,128]{3,2,1,0:T(8,128)(2,1)S(1)}, u32[]{:S(2)}, u32[]{:S(2)}) %collective-permute-start.5) | collective-permute-done | bytes 327712 | tf_op jit(solution)/shard_map/ppermute | solution.py:173
  144.8 11.0 %shard_map.38 = (bf16[2,8,64,128]{3,2,1,0:T(8,128)(2,1)S(1)}, bf16[2,8,64,128]{3,2,1,0:T(8,128)(2,1)S(1)}, bf16[2,8,64,128]{3,2,1,0:T(8,128)(2,1)S(1)}, bf16[2,8,64,128]{3,2,1,0:T(8,128)(2,1)S(1)}) custom-call(s32[8]{0:T(128)S(1)} %stack.125.refs_0_, bf16[2,10,64,128]{3,2,1,0:T(8,128)(2,1)S(1)} %pad_maximum_fusion.6.refs_1_, ...), custom_call_target="tpu_custom_call" | custom-call | flops 7247757312 | bytes 10000000 | tf_op jit(solution)/shard_map/pallas_call | solution.py:142
  155.8 1.7 collective-permute-start.16
  157.7 1.6 collective-permute-start.17
  159.3 10.5 %shard_map.39 = (bf16[2,8,64,128]{3,2,1,0:T(8,128)(2,1)S(1)}, bf16[2,8,64,128]{3,2,1,0:T(8,128)(2,1)S(1)}, bf16[2,8,64,128]{3,2,1,0:T(8,128)(2,1)S(1)}, bf16[2,8,64,128]{3,2,1,0:T(8,128)(2,1)S(1)}) custom-call(s32[8]{0:T(128)S(1)} %stack.125.refs_0_, bf16[2,10,64,128]{3,2,1,0:T(8,128)(2,1)S(1)} %pad_maximum_fusion.6.refs_1_, ...), custom_call_target="tpu_custom_call" | custom-call | flops 7247757312 | bytes 10000000 | tf_op jit(solution)/shard_map/pallas_call | solution.py:142
  171.3 1.6 collective-permute-start.20
  173.8 5.6 %collective-permute-done.21 = bf16[2,8,64,128]{3,2,1,0:T(8,128)(2,1)S(1)} collective-permute-done((bf16[2,8,64,128]{3,2,1,0:T(8,128)(2,1)S(1)}, bf16[2,8,64,128]{3,2,1,0:T(8,128)(2,1)S(1)}, u32[]{:S(2)}, u32[]{:S(2)}) %collective-permute-start.21) | collective-permute-done | bytes 262176 | tf_op jit(solution)/shard_map/ppermute | solution.py:173
  179.4 2.6 %collective-permute-done.20 = bf16[2,8,64,128]{3,2,1,0:T(8,128)(2,1)S(1)} collective-permute-done((bf16[2,8,64,128]{3,2,1,0:T(8,128)(2,1)S(1)}, bf16[2,8,64,128]{3,2,1,0:T(8,128)(2,1)S(1)}, u32[]{:S(2)}, u32[]{:S(2)}) %collective-permute-start.20) | collective-permute-done | bytes 262176 | tf_op jit(solution)/shard_map/ppermute | solution.py:173
  185.7 1.6 pad_maximum_fusion
  (104 shorter events, 19.5 us)
Async XLA Ops:
  1.6 95.5 %collective-permute-start.10 = (bf16[3,3,3,16,256]{4,3,2,1,0:T(8,128)(2,1)}, bf16[3,3,3,16,256]{4,3,2,1,0:T(8,128)(2,1)S(1)}, u32[]{:S(2)}, u32[]{:S(2)}) collective-permute-start(bf16[3,3,3,16,256]{4,3,2,1,0:T(8,128)(2,1)} %constant_dynamic-slice_fusion), channel_id=1, source_target_pairs={{0,2},{1,3},{2,0},{3,1},{4,6},{5,7},{6,4},{7,5},{8,10},{9,11},{10,... | collective-permute-start | bytes 663560 | tf_op jit(solution)/shard_map/ppermute | solution.py:173
  4.6 92.5 %collective-permute-start.11 = (bf16[3,3,3,16,256]{4,3,2,1,0:T(8,128)(2,1)}, bf16[3,3,3,16,256]{4,3,2,1,0:T(8,128)(2,1)S(1)}, u32[]{:S(2)}, u32[]{:S(2)}) collective-permute-start(bf16[3,3,3,16,256]{4,3,2,1,0:T(8,128)(2,1)} %constant_dynamic-slice_fusion), channel_id=1, source_target_pairs={{0,4},{1,5},{2,6},{3,7},{4,0},{5,1},{6,2},{7,3},{8,12},{9,13},{10,... | collective-permute-start | bytes 663560 | tf_op jit(solution)/shard_map/ppermute | solution.py:173
  6.1 91.0 %collective-permute-start.12 = (bf16[3,3,3,16,256]{4,3,2,1,0:T(8,128)(2,1)}, bf16[3,3,3,16,256]{4,3,2,1,0:T(8,128)(2,1)S(1)}, u32[]{:S(2)}, u32[]{:S(2)}) collective-permute-start(bf16[3,3,3,16,256]{4,3,2,1,0:T(8,128)(2,1)} %constant_dynamic-slice_fusion), channel_id=1, source_target_pairs={{0,6},{1,7},{2,4},{3,5},{4,2},{5,3},{6,0},{7,1},{8,14},{9,15},{10,... | collective-permute-start | bytes 663560 | tf_op jit(solution)/shard_map/ppermute | solution.py:173
  10.8 81.8 %copy-start.2 = (f32[256]{0:T(256)S(1)}, f32[256]{0:T(256)}, u32[]{:S(2)}) copy-start(f32[256]{0:T(256)} %param.5) | copy-start | bytes 3076
  92.4 2.4 %collective-permute-start = (bf16[4,2,10,32,128]{4,3,2,1,0:T(8,128)(2,1)}, bf16[4,2,10,32,128]{4,3,2,1,0:T(8,128)(2,1)S(1)}, u32[]{:S(2)}, u32[]{:S(2)}) collective-permute-start(bf16[4,2,10,32,128]{4,3,2,1,0:T(8,128)(2,1)} %get-tuple-element.25), channel_id=1, source_target_pairs={{0,1},{1,0},{2,3},{3,2},{4,5},{5,4},{6,7},{7,6},{8,9},{9,8},{10,11... | collective-permute-start | bytes 1966088 | tf_op jit(solution)/shard_map/ppermute | solution.py:173
  97.2 17.5 %collective-permute-start.13 = (bf16[3,3,3,3,16,256]{5,4,3,2,1,0:T(8,128)(2,1)S(1)}, bf16[3,3,3,3,16,256]{5,4,3,2,1,0:T(8,128)(2,1)S(1)}, u32[]{:S(2)}, u32[]{:S(2)}) collective-permute-start(bf16[3,3,3,3,16,256]{5,4,3,2,1,0:T(8,128)(2,1)S(1)} %pad_maximum_fusion.1), channel_id=1, source_target_pairs={{0,8},{8,0},{16,24},{24,16},{1,9},{9,1},{17,25},{25,17},{2,10},{10... | collective-permute-start | bytes 1990664 | tf_op jit(solution)/shard_map/ppermute | solution.py:173
  99.5 11.8 %collective-permute-start.3 = (bf16[2,10,64,128]{3,2,1,0:T(8,128)(2,1)}, bf16[2,10,64,128]{3,2,1,0:T(8,128)(2,1)S(1)}, u32[]{:S(2)}, u32[]{:S(2)}) collective-permute-start(bf16[2,10,64,128]{3,2,1,0:T(8,128)(2,1)} %pad_maximum_fusion.9), channel_id=1, source_target_pairs={{0,6},{1,7},{2,4},{3,5},{4,2},{5,3},{6,0},{7,1},{8,14},{9,15},{10,... | collective-permute-start | bytes 983048 | tf_op jit(solution)/shard_map/ppermute | solution.py:173
  102.0 15.2 %collective-permute-start.2 = (bf16[2,10,64,128]{3,2,1,0:T(8,128)(2,1)}, bf16[2,10,64,128]{3,2,1,0:T(8,128)(2,1)S(1)}, u32[]{:S(2)}, u32[]{:S(2)}) collective-permute-start(bf16[2,10,64,128]{3,2,1,0:T(8,128)(2,1)} %pad_maximum_fusion.8), channel_id=1, source_target_pairs={{0,4},{1,5},{2,6},{3,7},{4,0},{5,1},{6,2},{7,3},{8,12},{9,13},{10,... | collective-permute-start | bytes 983048 | tf_op jit(solution)/shard_map/ppermute | solution.py:173
  102.6 14.8 %collective-permute-start.1 = (bf16[2,10,64,128]{3,2,1,0:T(8,128)(2,1)}, bf16[2,10,64,128]{3,2,1,0:T(8,128)(2,1)S(1)}, u32[]{:S(2)}, u32[]{:S(2)}) collective-permute-start(bf16[2,10,64,128]{3,2,1,0:T(8,128)(2,1)} %pad_maximum_fusion.7), channel_id=1, source_target_pairs={{0,2},{1,3},{2,0},{3,1},{4,6},{5,7},{6,4},{7,5},{8,10},{9,11},{10,... | collective-permute-start | bytes 983048 | tf_op jit(solution)/shard_map/ppermute | solution.py:173
  103.1 20.3 %collective-permute-start.4 = (bf16[4,2,10,32,128]{4,3,2,1,0:T(8,128)(2,1)}, bf16[4,2,10,32,128]{4,3,2,1,0:T(8,128)(2,1)S(1)}, u32[]{:S(2)}, u32[]{:S(2)}) collective-permute-start(bf16[4,2,10,32,128]{4,3,2,1,0:T(8,128)(2,1)} %get-tuple-element.28), channel_id=1, source_target_pairs={{0,1},{1,0},{2,3},{3,2},{4,5},{5,4},{6,7},{7,6},{8,9},{9,8},{10,11... | collective-permute-start | bytes 1966088 | tf_op jit(solution)/shard_map/ppermute | solution.py:173
  115.0 29.7 %collective-permute-start.14 = (bf16[4,3,3,3,32,256]{5,4,3,2,1,0:T(8,128)(2,1)S(1)}, bf16[4,3,3,3,32,256]{5,4,3,2,1,0:T(8,128)(2,1)S(1)}, u32[]{:S(2)}, u32[]{:S(2)}) collective-permute-start(bf16[4,3,3,3,32,256]{5,4,3,2,1,0:T(8,128)(2,1)S(1)} %maximum_maximum_fusion.refs_17_.refs_9_), channel_id=1, source_target_pairs={{0,1},{1,0},{2,3},{3,2},{4,5},{5,4},{6,7},{7,6},{8,9},{9,8},{10,11... | collective-permute-start | bytes 5308424 | tf_op jit(solution)/shard_map/ppermute | solution.py:173
  117.5 18.5 %collective-permute-start.9 = (bf16[4,1,10,64,128]{4,3,2,1,0:T(8,128)(2,1)S(1)}, bf16[4,1,10,64,128]{4,3,2,1,0:T(8,128)(2,1)S(1)}, u32[]{:S(2)}, u32[]{:S(2)}) collective-permute-start(bf16[4,1,10,64,128]{4,3,2,1,0:T(8,128)(2,1)S(1)} %pad_maximum_fusion.3), channel_id=1, source_target_pairs={{8,0},{16,8},{24,16},{9,1},{17,9},{25,17},{10,2},{18,10},{26,18},{... | collective-permute-start | bytes 1966088 | tf_op jit(solution)/shard_map/ppermute | solution.py:198
  118.9 18.6 %collective-permute-start.8 = (bf16[4,1,10,64,128]{4,3,2,1,0:T(8,128)(2,1)S(1)}, bf16[4,1,10,64,128]{4,3,2,1,0:T(8,128)(2,1)S(1)}, u32[]{:S(2)}, u32[]{:S(2)}) collective-permute-start(bf16[4,1,10,64,128]{4,3,2,1,0:T(8,128)(2,1)S(1)} %pad_maximum_fusion.2), channel_id=1, source_target_pairs={{0,8},{8,16},{16,24},{1,9},{9,17},{17,25},{2,10},{10,18},{18,26},{... | collective-permute-start | bytes 1966088 | tf_op jit(solution)/shard_map/ppermute | solution.py:199
  123.6 14.0 %collective-permute-start.7 = (bf16[2,10,64,128]{3,2,1,0:T(8,128)(2,1)S(1)}, bf16[2,10,64,128]{3,2,1,0:T(8,128)(2,1)S(1)}, u32[]{:S(2)}, u32[]{:S(2)}) collective-permute-start(bf16[2,10,64,128]{3,2,1,0:T(8,128)(2,1)S(1)} %pad_maximum_fusion.13), channel_id=1, source_target_pairs={{0,6},{1,7},{2,4},{3,5},{4,2},{5,3},{6,0},{7,1},{8,14},{9,15},{10,... | collective-permute-start | bytes 983048 | tf_op jit(solution)/shard_map/ppermute | solution.py:173
  125.5 15.1 %collective-permute-start.6 = (bf16[2,10,64,128]{3,2,1,0:T(8,128)(2,1)S(1)}, bf16[2,10,64,128]{3,2,1,0:T(8,128)(2,1)S(1)}, u32[]{:S(2)}, u32[]{:S(2)}) collective-permute-start(bf16[2,10,64,128]{3,2,1,0:T(8,128)(2,1)S(1)} %pad_maximum_fusion.12), channel_id=1, source_target_pairs={{0,4},{1,5},{2,6},{3,7},{4,0},{5,1},{6,2},{7,3},{8,12},{9,13},{10,... | collective-permute-start | bytes 983048 | tf_op jit(solution)/shard_map/ppermute | solution.py:173
  136.0 8.7 %collective-permute-start.5 = (bf16[2,10,64,128]{3,2,1,0:T(8,128)(2,1)S(1)}, bf16[2,10,64,128]{3,2,1,0:T(8,128)(2,1)S(1)}, u32[]{:S(2)}, u32[]{:S(2)}) collective-permute-start(bf16[2,10,64,128]{3,2,1,0:T(8,128)(2,1)S(1)} %pad_maximum_fusion.11), channel_id=1, source_target_pairs={{0,2},{1,3},{2,0},{3,1},{4,6},{5,7},{6,4},{7,5},{8,10},{9,11},{10,... | collective-permute-start | bytes 983048 | tf_op jit(solution)/shard_map/ppermute | solution.py:173
  155.8 17.2 %collective-permute-start.16 = (bf16[2,8,64,128]{3,2,1,0:T(8,128)(2,1)S(1)}, bf16[2,8,64,128]{3,2,1,0:T(8,128)(2,1)S(1)}, u32[]{:S(2)}, u32[]{:S(2)}) collective-permute-start(bf16[2,8,64,128]{3,2,1,0:T(8,128)(2,1)S(1)} %get-tuple-element.37), channel_id=1, source_target_pairs={{0,4},{1,5},{2,6},{3,7},{4,0},{5,1},{6,2},{7,3},{8,12},{9,13},{10,... | collective-permute-start | bytes 786440 | tf_op jit(solution)/shard_map/ppermute | solution.py:173
  157.4 16.1 %collective-permute-start.15 = (bf16[2,8,64,128]{3,2,1,0:T(8,128)(2,1)S(1)}, bf16[2,8,64,128]{3,2,1,0:T(8,128)(2,1)S(1)}, u32[]{:S(2)}, u32[]{:S(2)}) collective-permute-start(bf16[2,8,64,128]{3,2,1,0:T(8,128)(2,1)S(1)} %get-tuple-element.36), channel_id=1, source_target_pairs={{0,2},{1,3},{2,0},{3,1},{4,6},{5,7},{6,4},{7,5},{8,10},{9,11},{10,... | collective-permute-start | bytes 786440 | tf_op jit(solution)/shard_map/ppermute | solution.py:173
  157.7 15.9 %collective-permute-start.17 = (bf16[2,8,64,128]{3,2,1,0:T(8,128)(2,1)S(1)}, bf16[2,8,64,128]{3,2,1,0:T(8,128)(2,1)S(1)}, u32[]{:S(2)}, u32[]{:S(2)}) collective-permute-start(bf16[2,8,64,128]{3,2,1,0:T(8,128)(2,1)S(1)} %get-tuple-element.38), channel_id=1, source_target_pairs={{0,6},{1,7},{2,4},{3,5},{4,2},{5,3},{6,0},{7,1},{8,14},{9,15},{10,... | collective-permute-start | bytes 786440 | tf_op jit(solution)/shard_map/ppermute | solution.py:173
  169.9 9.5 %collective-permute-start.21 = (bf16[2,8,64,128]{3,2,1,0:T(8,128)(2,1)S(1)}, bf16[2,8,64,128]{3,2,1,0:T(8,128)(2,1)S(1)}, u32[]{:S(2)}, u32[]{:S(2)}) collective-permute-start(bf16[2,8,64,128]{3,2,1,0:T(8,128)(2,1)S(1)} %get-tuple-element.42), channel_id=1, source_target_pairs={{0,6},{1,7},{2,4},{3,5},{4,2},{5,3},{6,0},{7,1},{8,14},{9,15},{10,... | collective-permute-start | bytes 786440 | tf_op jit(solution)/shard_map/ppermute | solution.py:173
  171.3 10.8 %collective-permute-start.20 = (bf16[2,8,64,128]{3,2,1,0:T(8,128)(2,1)S(1)}, bf16[2,8,64,128]{3,2,1,0:T(8,128)(2,1)S(1)}, u32[]{:S(2)}, u32[]{:S(2)}) collective-permute-start(bf16[2,8,64,128]{3,2,1,0:T(8,128)(2,1)S(1)} %get-tuple-element.41), channel_id=1, source_target_pairs={{0,4},{1,5},{2,6},{3,7},{4,0},{5,1},{6,2},{7,3},{8,12},{9,13},{10,... | collective-permute-start | bytes 786440 | tf_op jit(solution)/shard_map/ppermute | solution.py:173
  172.9 9.3 %collective-permute-start.19 = (bf16[2,8,64,128]{3,2,1,0:T(8,128)(2,1)S(1)}, bf16[2,8,64,128]{3,2,1,0:T(8,128)(2,1)S(1)}, u32[]{:S(2)}, u32[]{:S(2)}) collective-permute-start(bf16[2,8,64,128]{3,2,1,0:T(8,128)(2,1)S(1)} %get-tuple-element.40), channel_id=1, source_target_pairs={{0,2},{1,3},{2,0},{3,1},{4,6},{5,7},{6,4},{7,5},{8,10},{9,11},{10,... | collective-permute-start | bytes 786440 | tf_op jit(solution)/shard_map/ppermute | solution.py:173
  173.7 9.4 %collective-permute-start.18 = (bf16[4,2,8,32,128]{4,3,2,1,0:T(8,128)(2,1)S(1)}, bf16[4,2,8,32,128]{4,3,2,1,0:T(8,128)(2,1)S(1)}, u32[]{:S(2)}, u32[]{:S(2)}) collective-permute-start(bf16[4,2,8,32,128]{4,3,2,1,0:T(8,128)(2,1)S(1)} %pad_maximum_fusion.4), channel_id=1, source_target_pairs={{0,1},{1,0},{2,3},{3,2},{4,5},{5,4},{6,7},{7,6},{8,9},{9,8},{10,11... | collective-permute-start | bytes 1572872 | tf_op jit(solution)/shard_map/ppermute | solution.py:173
  182.4 2.0 %collective-permute-start.22 = (bf16[4,2,8,32,128]{4,3,2,1,0:T(8,128)(2,1)S(1)}, bf16[4,2,8,32,128]{4,3,2,1,0:T(8,128)(2,1)S(1)}, u32[]{:S(2)}, u32[]{:S(2)}) collective-permute-start(bf16[4,2,8,32,128]{4,3,2,1,0:T(8,128)(2,1)S(1)} %pad_maximum_fusion.5), channel_id=1, source_target_pairs={{0,1},{1,0},{2,3},{3,2},{4,5},{5,4},{6,7},{7,6},{8,9},{9,8},{10,11... | collective-permute-start | bytes 1572872 | tf_op jit(solution)/shard_map/ppermute | solution.py:173
  (3 other events, 21.2 us)

commit v7 on v6

--- a/solution.py
+++ b/solution.py
@@ -11,58 +11,78 @@
 PAIR = 2
 
 
-def cut_kernel(rows, me_ref, vol_ref, nothing_ref, *refs):
-    outs, sems = refs[:-2], refs[-2:]
+def cut_kernel(parts, me_ref, vol_ref, *outs):
     planes, y_cells = vol_ref.shape[:2]
-    parts = y_cells // rows
-    main, edge = sems
+    rows = y_cells // parts
     me = me_ref[0]
-
-    def moves(out, n, block, source):
-        top = block * rows
-        return [
-            (None, vol_ref.at[source, pl.ds(top, rows)], out.at[:, pl.ds(1, rows)], main.at[n]),
-            (block > 0, vol_ref.at[source, pl.ds(jnp.maximum(top - 1, 0), 1)], out.at[:, pl.ds(0, 1)], edge.at[n, 0]),
-            (block == 0, nothing_ref, out.at[:, pl.ds(0, 1)], edge.at[n, 0]),
-            (
-                block < parts - 1,
-                vol_ref.at[source, pl.ds(jnp.minimum(top + rows, y_cells - 1), 1)],
-                out.at[:, pl.ds(rows + 1, 1)],
-                edge.at[n, 1],
-            ),
-            (block == parts - 1, nothing_ref, out.at[:, pl.ds(rows + 1, 1)], edge.at[n, 1]),
-        ]
-
-    work = []
-    n = 0
-    for source, (kept, given) in ((pl.ds(0, 2), outs[:2]), (pl.ds(2, planes - 2), outs[2:])):
-        for k in range(parts // 2):
-            for core, out in enumerate((kept, given)):
-                work += moves(out.at[k], n, me ^ (2 * k + core), source)
-                n += 1
-    for act in ("start", "wait"):
-        for condition, src, dst, sem in work:
-            copy = pltpu.make_async_copy(src, dst, sem)
-            if condition is None:
-                getattr(copy, act)()
-            else:
-                pl.when(condition)(getattr(copy, act))
+    for k in range(parts // 2):
+        for core in range(2):
+            block = me ^ (2 * k + core)
+            for plane in range(planes):
+                inside = 0 < plane < planes - 1
+                out, slot = outs[2 * inside + core], (plane - 1 if inside else min(plane, 1))
+                for r in range(rows + 2):
+                    row = jnp.clip(block * rows + r - 1, 0, y_cells - 1)
+                    line = vol_ref[plane, row]
+                    if r == 0:
+                        line = jnp.where(block > 0, line, jnp.zeros_like(line))
+                    if r == rows + 1:
+                        line = jnp.where(block < parts - 1, line, jnp.zeros_like(line))
+                    out[k, slot, r] = line
 
 
 def cut(me, volume, parts):
     planes, y_cells, chan, cols = volume.shape
     rows = y_cells // parts
-    count = planes - 2
-    any_space = pl.BlockSpec(memory_space=pl.ANY)
-    assert count == 2
-    shape = jax.ShapeDtypeStruct((parts // 2, 2, rows + 2, chan, cols), volume.dtype)
-    return pl.pallas_call(
-        functools.partial(cut_kernel, rows),
-        out_shape=[shape] * 4,
-        in_specs=[pl.BlockSpec(memory_space=pltpu.SMEM), any_space, any_space],
-        out_specs=[any_space] * 4,
-        scratch_shapes=[pltpu.SemaphoreType.DMA((2 * parts,)), pltpu.SemaphoreType.DMA((2 * parts, 2))],
-    )(jnp.full((1,), me, jnp.int32), volume, jnp.zeros((2, 1, chan, cols), volume.dtype))
+    shapes = [
+        jax.ShapeDtypeStruct((parts // 2, count, rows + 2, chan, cols), volume.dtype) for count in (2, 2, planes - 2, planes - 2)
+    ]
+    in_vmem = pl.BlockSpec(memory_space=pltpu.VMEM)
+    return pl.pallas_call(
+        functools.partial(cut_kernel, parts),
+        out_shape=shapes,
+        in_specs=[pl.BlockSpec(memory_space=pltpu.SMEM), in_vmem],
+        out_specs=[in_vmem] * 4,
+        compiler_params=pltpu.CompilerParams(vmem_limit_bytes=16 * 2**20),
+    )(jnp.full((1,), me, jnp.int32), volume)
+
+
+def join_kernel(kept_ref, given_ref, *outs):
+    chan = kept_ref.shape[3]
+    for k, out in enumerate(outs):
+        out[:, :, :chan] = kept_ref[k]
+        out[:, :, chan:] = given_ref[k]
+
+
+def join(kept, given):
+    chips, count, rows_in, chan, cols = kept.shape
+    if chan % 16:
+        return [jnp.concatenate([kept[k], given[k]], axis=2) for k in range(chips)]
+    in_vmem = pl.BlockSpec(memory_space=pltpu.VMEM)
+    return pl.pallas_call(
+        join_kernel,
+        out_shape=[jax.ShapeDtypeStruct((count, rows_in, 2 * chan, cols), kept.dtype)] * chips,
+        in_specs=[in_vmem] * 2,
+        out_specs=[in_vmem] * chips,
+    )(kept, given)
+
+
+def edges_kernel(*refs):
+    blocks, (first, last) = refs[:-2], refs[-2:]
+    for k, block in enumerate(blocks):
+        first[k] = block[0]
+        last[k] = block[1]
+
+
+def edges_of(blocks):
+    _, rows_in, chan, cols = blocks[0].shape
+    in_vmem = pl.BlockSpec(memory_space=pltpu.VMEM)
+    return pl.pallas_call(
+        edges_kernel,
+        out_shape=[jax.ShapeDtypeStruct((len(blocks), rows_in, chan, cols), blocks[0].dtype)] * 2,
+        in_specs=[in_vmem] * len(blocks),
+        out_specs=[in_vmem] * 2,
+    )(*blocks)
 
 
 def conv_kernel(first, stride, count, plan, piece_count, tap_count, *refs):
@@ -71,26 +91,23 @@
     pieces = [refs.pop(0) for _ in range(piece_count)]
     tap_parts = [refs.pop(0) for _ in range(tap_count)]
     bias_ref = refs.pop(0)
-    outs = refs[:-2]
-    vol, vol_sem = refs[-2:]
+    outs, vol = refs[:-1], refs[-1]
     rows_in, total_in, cols = vol.shape[1:]
     total_out = bias_ref.shape[0]
     rows = rows_in - 2
-    copies = []
-    for n, (source, index, begin, slot, plane_count) in enumerate(plan):
-        piece = pieces[source].at[pl.ds(begin, plane_count)]
-        into = vol.at[pl.ds(slot, plane_count)]
-        chan = piece.shape[2] // (1 if index is None else 2)
-        for c in range(piece.shape[2] // chan):
-            place = 0 if index is None else place_ref[2 * index + c]
-            part = pl.ds(pl.multiple_of(place * chan, chan), chan)
-            copies.append(
-                pltpu.make_async_copy(piece.at[:, :, pl.ds(c * chan, chan)], into.at[:, :, part], vol_sem.at[n, c])
-            )
-    for copy in copies:
-        copy.start()
-    for copy in copies:
-        copy.wait()
+
+    def fill(row, carry):
+        for source, index, begin, slot, plane_count in plan:
+            piece = pieces[source]
+            chan = piece.shape[2] // (1 if index is None else 2)
+            for c in range(piece.shape[2] // chan):
+                place = 0 if index is None else place_ref[2 * index + c]
+                part = pl.ds(pl.multiple_of(place * chan, chan), chan)
+                for p in range(plane_count):
+                    vol[slot + p, row, part, :] = piece[begin + p, row, c * chan : (c + 1) * chan, :]
+        return carry
+
+    lax.fori_loop(0, rows_in, fill, 0)
 
     lane = lax.broadcasted_iota(jnp.int32, (total_out, cols), 1)
     per_plane = rows // PAIR
@@ -136,18 +153,14 @@
     depth = max(slot + n for _, _, _, slot, n in plan)
     wide_bias = jnp.broadcast_to(bias[:, None], (total_out, cols))
     macs = 27 * total_out * in_chan * count * rows * cols
-    any_space = pl.BlockSpec(memory_space=pl.ANY)
     in_vmem = pl.BlockSpec(memory_space=pltpu.VMEM)
     in_smem = pl.BlockSpec(memory_space=pltpu.SMEM)
     return pl.pallas_call(
         functools.partial(conv_kernel, first, stride, count, plan, len(pieces), len(tap_parts)),
         out_shape=[jax.ShapeDtypeStruct((count, rows, total_out // blocks, cols), jnp.bfloat16)] * blocks,
-        in_specs=[in_smem] + [any_space] * len(pieces) + [in_vmem] * (len(tap_parts) + 1),
+        in_specs=[in_smem] + [in_vmem] * (len(pieces) + len(tap_parts) + 1),
         out_specs=[in_vmem] * blocks,
-        scratch_shapes=[
-            pltpu.VMEM((depth, rows_in, in_chan, cols), jnp.bfloat16),
-            pltpu.SemaphoreType.DMA((len(plan), 2)),
-        ],
+        scratch_shapes=[pltpu.VMEM((depth, rows_in, in_chan, cols), jnp.bfloat16)],
         cost_estimate=pl.CostEstimate(flops=2 * macs, bytes_accessed=10_000_000, transcendentals=0),
         compiler_params=pltpu.CompilerParams(vmem_limit_bytes=20 * 2**20),
     )(places, *pieces, *tap_parts, wide_bias)
@@ -172,33 +185,29 @@
             return array
         return lax.ppermute(array, axis, [(i, i ^ k) for i in range(lax.axis_size(axis))])
 
-    half = out_chan // 2
-    odd = lax.axis_index("slab") % 2
-    mine = lax.dynamic_slice_in_dim(kernel, odd * half, half, 3)
-    mine = [swap(mine, k) for k in across[1:]]
-
-    ordered = jnp.concatenate([features[:1], features[-1:], features[1:-1]])
-    outer_kept, outer_given, inner_kept, inner_given = cut(me, ordered.transpose(0, 2, 1, 3), parts)
-    outer_given = swap(outer_given, 1)
-    outer_out = [jnp.concatenate([outer_kept[n], outer_given[n]], axis=2) for n in range(len(across))]
-    inner_given = swap(tie(inner_given, outer_given), 1)
-    inner_out = [jnp.concatenate([inner_kept[n], inner_given[n]], axis=2) for n in range(len(across))]
-
-    mine = jnp.stack(tie(mine, outer_out))
-    theirs = swap(mine, 1, "slab")
-    rest = jnp.concatenate([jnp.where(odd == 0, mine, theirs), jnp.where(odd == 0, theirs, mine)], axis=4)
-    same = jnp.concatenate([kernel[None], rest])
+    fetched = [swap(kernel, k) for k in (across[:3] if len(across) == 4 else across)]
+    outer_kept, outer_given, inner_kept, inner_given = cut(me, features.transpose(0, 2, 1, 3), parts)
+    outer_out = join(outer_kept, swap(outer_given, 1))
+    inner_out = join(inner_kept, swap(tie(inner_given, outer_out), 1))
+
+    if len(across) == 4:
+        half = out_chan // 2
+        across_x, across_y = tie(fetched[1:], outer_out)
+        far = [swap(across_x[:, :, :, :half], across[2]), swap(across_y[:, :, :, half:], across[1])]
+        fetched = [kernel, across_x, across_y, jnp.concatenate(far, axis=3)]
+    same = jnp.stack(fetched)
     other = swap(same, 1)
     tap_parts = [same, other]
 
     outer = [swap(block, k) for block, k in zip(outer_out, across)]
-    inner = [swap(tie(block, got) if k else block, k) for block, got, k in zip(inner_out, outer, across)]
+    inner = [swap(tie(block, got, other) if k else block, k) for block, got, k in zip(inner_out, outer, across)]
     up = [(i, i + 1) for i in range(slabs - 1)]
     down = [(i + 1, i) for i in range(slabs - 1)]
-    after = lax.ppermute(jnp.stack([block[:1] for block in outer]), "slab", down)
-    before = lax.ppermute(jnp.stack([block[1:] for block in outer]), "slab", up)
-    after = [after[n] for n in range(len(across))]
-    before = [before[n] for n in range(len(across))]
+    first, last = edges_of(outer)
+    after = lax.ppermute(first, "slab", down)
+    before = lax.ppermute(last, "slab", up)
+    after = [after[n : n + 1] for n in range(len(across))]
+    before = [before[n : n + 1] for n in range(len(across))]
 
     order = jnp.stack([me ^ k ^ c for k in across for c in range(2)])
     bias = jnp.take(bias_vector.reshape(parts, out_chan), order, axis=0).reshape(-1)

time: 188 us -> 124 us (0.66)
  Pallas kernels: 102 us -> 29.8 us
  waiting for transfers between devices: 39.8 us -> 49.6 us
  other arithmetic: 6.36 us -> 3.07 us
  local copies, waits for them, and re-layouts: 10 us -> 12.5 us
    pallas_call x1 -> x4, Pallas kernels: 80.9 us -> 7.55 us  [the longest x2 4.88 us: join(): pl.pallas_call(join_kernel, out_shape=[jax.ShapeDtypeStruct((count, rows_...]
    ppermute x21, waiting for transfers between devices: 30.6 us -> 44.3 us  [swap(): lax.ppermute(array, axis, [(i, i ^ k) for i in range(lax.axis_size(axis))])]
    unnamed x9 -> x27, local copies, waits for them, and re-layouts: 1.38 us -> 6.99 us
    ppermute x2, waiting for transfers between devices: 9.21 us -> 5.3 us  [the longest x1 4.52 us: body(): after = lax.ppermute(first, 'slab', down)]
    concatenate x9 -> x0, other arithmetic: 2.65 us -> none  [the longest x4 2.32 us: body(): jnp.concatenate([outer_kept[n], outer_given[n]], axis=2)]
  transfers between devices with their start and end apart: 23 -> 23, of which waited for: 12 -> 15; matrix products, arithmetic and copies ran while one was open for 6% -> 4% of each run, Pallas kernels for 49% -> 15%
where the time goes in v7:
time: 124 us; the launch traced here: 123 us
  waiting for transfers between devices  49.6 us (40%)
  Pallas kernels  29.8 us (24%)
  starting transfers between devices  27.8 us (22%)
  local copies, waits for them, and re-layouts  12.5 us (10%)
  other arithmetic  3.07 us (2%)
    ppermute x21, waiting for transfers between devices, swap(): lax.ppermute(array, axis, [(i, i ^ k) for i in range(lax.axis_size(axis))])  44.3 us
    pallas_call x2, Pallas kernels, convolve(): pl.pallas_call(functools.partial(conv_kernel, first, stride, count, plan,...  22.2 us
    ppermute x21, starting transfers between devices, swap(): lax.ppermute(array, axis, [(i, i ^ k) for i in range(lax.axis_size(axis))])  21.1 us
    unnamed x27, local copies, waits for them, and re-layouts  6.99 us
    ppermute x1, starting transfers between devices, body(): before = lax.ppermute(last, 'slab', up)  5.42 us
    pallas_call x2, Pallas kernels, join(): pl.pallas_call(join_kernel, out_shape=[jax.ShapeDtypeStruct((count, rows_...  4.88 us
    ppermute x1, waiting for transfers between devices, body(): after = lax.ppermute(first, 'slab', down)  4.52 us
  transfers between devices with their start and end apart: 23, of which 15 were waited for; matrix products, arithmetic and copies ran while one was open for 4% of the time, Pallas kernels for 15%

profile of v7, /device:TPU:0, one launch (start us, length us, event | category | flops | bytes accessed | tf_op | source)
XLA Modules:
  0.0 123.4 jit_solution(8734134328903848336)
XLA Ops:
  0.0 2.9 %copy.38 = bf16[4,32,64,128]{3,1,2,0:T(8,128)(2,1)S(1)} copy(bf16[4,32,64,128]{3,2,1,0:T(8,128)(2,1)} %param.3) | data formatting | bytes 4194304 | tf_op args[0]
  5.4 2.5 %collective-permute-start.5 = (bf16[3,3,3,32,256]{4,3,2,1,0:T(8,128)(2,1)S(1)}, bf16[3,3,3,32,256]{4,3,2,1,0:T(8,128)(2,1)S(1)}, u32[]{:S(2)}, u32[]{:S(2)}) collective-permute-start(bf16[3,3,3,32,256]{4,3,2,1,0:T(8,128)(2,1)S(1)} %copy-done.11), channel_id=1, source_target_pairs={{0,2},{1,3},{2,0},{3,1},{4,6},{5,7},{6,4},{7,5},{8,10},{9,11},{10,... | collective-permute-start | bytes 1327112 | tf_op jit(solution)/shard_map/ppermute | solution.py:186
  7.9 1.5 %collective-permute-start.6 = (bf16[3,3,3,32,256]{4,3,2,1,0:T(8,128)(2,1)S(1)}, bf16[3,3,3,32,256]{4,3,2,1,0:T(8,128)(2,1)S(1)}, u32[]{:S(2)}, u32[]{:S(2)}) collective-permute-start(bf16[3,3,3,32,256]{4,3,2,1,0:T(8,128)(2,1)S(1)} %copy-done.11), channel_id=1, source_target_pairs={{0,4},{1,5},{2,6},{3,7},{4,0},{5,1},{6,2},{7,3},{8,12},{9,13},{10,... | collective-permute-start | bytes 1327112 | tf_op jit(solution)/shard_map/ppermute | solution.py:186
  10.3 2.4 %shard_map.38 = (bf16[2,10,64,128]{3,2,1,0:T(8,128)(2,1)}, bf16[2,10,64,128]{3,2,1,0:T(8,128)(2,1)}, bf16[2,10,64,128]{3,2,1,0:T(8,128)(2,1)}, bf16[2,10,64,128]{3,2,1,0:T(8,128)(2,1)}) custom-call(bf16[4,2,10,32,128]{4,3,2,1,0:T(8,128)(2,1)} %copy-done.1, bf16[4,2,10,32,128]{4,3,2,1,0:T(8,128)(2,1)} %copy-done.10), custom_call_target="tpu_custom_call" | custom-call | tf_op jit(solution)/shard_map/pallas_call | solution.py:62
  12.6 6.1 %collective-permute-done.5 = bf16[3,3,3,32,256]{4,3,2,1,0:T(8,128)(2,1)S(1)} collective-permute-done((bf16[3,3,3,32,256]{4,3,2,1,0:T(8,128)(2,1)S(1)}, bf16[3,3,3,32,256]{4,3,2,1,0:T(8,128)(2,1)S(1)}, u32[]{:S(2)}, u32[]{:S(2)}) %collective-permute-start.5) | collective-permute-done | bytes 442400 | tf_op jit(solution)/shard_map/ppermute | solution.py:186
  18.7 1.5 %collective-permute-done.6 = bf16[3,3,3,32,256]{4,3,2,1,0:T(8,128)(2,1)S(1)} collective-permute-done((bf16[3,3,3,32,256]{4,3,2,1,0:T(8,128)(2,1)S(1)}, bf16[3,3,3,32,256]{4,3,2,1,0:T(8,128)(2,1)S(1)}, u32[]{:S(2)}, u32[]{:S(2)}) %collective-permute-start.6) | collective-permute-done | bytes 442400 | tf_op jit(solution)/shard_map/ppermute | solution.py:186
  20.2 1.6 %collective-permute-start.7 = (bf16[3,3,3,16,256]{4,3,2,1,0:T(8,128)(2,1)S(1)}, bf16[3,3,3,16,256]{4,3,2,1,0:T(8,128)(2,1)S(1)}, u32[]{:S(2)}, u32[]{:S(2)}) collective-permute-start(bf16[3,3,3,16,256]{4,3,2,1,0:T(8,128)(2,1)S(1)} %slice.108), channel_id=1, source_target_pairs={{0,4},{1,5},{2,6},{3,7},{4,0},{5,1},{6,2},{7,3},{8,12},{9,13},{10,... | collective-permute-start | bytes 663560 | tf_op jit(solution)/shard_map/ppermute | solution.py:186
  22.4 4.6 %collective-permute-done.7 = bf16[3,3,3,16,256]{4,3,2,1,0:T(8,128)(2,1)S(1)} collective-permute-done((bf16[3,3,3,16,256]{4,3,2,1,0:T(8,128)(2,1)S(1)}, bf16[3,3,3,16,256]{4,3,2,1,0:T(8,128)(2,1)S(1)}, u32[]{:S(2)}, u32[]{:S(2)}) %collective-permute-start.7) | collective-permute-done | bytes 221216 | tf_op jit(solution)/shard_map/ppermute | solution.py:186
  30.3 1.5 %collective-permute-start.2 = (bf16[2,10,64,128]{3,2,1,0:T(8,128)(2,1)}, bf16[2,10,64,128]{3,2,1,0:T(8,128)(2,1)S(1)}, u32[]{:S(2)}, u32[]{:S(2)}) collective-permute-start(bf16[2,10,64,128]{3,2,1,0:T(8,128)(2,1)} %get-tuple-element.37), channel_id=1, source_target_pairs={{0,4},{1,5},{2,6},{3,7},{4,0},{5,1},{6,2},{7,3},{8,12},{9,13},{10,... | collective-permute-start | bytes 983048 | tf_op jit(solution)/shard_map/ppermute | solution.py:186
  33.4 8.0 %collective-permute-done.3.refs_3_.refs_4_ = bf16[2,10,64,128]{3,2,1,0:T(8,128)(2,1)S(1)} collective-permute-done((bf16[2,10,64,128]{3,2,1,0:T(8,128)(2,1)}, bf16[2,10,64,128]{3,2,1,0:T(8,128)(2,1)S(1)}, u32[]{:S(2)}, u32[]{:S(2)}) %collective-permute-start.3) | collective-permute-done | bytes 327712 | tf_op jit(solution)/shard_map/ppermute | solution.py:186
  41.4 5.9 %collective-permute-done.2.refs_2_.refs_3_ = bf16[2,10,64,128]{3,2,1,0:T(8,128)(2,1)S(1)} collective-permute-done((bf16[2,10,64,128]{3,2,1,0:T(8,128)(2,1)}, bf16[2,10,64,128]{3,2,1,0:T(8,128)(2,1)S(1)}, u32[]{:S(2)}, u32[]{:S(2)}) %collective-permute-start.2) | collective-permute-done | bytes 327712 | tf_op jit(solution)/shard_map/ppermute | solution.py:186
  48.8 2.4 %shard_map.40 = (bf16[4,10,64,128]{3,2,1,0:T(8,128)(2,1)}, bf16[4,10,64,128]{3,2,1,0:T(8,128)(2,1)}) custom-call(bf16[2,10,64,128]{3,2,1,0:T(8,128)(2,1)} %get-tuple-element.35.refs_0_.refs_1_, bf16[2,10,64,128]{3,2,1,0:T(8,128)(2,1)} %copy-done.7, bf16[2,10,64,128]{3,2,1,0:T(8,128)(2,1)} %copy-done.5, bf16[2,10,64,128]{3,2,1,0:T(8,128)(2,1)} %copy-done.3), custom_call_target="tpu_custom_call" | custom-call | tf_op jit(solution)/shard_map/pallas_call | solution.py:80
  53.3 5.4 %collective-permute-start.13 = (bf16[4,10,64,128]{3,2,1,0:T(8,128)(2,1)}, bf16[4,10,64,128]{3,2,1,0:T(8,128)(2,1)}, u32[]{:S(2)}, u32[]{:S(2)}) collective-permute-start(bf16[4,10,64,128]{3,2,1,0:T(8,128)(2,1)} %get-tuple-element.51), channel_id=1, source_target_pairs={{0,8},{8,16},{16,24},{1,9},{9,17},{17,25},{2,10},{10,18},{18,26},{... | collective-permute-start | bytes 1966088 | tf_op jit(solution)/shard_map/ppermute | solution.py:208
  58.9 2.5 %shard_map.39 = (bf16[2,10,64,128]{3,2,1,0:T(8,128)(2,1)}, bf16[2,10,64,128]{3,2,1,0:T(8,128)(2,1)}, bf16[2,10,64,128]{3,2,1,0:T(8,128)(2,1)}, bf16[2,10,64,128]{3,2,1,0:T(8,128)(2,1)}) custom-call(bf16[4,2,10,32,128]{4,3,2,1,0:T(8,128)(2,1)} %copy-done, bf16[4,2,10,32,128]{4,3,2,1,0:T(8,128)(2,1)} %collective-permute-done.4.given_ref), custom_call_target="tpu_custom_call" | custom-call | tf_op jit(solution)/shard_map/pallas_call | solution.py:62
  62.6 1.5 %collective-permute-start.11 = (bf16[2,10,64,128]{3,2,1,0:T(8,128)(2,1)}, bf16[2,10,64,128]{3,2,1,0:T(8,128)(2,1)S(1)}, u32[]{:S(2)}, u32[]{:S(2)}) collective-permute-start(bf16[2,10,64,128]{3,2,1,0:T(8,128)(2,1)} %get-tuple-element.48), channel_id=1, source_target_pairs={{0,4},{1,5},{2,6},{3,7},{4,0},{5,1},{6,2},{7,3},{8,12},{9,13},{10,... | collective-permute-start | bytes 983048 | tf_op jit(solution)/shard_map/ppermute | solution.py:186
  64.9 4.5 %collective-permute-done.14 = bf16[4,10,64,128]{3,2,1,0:T(8,128)(2,1)} collective-permute-done((bf16[4,10,64,128]{3,2,1,0:T(8,128)(2,1)}, bf16[4,10,64,128]{3,2,1,0:T(8,128)(2,1)}, u32[]{:S(2)}, u32[]{:S(2)}) %collective-permute-start.14) | collective-permute-done | bytes 655392 | tf_op jit(solution)/shard_map/ppermute | solution.py:207
  73.2 4.8 %collective-permute-done.11.refs_7_ = bf16[2,10,64,128]{3,2,1,0:T(8,128)(2,1)S(1)} collective-permute-done((bf16[2,10,64,128]{3,2,1,0:T(8,128)(2,1)}, bf16[2,10,64,128]{3,2,1,0:T(8,128)(2,1)S(1)}, u32[]{:S(2)}, u32[]{:S(2)}) %collective-permute-start.11) | collective-permute-done | bytes 327712 | tf_op jit(solution)/shard_map/ppermute | solution.py:186
  78.5 11.2 %shard_map.41 = (bf16[2,8,64,128]{3,2,1,0:T(8,128)(2,1)S(1)}, bf16[2,8,64,128]{3,2,1,0:T(8,128)(2,1)S(1)}, bf16[2,8,64,128]{3,2,1,0:T(8,128)(2,1)S(1)}, bf16[2,8,64,128]{3,2,1,0:T(8,128)(2,1)S(1)}) custom-call(s32[8]{0:T(128)S(1)} %stack.98.refs_0_, bf16[2,10,64,128]{3,2,1,0:T(8,128)(2,1)S(1)} %copy-done.2, bf16[2,10,64,128]{3,2,1,0:T(8,128)(2,1)S(1)} %copy-done.8, ...), custom_call_target="tpu_custom_call" | custom-call | flops 7247757312 | bytes 10000000 | tf_op jit(solution)/shard_map/pallas_call | solution.py:158
  89.7 1.6 %collective-permute-start.17 = (bf16[2,8,64,128]{3,2,1,0:T(8,128)(2,1)S(1)}, bf16[2,8,64,128]{3,2,1,0:T(8,128)(2,1)S(1)}, u32[]{:S(2)}, u32[]{:S(2)}) collective-permute-start(bf16[2,8,64,128]{3,2,1,0:T(8,128)(2,1)S(1)} %get-tuple-element.56), channel_id=1, source_target_pairs={{0,6},{1,7},{2,4},{3,5},{4,2},{5,3},{6,0},{7,1},{8,14},{9,15},{10,... | collective-permute-start | bytes 786440 | tf_op jit(solution)/shard_map/ppermute | solution.py:186
  93.3 11.1 %shard_map.42 = (bf16[2,8,64,128]{3,2,1,0:T(8,128)(2,1)S(1)}, bf16[2,8,64,128]{3,2,1,0:T(8,128)(2,1)S(1)}, bf16[2,8,64,128]{3,2,1,0:T(8,128)(2,1)S(1)}, bf16[2,8,64,128]{3,2,1,0:T(8,128)(2,1)S(1)}) custom-call(s32[8]{0:T(128)S(1)} %stack.98.refs_0_, bf16[2,10,64,128]{3,2,1,0:T(8,128)(2,1)S(1)} %copy-done.2, bf16[2,10,64,128]{3,2,1,0:T(8,128)(2,1)S(1)} %copy-done.8, ...), custom_call_target="tpu_custom_call" | custom-call | flops 7247757312 | bytes 10000000 | tf_op jit(solution)/shard_map/pallas_call | solution.py:158
  104.4 1.6 %collective-permute-start.21 = (bf16[2,8,64,128]{3,2,1,0:T(8,128)(2,1)S(1)}, bf16[2,8,64,128]{3,2,1,0:T(8,128)(2,1)S(1)}, u32[]{:S(2)}, u32[]{:S(2)}) collective-permute-start(bf16[2,8,64,128]{3,2,1,0:T(8,128)(2,1)S(1)} %get-tuple-element.60), channel_id=1, source_target_pairs={{0,6},{1,7},{2,4},{3,5},{4,2},{5,3},{6,0},{7,1},{8,14},{9,15},{10,... | collective-permute-start | bytes 786440 | tf_op jit(solution)/shard_map/ppermute | solution.py:186
  108.3 6.3 %collective-permute-done.21 = bf16[2,8,64,128]{3,2,1,0:T(8,128)(2,1)S(1)} collective-permute-done((bf16[2,8,64,128]{3,2,1,0:T(8,128)(2,1)S(1)}, bf16[2,8,64,128]{3,2,1,0:T(8,128)(2,1)S(1)}, u32[]{:S(2)}, u32[]{:S(2)}) %collective-permute-start.21) | collective-permute-done | bytes 262176 | tf_op jit(solution)/shard_map/ppermute | solution.py:186
  114.6 3.5 %collective-permute-done.20 = bf16[2,8,64,128]{3,2,1,0:T(8,128)(2,1)S(1)} collective-permute-done((bf16[2,8,64,128]{3,2,1,0:T(8,128)(2,1)S(1)}, bf16[2,8,64,128]{3,2,1,0:T(8,128)(2,1)S(1)}, u32[]{:S(2)}, u32[]{:S(2)}) %collective-permute-start.20) | collective-permute-done | bytes 262176 | tf_op jit(solution)/shard_map/ppermute | solution.py:186
  121.8 1.6 %pad_maximum_fusion = bf16[4,32,64,128]{3,2,1,0:T(8,128)(2,1)} fusion(bf16[1,32,64,128]{3,2,1,0:T(8,128)(2,1)S(1)} %get-tuple-element.62, bf16[2,32,64,128]{3,2,1,0:T(8,128)(2,1)S(1)} %bitcast.62, bf16[1,32,64,128]{3,2,1,0:T(8,128)(2,1)S(1)} %get-tuple-element.61), kind=kLoop, calls=%fused_computation.1 | loop fusion | flops 2097152 | bytes 4194304 | tf_op jit(solution)/shard_map/concatenate | solution.py:249
  (102 shorter events, 26.3 us)
Async XLA Ops:
  4.9 4.5 %collective-permute-start = (bf16[4,2,10,32,128]{4,3,2,1,0:T(8,128)(2,1)S(1)}, bf16[4,2,10,32,128]{4,3,2,1,0:T(8,128)(2,1)S(1)}, u32[]{:S(2)}, u32[]{:S(2)}) collective-permute-start(bf16[4,2,10,32,128]{4,3,2,1,0:T(8,128)(2,1)S(1)} %get-tuple-element.34), channel_id=1, source_target_pairs={{0,1},{1,0},{2,3},{3,2},{4,5},{5,4},{6,7},{7,6},{8,9},{9,8},{10,11... | collective-permute-start | bytes 1966088 | tf_op jit(solution)/shard_map/ppermute | solution.py:186
  5.4 13.3 %collective-permute-start.5 = (bf16[3,3,3,32,256]{4,3,2,1,0:T(8,128)(2,1)S(1)}, bf16[3,3,3,32,256]{4,3,2,1,0:T(8,128)(2,1)S(1)}, u32[]{:S(2)}, u32[]{:S(2)}) collective-permute-start(bf16[3,3,3,32,256]{4,3,2,1,0:T(8,128)(2,1)S(1)} %copy-done.11), channel_id=1, source_target_pairs={{0,2},{1,3},{2,0},{3,1},{4,6},{5,7},{6,4},{7,5},{8,10},{9,11},{10,... | collective-permute-start | bytes 1327112 | tf_op jit(solution)/shard_map/ppermute | solution.py:186
  7.9 12.3 %collective-permute-start.6 = (bf16[3,3,3,32,256]{4,3,2,1,0:T(8,128)(2,1)S(1)}, bf16[3,3,3,32,256]{4,3,2,1,0:T(8,128)(2,1)S(1)}, u32[]{:S(2)}, u32[]{:S(2)}) collective-permute-start(bf16[3,3,3,32,256]{4,3,2,1,0:T(8,128)(2,1)S(1)} %copy-done.11), channel_id=1, source_target_pairs={{0,4},{1,5},{2,6},{3,7},{4,0},{5,1},{6,2},{7,3},{8,12},{9,13},{10,... | collective-permute-start | bytes 1327112 | tf_op jit(solution)/shard_map/ppermute | solution.py:186
  20.2 6.8 %collective-permute-start.7 = (bf16[3,3,3,16,256]{4,3,2,1,0:T(8,128)(2,1)S(1)}, bf16[3,3,3,16,256]{4,3,2,1,0:T(8,128)(2,1)S(1)}, u32[]{:S(2)}, u32[]{:S(2)}) collective-permute-start(bf16[3,3,3,16,256]{4,3,2,1,0:T(8,128)(2,1)S(1)} %slice.108), channel_id=1, source_target_pairs={{0,4},{1,5},{2,6},{3,7},{4,0},{5,1},{6,2},{7,3},{8,12},{9,13},{10,... | collective-permute-start | bytes 663560 | tf_op jit(solution)/shard_map/ppermute | solution.py:186
  21.8 6.5 %collective-permute-start.8 = (bf16[3,3,3,16,256]{4,3,2,1,0:T(8,128)(2,1)S(1)}, bf16[3,3,3,16,256]{4,3,2,1,0:T(8,128)(2,1)S(1)}, u32[]{:S(2)}, u32[]{:S(2)}) collective-permute-start(bf16[3,3,3,16,256]{4,3,2,1,0:T(8,128)(2,1)S(1)} %slice.109), channel_id=1, source_target_pairs={{0,2},{1,3},{2,0},{3,1},{4,6},{5,7},{6,4},{7,5},{8,10},{9,11},{10,... | collective-permute-start | bytes 663560 | tf_op jit(solution)/shard_map/ppermute | solution.py:186
  28.4 24.2 %copy-start.12 = (f32[256]{0:T(256)S(1)}, f32[256]{0:T(256)}, u32[]{:S(2)}) copy-start(f32[256]{0:T(256)} %param.5) | copy-start | bytes 3076
  29.6 31.8 %collective-permute-start.9 = (bf16[4,3,3,3,32,256]{5,4,3,2,1,0:T(8,128)(2,1)S(1)}, bf16[4,3,3,3,32,256]{5,4,3,2,1,0:T(8,128)(2,1)}, u32[]{:S(2)}, u32[]{:S(2)}) collective-permute-start(bf16[4,3,3,3,32,256]{5,4,3,2,1,0:T(8,128)(2,1)S(1)} %pad_maximum_fusion.1.refs_17_.refs_9_), channel_id=1, source_target_pairs={{0,1},{1,0},{2,3},{3,2},{4,5},{5,4},{6,7},{7,6},{8,9},{9,8},{10,11... | collective-permute-start | bytes 5308424 | tf_op jit(solution)/shard_map/ppermute | solution.py:186
  29.7 11.7 %collective-permute-start.3 = (bf16[2,10,64,128]{3,2,1,0:T(8,128)(2,1)}, bf16[2,10,64,128]{3,2,1,0:T(8,128)(2,1)S(1)}, u32[]{:S(2)}, u32[]{:S(2)}) collective-permute-start(bf16[2,10,64,128]{3,2,1,0:T(8,128)(2,1)} %get-tuple-element.38), channel_id=1, source_target_pairs={{0,6},{1,7},{2,4},{3,5},{4,2},{5,3},{6,0},{7,1},{8,14},{9,15},{10,... | collective-permute-start | bytes 983048 | tf_op jit(solution)/shard_map/ppermute | solution.py:186
  30.3 17.0 %collective-permute-start.2 = (bf16[2,10,64,128]{3,2,1,0:T(8,128)(2,1)}, bf16[2,10,64,128]{3,2,1,0:T(8,128)(2,1)S(1)}, u32[]{:S(2)}, u32[]{:S(2)}) collective-permute-start(bf16[2,10,64,128]{3,2,1,0:T(8,128)(2,1)} %get-tuple-element.37), channel_id=1, source_target_pairs={{0,4},{1,5},{2,6},{3,7},{4,0},{5,1},{6,2},{7,3},{8,12},{9,13},{10,... | collective-permute-start | bytes 983048 | tf_op jit(solution)/shard_map/ppermute | solution.py:186
  31.8 15.5 %collective-permute-start.1 = (bf16[2,10,64,128]{3,2,1,0:T(8,128)(2,1)}, bf16[2,10,64,128]{3,2,1,0:T(8,128)(2,1)S(1)}, u32[]{:S(2)}, u32[]{:S(2)}) collective-permute-start(bf16[2,10,64,128]{3,2,1,0:T(8,128)(2,1)} %get-tuple-element.36), channel_id=1, source_target_pairs={{0,2},{1,3},{2,0},{3,1},{4,6},{5,7},{6,4},{7,5},{8,10},{9,11},{10,... | collective-permute-start | bytes 983048 | tf_op jit(solution)/shard_map/ppermute | solution.py:186
  33.4 25.5 %collective-permute-start.4 = (bf16[4,2,10,32,128]{4,3,2,1,0:T(8,128)(2,1)S(1)}, bf16[4,2,10,32,128]{4,3,2,1,0:T(8,128)(2,1)}, u32[]{:S(2)}, u32[]{:S(2)}) collective-permute-start(bf16[4,2,10,32,128]{4,3,2,1,0:T(8,128)(2,1)S(1)} %get-tuple-element.41), channel_id=1, source_target_pairs={{0,1},{1,0},{2,3},{3,2},{4,5},{5,4},{6,7},{7,6},{8,9},{9,8},{10,11... | collective-permute-start | bytes 1966088 | tf_op jit(solution)/shard_map/ppermute | solution.py:186
  51.2 18.2 %collective-permute-start.14 = (bf16[4,10,64,128]{3,2,1,0:T(8,128)(2,1)}, bf16[4,10,64,128]{3,2,1,0:T(8,128)(2,1)}, u32[]{:S(2)}, u32[]{:S(2)}) collective-permute-start(bf16[4,10,64,128]{3,2,1,0:T(8,128)(2,1)} %get-tuple-element.52), channel_id=1, source_target_pairs={{8,0},{16,8},{24,16},{9,1},{17,9},{25,17},{10,2},{18,10},{26,18},{... | collective-permute-start | bytes 1966088 | tf_op jit(solution)/shard_map/ppermute | solution.py:207
  53.3 18.1 %collective-permute-start.13 = (bf16[4,10,64,128]{3,2,1,0:T(8,128)(2,1)}, bf16[4,10,64,128]{3,2,1,0:T(8,128)(2,1)}, u32[]{:S(2)}, u32[]{:S(2)}) collective-permute-start(bf16[4,10,64,128]{3,2,1,0:T(8,128)(2,1)} %get-tuple-element.51), channel_id=1, source_target_pairs={{0,8},{8,16},{16,24},{1,9},{9,17},{17,25},{2,10},{10,18},{18,26},{... | collective-permute-start | bytes 1966088 | tf_op jit(solution)/shard_map/ppermute | solution.py:208
  61.4 11.8 %collective-permute-start.12 = (bf16[2,10,64,128]{3,2,1,0:T(8,128)(2,1)}, bf16[2,10,64,128]{3,2,1,0:T(8,128)(2,1)S(1)}, u32[]{:S(2)}, u32[]{:S(2)}) collective-permute-start(bf16[2,10,64,128]{3,2,1,0:T(8,128)(2,1)} %get-tuple-element.50), channel_id=1, source_target_pairs={{0,6},{1,7},{2,4},{3,5},{4,2},{5,3},{6,0},{7,1},{8,14},{9,15},{10,... | collective-permute-start | bytes 983048 | tf_op jit(solution)/shard_map/ppermute | solution.py:186
  62.6 15.4 %collective-permute-start.11 = (bf16[2,10,64,128]{3,2,1,0:T(8,128)(2,1)}, bf16[2,10,64,128]{3,2,1,0:T(8,128)(2,1)S(1)}, u32[]{:S(2)}, u32[]{:S(2)}) collective-permute-start(bf16[2,10,64,128]{3,2,1,0:T(8,128)(2,1)} %get-tuple-element.48), channel_id=1, source_target_pairs={{0,4},{1,5},{2,6},{3,7},{4,0},{5,1},{6,2},{7,3},{8,12},{9,13},{10,... | collective-permute-start | bytes 983048 | tf_op jit(solution)/shard_map/ppermute | solution.py:186
  64.1 14.2 %collective-permute-start.10 = (bf16[2,10,64,128]{3,2,1,0:T(8,128)(2,1)}, bf16[2,10,64,128]{3,2,1,0:T(8,128)(2,1)S(1)}, u32[]{:S(2)}, u32[]{:S(2)}) collective-permute-start(bf16[2,10,64,128]{3,2,1,0:T(8,128)(2,1)} %get-tuple-element.46), channel_id=1, source_target_pairs={{0,2},{1,3},{2,0},{3,1},{4,6},{5,7},{6,4},{7,5},{8,10},{9,11},{10,... | collective-permute-start | bytes 983048 | tf_op jit(solution)/shard_map/ppermute | solution.py:186
  89.7 17.7 %collective-permute-start.17 = (bf16[2,8,64,128]{3,2,1,0:T(8,128)(2,1)S(1)}, bf16[2,8,64,128]{3,2,1,0:T(8,128)(2,1)S(1)}, u32[]{:S(2)}, u32[]{:S(2)}) collective-permute-start(bf16[2,8,64,128]{3,2,1,0:T(8,128)(2,1)S(1)} %get-tuple-element.56), channel_id=1, source_target_pairs={{0,6},{1,7},{2,4},{3,5},{4,2},{5,3},{6,0},{7,1},{8,14},{9,15},{10,... | collective-permute-start | bytes 786440 | tf_op jit(solution)/shard_map/ppermute | solution.py:186
  91.4 16.7 %collective-permute-start.16 = (bf16[2,8,64,128]{3,2,1,0:T(8,128)(2,1)S(1)}, bf16[2,8,64,128]{3,2,1,0:T(8,128)(2,1)S(1)}, u32[]{:S(2)}, u32[]{:S(2)}) collective-permute-start(bf16[2,8,64,128]{3,2,1,0:T(8,128)(2,1)S(1)} %get-tuple-element.55), channel_id=1, source_target_pairs={{0,4},{1,5},{2,6},{3,7},{4,0},{5,1},{6,2},{7,3},{8,12},{9,13},{10,... | collective-permute-start | bytes 786440 | tf_op jit(solution)/shard_map/ppermute | solution.py:186
  92.8 15.3 %collective-permute-start.15 = (bf16[2,8,64,128]{3,2,1,0:T(8,128)(2,1)S(1)}, bf16[2,8,64,128]{3,2,1,0:T(8,128)(2,1)S(1)}, u32[]{:S(2)}, u32[]{:S(2)}) collective-permute-start(bf16[2,8,64,128]{3,2,1,0:T(8,128)(2,1)S(1)} %get-tuple-element.54), channel_id=1, source_target_pairs={{0,2},{1,3},{2,0},{3,1},{4,6},{5,7},{6,4},{7,5},{8,10},{9,11},{10,... | collective-permute-start | bytes 786440 | tf_op jit(solution)/shard_map/ppermute | solution.py:186
  104.4 10.2 %collective-permute-start.21 = (bf16[2,8,64,128]{3,2,1,0:T(8,128)(2,1)S(1)}, bf16[2,8,64,128]{3,2,1,0:T(8,128)(2,1)S(1)}, u32[]{:S(2)}, u32[]{:S(2)}) collective-permute-start(bf16[2,8,64,128]{3,2,1,0:T(8,128)(2,1)S(1)} %get-tuple-element.60), channel_id=1, source_target_pairs={{0,6},{1,7},{2,4},{3,5},{4,2},{5,3},{6,0},{7,1},{8,14},{9,15},{10,... | collective-permute-start | bytes 786440 | tf_op jit(solution)/shard_map/ppermute | solution.py:186
  106.0 12.1 %collective-permute-start.20 = (bf16[2,8,64,128]{3,2,1,0:T(8,128)(2,1)S(1)}, bf16[2,8,64,128]{3,2,1,0:T(8,128)(2,1)S(1)}, u32[]{:S(2)}, u32[]{:S(2)}) collective-permute-start(bf16[2,8,64,128]{3,2,1,0:T(8,128)(2,1)S(1)} %get-tuple-element.59), channel_id=1, source_target_pairs={{0,4},{1,5},{2,6},{3,7},{4,0},{5,1},{6,2},{7,3},{8,12},{9,13},{10,... | collective-permute-start | bytes 786440 | tf_op jit(solution)/shard_map/ppermute | solution.py:186
  107.5 10.9 %collective-permute-start.19 = (bf16[2,8,64,128]{3,2,1,0:T(8,128)(2,1)S(1)}, bf16[2,8,64,128]{3,2,1,0:T(8,128)(2,1)S(1)}, u32[]{:S(2)}, u32[]{:S(2)}) collective-permute-start(bf16[2,8,64,128]{3,2,1,0:T(8,128)(2,1)S(1)} %get-tuple-element.58), channel_id=1, source_target_pairs={{0,2},{1,3},{2,0},{3,1},{4,6},{5,7},{6,4},{7,5},{8,10},{9,11},{10,... | collective-permute-start | bytes 786440 | tf_op jit(solution)/shard_map/ppermute | solution.py:186
  108.2 11.0 %collective-permute-start.18 = (bf16[4,2,8,32,128]{4,3,2,1,0:T(8,128)(2,1)S(1)}, bf16[4,2,8,32,128]{4,3,2,1,0:T(8,128)(2,1)S(1)}, u32[]{:S(2)}, u32[]{:S(2)}) collective-permute-start(bf16[4,2,8,32,128]{4,3,2,1,0:T(8,128)(2,1)S(1)} %pad_maximum_fusion.2), channel_id=1, source_target_pairs={{0,1},{1,0},{2,3},{3,2},{4,5},{5,4},{6,7},{7,6},{8,9},{9,8},{10,11... | collective-permute-start | bytes 1572872 | tf_op jit(solution)/shard_map/ppermute | solution.py:186
  118.4 2.0 %collective-permute-start.22 = (bf16[4,2,8,32,128]{4,3,2,1,0:T(8,128)(2,1)S(1)}, bf16[4,2,8,32,128]{4,3,2,1,0:T(8,128)(2,1)S(1)}, u32[]{:S(2)}, u32[]{:S(2)}) collective-permute-start(bf16[4,2,8,32,128]{4,3,2,1,0:T(8,128)(2,1)S(1)} %pad_maximum_fusion.3), channel_id=1, source_target_pairs={{0,1},{1,0},{2,3},{3,2},{4,5},{5,4},{6,7},{7,6},{8,9},{9,8},{10,11... | collective-permute-start | bytes 1572872 | tf_op jit(solution)/shard_map/ppermute | solution.py:186
  (12 other events, 107.9 us)

commit v8 on v5

v8 whole, which is shorter than its diff:
```python
import functools

import jax
import jax.numpy as jnp
from jax import lax
from jax.experimental import pallas as pl
from jax.experimental.pallas import tpu as pltpu
from jax.sharding import PartitionSpec as P

slope = 0.3
ROWS = 4


def cut_kernel(parts, vol_ref, outer, inner):
    planes, y_cells = vol_ref.shape[:2]
    rows = y_cells // parts
    for block in range(parts):
        for r in range(rows + 2):
            row = block * rows + r - 1
            for plane in range(planes):
                line = vol_ref[plane, min(max(row, 0), y_cells - 1)]
                line = line if 0 <= row < y_cells else jnp.zeros_like(line)
                if 0 < plane < planes - 1:
                    inner[block, plane - 1, r] = line
                else:
                    outer[block, min(plane, 1), r] = line


def cut(volume, parts):
    planes, y_cells, chan, cols = volume.shape
    in_vmem = pl.BlockSpec(memory_space=pltpu.VMEM)
    return pl.pallas_call(
        functools.partial(cut_kernel, parts),
        out_shape=[
            jax.ShapeDtypeStruct((parts, count, y_cells // parts + 2, chan, cols), volume.dtype)
            for count in (2, planes - 2)
        ],
        in_specs=[in_vmem],
        out_specs=[in_vmem] * 2,
        compiler_params=pltpu.CompilerParams(vmem_limit_bytes=8 * 2**20),
    )(volume)


def edges_kernel(vol_ref, first, last):
    for s in range(vol_ref.shape[0]):
        for r in range(vol_ref.shape[2]):
            first[s, 0, r] = vol_ref[s, 0, r]
            last[s, 0, r] = vol_ref[s, 1, r]


def edges_of(volume):
    sources, _, rows_in, chan, cols = volume.shape
    in_vmem = pl.BlockSpec(memory_space=pltpu.VMEM)
    return pl.pallas_call(
        edges_kernel,
        out_shape=[jax.ShapeDtypeStruct((sources, 1, rows_in, chan, cols), volume.dtype)] * 2,
        in_specs=[in_vmem],
        out_specs=[in_vmem] * 2,
        compiler_params=pltpu.CompilerParams(vmem_limit_bytes=4 * 2**20),
    )(volume)


def conv_kernel(plan, rows_at_once, pieces_count, tap_count, *refs):
    refs = list(refs)
    pieces = [refs.pop(0) for _ in range(pieces_count)]
    tap_parts = [refs.pop(0) for _ in range(tap_count)]
    bias_ref, outs = refs[0], refs[1:]
    rows_in, cols = pieces[0].shape[2], pieces[0].shape[4]
    rows = rows_in - 2
    total_out = bias_ref.shape[0]
    block = total_out // len(outs)
    groups, size = tap_parts[0].shape[0], tap_parts[0].shape[4]
    lane = lax.broadcasted_iota(jnp.int32, (total_out, cols), 1)

    def tile(slot, row):
        cells = []
        weights = []
        for a, (source, plane) in enumerate(plan[slot]):
            piece = pieces[source]
            lines = [
                jnp.concatenate([piece[s, plane, row + r] for s in range(piece.shape[0])], axis=0)
                for r in range(rows_at_once + 2)
            ]
            for b in range(3):
                cells.append(jnp.concatenate(lines[b : b + rows_at_once], axis=1))
                weights.append(
                    jnp.concatenate(
                        [part[g, a, b].reshape(3 * size, -1) for g in range(groups) for part in tap_parts], axis=0
                    )
                )
        total = jnp.dot(
            jnp.concatenate(weights, axis=1), jnp.concatenate(cells, axis=0), preferred_element_type=jnp.float32
        )
        for r in range(rows_at_once):
            part = total[:, r * cols : (r + 1) * cols].reshape(groups * tap_count, 3, size, cols)
            side = [part[:, c].reshape(total_out, cols) for c in range(3)]
            left = jnp.where(lane == 0, 0.0, pltpu.roll(side[0], 1, 1))
            right = jnp.where(lane == cols - 1, 0.0, pltpu.roll(side[2], cols - 1, 1))
            shifted = side[1] + left + right + bias_ref[...]
            done = jnp.where(shifted > 0, shifted, slope * shifted).astype(jnp.bfloat16)
            for n, out_ref in enumerate(outs):
                out_ref[slot, row + r] = done[n * block : (n + 1) * block]

    for slot in range(len(plan)):

        @pl.loop(0, rows // rows_at_once)
        def _(step):
            tile(slot, step * rows_at_once)


def convolve(plan, pieces, tap_parts, bias, blocks):
    rows, cols = pieces[0].shape[2] - 2, pieces[0].shape[4]
    in_chan = tap_parts[0].shape[5]
    total_out = bias.shape[0]
    wide_bias = jnp.broadcast_to(bias[:, None], (total_out, cols))
    macs = 27 * total_out * in_chan * len(plan) * rows * cols
    in_vmem = pl.BlockSpec(memory_space=pltpu.VMEM)
    shape = jax.ShapeDtypeStruct((len(plan), rows, total_out // blocks, cols), jnp.bfloat16)
    return pl.pallas_call(
        functools.partial(conv_kernel, plan, min(ROWS, rows), len(pieces), len(tap_parts)),
        out_shape=[shape] * blocks,
        in_specs=[in_vmem] * (len(pieces) + len(tap_parts) + 1),
        out_specs=[in_vmem] * blocks,
        cost_estimate=pl.CostEstimate(flops=2 * macs, bytes_accessed=10_000_000, transcendentals=0),
        compiler_params=pltpu.CompilerParams(vmem_limit_bytes=20 * 2**20),
    )(*pieces, *tap_parts, wide_bias)


def body(features, kernel, bias_vector):
    planes, chan, y_cells, cols = features.shape
    out_chan = kernel.shape[3]
    parts = lax.axis_size("filt")
    slabs = lax.axis_size("slab")
    me = lax.axis_index("filt")
    rows = y_cells // parts
    aligned = chan % 16 == 0 and out_chan % 16 == 0
    across = list(range(0, parts, 2))

    def swap(array, k, axis="filt"):
        if k == 0:
            return array
        return lax.ppermute(array, axis, [(i, i ^ k) for i in range(lax.axis_size(axis))])

    same = jnp.stack([swap(kernel, k) for k in across])
    tap_parts = [same, swap(same, 1)]

    outer_rows, inner_rows = cut(features.transpose(0, 2, 1, 3), parts)
    outer = lax.all_to_all(outer_rows, "filt", 0, 0)
    inner = lax.all_to_all(inner_rows, "filt", 0, 0)
    up = [(i, i + 1) for i in range(slabs - 1)]
    down = [(i + 1, i) for i in range(slabs - 1)]
    first, last = edges_of(outer)
    after = lax.ppermute(first, "slab", down)
    before = lax.ppermute(last, "slab", up)

    order = jnp.stack([me ^ k ^ c for k in across for c in range(2)])
    bias = jnp.take(bias_vector.reshape(parts, out_chan), order, axis=0).reshape(-1)
    if not aligned:
        joined = jnp.stack(tap_parts, axis=1).transpose(2, 3, 4, 0, 1, 5, 6)
        tap_parts = [joined.reshape(1, 3, 3, 3, parts * out_chan, -1)]
        outer, inner, before, after = (
            array.transpose(1, 2, 0, 3, 4).reshape(1, -1, rows + 2, parts * chan, cols)
            for array in (outer, inner, before, after)
        )

    def send_back(results):
        count = results[0].shape[0]
        got = [swap(result, k) for result, k in zip(results, across)]
        mine = [block[:, :, :out_chan] for block in got]
        theirs = swap(jnp.stack([block[:, :, out_chan:] for block in got]), 1)
        final = jnp.zeros((count, y_cells, out_chan, cols), jnp.bfloat16)
        for n, k in enumerate(across):
            final = lax.dynamic_update_slice_in_dim(final, mine[n], (me ^ k) * rows, 1)
            final = lax.dynamic_update_slice_in_dim(final, theirs[n], (me ^ k ^ 1) * rows, 1)
        return final.transpose(0, 2, 1, 3)

    blocks = len(across)
    where = [(0, 0)] + [(1, plane) for plane in range(planes - 2)] + [(0, 1)]
    middle = tuple(tuple(where[plane - 1 : plane + 2]) for plane in range(1, planes - 1))
    inside = send_back(convolve(middle, [outer, inner], tap_parts, bias, blocks))
    ends = (((2, 0), *where[:2]), (*where[-2:], (3, 0)))
    outside = send_back(convolve(ends, [outer, inner, before, after], tap_parts, bias, blocks))
    return jnp.concatenate([outside[:1], inside, outside[1:]])


def solution(mesh):
    placed = (P("slab", "filt", None, None), P(None, None, None, "filt", None), P())
    return jax.shard_map(
        body, mesh=mesh, in_specs=placed, out_specs=P("slab", "filt", None, None), check_vma=False
    )
```

time: 125 us -> 111 us (0.89)
  waiting for transfers between devices: 57.4 us -> 48.9 us
  other arithmetic: 7.36 us -> 3.29 us
  starting transfers between devices: 23.7 us -> 26.2 us
  Pallas kernels: 25.6 us -> 23.7 us
  local copies, waits for them, and re-layouts: 9.55 us -> 7.89 us
    ppermute x16 -> x12, waiting for transfers between devices: 57.3 us -> 21.5 us  [swap(): lax.ppermute(array, axis, [(i, i ^ k) for i in range(lax.axis_size(axis))])]
    all_to_all x1, waiting for transfers between devices: 0.01 us -> 10.8 us  [body(): outer = lax.all_to_all(outer_rows, 'filt', 0, 0)]
    all_to_all x0 -> x1, waiting for transfers between devices: none -> 10.4 us  [body(): inner = lax.all_to_all(inner_rows, 'filt', 0, 0)]
    ppermute x2, waiting for transfers between devices: 0.01 us -> 6.28 us  [the longest x1 4.94 us: body(): after = lax.ppermute(first, 'slab', down)]
    all_to_all x0 -> x1, starting transfers between devices: none -> 4.4 us  [body(): inner = lax.all_to_all(inner_rows, 'filt', 0, 0)]
    slice x6 -> x0, local copies, waits for them, and re-layouts: 3.73 us -> none  [the longest x1 1.31 us: body(): after = lax.ppermute(outer[:, :1], 'slab', down)]
    unnamed x9 -> x13, local copies, waits for them, and re-layouts: 1.38 us -> 4.79 us
    concatenate x4 -> x0, other arithmetic: 2.89 us -> none  [the longest x2 1.56 us: pack(): return jnp.concatenate([above, by_row, below], axis=2)]
  transfers between devices with their start and end apart: 19 -> 16, of which waited for: 7 -> 9; matrix products, arithmetic and copies ran while one was open for 5% -> 6% of each run, Pallas kernels for 10% -> 12%
where the time goes in v8:
time: 111 us; the launch traced here: 110 us
  waiting for transfers between devices  48.9 us (44%)
  starting transfers between devices  26.2 us (24%)
  Pallas kernels  23.7 us (21%)
  local copies, waits for them, and re-layouts  7.89 us (7%)
  other arithmetic  3.29 us (3%)
    ppermute x12, waiting for transfers between devices, swap(): lax.ppermute(array, axis, [(i, i ^ k) for i in range(lax.axis_size(axis))])  21.5 us
    pallas_call x2, Pallas kernels, convolve(): pl.pallas_call(functools.partial(conv_kernel, plan, min(ROWS, rows), len(...  21.2 us
    ppermute x12, starting transfers between devices, swap(): lax.ppermute(array, axis, [(i, i ^ k) for i in range(lax.axis_size(axis))])  11.8 us
    all_to_all x1, waiting for transfers between devices, body(): outer = lax.all_to_all(outer_rows, 'filt', 0, 0)  10.8 us
    all_to_all x1, waiting for transfers between devices, body(): inner = lax.all_to_all(inner_rows, 'filt', 0, 0)  10.4 us
    ppermute x1, waiting for transfers between devices, body(): after = lax.ppermute(first, 'slab', down)  4.94 us
    unnamed x13, local copies, waits for them, and re-layouts  4.79 us
    all_to_all x1, starting transfers between devices, body(): inner = lax.all_to_all(inner_rows, 'filt', 0, 0)  4.4 us
  transfers between devices with their start and end apart: 16, of which 9 were waited for; matrix products, arithmetic and copies ran while one was open for 6% of the time, Pallas kernels for 12%

profile of v8, /device:TPU:0, one launch (start us, length us, event | category | flops | bytes accessed | tf_op | source)
XLA Modules:
  0.0 110.4 jit_solution(1376145076018668484)
XLA Ops:
  0.0 2.9 %collective-permute-start.2 = (bf16[3,3,3,32,256]{4,3,2,1,0:T(8,128)(2,1)}, bf16[3,3,3,32,256]{4,3,2,1,0:T(8,128)(2,1)S(1)}, u32[]{:S(2)}, u32[]{:S(2)}) collective-permute-start(bf16[3,3,3,32,256]{4,3,2,1,0:T(8,128)(2,1)} %param.4), channel_id=1, source_target_pairs={{0,2},{1,3},{2,0},{3,1},{4,6},{5,7},{6,4},{7,5},{8,10},{9,11},{10,... | collective-permute-start | bytes 1327112 | tf_op jit(solution)/shard_map/ppermute | solution.py:142
  2.9 1.5 %collective-permute-start.3 = (bf16[3,3,3,32,256]{4,3,2,1,0:T(8,128)(2,1)}, bf16[3,3,3,32,256]{4,3,2,1,0:T(8,128)(2,1)S(1)}, u32[]{:S(2)}, u32[]{:S(2)}) collective-permute-start(bf16[3,3,3,32,256]{4,3,2,1,0:T(8,128)(2,1)} %param.4), channel_id=1, source_target_pairs={{0,4},{1,5},{2,6},{3,7},{4,0},{5,1},{6,2},{7,3},{8,12},{9,13},{10,... | collective-permute-start | bytes 1327112 | tf_op jit(solution)/shard_map/ppermute | solution.py:142
  4.5 2.9 %copy.38 = bf16[4,32,64,128]{3,1,2,0:T(8,128)(2,1)S(1)} copy(bf16[4,32,64,128]{3,2,1,0:T(8,128)(2,1)} %param.3) | data formatting | bytes 4194304 | tf_op args[0]
  7.4 1.3 %shard_map.37 = (bf16[8,2,10,32,128]{4,3,2,1,0:T(8,128)(2,1)}, bf16[8,2,10,32,128]{4,3,2,1,0:T(8,128)(2,1)S(1)}) custom-call(bf16[4,64,32,128]{3,2,1,0:T(8,128)(2,1)S(1)} %bitcast.59), custom_call_target="tpu_custom_call" | custom-call | tf_op jit(solution)/shard_map/pallas_call | solution.py:32
  8.7 1.1 copy-done
  9.8 4.3 %all-to-all-start = ((bf16[8,2,10,32,128]{4,3,2,1,0:T(8,128)(2,1)}), bf16[8,2,10,32,128]{4,3,2,1,0:T(8,128)(2,1)S(1)}, u32[]{:S(2)}, u32[]{:S(2)}) async-start(bf16[8,2,10,32,128]{4,3,2,1,0:T(8,128)(2,1)} %get-tuple-element.17), calls=%async_computation | async-start | bytes 2621440 | tf_op jit(solution)/shard_map/all_to_all | solution.py:148
  14.1 10.7 %collective-permute-done.3 = bf16[3,3,3,32,256]{4,3,2,1,0:T(8,128)(2,1)S(1)} collective-permute-done((bf16[3,3,3,32,256]{4,3,2,1,0:T(8,128)(2,1)}, bf16[3,3,3,32,256]{4,3,2,1,0:T(8,128)(2,1)S(1)}, u32[]{:S(2)}, u32[]{:S(2)}) %collective-permute-start.3) | collective-permute-done | bytes 442400 | tf_op jit(solution)/shard_map/ppermute | solution.py:142
  26.0 1.5 %pad_maximum_fusion.1.refs_4_.refs_2_ = bf16[4,3,3,3,32,256]{5,4,3,2,1,0:T(8,128)(2,1)S(1)} fusion(bf16[1,3,3,3,32,256]{5,4,3,2,1,0:T(8,128)(2,1)} %bitcast.65, bf16[1,3,3,3,32,256]{5,4,3,2,1,0:T(8,128)(2,1)} %bitcast.64, bf16[1,3,3,3,32,256]{5,4,3,2,1,0:T(8,128)(2,1)} %bitcast.63, bf16[1,3,3,3,32,256]{5,4,3,2,1,0:T(8,128)(2,1)S(1)} %bitcast.62), kind=kLoop, calls=%fused_computation.3 | loop fusion | flops 2654208 | bytes 3538944 | tf_op jit(solution)/shard_map/stack | solution.py:144
  27.5 10.8 %all-to-all-done.vol_ref.refs_0_ = bf16[8,2,10,32,128]{4,3,2,1,0:T(8,128)(2,1)S(1)} async-done(((bf16[8,2,10,32,128]{4,3,2,1,0:T(8,128)(2,1)}), bf16[8,2,10,32,128]{4,3,2,1,0:T(8,128)(2,1)S(1)}, u32[]{:S(2)}, u32[]{:S(2)}) %all-to-all-start) | async-done | bytes 1310752 | tf_op jit(solution)/shard_map/all_to_all | solution.py:148
  38.3 4.4 %all-to-all-start.1 = ((bf16[8,2,10,32,128]{4,3,2,1,0:T(8,128)(2,1)}), bf16[8,2,10,32,128]{4,3,2,1,0:T(8,128)(2,1)}, u32[]{:S(2)}, u32[]{:S(2)}) async-start(bf16[8,2,10,32,128]{4,3,2,1,0:T(8,128)(2,1)} %copy-done), calls=%async_computation.1 | async-start | bytes 2621440 | tf_op jit(solution)/shard_map/all_to_all | solution.py:149
  42.8 1.2 %shard_map.38 = (bf16[8,1,10,32,128]{4,3,2,1,0:T(8,128)(2,1)}, bf16[8,1,10,32,128]{4,3,2,1,0:T(8,128)(2,1)}) custom-call(bf16[8,2,10,32,128]{4,3,2,1,0:T(8,128)(2,1)S(1)} %all-to-all-done.vol_ref.refs_0_), custom_call_target="tpu_custom_call" | custom-call | tf_op jit(solution)/shard_map/pallas_call | solution.py:54
  44.0 4.3 %collective-permute-start = (bf16[8,1,10,32,128]{4,3,2,1,0:T(8,128)(2,1)}, bf16[8,1,10,32,128]{4,3,2,1,0:T(8,128)(2,1)}, u32[]{:S(2)}, u32[]{:S(2)}) collective-permute-start(bf16[8,1,10,32,128]{4,3,2,1,0:T(8,128)(2,1)} %get-tuple-element.19), channel_id=1, source_target_pairs={{0,8},{8,16},{16,24},{1,9},{9,17},{17,25},{2,10},{10,18},{18,26},{... | collective-permute-start | bytes 1966088 | tf_op jit(solution)/shard_map/ppermute | solution.py:154
  48.3 1.3 %collective-permute-start.1 = (bf16[8,1,10,32,128]{4,3,2,1,0:T(8,128)(2,1)}, bf16[8,1,10,32,128]{4,3,2,1,0:T(8,128)(2,1)}, u32[]{:S(2)}, u32[]{:S(2)}) collective-permute-start(bf16[8,1,10,32,128]{4,3,2,1,0:T(8,128)(2,1)} %get-tuple-element.20), channel_id=1, source_target_pairs={{8,0},{16,8},{24,16},{9,1},{17,9},{25,17},{10,2},{18,10},{26,18},{... | collective-permute-start | bytes 1966088 | tf_op jit(solution)/shard_map/ppermute | solution.py:153
  50.6 10.4 %all-to-all-done.1.refs_1_ = bf16[8,2,10,32,128]{4,3,2,1,0:T(8,128)(2,1)} async-done(((bf16[8,2,10,32,128]{4,3,2,1,0:T(8,128)(2,1)}), bf16[8,2,10,32,128]{4,3,2,1,0:T(8,128)(2,1)}, u32[]{:S(2)}, u32[]{:S(2)}) %all-to-all-start.1) | async-done | bytes 1310752 | tf_op jit(solution)/shard_map/all_to_all | solution.py:149
  60.9 1.3 %collective-permute-done.refs_2_ = bf16[8,1,10,32,128]{4,3,2,1,0:T(8,128)(2,1)} collective-permute-done((bf16[8,1,10,32,128]{4,3,2,1,0:T(8,128)(2,1)}, bf16[8,1,10,32,128]{4,3,2,1,0:T(8,128)(2,1)}, u32[]{:S(2)}, u32[]{:S(2)}) %collective-permute-start) | collective-permute-done | bytes 655392 | tf_op jit(solution)/shard_map/ppermute | solution.py:154
  62.3 4.9 %collective-permute-done.1.refs_3_ = bf16[8,1,10,32,128]{4,3,2,1,0:T(8,128)(2,1)} collective-permute-done((bf16[8,1,10,32,128]{4,3,2,1,0:T(8,128)(2,1)}, bf16[8,1,10,32,128]{4,3,2,1,0:T(8,128)(2,1)}, u32[]{:S(2)}, u32[]{:S(2)}) %collective-permute-start.1) | collective-permute-done | bytes 655392 | tf_op jit(solution)/shard_map/ppermute | solution.py:153
  67.3 10.8 %shard_map.39 = (bf16[2,8,64,128]{3,2,1,0:T(8,128)(2,1)S(1)}, bf16[2,8,64,128]{3,2,1,0:T(8,128)(2,1)S(1)}, bf16[2,8,64,128]{3,2,1,0:T(8,128)(2,1)S(1)}, bf16[2,8,64,128]{3,2,1,0:T(8,128)(2,1)S(1)}) custom-call(bf16[8,2,10,32,128]{4,3,2,1,0:T(8,128)(2,1)S(1)} %all-to-all-done.vol_ref.refs_0_, bf16[8,2,10,32,128]{4,3,2,1,0:T(8,128)(2,1)} %all-to-all-done.1.refs_1_, ...), custom_call_target="tpu_custom_call" | custom-call | flops 7247757312 | bytes 10000000 | tf_op jit(solution)/shard_map/pallas_call | solution.py:119
  78.1 2.7 %collective-permute-start.8 = (bf16[2,8,64,128]{3,2,1,0:T(8,128)(2,1)S(1)}, bf16[2,8,64,128]{3,2,1,0:T(8,128)(2,1)S(1)}, u32[]{:S(2)}, u32[]{:S(2)}) collective-permute-start(bf16[2,8,64,128]{3,2,1,0:T(8,128)(2,1)S(1)} %get-tuple-element.24), channel_id=1, source_target_pairs={{0,6},{1,7},{2,4},{3,5},{4,2},{5,3},{6,0},{7,1},{8,14},{9,15},{10,... | collective-permute-start | bytes 786440 | tf_op jit(solution)/shard_map/ppermute | solution.py:142
  81.7 10.4 %shard_map.40 = (bf16[2,8,64,128]{3,2,1,0:T(8,128)(2,1)S(1)}, bf16[2,8,64,128]{3,2,1,0:T(8,128)(2,1)S(1)}, bf16[2,8,64,128]{3,2,1,0:T(8,128)(2,1)S(1)}, bf16[2,8,64,128]{3,2,1,0:T(8,128)(2,1)S(1)}) custom-call(bf16[8,2,10,32,128]{4,3,2,1,0:T(8,128)(2,1)S(1)} %all-to-all-done.vol_ref.refs_0_, bf16[8,2,10,32,128]{4,3,2,1,0:T(8,128)(2,1)} %all-to-all-done.1.refs_1_, ...), custom_call_target="tpu_custom_call" | custom-call | flops 7247757312 | bytes 10000000 | tf_op jit(solution)/shard_map/pallas_call | solution.py:119
  92.1 2.7 %collective-permute-start.12 = (bf16[2,8,64,128]{3,2,1,0:T(8,128)(2,1)S(1)}, bf16[2,8,64,128]{3,2,1,0:T(8,128)(2,1)S(1)}, u32[]{:S(2)}, u32[]{:S(2)}) collective-permute-start(bf16[2,8,64,128]{3,2,1,0:T(8,128)(2,1)S(1)} %get-tuple-element.28), channel_id=1, source_target_pairs={{0,6},{1,7},{2,4},{3,5},{4,2},{5,3},{6,0},{7,1},{8,14},{9,15},{10,... | collective-permute-start | bytes 786440 | tf_op jit(solution)/shard_map/ppermute | solution.py:142
  96.0 6.3 %collective-permute-done.12 = bf16[2,8,64,128]{3,2,1,0:T(8,128)(2,1)S(1)} collective-permute-done((bf16[2,8,64,128]{3,2,1,0:T(8,128)(2,1)S(1)}, bf16[2,8,64,128]{3,2,1,0:T(8,128)(2,1)S(1)}, u32[]{:S(2)}, u32[]{:S(2)}) %collective-permute-start.12) | collective-permute-done | bytes 262176 | tf_op jit(solution)/shard_map/ppermute | solution.py:142
  102.4 2.9 %collective-permute-done.11 = bf16[2,8,64,128]{3,2,1,0:T(8,128)(2,1)S(1)} collective-permute-done((bf16[2,8,64,128]{3,2,1,0:T(8,128)(2,1)S(1)}, bf16[2,8,64,128]{3,2,1,0:T(8,128)(2,1)S(1)}, u32[]{:S(2)}, u32[]{:S(2)}) %collective-permute-start.11) | collective-permute-done | bytes 262176 | tf_op jit(solution)/shard_map/ppermute | solution.py:142
  106.3 1.2 %collective-permute-done.13 = bf16[4,2,8,32,128]{4,3,2,1,0:T(8,128)(2,1)S(1)} collective-permute-done((bf16[4,2,8,32,128]{4,3,2,1,0:T(8,128)(2,1)S(1)}, bf16[4,2,8,32,128]{4,3,2,1,0:T(8,128)(2,1)S(1)}, u32[]{:S(2)}, u32[]{:S(2)}) %collective-permute-start.13) | collective-permute-done | bytes 524320 | tf_op jit(solution)/shard_map/ppermute | solution.py:142
  108.8 1.6 %pad_maximum_fusion = bf16[4,32,64,128]{3,2,1,0:T(8,128)(2,1)} fusion(bf16[1,32,64,128]{3,2,1,0:T(8,128)(2,1)S(1)} %get-tuple-element.30, bf16[2,32,64,128]{3,2,1,0:T(8,128)(2,1)S(1)} %bitcast.61, bf16[1,32,64,128]{3,2,1,0:T(8,128)(2,1)S(1)} %get-tuple-element.29), kind=kLoop, calls=%fused_computation.1 | loop fusion | flops 2097152 | bytes 4194304 | tf_op jit(solution)/shard_map/concatenate | solution.py:183
  (67 shorter events, 6.6 us)
Async XLA Ops:
  0.0 14.1 %collective-permute-start.2 = (bf16[3,3,3,32,256]{4,3,2,1,0:T(8,128)(2,1)}, bf16[3,3,3,32,256]{4,3,2,1,0:T(8,128)(2,1)S(1)}, u32[]{:S(2)}, u32[]{:S(2)}) collective-permute-start(bf16[3,3,3,32,256]{4,3,2,1,0:T(8,128)(2,1)} %param.4), channel_id=1, source_target_pairs={{0,2},{1,3},{2,0},{3,1},{4,6},{5,7},{6,4},{7,5},{8,10},{9,11},{10,... | collective-permute-start | bytes 1327112 | tf_op jit(solution)/shard_map/ppermute | solution.py:142
  2.9 21.9 %collective-permute-start.3 = (bf16[3,3,3,32,256]{4,3,2,1,0:T(8,128)(2,1)}, bf16[3,3,3,32,256]{4,3,2,1,0:T(8,128)(2,1)S(1)}, u32[]{:S(2)}, u32[]{:S(2)}) collective-permute-start(bf16[3,3,3,32,256]{4,3,2,1,0:T(8,128)(2,1)} %param.4), channel_id=1, source_target_pairs={{0,4},{1,5},{2,6},{3,7},{4,0},{5,1},{6,2},{7,3},{8,12},{9,13},{10,... | collective-permute-start | bytes 1327112 | tf_op jit(solution)/shard_map/ppermute | solution.py:142
  4.5 20.7 %collective-permute-start.4 = (bf16[3,3,3,32,256]{4,3,2,1,0:T(8,128)(2,1)}, bf16[3,3,3,32,256]{4,3,2,1,0:T(8,128)(2,1)S(1)}, u32[]{:S(2)}, u32[]{:S(2)}) collective-permute-start(bf16[3,3,3,32,256]{4,3,2,1,0:T(8,128)(2,1)} %param.4), channel_id=1, source_target_pairs={{0,6},{1,7},{2,4},{3,5},{4,2},{5,3},{6,0},{7,1},{8,14},{9,15},{10,... | collective-permute-start | bytes 1327112 | tf_op jit(solution)/shard_map/ppermute | solution.py:142
  8.7 1.1 copy-start
  9.8 16.2 %copy-start.1 = (bf16[3,3,3,32,256]{4,3,2,1,0:T(8,128)(2,1)S(1)}, bf16[3,3,3,32,256]{4,3,2,1,0:T(8,128)(2,1)}, u32[]{:S(2)}) copy-start(bf16[3,3,3,32,256]{4,3,2,1,0:T(8,128)(2,1)} %param.4) | copy-start | bytes 1327108
  9.8 28.5 %all-to-all-start = ((bf16[8,2,10,32,128]{4,3,2,1,0:T(8,128)(2,1)}), bf16[8,2,10,32,128]{4,3,2,1,0:T(8,128)(2,1)S(1)}, u32[]{:S(2)}, u32[]{:S(2)}) async-start(bf16[8,2,10,32,128]{4,3,2,1,0:T(8,128)(2,1)} %get-tuple-element.17), calls=%async_computation | async-start | bytes 2621440 | tf_op jit(solution)/shard_map/all_to_all | solution.py:148
  14.1 11.1 %copy-start.2 = (bf16[3,3,3,32,256]{4,3,2,1,0:T(8,128)(2,1)}, bf16[3,3,3,32,256]{4,3,2,1,0:T(8,128)(2,1)S(1)}, u32[]{:S(2)}) copy-start(bf16[3,3,3,32,256]{4,3,2,1,0:T(8,128)(2,1)S(1)} %collective-permute-done.2) | copy-start | bytes 1327108
  24.8 0.8 copy-start.3
  25.2 0.8 copy-start.4
  27.5 39.8 %collective-permute-start.5 = (bf16[4,3,3,3,32,256]{5,4,3,2,1,0:T(8,128)(2,1)S(1)}, bf16[4,3,3,3,32,256]{5,4,3,2,1,0:T(8,128)(2,1)}, u32[]{:S(2)}, u32[]{:S(2)}) collective-permute-start(bf16[4,3,3,3,32,256]{5,4,3,2,1,0:T(8,128)(2,1)S(1)} %pad_maximum_fusion.1.refs_4_.refs_2_), channel_id=1, source_target_pairs={{0,1},{1,0},{2,3},{3,2},{4,5},{5,4},{6,7},{7,6},{8,9},{9,8},{10,11... | collective-permute-start | bytes 5308424 | tf_op jit(solution)/shard_map/ppermute | solution.py:142
  38.3 11.4 %copy-start.5 = (f32[256]{0:T(256)S(1)}, f32[256]{0:T(256)}, u32[]{:S(2)}) copy-start(f32[256]{0:T(256)} %param.5) | copy-start | bytes 3076
  38.3 22.6 %all-to-all-start.1 = ((bf16[8,2,10,32,128]{4,3,2,1,0:T(8,128)(2,1)}), bf16[8,2,10,32,128]{4,3,2,1,0:T(8,128)(2,1)}, u32[]{:S(2)}, u32[]{:S(2)}) async-start(bf16[8,2,10,32,128]{4,3,2,1,0:T(8,128)(2,1)} %copy-done), calls=%async_computation.1 | async-start | bytes 2621440 | tf_op jit(solution)/shard_map/all_to_all | solution.py:149
  44.0 18.3 %collective-permute-start = (bf16[8,1,10,32,128]{4,3,2,1,0:T(8,128)(2,1)}, bf16[8,1,10,32,128]{4,3,2,1,0:T(8,128)(2,1)}, u32[]{:S(2)}, u32[]{:S(2)}) collective-permute-start(bf16[8,1,10,32,128]{4,3,2,1,0:T(8,128)(2,1)} %get-tuple-element.19), channel_id=1, source_target_pairs={{0,8},{8,16},{16,24},{1,9},{9,17},{17,25},{2,10},{10,18},{18,26},{... | collective-permute-start | bytes 1966088 | tf_op jit(solution)/shard_map/ppermute | solution.py:154
  48.3 18.9 %collective-permute-start.1 = (bf16[8,1,10,32,128]{4,3,2,1,0:T(8,128)(2,1)}, bf16[8,1,10,32,128]{4,3,2,1,0:T(8,128)(2,1)}, u32[]{:S(2)}, u32[]{:S(2)}) collective-permute-start(bf16[8,1,10,32,128]{4,3,2,1,0:T(8,128)(2,1)} %get-tuple-element.20), channel_id=1, source_target_pairs={{8,0},{16,8},{24,16},{9,1},{17,9},{25,17},{10,2},{18,10},{26,18},{... | collective-permute-start | bytes 1966088 | tf_op jit(solution)/shard_map/ppermute | solution.py:153
  78.1 17.2 %collective-permute-start.8 = (bf16[2,8,64,128]{3,2,1,0:T(8,128)(2,1)S(1)}, bf16[2,8,64,128]{3,2,1,0:T(8,128)(2,1)S(1)}, u32[]{:S(2)}, u32[]{:S(2)}) collective-permute-start(bf16[2,8,64,128]{3,2,1,0:T(8,128)(2,1)S(1)} %get-tuple-element.24), channel_id=1, source_target_pairs={{0,6},{1,7},{2,4},{3,5},{4,2},{5,3},{6,0},{7,1},{8,14},{9,15},{10,... | collective-permute-start | bytes 786440 | tf_op jit(solution)/shard_map/ppermute | solution.py:142
  80.8 15.0 %collective-permute-start.7 = (bf16[2,8,64,128]{3,2,1,0:T(8,128)(2,1)S(1)}, bf16[2,8,64,128]{3,2,1,0:T(8,128)(2,1)S(1)}, u32[]{:S(2)}, u32[]{:S(2)}) collective-permute-start(bf16[2,8,64,128]{3,2,1,0:T(8,128)(2,1)S(1)} %get-tuple-element.23), channel_id=1, source_target_pairs={{0,4},{1,5},{2,6},{3,7},{4,0},{5,1},{6,2},{7,3},{8,12},{9,13},{10,... | collective-permute-start | bytes 786440 | tf_op jit(solution)/shard_map/ppermute | solution.py:142
  81.3 14.5 %collective-permute-start.6 = (bf16[2,8,64,128]{3,2,1,0:T(8,128)(2,1)S(1)}, bf16[2,8,64,128]{3,2,1,0:T(8,128)(2,1)S(1)}, u32[]{:S(2)}, u32[]{:S(2)}) collective-permute-start(bf16[2,8,64,128]{3,2,1,0:T(8,128)(2,1)S(1)} %get-tuple-element.22), channel_id=1, source_target_pairs={{0,2},{1,3},{2,0},{3,1},{4,6},{5,7},{6,4},{7,5},{8,10},{9,11},{10,... | collective-permute-start | bytes 786440 | tf_op jit(solution)/shard_map/ppermute | solution.py:142
  92.1 10.2 %collective-permute-start.12 = (bf16[2,8,64,128]{3,2,1,0:T(8,128)(2,1)S(1)}, bf16[2,8,64,128]{3,2,1,0:T(8,128)(2,1)S(1)}, u32[]{:S(2)}, u32[]{:S(2)}) collective-permute-start(bf16[2,8,64,128]{3,2,1,0:T(8,128)(2,1)S(1)} %get-tuple-element.28), channel_id=1, source_target_pairs={{0,6},{1,7},{2,4},{3,5},{4,2},{5,3},{6,0},{7,1},{8,14},{9,15},{10,... | collective-permute-start | bytes 786440 | tf_op jit(solution)/shard_map/ppermute | solution.py:142
  94.8 10.5 %collective-permute-start.11 = (bf16[2,8,64,128]{3,2,1,0:T(8,128)(2,1)S(1)}, bf16[2,8,64,128]{3,2,1,0:T(8,128)(2,1)S(1)}, u32[]{:S(2)}, u32[]{:S(2)}) collective-permute-start(bf16[2,8,64,128]{3,2,1,0:T(8,128)(2,1)S(1)} %get-tuple-element.27), channel_id=1, source_target_pairs={{0,4},{1,5},{2,6},{3,7},{4,0},{5,1},{6,2},{7,3},{8,12},{9,13},{10,... | collective-permute-start | bytes 786440 | tf_op jit(solution)/shard_map/ppermute | solution.py:142
  95.4 10.0 %collective-permute-start.10 = (bf16[2,8,64,128]{3,2,1,0:T(8,128)(2,1)S(1)}, bf16[2,8,64,128]{3,2,1,0:T(8,128)(2,1)S(1)}, u32[]{:S(2)}, u32[]{:S(2)}) collective-permute-start(bf16[2,8,64,128]{3,2,1,0:T(8,128)(2,1)S(1)} %get-tuple-element.26), channel_id=1, source_target_pairs={{0,2},{1,3},{2,0},{3,1},{4,6},{5,7},{6,4},{7,5},{8,10},{9,11},{10,... | collective-permute-start | bytes 786440 | tf_op jit(solution)/shard_map/ppermute | solution.py:142
  96.0 10.3 %collective-permute-start.9 = (bf16[4,2,8,32,128]{4,3,2,1,0:T(8,128)(2,1)S(1)}, bf16[4,2,8,32,128]{4,3,2,1,0:T(8,128)(2,1)S(1)}, u32[]{:S(2)}, u32[]{:S(2)}) collective-permute-start(bf16[4,2,8,32,128]{4,3,2,1,0:T(8,128)(2,1)S(1)} %pad_maximum_fusion.2), channel_id=1, source_target_pairs={{0,1},{1,0},{2,3},{3,2},{4,5},{5,4},{6,7},{7,6},{8,9},{9,8},{10,11... | collective-permute-start | bytes 1572872 | tf_op jit(solution)/shard_map/ppermute | solution.py:142
  105.5 2.0 %collective-permute-start.13 = (bf16[4,2,8,32,128]{4,3,2,1,0:T(8,128)(2,1)S(1)}, bf16[4,2,8,32,128]{4,3,2,1,0:T(8,128)(2,1)S(1)}, u32[]{:S(2)}, u32[]{:S(2)}) collective-permute-start(bf16[4,2,8,32,128]{4,3,2,1,0:T(8,128)(2,1)S(1)} %pad_maximum_fusion.3), channel_id=1, source_target_pairs={{0,1},{1,0},{2,3},{3,2},{4,5},{5,4},{6,7},{7,6},{8,9},{9,8},{10,11... | collective-permute-start | bytes 1572872 | tf_op jit(solution)/shard_map/ppermute | solution.py:142

commit v9 on v8

--- a/solution.py
+++ b/solution.py
@@ -141,27 +141,31 @@
             return array
         return lax.ppermute(array, axis, [(i, i ^ k) for i in range(lax.axis_size(axis))])
 
-    same = jnp.stack([swap(kernel, k) for k in across])
+    if len(across) == 4:
+        half = out_chan // 2
+        by_x, by_y = swap(kernel, across[1]), swap(kernel, across[2])
+        far = [swap(by_x[:, :, :, :half], across[2]), swap(by_y[:, :, :, half:], across[1])]
+        fetched = [kernel, by_x, by_y, jnp.concatenate(far, axis=3)]
+    else:
+        fetched = [swap(kernel, k) for k in across]
+    same = jnp.stack(fetched)
     tap_parts = [same, swap(same, 1)]
 
     outer_rows, inner_rows = cut(features.transpose(0, 2, 1, 3), parts)
     outer = lax.all_to_all(outer_rows, "filt", 0, 0)
     inner = lax.all_to_all(inner_rows, "filt", 0, 0)
-    up = [(i, i + 1) for i in range(slabs - 1)]
-    down = [(i + 1, i) for i in range(slabs - 1)]
-    first, last = edges_of(outer)
-    after = lax.ppermute(first, "slab", down)
-    before = lax.ppermute(last, "slab", up)
-
+    arrived = outer
     order = jnp.stack([me ^ k ^ c for k in across for c in range(2)])
     bias = jnp.take(bias_vector.reshape(parts, out_chan), order, axis=0).reshape(-1)
+    def settle(array):
+        if aligned:
+            return array
+        return array.transpose(1, 2, 0, 3, 4).reshape(1, -1, rows + 2, parts * chan, cols)
+
     if not aligned:
         joined = jnp.stack(tap_parts, axis=1).transpose(2, 3, 4, 0, 1, 5, 6)
         tap_parts = [joined.reshape(1, 3, 3, 3, parts * out_chan, -1)]
-        outer, inner, before, after = (
-            array.transpose(1, 2, 0, 3, 4).reshape(1, -1, rows + 2, parts * chan, cols)
-            for array in (outer, inner, before, after)
-        )
+        outer, inner = settle(outer), settle(inner)
 
     def send_back(results):
         count = results[0].shape[0]
@@ -178,9 +182,17 @@
     where = [(0, 0)] + [(1, plane) for plane in range(planes - 2)] + [(0, 1)]
     middle = tuple(tuple(where[plane - 1 : plane + 2]) for plane in range(1, planes - 1))
     inside = send_back(convolve(middle, [outer, inner], tap_parts, bias, blocks))
+    up = [(i, i + 1) for i in range(slabs - 1)]
+    down = [(i + 1, i) for i in range(slabs - 1)]
+    first, last = edges_of(arrived)
+    after = lax.ppermute(first, "slab", down)
+    before = lax.ppermute(last, "slab", up)
+
     ends = (((2, 0), *where[:2]), (*where[-2:], (3, 0)))
-    outside = send_back(convolve(ends, [outer, inner, before, after], tap_parts, bias, blocks))
-    return jnp.concatenate([outside[:1], inside, outside[1:]])
+    outside = send_back(convolve(ends, [outer, inner, settle(before), settle(after)], tap_parts, bias, blocks))
+    whole = jnp.pad(inside, ((1, 1), (0, 0), (0, 0), (0, 0)))
+    whole = lax.dynamic_update_slice_in_dim(whole, outside[:1], 0, 0)
+    return lax.dynamic_update_slice_in_dim(whole, outside[1:], planes - 1, 0)
 
 
 def solution(mesh):

time: 111 us -> 103 us (0.928)
  waiting for transfers between devices: 48.9 us -> 37.7 us
  starting transfers between devices: 26.2 us -> 29.9 us
  local copies, waits for them, and re-layouts: 7.89 us -> 9.72 us
  other arithmetic: 3.29 us -> 1.52 us
    all_to_all x1, waiting for transfers between devices: 10.8 us -> 0.01 us  [body(): outer = lax.all_to_all(outer_rows, 'filt', 0, 0)]
    ppermute x12 -> x13, waiting for transfers between devices: 21.5 us -> 28.4 us  [swap(): lax.ppermute(array, axis, [(i, i ^ k) for i in range(lax.axis_size(axis))])]
    ppermute x1, waiting for transfers between devices: 4.94 us -> 0.01 us  [body(): after = lax.ppermute(first, 'slab', down)]
    ppermute x12 -> x13, starting transfers between devices: 11.8 us -> 15.4 us  [swap(): lax.ppermute(array, axis, [(i, i ^ k) for i in range(lax.axis_size(axis))])]
    concatenate x1 -> x0, other arithmetic: 1.56 us -> none  [body(): return jnp.concatenate([outside[:1], inside, outside[1:]])]
    ppermute x1, waiting for transfers between devices: 1.34 us -> 0.01 us  [body(): before = lax.ppermute(last, 'slab', up)]
    unnamed x13 -> x11, local copies, waits for them, and re-layouts: 4.79 us -> 5.35 us
  transfers between devices with their start and end apart: 16 -> 17, of which waited for: 9 -> 6; matrix products, arithmetic and copies ran while one was open for 6% -> 6% of each run, Pallas kernels for 12% -> 23%
where the time goes in v9:
time: 103 us
  waiting for transfers between devices  37.7 us (37%)
  starting transfers between devices  29.9 us (29%)
  Pallas kernels  23.7 us (23%)
  local copies, waits for them, and re-layouts  9.72 us (9%)
  other arithmetic  1.52 us (1%)
    ppermute x13, waiting for transfers between devices, swap(): lax.ppermute(array, axis, [(i, i ^ k) for i in range(lax.axis_size(axis))])  28.4 us
    pallas_call x2, Pallas kernels, convolve(): pl.pallas_call(functools.partial(conv_kernel, plan, min(ROWS, rows), len(...  21.2 us
    ppermute x13, starting transfers between devices, swap(): lax.ppermute(array, axis, [(i, i ^ k) for i in range(lax.axis_size(axis))])  15.4 us
    all_to_all x1, waiting for transfers between devices, body(): inner = lax.all_to_all(inner_rows, 'filt', 0, 0)  9.3 us
    ppermute x1, starting transfers between devices, body(): before = lax.ppermute(last, 'slab', up)  5.41 us
    unnamed x11, local copies, waits for them, and re-layouts  5.35 us
    all_to_all x1, starting transfers between devices, body(): inner = lax.all_to_all(inner_rows, 'filt', 0, 0)  4.28 us
    all_to_all x1, starting transfers between devices, body(): outer = lax.all_to_all(outer_rows, 'filt', 0, 0)  3.57 us
  transfers between devices with their start and end apart: 17, of which 6 were waited for; matrix products, arithmetic and copies ran while one was open for 6% of the time, Pallas kernels for 23%

profile of v9, /device:TPU:0, one launch (start us, length us, event | category | flops | bytes accessed | tf_op | source)
XLA Modules:
  0.0 103.1 jit_solution(14542243481440480869)
XLA Ops:
  0.0 2.9 %collective-permute-start = (bf16[3,3,3,32,256]{4,3,2,1,0:T(8,128)(2,1)}, bf16[3,3,3,32,256]{4,3,2,1,0:T(8,128)(2,1)S(1)}, u32[]{:S(2)}, u32[]{:S(2)}) collective-permute-start(bf16[3,3,3,32,256]{4,3,2,1,0:T(8,128)(2,1)} %param.4), channel_id=1, source_target_pairs={{0,2},{1,3},{2,0},{3,1},{4,6},{5,7},{6,4},{7,5},{8,10},{9,11},{10,... | collective-permute-start | bytes 1327112 | tf_op jit(solution)/shard_map/ppermute | solution.py:142
  2.9 1.5 %collective-permute-start.1 = (bf16[3,3,3,32,256]{4,3,2,1,0:T(8,128)(2,1)}, bf16[3,3,3,32,256]{4,3,2,1,0:T(8,128)(2,1)S(1)}, u32[]{:S(2)}, u32[]{:S(2)}) collective-permute-start(bf16[3,3,3,32,256]{4,3,2,1,0:T(8,128)(2,1)} %param.4), channel_id=1, source_target_pairs={{0,4},{1,5},{2,6},{3,7},{4,0},{5,1},{6,2},{7,3},{8,12},{9,13},{10,... | collective-permute-start | bytes 1327112 | tf_op jit(solution)/shard_map/ppermute | solution.py:142
  4.5 2.9 %copy.38 = bf16[4,32,64,128]{3,1,2,0:T(8,128)(2,1)S(1)} copy(bf16[4,32,64,128]{3,2,1,0:T(8,128)(2,1)} %param.3) | data formatting | bytes 4194304 | tf_op args[0]
  7.4 1.3 %shard_map.37 = (bf16[8,2,10,32,128]{4,3,2,1,0:T(8,128)(2,1)}, bf16[8,2,10,32,128]{4,3,2,1,0:T(8,128)(2,1)S(1)}) custom-call(bf16[4,64,32,128]{3,2,1,0:T(8,128)(2,1)S(1)} %bitcast.60), custom_call_target="tpu_custom_call" | custom-call | tf_op jit(solution)/shard_map/pallas_call | solution.py:32
  9.8 3.6 %all-to-all-start = ((bf16[8,2,10,32,128]{4,3,2,1,0:T(8,128)(2,1)}), bf16[8,2,10,32,128]{4,3,2,1,0:T(8,128)(2,1)S(1)}, u32[]{:S(2)}, u32[]{:S(2)}) async-start(bf16[8,2,10,32,128]{4,3,2,1,0:T(8,128)(2,1)} %get-tuple-element.17), calls=%async_computation | async-start | bytes 2621440 | tf_op jit(solution)/shard_map/all_to_all | solution.py:155
  13.4 2.0 %collective-permute-start.2 = (bf16[3,3,3,16,256]{4,3,2,1,0:T(8,128)(2,1)S(1)}, bf16[3,3,3,16,256]{4,3,2,1,0:T(8,128)(2,1)S(1)}, u32[]{:S(2)}, u32[]{:S(2)}) collective-permute-start(bf16[3,3,3,16,256]{4,3,2,1,0:T(8,128)(2,1)S(1)} %slice.114), channel_id=1, source_target_pairs={{0,4},{1,5},{2,6},{3,7},{4,0},{5,1},{6,2},{7,3},{8,12},{9,13},{10,... | collective-permute-start | bytes 663560 | tf_op jit(solution)/shard_map/ppermute | solution.py:142
  15.4 1.5 %collective-permute-start.3 = (bf16[3,3,3,16,256]{4,3,2,1,0:T(8,128)(2,1)S(1)}, bf16[3,3,3,16,256]{4,3,2,1,0:T(8,128)(2,1)S(1)}, u32[]{:S(2)}, u32[]{:S(2)}) collective-permute-start(bf16[3,3,3,16,256]{4,3,2,1,0:T(8,128)(2,1)S(1)} %slice.115), channel_id=1, source_target_pairs={{0,2},{1,3},{2,0},{3,1},{4,6},{5,7},{6,4},{7,5},{8,10},{9,11},{10,... | collective-permute-start | bytes 663560 | tf_op jit(solution)/shard_map/ppermute | solution.py:142
  17.0 18.3 %collective-permute-done.2 = bf16[3,3,3,16,256]{4,3,2,1,0:T(8,128)(2,1)S(1)} collective-permute-done((bf16[3,3,3,16,256]{4,3,2,1,0:T(8,128)(2,1)S(1)}, bf16[3,3,3,16,256]{4,3,2,1,0:T(8,128)(2,1)S(1)}, u32[]{:S(2)}, u32[]{:S(2)}) %collective-permute-start.2) | collective-permute-done | bytes 221216 | tf_op jit(solution)/shard_map/ppermute | solution.py:142
  35.4 1.2 %pad_maximum_fusion.refs_2_.refs_4_ = bf16[4,3,3,3,32,256]{5,4,3,2,1,0:T(8,128)(2,1)S(1)} fusion(bf16[1,3,3,3,32,256]{5,4,3,2,1,0:T(8,128)(2,1)S(1)} %maximum_bitcast_fusion, bf16[1,3,3,3,32,256]{5,4,3,2,1,0:T(8,128)(2,1)} %bitcast.65, bf16[1,3,3,3,32,256]{5,4,3,2,1,0:T(8,128)(2,1)S(1)} %bitcast.64, bf16[1,3,3,3,32,256]{5,4,3,2,1,0:T(8,128)(2,1)S(1)} %bitcast.66), kind=kLoop, calls=%fused_computation.2 | loop fusion | flops 2654208 | bytes 3538944 | tf_op jit(solution)/shard_map/stack | solution.py:151
  36.8 4.3 %all-to-all-start.1 = ((bf16[8,2,10,32,128]{4,3,2,1,0:T(8,128)(2,1)}), bf16[8,2,10,32,128]{4,3,2,1,0:T(8,128)(2,1)}, u32[]{:S(2)}, u32[]{:S(2)}) async-start(bf16[8,2,10,32,128]{4,3,2,1,0:T(8,128)(2,1)} %copy-done), calls=%async_computation.1 | async-start | bytes 2621440 | tf_op jit(solution)/shard_map/all_to_all | solution.py:156
  42.1 1.2 %shard_map.39 = (bf16[8,1,10,32,128]{4,3,2,1,0:T(8,128)(2,1)}, bf16[8,1,10,32,128]{4,3,2,1,0:T(8,128)(2,1)}) custom-call(bf16[8,2,10,32,128]{4,3,2,1,0:T(8,128)(2,1)S(1)} %all-to-all-done.refs_0_.vol_ref), custom_call_target="tpu_custom_call" | custom-call | tf_op jit(solution)/shard_map/pallas_call | solution.py:54
  43.3 1.3 %collective-permute-start.10 = (bf16[8,1,10,32,128]{4,3,2,1,0:T(8,128)(2,1)}, bf16[8,1,10,32,128]{4,3,2,1,0:T(8,128)(2,1)}, u32[]{:S(2)}, u32[]{:S(2)}) collective-permute-start(bf16[8,1,10,32,128]{4,3,2,1,0:T(8,128)(2,1)} %get-tuple-element.24), channel_id=1, source_target_pairs={{8,0},{16,8},{24,16},{9,1},{17,9},{25,17},{10,2},{18,10},{26,18},{... | collective-permute-start | bytes 1966088 | tf_op jit(solution)/shard_map/ppermute | solution.py:188
  44.6 5.4 %collective-permute-start.9 = (bf16[8,1,10,32,128]{4,3,2,1,0:T(8,128)(2,1)}, bf16[8,1,10,32,128]{4,3,2,1,0:T(8,128)(2,1)}, u32[]{:S(2)}, u32[]{:S(2)}) collective-permute-start(bf16[8,1,10,32,128]{4,3,2,1,0:T(8,128)(2,1)} %get-tuple-element.23), channel_id=1, source_target_pairs={{0,8},{8,16},{16,24},{1,9},{9,17},{17,25},{2,10},{10,18},{18,26},{... | collective-permute-start | bytes 1966088 | tf_op jit(solution)/shard_map/ppermute | solution.py:189
  50.0 9.3 %all-to-all-done.1.refs_1_ = bf16[8,2,10,32,128]{4,3,2,1,0:T(8,128)(2,1)} async-done(((bf16[8,2,10,32,128]{4,3,2,1,0:T(8,128)(2,1)}), bf16[8,2,10,32,128]{4,3,2,1,0:T(8,128)(2,1)}, u32[]{:S(2)}, u32[]{:S(2)}) %all-to-all-start.1) | async-done | bytes 1310752 | tf_op jit(solution)/shard_map/all_to_all | solution.py:156
  59.4 10.4 %shard_map.38 = (bf16[2,8,64,128]{3,2,1,0:T(8,128)(2,1)S(1)}, bf16[2,8,64,128]{3,2,1,0:T(8,128)(2,1)S(1)}, bf16[2,8,64,128]{3,2,1,0:T(8,128)(2,1)S(1)}, bf16[2,8,64,128]{3,2,1,0:T(8,128)(2,1)S(1)}) custom-call(bf16[8,2,10,32,128]{4,3,2,1,0:T(8,128)(2,1)S(1)} %all-to-all-done.refs_0_.vol_ref, bf16[8,2,10,32,128]{4,3,2,1,0:T(8,128)(2,1)} %all-to-all-done.1.refs_1_, ...), custom_call_target="tpu_custom_call" | custom-call | flops 7247757312 | bytes 10000000 | tf_op jit(solution)/shard_map/pallas_call | solution.py:119
  70.5 1.4 %collective-permute-start.6 = (bf16[2,8,64,128]{3,2,1,0:T(8,128)(2,1)S(1)}, bf16[2,8,64,128]{3,2,1,0:T(8,128)(2,1)S(1)}, u32[]{:S(2)}, u32[]{:S(2)}) collective-permute-start(bf16[2,8,64,128]{3,2,1,0:T(8,128)(2,1)S(1)} %get-tuple-element.21), channel_id=1, source_target_pairs={{0,4},{1,5},{2,6},{3,7},{4,0},{5,1},{6,2},{7,3},{8,12},{9,13},{10,... | collective-permute-start | bytes 786440 | tf_op jit(solution)/shard_map/ppermute | solution.py:142
  71.8 1.5 %collective-permute-start.5 = (bf16[2,8,64,128]{3,2,1,0:T(8,128)(2,1)S(1)}, bf16[2,8,64,128]{3,2,1,0:T(8,128)(2,1)S(1)}, u32[]{:S(2)}, u32[]{:S(2)}) collective-permute-start(bf16[2,8,64,128]{3,2,1,0:T(8,128)(2,1)S(1)} %get-tuple-element.20), channel_id=1, source_target_pairs={{0,2},{1,3},{2,0},{3,1},{4,6},{5,7},{6,4},{7,5},{8,10},{9,11},{10,... | collective-permute-start | bytes 786440 | tf_op jit(solution)/shard_map/ppermute | solution.py:142
  73.4 10.8 %shard_map.40 = (bf16[2,8,64,128]{3,2,1,0:T(8,128)(2,1)S(1)}, bf16[2,8,64,128]{3,2,1,0:T(8,128)(2,1)S(1)}, bf16[2,8,64,128]{3,2,1,0:T(8,128)(2,1)S(1)}, bf16[2,8,64,128]{3,2,1,0:T(8,128)(2,1)S(1)}) custom-call(bf16[8,2,10,32,128]{4,3,2,1,0:T(8,128)(2,1)S(1)} %all-to-all-done.refs_0_.vol_ref, bf16[8,2,10,32,128]{4,3,2,1,0:T(8,128)(2,1)} %all-to-all-done.1.refs_1_, ...), custom_call_target="tpu_custom_call" | custom-call | flops 7247757312 | bytes 10000000 | tf_op jit(solution)/shard_map/pallas_call | solution.py:119
  84.9 1.4 %collective-permute-start.12 = (bf16[2,8,64,128]{3,2,1,0:T(8,128)(2,1)S(1)}, bf16[2,8,64,128]{3,2,1,0:T(8,128)(2,1)S(1)}, u32[]{:S(2)}, u32[]{:S(2)}) collective-permute-start(bf16[2,8,64,128]{3,2,1,0:T(8,128)(2,1)S(1)} %get-tuple-element.27), channel_id=1, source_target_pairs={{0,4},{1,5},{2,6},{3,7},{4,0},{5,1},{6,2},{7,3},{8,12},{9,13},{10,... | collective-permute-start | bytes 786440 | tf_op jit(solution)/shard_map/ppermute | solution.py:142
  86.3 1.6 %collective-permute-start.11 = (bf16[2,8,64,128]{3,2,1,0:T(8,128)(2,1)S(1)}, bf16[2,8,64,128]{3,2,1,0:T(8,128)(2,1)S(1)}, u32[]{:S(2)}, u32[]{:S(2)}) collective-permute-start(bf16[2,8,64,128]{3,2,1,0:T(8,128)(2,1)S(1)} %get-tuple-element.26), channel_id=1, source_target_pairs={{0,2},{1,3},{2,0},{3,1},{4,6},{5,7},{6,4},{7,5},{8,10},{9,11},{10,... | collective-permute-start | bytes 786440 | tf_op jit(solution)/shard_map/ppermute | solution.py:142
  88.1 6.1 %collective-permute-done.13 = bf16[2,8,64,128]{3,2,1,0:T(8,128)(2,1)S(1)} collective-permute-done((bf16[2,8,64,128]{3,2,1,0:T(8,128)(2,1)S(1)}, bf16[2,8,64,128]{3,2,1,0:T(8,128)(2,1)S(1)}, u32[]{:S(2)}, u32[]{:S(2)}) %collective-permute-start.13) | collective-permute-done | bytes 262176 | tf_op jit(solution)/shard_map/ppermute | solution.py:142
  94.3 2.7 %collective-permute-done.12 = bf16[2,8,64,128]{3,2,1,0:T(8,128)(2,1)S(1)} collective-permute-done((bf16[2,8,64,128]{3,2,1,0:T(8,128)(2,1)S(1)}, bf16[2,8,64,128]{3,2,1,0:T(8,128)(2,1)S(1)}, u32[]{:S(2)}, u32[]{:S(2)}) %collective-permute-start.12) | collective-permute-done | bytes 262176 | tf_op jit(solution)/shard_map/ppermute | solution.py:142
  98.0 1.2 %collective-permute-done.14 = bf16[4,2,8,32,128]{4,3,2,1,0:T(8,128)(2,1)S(1)} collective-permute-done((bf16[4,2,8,32,128]{4,3,2,1,0:T(8,128)(2,1)S(1)}, bf16[4,2,8,32,128]{4,3,2,1,0:T(8,128)(2,1)S(1)}, u32[]{:S(2)}, u32[]{:S(2)}) %collective-permute-start.14) | collective-permute-done | bytes 524320 | tf_op jit(solution)/shard_map/ppermute | solution.py:142
  100.9 1.3 %copy-done.1 = bf16[4,32,64,128]{3,2,1,0:T(8,128)(2,1)} copy-done((bf16[4,32,64,128]{3,2,1,0:T(8,128)(2,1)}, bf16[4,32,64,128]{3,2,1,0:T(8,128)(2,1)S(1)}, u32[]{:S(2)}) %copy-start.1) | copy-done | bytes 2097176
  (71 shorter events, 7.4 us)
Async XLA Ops:
  0.0 13.4 %collective-permute-start = (bf16[3,3,3,32,256]{4,3,2,1,0:T(8,128)(2,1)}, bf16[3,3,3,32,256]{4,3,2,1,0:T(8,128)(2,1)S(1)}, u32[]{:S(2)}, u32[]{:S(2)}) collective-permute-start(bf16[3,3,3,32,256]{4,3,2,1,0:T(8,128)(2,1)} %param.4), channel_id=1, source_target_pairs={{0,2},{1,3},{2,0},{3,1},{4,6},{5,7},{6,4},{7,5},{8,10},{9,11},{10,... | collective-permute-start | bytes 1327112 | tf_op jit(solution)/shard_map/ppermute | solution.py:142
  2.9 12.5 %collective-permute-start.1 = (bf16[3,3,3,32,256]{4,3,2,1,0:T(8,128)(2,1)}, bf16[3,3,3,32,256]{4,3,2,1,0:T(8,128)(2,1)S(1)}, u32[]{:S(2)}, u32[]{:S(2)}) collective-permute-start(bf16[3,3,3,32,256]{4,3,2,1,0:T(8,128)(2,1)} %param.4), channel_id=1, source_target_pairs={{0,4},{1,5},{2,6},{3,7},{4,0},{5,1},{6,2},{7,3},{8,12},{9,13},{10,... | collective-permute-start | bytes 1327112 | tf_op jit(solution)/shard_map/ppermute | solution.py:142
  8.7 1.1 %copy-start = (bf16[8,2,10,32,128]{4,3,2,1,0:T(8,128)(2,1)}, bf16[8,2,10,32,128]{4,3,2,1,0:T(8,128)(2,1)S(1)}, u32[]{:S(2)}) copy-start(bf16[8,2,10,32,128]{4,3,2,1,0:T(8,128)(2,1)S(1)} %get-tuple-element.18) | copy-start | bytes 3932164
  9.8 27.0 %all-to-all-start = ((bf16[8,2,10,32,128]{4,3,2,1,0:T(8,128)(2,1)}), bf16[8,2,10,32,128]{4,3,2,1,0:T(8,128)(2,1)S(1)}, u32[]{:S(2)}, u32[]{:S(2)}) async-start(bf16[8,2,10,32,128]{4,3,2,1,0:T(8,128)(2,1)} %get-tuple-element.17), calls=%async_computation | async-start | bytes 2621440 | tf_op jit(solution)/shard_map/all_to_all | solution.py:155
  13.3 22.1 %copy-start.3 = (bf16[3,3,3,32,256]{4,3,2,1,0:T(8,128)(2,1)S(1)}, bf16[3,3,3,32,256]{4,3,2,1,0:T(8,128)(2,1)}, u32[]{:S(2)}) copy-start(bf16[3,3,3,32,256]{4,3,2,1,0:T(8,128)(2,1)} %param.4) | copy-start | bytes 1327108
  13.4 21.9 %collective-permute-start.2 = (bf16[3,3,3,16,256]{4,3,2,1,0:T(8,128)(2,1)S(1)}, bf16[3,3,3,16,256]{4,3,2,1,0:T(8,128)(2,1)S(1)}, u32[]{:S(2)}, u32[]{:S(2)}) collective-permute-start(bf16[3,3,3,16,256]{4,3,2,1,0:T(8,128)(2,1)S(1)} %slice.114), channel_id=1, source_target_pairs={{0,4},{1,5},{2,6},{3,7},{4,0},{5,1},{6,2},{7,3},{8,12},{9,13},{10,... | collective-permute-start | bytes 663560 | tf_op jit(solution)/shard_map/ppermute | solution.py:142
  15.4 20.0 %copy-start.2 = (bf16[3,3,3,32,256]{4,3,2,1,0:T(8,128)(2,1)}, bf16[3,3,3,32,256]{4,3,2,1,0:T(8,128)(2,1)S(1)}, u32[]{:S(2)}) copy-start(bf16[3,3,3,32,256]{4,3,2,1,0:T(8,128)(2,1)S(1)} %collective-permute-done.1) | copy-start | bytes 1327108
  15.4 19.9 %collective-permute-start.3 = (bf16[3,3,3,16,256]{4,3,2,1,0:T(8,128)(2,1)S(1)}, bf16[3,3,3,16,256]{4,3,2,1,0:T(8,128)(2,1)S(1)}, u32[]{:S(2)}, u32[]{:S(2)}) collective-permute-start(bf16[3,3,3,16,256]{4,3,2,1,0:T(8,128)(2,1)S(1)} %slice.115), channel_id=1, source_target_pairs={{0,2},{1,3},{2,0},{3,1},{4,6},{5,7},{6,4},{7,5},{8,10},{9,11},{10,... | collective-permute-start | bytes 663560 | tf_op jit(solution)/shard_map/ppermute | solution.py:142
  36.7 4.4 %copy-start.4 = (f32[256]{0:T(256)S(1)}, f32[256]{0:T(256)}, u32[]{:S(2)}) copy-start(f32[256]{0:T(256)} %param.5) | copy-start | bytes 3076
  36.7 22.6 %collective-permute-start.4 = (bf16[4,3,3,3,32,256]{5,4,3,2,1,0:T(8,128)(2,1)S(1)}, bf16[4,3,3,3,32,256]{5,4,3,2,1,0:T(8,128)(2,1)}, u32[]{:S(2)}, u32[]{:S(2)}) collective-permute-start(bf16[4,3,3,3,32,256]{5,4,3,2,1,0:T(8,128)(2,1)S(1)} %pad_maximum_fusion.refs_2_.refs_4_), channel_id=1, source_target_pairs={{0,1},{1,0},{2,3},{3,2},{4,5},{5,4},{6,7},{7,6},{8,9},{9,8},{10,11... | collective-permute-start | bytes 5308424 | tf_op jit(solution)/shard_map/ppermute | solution.py:142
  36.8 22.5 %all-to-all-start.1 = ((bf16[8,2,10,32,128]{4,3,2,1,0:T(8,128)(2,1)}), bf16[8,2,10,32,128]{4,3,2,1,0:T(8,128)(2,1)}, u32[]{:S(2)}, u32[]{:S(2)}) async-start(bf16[8,2,10,32,128]{4,3,2,1,0:T(8,128)(2,1)} %copy-done), calls=%async_computation.1 | async-start | bytes 2621440 | tf_op jit(solution)/shard_map/all_to_all | solution.py:156
  43.3 30.1 %collective-permute-start.10 = (bf16[8,1,10,32,128]{4,3,2,1,0:T(8,128)(2,1)}, bf16[8,1,10,32,128]{4,3,2,1,0:T(8,128)(2,1)}, u32[]{:S(2)}, u32[]{:S(2)}) collective-permute-start(bf16[8,1,10,32,128]{4,3,2,1,0:T(8,128)(2,1)} %get-tuple-element.24), channel_id=1, source_target_pairs={{8,0},{16,8},{24,16},{9,1},{17,9},{25,17},{10,2},{18,10},{26,18},{... | collective-permute-start | bytes 1966088 | tf_op jit(solution)/shard_map/ppermute | solution.py:188
  44.6 28.8 %collective-permute-start.9 = (bf16[8,1,10,32,128]{4,3,2,1,0:T(8,128)(2,1)}, bf16[8,1,10,32,128]{4,3,2,1,0:T(8,128)(2,1)}, u32[]{:S(2)}, u32[]{:S(2)}) collective-permute-start(bf16[8,1,10,32,128]{4,3,2,1,0:T(8,128)(2,1)} %get-tuple-element.23), channel_id=1, source_target_pairs={{0,8},{8,16},{16,24},{1,9},{9,17},{17,25},{2,10},{10,18},{18,26},{... | collective-permute-start | bytes 1966088 | tf_op jit(solution)/shard_map/ppermute | solution.py:189
  69.8 16.5 %collective-permute-start.7 = (bf16[2,8,64,128]{3,2,1,0:T(8,128)(2,1)S(1)}, bf16[2,8,64,128]{3,2,1,0:T(8,128)(2,1)S(1)}, u32[]{:S(2)}, u32[]{:S(2)}) collective-permute-start(bf16[2,8,64,128]{3,2,1,0:T(8,128)(2,1)S(1)} %get-tuple-element.22), channel_id=1, source_target_pairs={{0,6},{1,7},{2,4},{3,5},{4,2},{5,3},{6,0},{7,1},{8,14},{9,15},{10,... | collective-permute-start | bytes 786440 | tf_op jit(solution)/shard_map/ppermute | solution.py:142
  70.5 17.4 %collective-permute-start.6 = (bf16[2,8,64,128]{3,2,1,0:T(8,128)(2,1)S(1)}, bf16[2,8,64,128]{3,2,1,0:T(8,128)(2,1)S(1)}, u32[]{:S(2)}, u32[]{:S(2)}) collective-permute-start(bf16[2,8,64,128]{3,2,1,0:T(8,128)(2,1)S(1)} %get-tuple-element.21), channel_id=1, source_target_pairs={{0,4},{1,5},{2,6},{3,7},{4,0},{5,1},{6,2},{7,3},{8,12},{9,13},{10,... | collective-permute-start | bytes 786440 | tf_op jit(solution)/shard_map/ppermute | solution.py:142
  71.8 16.1 %collective-permute-start.5 = (bf16[2,8,64,128]{3,2,1,0:T(8,128)(2,1)S(1)}, bf16[2,8,64,128]{3,2,1,0:T(8,128)(2,1)S(1)}, u32[]{:S(2)}, u32[]{:S(2)}) collective-permute-start(bf16[2,8,64,128]{3,2,1,0:T(8,128)(2,1)S(1)} %get-tuple-element.20), channel_id=1, source_target_pairs={{0,2},{1,3},{2,0},{3,1},{4,6},{5,7},{6,4},{7,5},{8,10},{9,11},{10,... | collective-permute-start | bytes 786440 | tf_op jit(solution)/shard_map/ppermute | solution.py:142
  84.2 10.0 %collective-permute-start.13 = (bf16[2,8,64,128]{3,2,1,0:T(8,128)(2,1)S(1)}, bf16[2,8,64,128]{3,2,1,0:T(8,128)(2,1)S(1)}, u32[]{:S(2)}, u32[]{:S(2)}) collective-permute-start(bf16[2,8,64,128]{3,2,1,0:T(8,128)(2,1)S(1)} %get-tuple-element.28), channel_id=1, source_target_pairs={{0,6},{1,7},{2,4},{3,5},{4,2},{5,3},{6,0},{7,1},{8,14},{9,15},{10,... | collective-permute-start | bytes 786440 | tf_op jit(solution)/shard_map/ppermute | solution.py:142
  84.9 12.1 %collective-permute-start.12 = (bf16[2,8,64,128]{3,2,1,0:T(8,128)(2,1)S(1)}, bf16[2,8,64,128]{3,2,1,0:T(8,128)(2,1)S(1)}, u32[]{:S(2)}, u32[]{:S(2)}) collective-permute-start(bf16[2,8,64,128]{3,2,1,0:T(8,128)(2,1)S(1)} %get-tuple-element.27), channel_id=1, source_target_pairs={{0,4},{1,5},{2,6},{3,7},{4,0},{5,1},{6,2},{7,3},{8,12},{9,13},{10,... | collective-permute-start | bytes 786440 | tf_op jit(solution)/shard_map/ppermute | solution.py:142
  86.3 10.7 %collective-permute-start.11 = (bf16[2,8,64,128]{3,2,1,0:T(8,128)(2,1)S(1)}, bf16[2,8,64,128]{3,2,1,0:T(8,128)(2,1)S(1)}, u32[]{:S(2)}, u32[]{:S(2)}) collective-permute-start(bf16[2,8,64,128]{3,2,1,0:T(8,128)(2,1)S(1)} %get-tuple-element.26), channel_id=1, source_target_pairs={{0,2},{1,3},{2,0},{3,1},{4,6},{5,7},{6,4},{7,5},{8,10},{9,11},{10,... | collective-permute-start | bytes 786440 | tf_op jit(solution)/shard_map/ppermute | solution.py:142
  88.0 9.9 %collective-permute-start.8 = (bf16[4,2,8,32,128]{4,3,2,1,0:T(8,128)(2,1)S(1)}, bf16[4,2,8,32,128]{4,3,2,1,0:T(8,128)(2,1)S(1)}, u32[]{:S(2)}, u32[]{:S(2)}) collective-permute-start(bf16[4,2,8,32,128]{4,3,2,1,0:T(8,128)(2,1)S(1)} %pad_maximum_fusion.1), channel_id=1, source_target_pairs={{0,1},{1,0},{2,3},{3,2},{4,5},{5,4},{6,7},{7,6},{8,9},{9,8},{10,11... | collective-permute-start | bytes 1572872 | tf_op jit(solution)/shard_map/ppermute | solution.py:142
  97.1 2.0 %collective-permute-start.14 = (bf16[4,2,8,32,128]{4,3,2,1,0:T(8,128)(2,1)S(1)}, bf16[4,2,8,32,128]{4,3,2,1,0:T(8,128)(2,1)S(1)}, u32[]{:S(2)}, u32[]{:S(2)}) collective-permute-start(bf16[4,2,8,32,128]{4,3,2,1,0:T(8,128)(2,1)S(1)} %pad_maximum_fusion.2), channel_id=1, source_target_pairs={{0,1},{1,0},{2,3},{3,2},{4,5},{5,4},{6,7},{7,6},{8,9},{9,8},{10,11... | collective-permute-start | bytes 1572872 | tf_op jit(solution)/shard_map/ppermute | solution.py:142
  100.9 1.3 %copy-start.1 = (bf16[4,32,64,128]{3,2,1,0:T(8,128)(2,1)}, bf16[4,32,64,128]{3,2,1,0:T(8,128)(2,1)S(1)}, u32[]{:S(2)}) copy-start(bf16[4,32,64,128]{3,2,1,0:T(8,128)(2,1)S(1)} %slice_dynamic-update-slice_fusion.1) | copy-start | bytes 6291460

commit v10 on v9

--- a/solution.py
+++ b/solution.py
@@ -60,8 +60,9 @@
     )(volume)
 
 
-def conv_kernel(plan, rows_at_once, pieces_count, tap_count, *refs):
+def conv_kernel(plan, rows_at_once, sums_count, pieces_count, tap_count, final, *refs):
     refs = list(refs)
+    sums = [refs.pop(0) for _ in range(sums_count)]
     pieces = [refs.pop(0) for _ in range(pieces_count)]
     tap_parts = [refs.pop(0) for _ in range(tap_count)]
     bias_ref, outs = refs[0], refs[1:]
@@ -75,7 +76,7 @@
     def tile(slot, row):
         cells = []
         weights = []
-        for a, (source, plane) in enumerate(plan[slot]):
+        for a, source, plane in plan[slot]:
             piece = pieces[source]
             lines = [
                 jnp.concatenate([piece[s, plane, row + r] for s in range(piece.shape[0])], axis=0)
@@ -96,7 +97,11 @@
             side = [part[:, c].reshape(total_out, cols) for c in range(3)]
             left = jnp.where(lane == 0, 0.0, pltpu.roll(side[0], 1, 1))
             right = jnp.where(lane == cols - 1, 0.0, pltpu.roll(side[2], cols - 1, 1))
-            shifted = side[1] + left + right + bias_ref[...]
+            found = side[1] + left + right
+            if not final:
+                outs[slot // 2][slot % 2, row + r] = found
+                continue
+            shifted = found + sums[0][slot, row + r] + bias_ref[...]
             done = jnp.where(shifted > 0, shifted, slope * shifted).astype(jnp.bfloat16)
             for n, out_ref in enumerate(outs):
                 out_ref[slot, row + r] = done[n * block : (n + 1) * block]
@@ -108,22 +113,27 @@
             tile(slot, step * rows_at_once)
 
 
-def convolve(plan, pieces, tap_parts, bias, blocks):
+def convolve(plan, sums, pieces, tap_parts, bias, blocks):
     rows, cols = pieces[0].shape[2] - 2, pieces[0].shape[4]
     in_chan = tap_parts[0].shape[5]
     total_out = bias.shape[0]
     wide_bias = jnp.broadcast_to(bias[:, None], (total_out, cols))
-    macs = 27 * total_out * in_chan * len(plan) * rows * cols
+    macs = 9 * total_out * in_chan * sum(len(terms) for terms in plan) * rows * cols
     in_vmem = pl.BlockSpec(memory_space=pltpu.VMEM)
-    shape = jax.ShapeDtypeStruct((len(plan), rows, total_out // blocks, cols), jnp.bfloat16)
+    if blocks:
+        shapes = [jax.ShapeDtypeStruct((len(plan), rows, total_out // blocks, cols), jnp.bfloat16)] * blocks
+    else:
+        shapes = [jax.ShapeDtypeStruct((2, rows, total_out, cols), jnp.float32)] * (len(plan) // 2)
     return pl.pallas_call(
-        functools.partial(conv_kernel, plan, min(ROWS, rows), len(pieces), len(tap_parts)),
-        out_shape=[shape] * blocks,
-        in_specs=[in_vmem] * (len(pieces) + len(tap_parts) + 1),
-        out_specs=[in_vmem] * blocks,
+        functools.partial(
+            conv_kernel, plan, min(ROWS, rows), len(sums), len(pieces), len(tap_parts), bool(blocks)
+        ),
+        out_shape=shapes,
+        in_specs=[in_vmem] * (len(sums) + len(pieces) + len(tap_parts) + 1),
+        out_specs=[in_vmem] * len(shapes),
         cost_estimate=pl.CostEstimate(flops=2 * macs, bytes_accessed=10_000_000, transcendentals=0),
         compiler_params=pltpu.CompilerParams(vmem_limit_bytes=20 * 2**20),
-    )(*pieces, *tap_parts, wide_bias)
+    )(*sums, *pieces, *tap_parts, wide_bias)
 
 
 def body(features, kernel, bias_vector):
@@ -179,20 +189,22 @@
         return final.transpose(0, 2, 1, 3)
 
     blocks = len(across)
-    where = [(0, 0)] + [(1, plane) for plane in range(planes - 2)] + [(0, 1)]
-    middle = tuple(tuple(where[plane - 1 : plane + 2]) for plane in range(1, planes - 1))
-    inside = send_back(convolve(middle, [outer, inner], tap_parts, bias, blocks))
+    assert planes == 4
+    begun = ((0, 0, 0),), ((2, 0, 1),), ((1, 0, 0),), ((1, 0, 1),)
+    middle_sums, end_sums = convolve(begun, [], [outer], tap_parts, bias, 0)
+    middle = ((1, 0, 0), (2, 0, 1)), ((0, 0, 0), (1, 0, 1))
+    inside = send_back(convolve(middle, [middle_sums], [inner], tap_parts, bias, blocks))
     up = [(i, i + 1) for i in range(slabs - 1)]
     down = [(i + 1, i) for i in range(slabs - 1)]
     first, last = edges_of(arrived)
     after = lax.ppermute(first, "slab", down)
     before = lax.ppermute(last, "slab", up)
-
-    ends = (((2, 0), *where[:2]), (*where[-2:], (3, 0)))
-    outside = send_back(convolve(ends, [outer, inner, settle(before), settle(after)], tap_parts, bias, blocks))
-    whole = jnp.pad(inside, ((1, 1), (0, 0), (0, 0), (0, 0)))
-    whole = lax.dynamic_update_slice_in_dim(whole, outside[:1], 0, 0)
-    return lax.dynamic_update_slice_in_dim(whole, outside[1:], planes - 1, 0)
+    ends = ((0, 1, 0), (2, 0, 0)), ((0, 0, 1), (2, 2, 0))
+    outside = send_back(
+        convolve(ends, [end_sums], [inner, settle(before), settle(after)], tap_parts, bias, blocks)
+    )
+    inside, outside = lax.optimization_barrier((inside, outside))
+    return jnp.concatenate([outside[:1], inside, outside[1:]])
 
 
 def solution(mesh):

time: 103 us -> 110 us (1.068)
  Pallas kernels: 23.7 us -> 27.8 us
  local copies, waits for them, and re-layouts: 9.72 us -> 11.5 us
  other arithmetic: 1.52 us -> 3.22 us
  waiting for transfers between devices: 37.7 us -> 36.3 us
    all_to_all x1, waiting for transfers between devices: 0.01 us -> 16 us  [body(): outer = lax.all_to_all(outer_rows, 'filt', 0, 0)]
    all_to_all x1, waiting for transfers between devices: 9.3 us -> 0.01 us  [body(): inner = lax.all_to_all(inner_rows, 'filt', 0, 0)]
    ppermute x13, waiting for transfers between devices: 28.4 us -> 20.2 us  [swap(): lax.ppermute(array, axis, [(i, i ^ k) for i in range(lax.axis_size(axis))])]
    pallas_call x2 -> x3, Pallas kernels: 21.2 us -> 25.3 us  [convolve(): pl.pallas_call(functools.partial(conv_kernel, plan, min(ROWS, rows), len(...]
    unnamed x11 -> x15, local copies, waits for them, and re-layouts: 5.35 us -> 8.33 us
    concatenate x0 -> x1, other arithmetic: none -> 1.56 us  [body(): return jnp.concatenate([outside[:1], inside, outside[1:]])]
  transfers between devices with their start and end apart: 17 -> 17, of which waited for: 6 -> 6; matrix products, arithmetic and copies ran while one was open for 6% -> 6% of each run, Pallas kernels for 23% -> 25%
where the time goes in v10:
time: 110 us; the launch traced here: 109 us
  waiting for transfers between devices  36.3 us (33%)
  starting transfers between devices  30.2 us (27%)
  Pallas kernels  27.8 us (25%)
  local copies, waits for them, and re-layouts  11.5 us (10%)
  other arithmetic  3.22 us (3%)
    pallas_call x3, Pallas kernels, convolve(): pl.pallas_call(functools.partial(conv_kernel, plan, min(ROWS, rows), len(...  25.3 us
    ppermute x13, waiting for transfers between devices, swap(): lax.ppermute(array, axis, [(i, i ^ k) for i in range(lax.axis_size(axis))])  20.2 us
    all_to_all x1, waiting for transfers between devices, body(): outer = lax.all_to_all(outer_rows, 'filt', 0, 0)  16 us
    ppermute x13, starting transfers between devices, swap(): lax.ppermute(array, axis, [(i, i ^ k) for i in range(lax.axis_size(axis))])  15.6 us
    unnamed x15, local copies, waits for them, and re-layouts  8.33 us
    ppermute x1, starting transfers between devices, body(): before = lax.ppermute(last, 'slab', up)  5.4 us
    all_to_all x1, starting transfers between devices, body(): inner = lax.all_to_all(inner_rows, 'filt', 0, 0)  4.29 us
    all_to_all x1, starting transfers between devices, body(): outer = lax.all_to_all(outer_rows, 'filt', 0, 0)  3.57 us
  transfers between devices with their start and end apart: 17, of which 6 were waited for; matrix products, arithmetic and copies ran while one was open for 6% of the time, Pallas kernels for 25%

profile of v10, /device:TPU:0, one launch (start us, length us, event | category | flops | bytes accessed | tf_op | source)
XLA Modules:
  0.0 109.4 jit_solution(11669497748809681165)
XLA Ops:
  0.0 2.9 %collective-permute-start = (bf16[3,3,3,32,256]{4,3,2,1,0:T(8,128)(2,1)}, bf16[3,3,3,32,256]{4,3,2,1,0:T(8,128)(2,1)S(1)}, u32[]{:S(2)}, u32[]{:S(2)}) collective-permute-start(bf16[3,3,3,32,256]{4,3,2,1,0:T(8,128)(2,1)} %param.4), channel_id=1, source_target_pairs={{0,2},{1,3},{2,0},{3,1},{4,6},{5,7},{6,4},{7,5},{8,10},{9,11},{10,... | collective-permute-start | bytes 1327112 | tf_op jit(solution)/shard_map/ppermute | solution.py:152
  2.9 1.5 %collective-permute-start.1 = (bf16[3,3,3,32,256]{4,3,2,1,0:T(8,128)(2,1)}, bf16[3,3,3,32,256]{4,3,2,1,0:T(8,128)(2,1)S(1)}, u32[]{:S(2)}, u32[]{:S(2)}) collective-permute-start(bf16[3,3,3,32,256]{4,3,2,1,0:T(8,128)(2,1)} %param.4), channel_id=1, source_target_pairs={{0,4},{1,5},{2,6},{3,7},{4,0},{5,1},{6,2},{7,3},{8,12},{9,13},{10,... | collective-permute-start | bytes 1327112 | tf_op jit(solution)/shard_map/ppermute | solution.py:152
  4.5 8.9 %collective-permute-done = bf16[3,3,3,32,256]{4,3,2,1,0:T(8,128)(2,1)S(1)} collective-permute-done((bf16[3,3,3,32,256]{4,3,2,1,0:T(8,128)(2,1)}, bf16[3,3,3,32,256]{4,3,2,1,0:T(8,128)(2,1)S(1)}, u32[]{:S(2)}, u32[]{:S(2)}) %collective-permute-start) | collective-permute-done | bytes 442400 | tf_op jit(solution)/shard_map/ppermute | solution.py:152
  13.3 1.8 %collective-permute-start.2 = (bf16[3,3,3,16,256]{4,3,2,1,0:T(8,128)(2,1)S(1)}, bf16[3,3,3,16,256]{4,3,2,1,0:T(8,128)(2,1)S(1)}, u32[]{:S(2)}, u32[]{:S(2)}) collective-permute-start(bf16[3,3,3,16,256]{4,3,2,1,0:T(8,128)(2,1)S(1)} %slice.114), channel_id=1, source_target_pairs={{0,4},{1,5},{2,6},{3,7},{4,0},{5,1},{6,2},{7,3},{8,12},{9,13},{10,... | collective-permute-start | bytes 663560 | tf_op jit(solution)/shard_map/ppermute | solution.py:152
  15.2 1.6 %collective-permute-start.3 = (bf16[3,3,3,16,256]{4,3,2,1,0:T(8,128)(2,1)S(1)}, bf16[3,3,3,16,256]{4,3,2,1,0:T(8,128)(2,1)S(1)}, u32[]{:S(2)}, u32[]{:S(2)}) collective-permute-start(bf16[3,3,3,16,256]{4,3,2,1,0:T(8,128)(2,1)S(1)} %slice.115), channel_id=1, source_target_pairs={{0,2},{1,3},{2,0},{3,1},{4,6},{5,7},{6,4},{7,5},{8,10},{9,11},{10,... | collective-permute-start | bytes 663560 | tf_op jit(solution)/shard_map/ppermute | solution.py:152
  16.8 2.9 %copy.38 = bf16[4,32,64,128]{3,1,2,0:T(8,128)(2,1)S(1)} copy(bf16[4,32,64,128]{3,2,1,0:T(8,128)(2,1)} %param.3) | data formatting | bytes 4194304 | tf_op args[0]
  19.7 1.3 %shard_map.37 = (bf16[8,2,10,32,128]{4,3,2,1,0:T(8,128)(2,1)}, bf16[8,2,10,32,128]{4,3,2,1,0:T(8,128)(2,1)S(1)}) custom-call(bf16[4,64,32,128]{3,2,1,0:T(8,128)(2,1)S(1)} %bitcast.60), custom_call_target="tpu_custom_call" | custom-call | tf_op jit(solution)/shard_map/pallas_call | solution.py:32
  22.1 3.6 %all-to-all-start = ((bf16[8,2,10,32,128]{4,3,2,1,0:T(8,128)(2,1)}), bf16[8,2,10,32,128]{4,3,2,1,0:T(8,128)(2,1)S(1)}, u32[]{:S(2)}, u32[]{:S(2)}) async-start(bf16[8,2,10,32,128]{4,3,2,1,0:T(8,128)(2,1)} %get-tuple-element.21), calls=%async_computation | async-start | bytes 2621440 | tf_op jit(solution)/shard_map/all_to_all | solution.py:165
  25.8 1.4 %pad_maximum_fusion.1.refs_1_.refs_2_.refs_4_ = bf16[4,3,3,3,32,256]{5,4,3,2,1,0:T(8,128)(2,1)S(1)} fusion(bf16[1,3,3,3,32,256]{5,4,3,2,1,0:T(8,128)(2,1)S(1)} %maximum_bitcast_fusion, bf16[1,3,3,3,32,256]{5,4,3,2,1,0:T(8,128)(2,1)} %bitcast.64, bf16[1,3,3,3,32,256]{5,4,3,2,1,0:T(8,128)(2,1)S(1)} %bitcast.63, bf16[1,3,3,3,32,256]{5,4,3,2,1,0:T(8,128)(2,1)} %bitcast.65), kind=kLoop, calls=%fused_computation.3 | loop fusion | flops 2654208 | bytes 3538944 | tf_op jit(solution)/shard_map/stack | solution.py:161
  27.8 16.0 %all-to-all-done.refs_0_.vol_ref = bf16[8,2,10,32,128]{4,3,2,1,0:T(8,128)(2,1)S(1)} async-done(((bf16[8,2,10,32,128]{4,3,2,1,0:T(8,128)(2,1)}), bf16[8,2,10,32,128]{4,3,2,1,0:T(8,128)(2,1)S(1)}, u32[]{:S(2)}, u32[]{:S(2)}) %all-to-all-start) | async-done | bytes 1310752 | tf_op jit(solution)/shard_map/all_to_all | solution.py:165
  43.8 4.3 %all-to-all-start.1 = ((bf16[8,2,10,32,128]{4,3,2,1,0:T(8,128)(2,1)}), bf16[8,2,10,32,128]{4,3,2,1,0:T(8,128)(2,1)}, u32[]{:S(2)}, u32[]{:S(2)}) async-start(bf16[8,2,10,32,128]{4,3,2,1,0:T(8,128)(2,1)} %copy-done), calls=%async_computation.1 | async-start | bytes 2621440 | tf_op jit(solution)/shard_map/all_to_all | solution.py:166
  50.2 1.3 %collective-permute-start.10 = (bf16[8,1,10,32,128]{4,3,2,1,0:T(8,128)(2,1)}, bf16[8,1,10,32,128]{4,3,2,1,0:T(8,128)(2,1)}, u32[]{:S(2)}, u32[]{:S(2)}) collective-permute-start(bf16[8,1,10,32,128]{4,3,2,1,0:T(8,128)(2,1)} %get-tuple-element.30), channel_id=1, source_target_pairs={{8,0},{16,8},{24,16},{9,1},{17,9},{25,17},{10,2},{18,10},{26,18},{... | collective-permute-start | bytes 1966088 | tf_op jit(solution)/shard_map/ppermute | solution.py:200
  51.5 5.4 %collective-permute-start.9 = (bf16[8,1,10,32,128]{4,3,2,1,0:T(8,128)(2,1)}, bf16[8,1,10,32,128]{4,3,2,1,0:T(8,128)(2,1)}, u32[]{:S(2)}, u32[]{:S(2)}) collective-permute-start(bf16[8,1,10,32,128]{4,3,2,1,0:T(8,128)(2,1)} %get-tuple-element.29), channel_id=1, source_target_pairs={{0,8},{8,16},{16,24},{1,9},{9,17},{17,25},{2,10},{10,18},{18,26},{... | collective-permute-start | bytes 1966088 | tf_op jit(solution)/shard_map/ppermute | solution.py:201
  57.0 8.8 %shard_map.38 = (f32[2,8,256,128]{3,2,1,0:T(8,128)S(1)}, f32[2,8,256,128]{3,2,1,0:T(8,128)S(1)}) custom-call(bf16[8,2,10,32,128]{4,3,2,1,0:T(8,128)(2,1)S(1)} %all-to-all-done.refs_0_.vol_ref, bf16[4,3,3,3,32,256]{5,4,3,2,1,0:T(8,128)(2,1)S(1)} %pad_maximum_fusion.1.refs_1_.refs_2_.refs_4_, ...), custom_call_target="tpu_custom_call" | custom-call | flops 4831838208 | bytes 10000000 | tf_op jit(solution)/shard_map/pallas_call | solution.py:127
  65.8 1.3 %copy-done.1 = f32[2,8,256,128]{3,2,1,0:T(8,128)} copy-done((f32[2,8,256,128]{3,2,1,0:T(8,128)}, f32[2,8,256,128]{3,2,1,0:T(8,128)S(1)}, u32[]{:S(2)}) %copy-start.1) | copy-done | bytes 2097176
  67.1 1.4 %copy-done.3 = f32[2,8,256,128]{3,2,1,0:T(8,128)} copy-done((f32[2,8,256,128]{3,2,1,0:T(8,128)}, f32[2,8,256,128]{3,2,1,0:T(8,128)S(1)}, u32[]{:S(2)}) %copy-start.3) | copy-done | bytes 2097176
  68.5 1.6 %copy-done.4 = f32[2,8,256,128]{3,2,1,0:T(8,128)S(1)} copy-done((f32[2,8,256,128]{3,2,1,0:T(8,128)S(1)}, f32[2,8,256,128]{3,2,1,0:T(8,128)}, u32[]{:S(2)}) %copy-start.4) | copy-done | bytes 2097176
  70.1 8.1 %shard_map.39 = (bf16[2,8,64,128]{3,2,1,0:T(8,128)(2,1)S(1)}, bf16[2,8,64,128]{3,2,1,0:T(8,128)(2,1)S(1)}, bf16[2,8,64,128]{3,2,1,0:T(8,128)(2,1)S(1)}, bf16[2,8,64,128]{3,2,1,0:T(8,128)(2,1)S(1)}) custom-call(f32[2,8,256,128]{3,2,1,0:T(8,128)S(1)} %copy-done.4, bf16[8,2,10,32,128]{4,3,2,1,0:T(8,128)(2,1)} %all-to-all-done.1.refs_1_, ...), custom_call_target="tpu_custom_call" | custom-call | flops 4831838208 | bytes 10000000 | tf_op jit(solution)/shard_map/pallas_call | solution.py:127
  78.2 2.9 %collective-permute-start.7 = (bf16[2,8,64,128]{3,2,1,0:T(8,128)(2,1)S(1)}, bf16[2,8,64,128]{3,2,1,0:T(8,128)(2,1)S(1)}, u32[]{:S(2)}, u32[]{:S(2)}) collective-permute-start(bf16[2,8,64,128]{3,2,1,0:T(8,128)(2,1)S(1)} %get-tuple-element.27), channel_id=1, source_target_pairs={{0,6},{1,7},{2,4},{3,5},{4,2},{5,3},{6,0},{7,1},{8,14},{9,15},{10,... | collective-permute-start | bytes 786440 | tf_op jit(solution)/shard_map/ppermute | solution.py:152
  81.8 8.4 %shard_map.41 = (bf16[2,8,64,128]{3,2,1,0:T(8,128)(2,1)S(1)}, bf16[2,8,64,128]{3,2,1,0:T(8,128)(2,1)S(1)}, bf16[2,8,64,128]{3,2,1,0:T(8,128)(2,1)S(1)}, bf16[2,8,64,128]{3,2,1,0:T(8,128)(2,1)S(1)}) custom-call(f32[2,8,256,128]{3,2,1,0:T(8,128)S(1)} %copy-done.2, bf16[8,2,10,32,128]{4,3,2,1,0:T(8,128)(2,1)} %all-to-all-done.1.refs_1_, ...), custom_call_target="tpu_custom_call" | custom-call | flops 4831838208 | bytes 10000000 | tf_op jit(solution)/shard_map/pallas_call | solution.py:127
  90.2 2.9 %collective-permute-start.13 = (bf16[2,8,64,128]{3,2,1,0:T(8,128)(2,1)S(1)}, bf16[2,8,64,128]{3,2,1,0:T(8,128)(2,1)S(1)}, u32[]{:S(2)}, u32[]{:S(2)}) collective-permute-start(bf16[2,8,64,128]{3,2,1,0:T(8,128)(2,1)S(1)} %get-tuple-element.34), channel_id=1, source_target_pairs={{0,6},{1,7},{2,4},{3,5},{4,2},{5,3},{6,0},{7,1},{8,14},{9,15},{10,... | collective-permute-start | bytes 786440 | tf_op jit(solution)/shard_map/ppermute | solution.py:152
  94.1 6.3 %collective-permute-done.13 = bf16[2,8,64,128]{3,2,1,0:T(8,128)(2,1)S(1)} collective-permute-done((bf16[2,8,64,128]{3,2,1,0:T(8,128)(2,1)S(1)}, bf16[2,8,64,128]{3,2,1,0:T(8,128)(2,1)S(1)}, u32[]{:S(2)}, u32[]{:S(2)}) %collective-permute-start.13) | collective-permute-done | bytes 262176 | tf_op jit(solution)/shard_map/ppermute | solution.py:152
  100.5 3.6 %collective-permute-done.12 = bf16[2,8,64,128]{3,2,1,0:T(8,128)(2,1)S(1)} collective-permute-done((bf16[2,8,64,128]{3,2,1,0:T(8,128)(2,1)S(1)}, bf16[2,8,64,128]{3,2,1,0:T(8,128)(2,1)S(1)}, u32[]{:S(2)}, u32[]{:S(2)}) %collective-permute-start.12) | collective-permute-done | bytes 262176 | tf_op jit(solution)/shard_map/ppermute | solution.py:152
  107.8 1.6 %pad_maximum_fusion = bf16[4,32,64,128]{3,2,1,0:T(8,128)(2,1)} fusion(bf16[1,32,64,128]{3,2,1,0:T(8,128)(2,1)S(1)} %get-tuple-element.38, bf16[2,32,64,128]{3,2,1,0:T(8,128)(2,1)S(1)} %bitcast.62, bf16[1,32,64,128]{3,2,1,0:T(8,128)(2,1)S(1)} %get-tuple-element.37), kind=kLoop, calls=%fused_computation.1 | loop fusion | flops 2097152 | bytes 4194304 | tf_op jit(solution)/shard_map/concatenate | solution.py:207
  (75 shorter events, 9.2 us)
Async XLA Ops:
  0.0 13.3 %collective-permute-start = (bf16[3,3,3,32,256]{4,3,2,1,0:T(8,128)(2,1)}, bf16[3,3,3,32,256]{4,3,2,1,0:T(8,128)(2,1)S(1)}, u32[]{:S(2)}, u32[]{:S(2)}) collective-permute-start(bf16[3,3,3,32,256]{4,3,2,1,0:T(8,128)(2,1)} %param.4), channel_id=1, source_target_pairs={{0,2},{1,3},{2,0},{3,1},{4,6},{5,7},{6,4},{7,5},{8,10},{9,11},{10,... | collective-permute-start | bytes 1327112 | tf_op jit(solution)/shard_map/ppermute | solution.py:152
  2.9 12.2 %collective-permute-start.1 = (bf16[3,3,3,32,256]{4,3,2,1,0:T(8,128)(2,1)}, bf16[3,3,3,32,256]{4,3,2,1,0:T(8,128)(2,1)S(1)}, u32[]{:S(2)}, u32[]{:S(2)}) collective-permute-start(bf16[3,3,3,32,256]{4,3,2,1,0:T(8,128)(2,1)} %param.4), channel_id=1, source_target_pairs={{0,4},{1,5},{2,6},{3,7},{4,0},{5,1},{6,2},{7,3},{8,12},{9,13},{10,... | collective-permute-start | bytes 1327112 | tf_op jit(solution)/shard_map/ppermute | solution.py:152
  13.3 12.3 %collective-permute-start.2 = (bf16[3,3,3,16,256]{4,3,2,1,0:T(8,128)(2,1)S(1)}, bf16[3,3,3,16,256]{4,3,2,1,0:T(8,128)(2,1)S(1)}, u32[]{:S(2)}, u32[]{:S(2)}) collective-permute-start(bf16[3,3,3,16,256]{4,3,2,1,0:T(8,128)(2,1)S(1)} %slice.114), channel_id=1, source_target_pairs={{0,4},{1,5},{2,6},{3,7},{4,0},{5,1},{6,2},{7,3},{8,12},{9,13},{10,... | collective-permute-start | bytes 663560 | tf_op jit(solution)/shard_map/ppermute | solution.py:152
  15.2 4.5 %copy-start.5 = (bf16[3,3,3,32,256]{4,3,2,1,0:T(8,128)(2,1)}, bf16[3,3,3,32,256]{4,3,2,1,0:T(8,128)(2,1)S(1)}, u32[]{:S(2)}) copy-start(bf16[3,3,3,32,256]{4,3,2,1,0:T(8,128)(2,1)S(1)} %collective-permute-done.1) | copy-start | bytes 1327108
  15.2 10.5 %collective-permute-start.3 = (bf16[3,3,3,16,256]{4,3,2,1,0:T(8,128)(2,1)S(1)}, bf16[3,3,3,16,256]{4,3,2,1,0:T(8,128)(2,1)S(1)}, u32[]{:S(2)}, u32[]{:S(2)}) collective-permute-start(bf16[3,3,3,16,256]{4,3,2,1,0:T(8,128)(2,1)S(1)} %slice.115), channel_id=1, source_target_pairs={{0,2},{1,3},{2,0},{3,1},{4,6},{5,7},{6,4},{7,5},{8,10},{9,11},{10,... | collective-permute-start | bytes 663560 | tf_op jit(solution)/shard_map/ppermute | solution.py:152
  21.0 1.1 %copy-start = (bf16[8,2,10,32,128]{4,3,2,1,0:T(8,128)(2,1)}, bf16[8,2,10,32,128]{4,3,2,1,0:T(8,128)(2,1)S(1)}, u32[]{:S(2)}) copy-start(bf16[8,2,10,32,128]{4,3,2,1,0:T(8,128)(2,1)S(1)} %get-tuple-element.23) | copy-start | bytes 3932164
  22.1 21.7 %all-to-all-start = ((bf16[8,2,10,32,128]{4,3,2,1,0:T(8,128)(2,1)}), bf16[8,2,10,32,128]{4,3,2,1,0:T(8,128)(2,1)S(1)}, u32[]{:S(2)}, u32[]{:S(2)}) async-start(bf16[8,2,10,32,128]{4,3,2,1,0:T(8,128)(2,1)} %get-tuple-element.21), calls=%async_computation | async-start | bytes 2621440 | tf_op jit(solution)/shard_map/all_to_all | solution.py:165
  25.8 1.9 %copy-start.6 = (f32[256]{0:T(256)S(1)}, f32[256]{0:T(256)}, u32[]{:S(2)}) copy-start(f32[256]{0:T(256)} %param.5) | copy-start | bytes 3076
  27.1 29.7 %collective-permute-start.4 = (bf16[4,3,3,3,32,256]{5,4,3,2,1,0:T(8,128)(2,1)S(1)}, bf16[4,3,3,3,32,256]{5,4,3,2,1,0:T(8,128)(2,1)}, u32[]{:S(2)}, u32[]{:S(2)}) collective-permute-start(bf16[4,3,3,3,32,256]{5,4,3,2,1,0:T(8,128)(2,1)S(1)} %pad_maximum_fusion.1.refs_1_.refs_2_.refs_4_), channel_id=1, source_target_pairs={{0,1},{1,0},{2,3},{3,2},{4,5},{5,4},{6,7},{7,6},{8,9},{9,8},{10,11... | collective-permute-start | bytes 5308424 | tf_op jit(solution)/shard_map/ppermute | solution.py:152
  43.8 24.7 %all-to-all-start.1 = ((bf16[8,2,10,32,128]{4,3,2,1,0:T(8,128)(2,1)}), bf16[8,2,10,32,128]{4,3,2,1,0:T(8,128)(2,1)}, u32[]{:S(2)}, u32[]{:S(2)}) async-start(bf16[8,2,10,32,128]{4,3,2,1,0:T(8,128)(2,1)} %copy-done), calls=%async_computation.1 | async-start | bytes 2621440 | tf_op jit(solution)/shard_map/all_to_all | solution.py:166
  50.2 31.6 %collective-permute-start.10 = (bf16[8,1,10,32,128]{4,3,2,1,0:T(8,128)(2,1)}, bf16[8,1,10,32,128]{4,3,2,1,0:T(8,128)(2,1)}, u32[]{:S(2)}, u32[]{:S(2)}) collective-permute-start(bf16[8,1,10,32,128]{4,3,2,1,0:T(8,128)(2,1)} %get-tuple-element.30), channel_id=1, source_target_pairs={{8,0},{16,8},{24,16},{9,1},{17,9},{25,17},{10,2},{18,10},{26,18},{... | collective-permute-start | bytes 1966088 | tf_op jit(solution)/shard_map/ppermute | solution.py:200
  51.5 30.3 %collective-permute-start.9 = (bf16[8,1,10,32,128]{4,3,2,1,0:T(8,128)(2,1)}, bf16[8,1,10,32,128]{4,3,2,1,0:T(8,128)(2,1)}, u32[]{:S(2)}, u32[]{:S(2)}) collective-permute-start(bf16[8,1,10,32,128]{4,3,2,1,0:T(8,128)(2,1)} %get-tuple-element.29), channel_id=1, source_target_pairs={{0,8},{8,16},{16,24},{1,9},{9,17},{17,25},{2,10},{10,18},{18,26},{... | collective-permute-start | bytes 1966088 | tf_op jit(solution)/shard_map/ppermute | solution.py:201
  65.8 1.3 %copy-start.1 = (f32[2,8,256,128]{3,2,1,0:T(8,128)}, f32[2,8,256,128]{3,2,1,0:T(8,128)S(1)}, u32[]{:S(2)}) copy-start(f32[2,8,256,128]{3,2,1,0:T(8,128)S(1)} %get-tuple-element.28.refs_0_) | copy-start | bytes 6291460
  67.1 1.4 %copy-start.3 = (f32[2,8,256,128]{3,2,1,0:T(8,128)}, f32[2,8,256,128]{3,2,1,0:T(8,128)S(1)}, u32[]{:S(2)}) copy-start(f32[2,8,256,128]{3,2,1,0:T(8,128)S(1)} %get-tuple-element.22.refs_0_) | copy-start | bytes 6291460
  68.5 1.6 %copy-start.4 = (f32[2,8,256,128]{3,2,1,0:T(8,128)S(1)}, f32[2,8,256,128]{3,2,1,0:T(8,128)}, u32[]{:S(2)}) copy-start(f32[2,8,256,128]{3,2,1,0:T(8,128)} %copy-done.3) | copy-start | bytes 6291460
  70.1 11.7 %copy-start.2 = (f32[2,8,256,128]{3,2,1,0:T(8,128)S(1)}, f32[2,8,256,128]{3,2,1,0:T(8,128)}, u32[]{:S(2)}) copy-start(f32[2,8,256,128]{3,2,1,0:T(8,128)} %copy-done.1) | copy-start | bytes 6291460
  78.2 15.4 %collective-permute-start.7 = (bf16[2,8,64,128]{3,2,1,0:T(8,128)(2,1)S(1)}, bf16[2,8,64,128]{3,2,1,0:T(8,128)(2,1)S(1)}, u32[]{:S(2)}, u32[]{:S(2)}) collective-permute-start(bf16[2,8,64,128]{3,2,1,0:T(8,128)(2,1)S(1)} %get-tuple-element.27), channel_id=1, source_target_pairs={{0,6},{1,7},{2,4},{3,5},{4,2},{5,3},{6,0},{7,1},{8,14},{9,15},{10,... | collective-permute-start | bytes 786440 | tf_op jit(solution)/shard_map/ppermute | solution.py:152
  81.1 12.8 %collective-permute-start.6 = (bf16[2,8,64,128]{3,2,1,0:T(8,128)(2,1)S(1)}, bf16[2,8,64,128]{3,2,1,0:T(8,128)(2,1)S(1)}, u32[]{:S(2)}, u32[]{:S(2)}) collective-permute-start(bf16[2,8,64,128]{3,2,1,0:T(8,128)(2,1)S(1)} %get-tuple-element.26), channel_id=1, source_target_pairs={{0,4},{1,5},{2,6},{3,7},{4,0},{5,1},{6,2},{7,3},{8,12},{9,13},{10,... | collective-permute-start | bytes 786440 | tf_op jit(solution)/shard_map/ppermute | solution.py:152
  81.6 12.3 %collective-permute-start.5 = (bf16[2,8,64,128]{3,2,1,0:T(8,128)(2,1)S(1)}, bf16[2,8,64,128]{3,2,1,0:T(8,128)(2,1)S(1)}, u32[]{:S(2)}, u32[]{:S(2)}) collective-permute-start(bf16[2,8,64,128]{3,2,1,0:T(8,128)(2,1)S(1)} %get-tuple-element.25), channel_id=1, source_target_pairs={{0,2},{1,3},{2,0},{3,1},{4,6},{5,7},{6,4},{7,5},{8,10},{9,11},{10,... | collective-permute-start | bytes 786440 | tf_op jit(solution)/shard_map/ppermute | solution.py:152
  90.2 10.3 %collective-permute-start.13 = (bf16[2,8,64,128]{3,2,1,0:T(8,128)(2,1)S(1)}, bf16[2,8,64,128]{3,2,1,0:T(8,128)(2,1)S(1)}, u32[]{:S(2)}, u32[]{:S(2)}) collective-permute-start(bf16[2,8,64,128]{3,2,1,0:T(8,128)(2,1)S(1)} %get-tuple-element.34), channel_id=1, source_target_pairs={{0,6},{1,7},{2,4},{3,5},{4,2},{5,3},{6,0},{7,1},{8,14},{9,15},{10,... | collective-permute-start | bytes 786440 | tf_op jit(solution)/shard_map/ppermute | solution.py:152
  93.1 11.0 %collective-permute-start.12 = (bf16[2,8,64,128]{3,2,1,0:T(8,128)(2,1)S(1)}, bf16[2,8,64,128]{3,2,1,0:T(8,128)(2,1)S(1)}, u32[]{:S(2)}, u32[]{:S(2)}) collective-permute-start(bf16[2,8,64,128]{3,2,1,0:T(8,128)(2,1)S(1)} %get-tuple-element.33), channel_id=1, source_target_pairs={{0,4},{1,5},{2,6},{3,7},{4,0},{5,1},{6,2},{7,3},{8,12},{9,13},{10,... | collective-permute-start | bytes 786440 | tf_op jit(solution)/shard_map/ppermute | solution.py:152
  93.6 10.7 %collective-permute-start.11 = (bf16[2,8,64,128]{3,2,1,0:T(8,128)(2,1)S(1)}, bf16[2,8,64,128]{3,2,1,0:T(8,128)(2,1)S(1)}, u32[]{:S(2)}, u32[]{:S(2)}) collective-permute-start(bf16[2,8,64,128]{3,2,1,0:T(8,128)(2,1)S(1)} %get-tuple-element.32), channel_id=1, source_target_pairs={{0,2},{1,3},{2,0},{3,1},{4,6},{5,7},{6,4},{7,5},{8,10},{9,11},{10,... | collective-permute-start | bytes 786440 | tf_op jit(solution)/shard_map/ppermute | solution.py:152
  94.0 11.2 %collective-permute-start.8 = (bf16[4,2,8,32,128]{4,3,2,1,0:T(8,128)(2,1)S(1)}, bf16[4,2,8,32,128]{4,3,2,1,0:T(8,128)(2,1)S(1)}, u32[]{:S(2)}, u32[]{:S(2)}) collective-permute-start(bf16[4,2,8,32,128]{4,3,2,1,0:T(8,128)(2,1)S(1)} %pad_maximum_fusion.2), channel_id=1, source_target_pairs={{0,1},{1,0},{2,3},{3,2},{4,5},{5,4},{6,7},{7,6},{8,9},{9,8},{10,11... | collective-permute-start | bytes 1572872 | tf_op jit(solution)/shard_map/ppermute | solution.py:152
  104.4 2.0 %collective-permute-start.14 = (bf16[4,2,8,32,128]{4,3,2,1,0:T(8,128)(2,1)S(1)}, bf16[4,2,8,32,128]{4,3,2,1,0:T(8,128)(2,1)S(1)}, u32[]{:S(2)}, u32[]{:S(2)}) collective-permute-start(bf16[4,2,8,32,128]{4,3,2,1,0:T(8,128)(2,1)S(1)} %pad_maximum_fusion.3), channel_id=1, source_target_pairs={{0,1},{1,0},{2,3},{3,2},{4,5},{5,4},{6,7},{7,6},{8,9},{9,8},{10,11... | collective-permute-start | bytes 1572872 | tf_op jit(solution)/shard_map/ppermute | solution.py:152

commit v11 on v9

--- a/solution.py
+++ b/solution.py
@@ -8,7 +8,7 @@
 from jax.sharding import PartitionSpec as P
 
 slope = 0.3
-ROWS = 4
+ROWS = 2
 
 
 def cut_kernel(parts, vol_ref, outer, inner):
@@ -73,8 +73,7 @@
     lane = lax.broadcasted_iota(jnp.int32, (total_out, cols), 1)
 
     def tile(slot, row):
-        cells = []
-        weights = []
+        total = jnp.zeros((3 * total_out, rows_at_once * cols), jnp.float32)
         for a, (source, plane) in enumerate(plan[slot]):
             piece = pieces[source]
             lines = [
@@ -82,15 +81,11 @@
                 for r in range(rows_at_once + 2)
             ]
             for b in range(3):
-                cells.append(jnp.concatenate(lines[b : b + rows_at_once], axis=1))
-                weights.append(
-                    jnp.concatenate(
-                        [part[g, a, b].reshape(3 * size, -1) for g in range(groups) for part in tap_parts], axis=0
-                    )
+                cells = jnp.concatenate(lines[b : b + rows_at_once], axis=1)
+                weights = jnp.concatenate(
+                    [part[g, a, b].reshape(3 * size, -1) for g in range(groups) for part in tap_parts], axis=0
                 )
-        total = jnp.dot(
-            jnp.concatenate(weights, axis=1), jnp.concatenate(cells, axis=0), preferred_element_type=jnp.float32
-        )
+                total = total + jnp.dot(weights, cells, preferred_element_type=jnp.float32)
         for r in range(rows_at_once):
             part = total[:, r * cols : (r + 1) * cols].reshape(groups * tap_count, 3, size, cols)
             side = [part[:, c].reshape(total_out, cols) for c in range(3)]
@@ -122,7 +117,7 @@
         in_specs=[in_vmem] * (len(pieces) + len(tap_parts) + 1),
         out_specs=[in_vmem] * blocks,
         cost_estimate=pl.CostEstimate(flops=2 * macs, bytes_accessed=10_000_000, transcendentals=0),
-        compiler_params=pltpu.CompilerParams(vmem_limit_bytes=20 * 2**20),
+        compiler_params=pltpu.CompilerParams(vmem_limit_bytes=12 * 2**20),
     )(*pieces, *tap_parts, wide_bias)
 
 
@@ -190,9 +185,8 @@
 
     ends = (((2, 0), *where[:2]), (*where[-2:], (3, 0)))
     outside = send_back(convolve(ends, [outer, inner, settle(before), settle(after)], tap_parts, bias, blocks))
-    whole = jnp.pad(inside, ((1, 1), (0, 0), (0, 0), (0, 0)))
-    whole = lax.dynamic_update_slice_in_dim(whole, outside[:1], 0, 0)
-    return lax.dynamic_update_slice_in_dim(whole, outside[1:], planes - 1, 0)
+    inside, outside = lax.optimization_barrier((inside, outside))
+    return jnp.concatenate([outside[:1], inside, outside[1:]])
 
 
 def solution(mesh):

time: 103 us -> 104 us (level)
  local copies, waits for them, and re-layouts: 9.72 us -> 7.17 us
  other arithmetic: 1.52 us -> 3.08 us
  Pallas kernels: 23.7 us -> 25.1 us
    concatenate x0 -> x1, other arithmetic: none -> 1.56 us  [body(): return jnp.concatenate([outside[:1], inside, outside[1:]])]
    pallas_call x2, Pallas kernels: 21.2 us -> 22.7 us  [convolve(): pl.pallas_call(functools.partial(conv_kernel, plan, min(ROWS, rows), len(...]
    unnamed x11 -> x9, local copies, waits for them, and re-layouts: 5.35 us -> 4.04 us
  transfers between devices with their start and end apart: 17 -> 17, of which waited for: 6 -> 6; matrix products, arithmetic and copies ran while one was open for 6% -> 6% of each run, Pallas kernels for 23% -> 24%
where the time goes in v11:
time: 104 us
  waiting for transfers between devices  37.7 us (36%)
  starting transfers between devices  29.9 us (29%)
  Pallas kernels  25.1 us (24%)
  local copies, waits for them, and re-layouts  7.17 us (7%)
  other arithmetic  3.08 us (3%)
    ppermute x13, waiting for transfers between devices, swap(): lax.ppermute(array, axis, [(i, i ^ k) for i in range(lax.axis_size(axis))])  28.4 us
    pallas_call x2, Pallas kernels, convolve(): pl.pallas_call(functools.partial(conv_kernel, plan, min(ROWS, rows), len(...  22.7 us
    ppermute x13, starting transfers between devices, swap(): lax.ppermute(array, axis, [(i, i ^ k) for i in range(lax.axis_size(axis))])  15.4 us
    all_to_all x1, waiting for transfers between devices, body(): inner = lax.all_to_all(inner_rows, 'filt', 0, 0)  9.3 us
    ppermute x1, starting transfers between devices, body(): before = lax.ppermute(last, 'slab', up)  5.41 us
    all_to_all x1, starting transfers between devices, body(): inner = lax.all_to_all(inner_rows, 'filt', 0, 0)  4.28 us
    unnamed x9, local copies, waits for them, and re-layouts  4.04 us
    all_to_all x1, starting transfers between devices, body(): outer = lax.all_to_all(outer_rows, 'filt', 0, 0)  3.57 us
  transfers between devices with their start and end apart: 17, of which 6 were waited for; matrix products, arithmetic and copies ran while one was open for 6% of the time, Pallas kernels for 24%

profile of v11, /device:TPU:0, one launch (start us, length us, event | category | flops | bytes accessed | tf_op | source)
XLA Modules:
  0.0 103.5 jit_solution(2473617116767538624)
XLA Ops:
  0.0 2.9 %collective-permute-start = (bf16[3,3,3,32,256]{4,3,2,1,0:T(8,128)(2,1)}, bf16[3,3,3,32,256]{4,3,2,1,0:T(8,128)(2,1)S(1)}, u32[]{:S(2)}, u32[]{:S(2)}) collective-permute-start(bf16[3,3,3,32,256]{4,3,2,1,0:T(8,128)(2,1)} %param.4), channel_id=1, source_target_pairs={{0,2},{1,3},{2,0},{3,1},{4,6},{5,7},{6,4},{7,5},{8,10},{9,11},{10,... | collective-permute-start | bytes 1327112 | tf_op jit(solution)/shard_map/ppermute | solution.py:137
  2.9 1.5 %collective-permute-start.1 = (bf16[3,3,3,32,256]{4,3,2,1,0:T(8,128)(2,1)}, bf16[3,3,3,32,256]{4,3,2,1,0:T(8,128)(2,1)S(1)}, u32[]{:S(2)}, u32[]{:S(2)}) collective-permute-start(bf16[3,3,3,32,256]{4,3,2,1,0:T(8,128)(2,1)} %param.4), channel_id=1, source_target_pairs={{0,4},{1,5},{2,6},{3,7},{4,0},{5,1},{6,2},{7,3},{8,12},{9,13},{10,... | collective-permute-start | bytes 1327112 | tf_op jit(solution)/shard_map/ppermute | solution.py:137
  4.5 2.9 %copy.38 = bf16[4,32,64,128]{3,1,2,0:T(8,128)(2,1)S(1)} copy(bf16[4,32,64,128]{3,2,1,0:T(8,128)(2,1)} %param.3) | data formatting | bytes 4194304 | tf_op args[0]
  7.4 1.3 %shard_map.37 = (bf16[8,2,10,32,128]{4,3,2,1,0:T(8,128)(2,1)}, bf16[8,2,10,32,128]{4,3,2,1,0:T(8,128)(2,1)S(1)}) custom-call(bf16[4,64,32,128]{3,2,1,0:T(8,128)(2,1)S(1)} %bitcast.60), custom_call_target="tpu_custom_call" | custom-call | tf_op jit(solution)/shard_map/pallas_call | solution.py:32
  9.8 3.6 %all-to-all-start = ((bf16[8,2,10,32,128]{4,3,2,1,0:T(8,128)(2,1)}), bf16[8,2,10,32,128]{4,3,2,1,0:T(8,128)(2,1)S(1)}, u32[]{:S(2)}, u32[]{:S(2)}) async-start(bf16[8,2,10,32,128]{4,3,2,1,0:T(8,128)(2,1)} %get-tuple-element.19), calls=%async_computation | async-start | bytes 2621440 | tf_op jit(solution)/shard_map/all_to_all | solution.py:150
  13.4 2.0 %collective-permute-start.2 = (bf16[3,3,3,16,256]{4,3,2,1,0:T(8,128)(2,1)S(1)}, bf16[3,3,3,16,256]{4,3,2,1,0:T(8,128)(2,1)S(1)}, u32[]{:S(2)}, u32[]{:S(2)}) collective-permute-start(bf16[3,3,3,16,256]{4,3,2,1,0:T(8,128)(2,1)S(1)} %slice.114), channel_id=1, source_target_pairs={{0,4},{1,5},{2,6},{3,7},{4,0},{5,1},{6,2},{7,3},{8,12},{9,13},{10,... | collective-permute-start | bytes 663560 | tf_op jit(solution)/shard_map/ppermute | solution.py:137
  15.4 1.5 %collective-permute-start.3 = (bf16[3,3,3,16,256]{4,3,2,1,0:T(8,128)(2,1)S(1)}, bf16[3,3,3,16,256]{4,3,2,1,0:T(8,128)(2,1)S(1)}, u32[]{:S(2)}, u32[]{:S(2)}) collective-permute-start(bf16[3,3,3,16,256]{4,3,2,1,0:T(8,128)(2,1)S(1)} %slice.115), channel_id=1, source_target_pairs={{0,2},{1,3},{2,0},{3,1},{4,6},{5,7},{6,4},{7,5},{8,10},{9,11},{10,... | collective-permute-start | bytes 663560 | tf_op jit(solution)/shard_map/ppermute | solution.py:137
  17.0 18.3 %collective-permute-done.2 = bf16[3,3,3,16,256]{4,3,2,1,0:T(8,128)(2,1)S(1)} collective-permute-done((bf16[3,3,3,16,256]{4,3,2,1,0:T(8,128)(2,1)S(1)}, bf16[3,3,3,16,256]{4,3,2,1,0:T(8,128)(2,1)S(1)}, u32[]{:S(2)}, u32[]{:S(2)}) %collective-permute-start.2) | collective-permute-done | bytes 221216 | tf_op jit(solution)/shard_map/ppermute | solution.py:137
  35.4 1.2 %pad_maximum_fusion.1.refs_2_.refs_4_ = bf16[4,3,3,3,32,256]{5,4,3,2,1,0:T(8,128)(2,1)S(1)} fusion(bf16[1,3,3,3,32,256]{5,4,3,2,1,0:T(8,128)(2,1)S(1)} %maximum_bitcast_fusion, bf16[1,3,3,3,32,256]{5,4,3,2,1,0:T(8,128)(2,1)} %bitcast.64, bf16[1,3,3,3,32,256]{5,4,3,2,1,0:T(8,128)(2,1)S(1)} %bitcast.63, bf16[1,3,3,3,32,256]{5,4,3,2,1,0:T(8,128)(2,1)S(1)} %bitcast.65), kind=kLoop, calls=%fused_computation.3 | loop fusion | flops 2654208 | bytes 3538944 | tf_op jit(solution)/shard_map/stack | solution.py:146
  36.8 4.3 %all-to-all-start.1 = ((bf16[8,2,10,32,128]{4,3,2,1,0:T(8,128)(2,1)}), bf16[8,2,10,32,128]{4,3,2,1,0:T(8,128)(2,1)}, u32[]{:S(2)}, u32[]{:S(2)}) async-start(bf16[8,2,10,32,128]{4,3,2,1,0:T(8,128)(2,1)} %copy-done), calls=%async_computation.1 | async-start | bytes 2621440 | tf_op jit(solution)/shard_map/all_to_all | solution.py:151
  42.1 1.2 %shard_map.39 = (bf16[8,1,10,32,128]{4,3,2,1,0:T(8,128)(2,1)}, bf16[8,1,10,32,128]{4,3,2,1,0:T(8,128)(2,1)}) custom-call(bf16[8,2,10,32,128]{4,3,2,1,0:T(8,128)(2,1)S(1)} %all-to-all-done.refs_0_.vol_ref), custom_call_target="tpu_custom_call" | custom-call | tf_op jit(solution)/shard_map/pallas_call | solution.py:54
  43.3 1.3 %collective-permute-start.10 = (bf16[8,1,10,32,128]{4,3,2,1,0:T(8,128)(2,1)}, bf16[8,1,10,32,128]{4,3,2,1,0:T(8,128)(2,1)}, u32[]{:S(2)}, u32[]{:S(2)}) collective-permute-start(bf16[8,1,10,32,128]{4,3,2,1,0:T(8,128)(2,1)} %get-tuple-element.26), channel_id=1, source_target_pairs={{8,0},{16,8},{24,16},{9,1},{17,9},{25,17},{10,2},{18,10},{26,18},{... | collective-permute-start | bytes 1966088 | tf_op jit(solution)/shard_map/ppermute | solution.py:183
  44.6 5.4 %collective-permute-start.9 = (bf16[8,1,10,32,128]{4,3,2,1,0:T(8,128)(2,1)}, bf16[8,1,10,32,128]{4,3,2,1,0:T(8,128)(2,1)}, u32[]{:S(2)}, u32[]{:S(2)}) collective-permute-start(bf16[8,1,10,32,128]{4,3,2,1,0:T(8,128)(2,1)} %get-tuple-element.25), channel_id=1, source_target_pairs={{0,8},{8,16},{16,24},{1,9},{9,17},{17,25},{2,10},{10,18},{18,26},{... | collective-permute-start | bytes 1966088 | tf_op jit(solution)/shard_map/ppermute | solution.py:184
  50.0 9.3 %all-to-all-done.1.refs_1_ = bf16[8,2,10,32,128]{4,3,2,1,0:T(8,128)(2,1)} async-done(((bf16[8,2,10,32,128]{4,3,2,1,0:T(8,128)(2,1)}), bf16[8,2,10,32,128]{4,3,2,1,0:T(8,128)(2,1)}, u32[]{:S(2)}, u32[]{:S(2)}) %all-to-all-start.1) | async-done | bytes 1310752 | tf_op jit(solution)/shard_map/all_to_all | solution.py:151
  59.4 11.1 %shard_map.38 = (bf16[2,8,64,128]{3,2,1,0:T(8,128)(2,1)S(1)}, bf16[2,8,64,128]{3,2,1,0:T(8,128)(2,1)S(1)}, bf16[2,8,64,128]{3,2,1,0:T(8,128)(2,1)S(1)}, bf16[2,8,64,128]{3,2,1,0:T(8,128)(2,1)S(1)}) custom-call(bf16[8,2,10,32,128]{4,3,2,1,0:T(8,128)(2,1)S(1)} %all-to-all-done.refs_0_.vol_ref, bf16[8,2,10,32,128]{4,3,2,1,0:T(8,128)(2,1)} %all-to-all-done.1.refs_1_, ...), custom_call_target="tpu_custom_call" | custom-call | flops 7247757312 | bytes 10000000 | tf_op jit(solution)/shard_map/pallas_call | solution.py:114
  71.2 1.4 %collective-permute-start.6 = (bf16[2,8,64,128]{3,2,1,0:T(8,128)(2,1)S(1)}, bf16[2,8,64,128]{3,2,1,0:T(8,128)(2,1)S(1)}, u32[]{:S(2)}, u32[]{:S(2)}) collective-permute-start(bf16[2,8,64,128]{3,2,1,0:T(8,128)(2,1)S(1)} %get-tuple-element.23), channel_id=1, source_target_pairs={{0,4},{1,5},{2,6},{3,7},{4,0},{5,1},{6,2},{7,3},{8,12},{9,13},{10,... | collective-permute-start | bytes 786440 | tf_op jit(solution)/shard_map/ppermute | solution.py:137
  72.6 1.5 %collective-permute-start.5 = (bf16[2,8,64,128]{3,2,1,0:T(8,128)(2,1)S(1)}, bf16[2,8,64,128]{3,2,1,0:T(8,128)(2,1)S(1)}, u32[]{:S(2)}, u32[]{:S(2)}) collective-permute-start(bf16[2,8,64,128]{3,2,1,0:T(8,128)(2,1)S(1)} %get-tuple-element.22), channel_id=1, source_target_pairs={{0,2},{1,3},{2,0},{3,1},{4,6},{5,7},{6,4},{7,5},{8,10},{9,11},{10,... | collective-permute-start | bytes 786440 | tf_op jit(solution)/shard_map/ppermute | solution.py:137
  74.1 11.5 %shard_map.40 = (bf16[2,8,64,128]{3,2,1,0:T(8,128)(2,1)S(1)}, bf16[2,8,64,128]{3,2,1,0:T(8,128)(2,1)S(1)}, bf16[2,8,64,128]{3,2,1,0:T(8,128)(2,1)S(1)}, bf16[2,8,64,128]{3,2,1,0:T(8,128)(2,1)S(1)}) custom-call(bf16[8,2,10,32,128]{4,3,2,1,0:T(8,128)(2,1)S(1)} %all-to-all-done.refs_0_.vol_ref, bf16[8,2,10,32,128]{4,3,2,1,0:T(8,128)(2,1)} %all-to-all-done.1.refs_1_, ...), custom_call_target="tpu_custom_call" | custom-call | flops 7247757312 | bytes 10000000 | tf_op jit(solution)/shard_map/pallas_call | solution.py:114
  86.3 1.4 %collective-permute-start.12 = (bf16[2,8,64,128]{3,2,1,0:T(8,128)(2,1)S(1)}, bf16[2,8,64,128]{3,2,1,0:T(8,128)(2,1)S(1)}, u32[]{:S(2)}, u32[]{:S(2)}) collective-permute-start(bf16[2,8,64,128]{3,2,1,0:T(8,128)(2,1)S(1)} %get-tuple-element.29), channel_id=1, source_target_pairs={{0,4},{1,5},{2,6},{3,7},{4,0},{5,1},{6,2},{7,3},{8,12},{9,13},{10,... | collective-permute-start | bytes 786440 | tf_op jit(solution)/shard_map/ppermute | solution.py:137
  87.7 1.6 %collective-permute-start.11 = (bf16[2,8,64,128]{3,2,1,0:T(8,128)(2,1)S(1)}, bf16[2,8,64,128]{3,2,1,0:T(8,128)(2,1)S(1)}, u32[]{:S(2)}, u32[]{:S(2)}) collective-permute-start(bf16[2,8,64,128]{3,2,1,0:T(8,128)(2,1)S(1)} %get-tuple-element.28), channel_id=1, source_target_pairs={{0,2},{1,3},{2,0},{3,1},{4,6},{5,7},{6,4},{7,5},{8,10},{9,11},{10,... | collective-permute-start | bytes 786440 | tf_op jit(solution)/shard_map/ppermute | solution.py:137
  89.6 6.1 %collective-permute-done.13 = bf16[2,8,64,128]{3,2,1,0:T(8,128)(2,1)S(1)} collective-permute-done((bf16[2,8,64,128]{3,2,1,0:T(8,128)(2,1)S(1)}, bf16[2,8,64,128]{3,2,1,0:T(8,128)(2,1)S(1)}, u32[]{:S(2)}, u32[]{:S(2)}) %collective-permute-start.13) | collective-permute-done | bytes 262176 | tf_op jit(solution)/shard_map/ppermute | solution.py:137
  95.7 2.7 %collective-permute-done.12 = bf16[2,8,64,128]{3,2,1,0:T(8,128)(2,1)S(1)} collective-permute-done((bf16[2,8,64,128]{3,2,1,0:T(8,128)(2,1)S(1)}, bf16[2,8,64,128]{3,2,1,0:T(8,128)(2,1)S(1)}, u32[]{:S(2)}, u32[]{:S(2)}) %collective-permute-start.12) | collective-permute-done | bytes 262176 | tf_op jit(solution)/shard_map/ppermute | solution.py:137
  99.4 1.2 %collective-permute-done.14 = bf16[4,2,8,32,128]{4,3,2,1,0:T(8,128)(2,1)S(1)} collective-permute-done((bf16[4,2,8,32,128]{4,3,2,1,0:T(8,128)(2,1)S(1)}, bf16[4,2,8,32,128]{4,3,2,1,0:T(8,128)(2,1)S(1)}, u32[]{:S(2)}, u32[]{:S(2)}) %collective-permute-start.14) | collective-permute-done | bytes 524320 | tf_op jit(solution)/shard_map/ppermute | solution.py:137
  102.0 1.6 %pad_maximum_fusion = bf16[4,32,64,128]{3,2,1,0:T(8,128)(2,1)} fusion(bf16[1,32,64,128]{3,2,1,0:T(8,128)(2,1)S(1)} %get-tuple-element.34, bf16[2,32,64,128]{3,2,1,0:T(8,128)(2,1)S(1)} %bitcast.62, bf16[1,32,64,128]{3,2,1,0:T(8,128)(2,1)S(1)} %get-tuple-element.33), kind=kLoop, calls=%fused_computation.1 | loop fusion | flops 2097152 | bytes 4194304 | tf_op jit(solution)/shard_map/concatenate | solution.py:189
  (68 shorter events, 6.2 us)
Async XLA Ops:
  0.0 13.4 %collective-permute-start = (bf16[3,3,3,32,256]{4,3,2,1,0:T(8,128)(2,1)}, bf16[3,3,3,32,256]{4,3,2,1,0:T(8,128)(2,1)S(1)}, u32[]{:S(2)}, u32[]{:S(2)}) collective-permute-start(bf16[3,3,3,32,256]{4,3,2,1,0:T(8,128)(2,1)} %param.4), channel_id=1, source_target_pairs={{0,2},{1,3},{2,0},{3,1},{4,6},{5,7},{6,4},{7,5},{8,10},{9,11},{10,... | collective-permute-start | bytes 1327112 | tf_op jit(solution)/shard_map/ppermute | solution.py:137
  2.9 12.5 %collective-permute-start.1 = (bf16[3,3,3,32,256]{4,3,2,1,0:T(8,128)(2,1)}, bf16[3,3,3,32,256]{4,3,2,1,0:T(8,128)(2,1)S(1)}, u32[]{:S(2)}, u32[]{:S(2)}) collective-permute-start(bf16[3,3,3,32,256]{4,3,2,1,0:T(8,128)(2,1)} %param.4), channel_id=1, source_target_pairs={{0,4},{1,5},{2,6},{3,7},{4,0},{5,1},{6,2},{7,3},{8,12},{9,13},{10,... | collective-permute-start | bytes 1327112 | tf_op jit(solution)/shard_map/ppermute | solution.py:137
  8.7 1.1 %copy-start = (bf16[8,2,10,32,128]{4,3,2,1,0:T(8,128)(2,1)}, bf16[8,2,10,32,128]{4,3,2,1,0:T(8,128)(2,1)S(1)}, u32[]{:S(2)}) copy-start(bf16[8,2,10,32,128]{4,3,2,1,0:T(8,128)(2,1)S(1)} %get-tuple-element.20) | copy-start | bytes 3932164
  9.8 27.0 %all-to-all-start = ((bf16[8,2,10,32,128]{4,3,2,1,0:T(8,128)(2,1)}), bf16[8,2,10,32,128]{4,3,2,1,0:T(8,128)(2,1)S(1)}, u32[]{:S(2)}, u32[]{:S(2)}) async-start(bf16[8,2,10,32,128]{4,3,2,1,0:T(8,128)(2,1)} %get-tuple-element.19), calls=%async_computation | async-start | bytes 2621440 | tf_op jit(solution)/shard_map/all_to_all | solution.py:150
  13.3 22.1 %copy-start.2 = (bf16[3,3,3,32,256]{4,3,2,1,0:T(8,128)(2,1)S(1)}, bf16[3,3,3,32,256]{4,3,2,1,0:T(8,128)(2,1)}, u32[]{:S(2)}) copy-start(bf16[3,3,3,32,256]{4,3,2,1,0:T(8,128)(2,1)} %param.4) | copy-start | bytes 1327108
  13.4 21.9 %collective-permute-start.2 = (bf16[3,3,3,16,256]{4,3,2,1,0:T(8,128)(2,1)S(1)}, bf16[3,3,3,16,256]{4,3,2,1,0:T(8,128)(2,1)S(1)}, u32[]{:S(2)}, u32[]{:S(2)}) collective-permute-start(bf16[3,3,3,16,256]{4,3,2,1,0:T(8,128)(2,1)S(1)} %slice.114), channel_id=1, source_target_pairs={{0,4},{1,5},{2,6},{3,7},{4,0},{5,1},{6,2},{7,3},{8,12},{9,13},{10,... | collective-permute-start | bytes 663560 | tf_op jit(solution)/shard_map/ppermute | solution.py:137
  15.4 20.0 %copy-start.1 = (bf16[3,3,3,32,256]{4,3,2,1,0:T(8,128)(2,1)}, bf16[3,3,3,32,256]{4,3,2,1,0:T(8,128)(2,1)S(1)}, u32[]{:S(2)}) copy-start(bf16[3,3,3,32,256]{4,3,2,1,0:T(8,128)(2,1)S(1)} %collective-permute-done.1) | copy-start | bytes 1327108
  15.4 19.9 %collective-permute-start.3 = (bf16[3,3,3,16,256]{4,3,2,1,0:T(8,128)(2,1)S(1)}, bf16[3,3,3,16,256]{4,3,2,1,0:T(8,128)(2,1)S(1)}, u32[]{:S(2)}, u32[]{:S(2)}) collective-permute-start(bf16[3,3,3,16,256]{4,3,2,1,0:T(8,128)(2,1)S(1)} %slice.115), channel_id=1, source_target_pairs={{0,2},{1,3},{2,0},{3,1},{4,6},{5,7},{6,4},{7,5},{8,10},{9,11},{10,... | collective-permute-start | bytes 663560 | tf_op jit(solution)/shard_map/ppermute | solution.py:137
  36.7 4.4 %copy-start.3 = (f32[256]{0:T(256)S(1)}, f32[256]{0:T(256)}, u32[]{:S(2)}) copy-start(f32[256]{0:T(256)} %param.5) | copy-start | bytes 3076
  36.7 22.6 %collective-permute-start.4 = (bf16[4,3,3,3,32,256]{5,4,3,2,1,0:T(8,128)(2,1)S(1)}, bf16[4,3,3,3,32,256]{5,4,3,2,1,0:T(8,128)(2,1)}, u32[]{:S(2)}, u32[]{:S(2)}) collective-permute-start(bf16[4,3,3,3,32,256]{5,4,3,2,1,0:T(8,128)(2,1)S(1)} %pad_maximum_fusion.1.refs_2_.refs_4_), channel_id=1, source_target_pairs={{0,1},{1,0},{2,3},{3,2},{4,5},{5,4},{6,7},{7,6},{8,9},{9,8},{10,11... | collective-permute-start | bytes 5308424 | tf_op jit(solution)/shard_map/ppermute | solution.py:137
  36.8 22.5 %all-to-all-start.1 = ((bf16[8,2,10,32,128]{4,3,2,1,0:T(8,128)(2,1)}), bf16[8,2,10,32,128]{4,3,2,1,0:T(8,128)(2,1)}, u32[]{:S(2)}, u32[]{:S(2)}) async-start(bf16[8,2,10,32,128]{4,3,2,1,0:T(8,128)(2,1)} %copy-done), calls=%async_computation.1 | async-start | bytes 2621440 | tf_op jit(solution)/shard_map/all_to_all | solution.py:151
  43.3 30.8 %collective-permute-start.10 = (bf16[8,1,10,32,128]{4,3,2,1,0:T(8,128)(2,1)}, bf16[8,1,10,32,128]{4,3,2,1,0:T(8,128)(2,1)}, u32[]{:S(2)}, u32[]{:S(2)}) collective-permute-start(bf16[8,1,10,32,128]{4,3,2,1,0:T(8,128)(2,1)} %get-tuple-element.26), channel_id=1, source_target_pairs={{8,0},{16,8},{24,16},{9,1},{17,9},{25,17},{10,2},{18,10},{26,18},{... | collective-permute-start | bytes 1966088 | tf_op jit(solution)/shard_map/ppermute | solution.py:183
  44.6 29.5 %collective-permute-start.9 = (bf16[8,1,10,32,128]{4,3,2,1,0:T(8,128)(2,1)}, bf16[8,1,10,32,128]{4,3,2,1,0:T(8,128)(2,1)}, u32[]{:S(2)}, u32[]{:S(2)}) collective-permute-start(bf16[8,1,10,32,128]{4,3,2,1,0:T(8,128)(2,1)} %get-tuple-element.25), channel_id=1, source_target_pairs={{0,8},{8,16},{16,24},{1,9},{9,17},{17,25},{2,10},{10,18},{18,26},{... | collective-permute-start | bytes 1966088 | tf_op jit(solution)/shard_map/ppermute | solution.py:184
  70.5 17.2 %collective-permute-start.7 = (bf16[2,8,64,128]{3,2,1,0:T(8,128)(2,1)S(1)}, bf16[2,8,64,128]{3,2,1,0:T(8,128)(2,1)S(1)}, u32[]{:S(2)}, u32[]{:S(2)}) collective-permute-start(bf16[2,8,64,128]{3,2,1,0:T(8,128)(2,1)S(1)} %get-tuple-element.24), channel_id=1, source_target_pairs={{0,6},{1,7},{2,4},{3,5},{4,2},{5,3},{6,0},{7,1},{8,14},{9,15},{10,... | collective-permute-start | bytes 786440 | tf_op jit(solution)/shard_map/ppermute | solution.py:137
  71.2 18.2 %collective-permute-start.6 = (bf16[2,8,64,128]{3,2,1,0:T(8,128)(2,1)S(1)}, bf16[2,8,64,128]{3,2,1,0:T(8,128)(2,1)S(1)}, u32[]{:S(2)}, u32[]{:S(2)}) collective-permute-start(bf16[2,8,64,128]{3,2,1,0:T(8,128)(2,1)S(1)} %get-tuple-element.23), channel_id=1, source_target_pairs={{0,4},{1,5},{2,6},{3,7},{4,0},{5,1},{6,2},{7,3},{8,12},{9,13},{10,... | collective-permute-start | bytes 786440 | tf_op jit(solution)/shard_map/ppermute | solution.py:137
  72.6 16.8 %collective-permute-start.5 = (bf16[2,8,64,128]{3,2,1,0:T(8,128)(2,1)S(1)}, bf16[2,8,64,128]{3,2,1,0:T(8,128)(2,1)S(1)}, u32[]{:S(2)}, u32[]{:S(2)}) collective-permute-start(bf16[2,8,64,128]{3,2,1,0:T(8,128)(2,1)S(1)} %get-tuple-element.22), channel_id=1, source_target_pairs={{0,2},{1,3},{2,0},{3,1},{4,6},{5,7},{6,4},{7,5},{8,10},{9,11},{10,... | collective-permute-start | bytes 786440 | tf_op jit(solution)/shard_map/ppermute | solution.py:137
  85.7 10.0 %collective-permute-start.13 = (bf16[2,8,64,128]{3,2,1,0:T(8,128)(2,1)S(1)}, bf16[2,8,64,128]{3,2,1,0:T(8,128)(2,1)S(1)}, u32[]{:S(2)}, u32[]{:S(2)}) collective-permute-start(bf16[2,8,64,128]{3,2,1,0:T(8,128)(2,1)S(1)} %get-tuple-element.30), channel_id=1, source_target_pairs={{0,6},{1,7},{2,4},{3,5},{4,2},{5,3},{6,0},{7,1},{8,14},{9,15},{10,... | collective-permute-start | bytes 786440 | tf_op jit(solution)/shard_map/ppermute | solution.py:137
  86.3 12.1 %collective-permute-start.12 = (bf16[2,8,64,128]{3,2,1,0:T(8,128)(2,1)S(1)}, bf16[2,8,64,128]{3,2,1,0:T(8,128)(2,1)S(1)}, u32[]{:S(2)}, u32[]{:S(2)}) collective-permute-start(bf16[2,8,64,128]{3,2,1,0:T(8,128)(2,1)S(1)} %get-tuple-element.29), channel_id=1, source_target_pairs={{0,4},{1,5},{2,6},{3,7},{4,0},{5,1},{6,2},{7,3},{8,12},{9,13},{10,... | collective-permute-start | bytes 786440 | tf_op jit(solution)/shard_map/ppermute | solution.py:137
  87.7 10.7 %collective-permute-start.11 = (bf16[2,8,64,128]{3,2,1,0:T(8,128)(2,1)S(1)}, bf16[2,8,64,128]{3,2,1,0:T(8,128)(2,1)S(1)}, u32[]{:S(2)}, u32[]{:S(2)}) collective-permute-start(bf16[2,8,64,128]{3,2,1,0:T(8,128)(2,1)S(1)} %get-tuple-element.28), channel_id=1, source_target_pairs={{0,2},{1,3},{2,0},{3,1},{4,6},{5,7},{6,4},{7,5},{8,10},{9,11},{10,... | collective-permute-start | bytes 786440 | tf_op jit(solution)/shard_map/ppermute | solution.py:137
  89.5 9.9 %collective-permute-start.8 = (bf16[4,2,8,32,128]{4,3,2,1,0:T(8,128)(2,1)S(1)}, bf16[4,2,8,32,128]{4,3,2,1,0:T(8,128)(2,1)S(1)}, u32[]{:S(2)}, u32[]{:S(2)}) collective-permute-start(bf16[4,2,8,32,128]{4,3,2,1,0:T(8,128)(2,1)S(1)} %pad_maximum_fusion.2), channel_id=1, source_target_pairs={{0,1},{1,0},{2,3},{3,2},{4,5},{5,4},{6,7},{7,6},{8,9},{9,8},{10,11... | collective-permute-start | bytes 1572872 | tf_op jit(solution)/shard_map/ppermute | solution.py:137
  98.6 2.0 %collective-permute-start.14 = (bf16[4,2,8,32,128]{4,3,2,1,0:T(8,128)(2,1)S(1)}, bf16[4,2,8,32,128]{4,3,2,1,0:T(8,128)(2,1)S(1)}, u32[]{:S(2)}, u32[]{:S(2)}) collective-permute-start(bf16[4,2,8,32,128]{4,3,2,1,0:T(8,128)(2,1)S(1)} %pad_maximum_fusion.3), channel_id=1, source_target_pairs={{0,1},{1,0},{2,3},{3,2},{4,5},{5,4},{6,7},{7,6},{8,9},{9,8},{10,11... | collective-permute-start | bytes 1572872 | tf_op jit(solution)/shard_map/ppermute | solution.py:137

commit v12 on v10

--- a/solution.py
+++ b/solution.py
@@ -8,7 +8,7 @@
 from jax.sharding import PartitionSpec as P
 
 slope = 0.3
-ROWS = 4
+ROWS = 2
 
 
 def cut_kernel(parts, vol_ref, outer, inner):
@@ -132,7 +132,7 @@
         in_specs=[in_vmem] * (len(sums) + len(pieces) + len(tap_parts) + 1),
         out_specs=[in_vmem] * len(shapes),
         cost_estimate=pl.CostEstimate(flops=2 * macs, bytes_accessed=10_000_000, transcendentals=0),
-        compiler_params=pltpu.CompilerParams(vmem_limit_bytes=20 * 2**20),
+        compiler_params=pltpu.CompilerParams(vmem_limit_bytes=12 * 2**20),
     )(*sums, *pieces, *tap_parts, wide_bias)
 
 
@@ -151,17 +151,12 @@
             return array
         return lax.ppermute(array, axis, [(i, i ^ k) for i in range(lax.axis_size(axis))])
 
-    if len(across) == 4:
-        half = out_chan // 2
-        by_x, by_y = swap(kernel, across[1]), swap(kernel, across[2])
-        far = [swap(by_x[:, :, :, :half], across[2]), swap(by_y[:, :, :, half:], across[1])]
-        fetched = [kernel, by_x, by_y, jnp.concatenate(far, axis=3)]
-    else:
-        fetched = [swap(kernel, k) for k in across]
+
+    outer_rows, inner_rows = cut(features.transpose(0, 2, 1, 3), parts)
+    fetched = [swap(kernel, k) for k in across]
+    fetched = lax.optimization_barrier((fetched, outer_rows))[0]
     same = jnp.stack(fetched)
     tap_parts = [same, swap(same, 1)]
-
-    outer_rows, inner_rows = cut(features.transpose(0, 2, 1, 3), parts)
     outer = lax.all_to_all(outer_rows, "filt", 0, 0)
     inner = lax.all_to_all(inner_rows, "filt", 0, 0)
     arrived = outer

time: 110 us -> 106 us (0.964)
  starting transfers between devices: 30.2 us -> 26.1 us
  waiting for transfers between devices: 36.3 us -> 33.1 us
  Pallas kernels: 27.8 us -> 30.6 us
    all_to_all x1, waiting for transfers between devices: 16 us -> 10.5 us  [body(): outer = lax.all_to_all(outer_rows, 'filt', 0, 0)]
    ppermute x13 -> x12, starting transfers between devices: 15.6 us -> 11.8 us  [swap(): lax.ppermute(array, axis, [(i, i ^ k) for i in range(lax.axis_size(axis))])]
    pallas_call x3, Pallas kernels: 25.3 us -> 28.1 us  [convolve(): pl.pallas_call(functools.partial(conv_kernel, plan, min(ROWS, rows), len(...]
    ppermute x13 -> x12, waiting for transfers between devices: 20.2 us -> 22.6 us  [swap(): lax.ppermute(array, axis, [(i, i ^ k) for i in range(lax.axis_size(axis))])]
    unnamed x15 -> x21, local copies, waits for them, and re-layouts: 8.33 us -> 9.07 us
  transfers between devices with their start and end apart: 17 -> 16, of which waited for: 6 -> 7; matrix products, arithmetic and copies ran while one was open for 6% -> 6% of each run, Pallas kernels for 25% -> 29%
where the time goes in v12:
time: 106 us
  waiting for transfers between devices  33.1 us (31%)
  Pallas kernels  30.6 us (29%)
  starting transfers between devices  26.1 us (25%)
  local copies, waits for them, and re-layouts  12.2 us (12%)
  other arithmetic  3.31 us (3%)
    pallas_call x3, Pallas kernels, convolve(): pl.pallas_call(functools.partial(conv_kernel, plan, min(ROWS, rows), len(...  28.1 us
    ppermute x12, waiting for transfers between devices, swap(): lax.ppermute(array, axis, [(i, i ^ k) for i in range(lax.axis_size(axis))])  22.6 us
    ppermute x12, starting transfers between devices, swap(): lax.ppermute(array, axis, [(i, i ^ k) for i in range(lax.axis_size(axis))])  11.8 us
    all_to_all x1, waiting for transfers between devices, body(): outer = lax.all_to_all(outer_rows, 'filt', 0, 0)  10.5 us
    unnamed x21, local copies, waits for them, and re-layouts  9.07 us
    ppermute x1, starting transfers between devices, body(): before = lax.ppermute(last, 'slab', up)  4.33 us
    all_to_all x1, starting transfers between devices, body(): outer = lax.all_to_all(outer_rows, 'filt', 0, 0)  4.33 us
    all_to_all x1, starting transfers between devices, body(): inner = lax.all_to_all(inner_rows, 'filt', 0, 0)  4.28 us
  transfers between devices with their start and end apart: 16, of which 7 were waited for; matrix products, arithmetic and copies ran while one was open for 6% of the time, Pallas kernels for 29%

profile of v12, /device:TPU:0, one launch (start us, length us, event | category | flops | bytes accessed | tf_op | source)
XLA Modules:
  0.0 105.7 jit_solution(5085729453208826725)
XLA Ops:
  0.0 2.9 %collective-permute-start = (bf16[3,3,3,32,256]{4,3,2,1,0:T(8,128)(2,1)}, bf16[3,3,3,32,256]{4,3,2,1,0:T(8,128)(2,1)S(1)}, u32[]{:S(2)}, u32[]{:S(2)}) collective-permute-start(bf16[3,3,3,32,256]{4,3,2,1,0:T(8,128)(2,1)} %param.4), channel_id=1, source_target_pairs={{0,2},{1,3},{2,0},{3,1},{4,6},{5,7},{6,4},{7,5},{8,10},{9,11},{10,... | collective-permute-start | bytes 1327112 | tf_op jit(solution)/shard_map/ppermute | solution.py:152
  2.9 1.5 %collective-permute-start.1 = (bf16[3,3,3,32,256]{4,3,2,1,0:T(8,128)(2,1)}, bf16[3,3,3,32,256]{4,3,2,1,0:T(8,128)(2,1)S(1)}, u32[]{:S(2)}, u32[]{:S(2)}) collective-permute-start(bf16[3,3,3,32,256]{4,3,2,1,0:T(8,128)(2,1)} %param.4), channel_id=1, source_target_pairs={{0,4},{1,5},{2,6},{3,7},{4,0},{5,1},{6,2},{7,3},{8,12},{9,13},{10,... | collective-permute-start | bytes 1327112 | tf_op jit(solution)/shard_map/ppermute | solution.py:152
  4.5 2.9 %copy.38 = bf16[4,32,64,128]{3,1,2,0:T(8,128)(2,1)S(1)} copy(bf16[4,32,64,128]{3,2,1,0:T(8,128)(2,1)} %param.3) | data formatting | bytes 4194304 | tf_op args[0]
  7.4 1.3 %shard_map.37 = (bf16[8,2,10,32,128]{4,3,2,1,0:T(8,128)(2,1)}, bf16[8,2,10,32,128]{4,3,2,1,0:T(8,128)(2,1)S(1)}) custom-call(bf16[4,64,32,128]{3,2,1,0:T(8,128)(2,1)S(1)} %bitcast.59), custom_call_target="tpu_custom_call" | custom-call | tf_op jit(solution)/shard_map/pallas_call | solution.py:32
  9.8 4.3 %all-to-all-start = ((bf16[8,2,10,32,128]{4,3,2,1,0:T(8,128)(2,1)}), bf16[8,2,10,32,128]{4,3,2,1,0:T(8,128)(2,1)S(1)}, u32[]{:S(2)}, u32[]{:S(2)}) async-start(bf16[8,2,10,32,128]{4,3,2,1,0:T(8,128)(2,1)} %get-tuple-element.25), calls=%async_computation | async-start | bytes 2621440 | tf_op jit(solution)/shard_map/all_to_all | solution.py:160
  14.1 10.7 %collective-permute-done.1 = bf16[3,3,3,32,256]{4,3,2,1,0:T(8,128)(2,1)S(1)} collective-permute-done((bf16[3,3,3,32,256]{4,3,2,1,0:T(8,128)(2,1)}, bf16[3,3,3,32,256]{4,3,2,1,0:T(8,128)(2,1)S(1)}, u32[]{:S(2)}, u32[]{:S(2)}) %collective-permute-start.1) | collective-permute-done | bytes 442400 | tf_op jit(solution)/shard_map/ppermute | solution.py:152
  26.0 1.5 %pad_maximum_fusion.1.refs_1_.refs_2_.refs_4_ = bf16[4,3,3,3,32,256]{5,4,3,2,1,0:T(8,128)(2,1)S(1)} fusion(bf16[1,3,3,3,32,256]{5,4,3,2,1,0:T(8,128)(2,1)} %bitcast.65, bf16[1,3,3,3,32,256]{5,4,3,2,1,0:T(8,128)(2,1)} %bitcast.64, bf16[1,3,3,3,32,256]{5,4,3,2,1,0:T(8,128)(2,1)} %bitcast.63, bf16[1,3,3,3,32,256]{5,4,3,2,1,0:T(8,128)(2,1)S(1)} %bitcast.62), kind=kLoop, calls=%fused_computation.3 | loop fusion | flops 2654208 | bytes 3538944 | tf_op jit(solution)/shard_map/stack | solution.py:158
  27.8 10.5 %all-to-all-done.refs_0_.vol_ref = bf16[8,2,10,32,128]{4,3,2,1,0:T(8,128)(2,1)S(1)} async-done(((bf16[8,2,10,32,128]{4,3,2,1,0:T(8,128)(2,1)}), bf16[8,2,10,32,128]{4,3,2,1,0:T(8,128)(2,1)S(1)}, u32[]{:S(2)}, u32[]{:S(2)}) %all-to-all-start) | async-done | bytes 1310752 | tf_op jit(solution)/shard_map/all_to_all | solution.py:160
  38.3 4.3 %all-to-all-start.1 = ((bf16[8,2,10,32,128]{4,3,2,1,0:T(8,128)(2,1)}), bf16[8,2,10,32,128]{4,3,2,1,0:T(8,128)(2,1)}, u32[]{:S(2)}, u32[]{:S(2)}) async-start(bf16[8,2,10,32,128]{4,3,2,1,0:T(8,128)(2,1)} %copy-done), calls=%async_computation.1 | async-start | bytes 2621440 | tf_op jit(solution)/shard_map/all_to_all | solution.py:161
  43.4 1.2 %shard_map.40 = (bf16[8,1,10,32,128]{4,3,2,1,0:T(8,128)(2,1)}, bf16[8,1,10,32,128]{4,3,2,1,0:T(8,128)(2,1)}) custom-call(bf16[8,2,10,32,128]{4,3,2,1,0:T(8,128)(2,1)S(1)} %all-to-all-done.refs_0_.vol_ref), custom_call_target="tpu_custom_call" | custom-call | tf_op jit(solution)/shard_map/pallas_call | solution.py:54
  44.7 4.3 %collective-permute-start.8 = (bf16[8,1,10,32,128]{4,3,2,1,0:T(8,128)(2,1)}, bf16[8,1,10,32,128]{4,3,2,1,0:T(8,128)(2,1)}, u32[]{:S(2)}, u32[]{:S(2)}) collective-permute-start(bf16[8,1,10,32,128]{4,3,2,1,0:T(8,128)(2,1)} %get-tuple-element.37), channel_id=1, source_target_pairs={{0,8},{8,16},{16,24},{1,9},{9,17},{17,25},{2,10},{10,18},{18,26},{... | collective-permute-start | bytes 1966088 | tf_op jit(solution)/shard_map/ppermute | solution.py:196
  49.0 1.3 %collective-permute-start.9 = (bf16[8,1,10,32,128]{4,3,2,1,0:T(8,128)(2,1)}, bf16[8,1,10,32,128]{4,3,2,1,0:T(8,128)(2,1)}, u32[]{:S(2)}, u32[]{:S(2)}) collective-permute-start(bf16[8,1,10,32,128]{4,3,2,1,0:T(8,128)(2,1)} %get-tuple-element.38), channel_id=1, source_target_pairs={{8,0},{16,8},{24,16},{9,1},{17,9},{25,17},{10,2},{18,10},{26,18},{... | collective-permute-start | bytes 1966088 | tf_op jit(solution)/shard_map/ppermute | solution.py:195
  50.4 10.2 %shard_map.38 = (f32[2,8,256,128]{3,2,1,0:T(8,128)S(1)}, f32[2,8,256,128]{3,2,1,0:T(8,128)S(1)}) custom-call(bf16[8,2,10,32,128]{4,3,2,1,0:T(8,128)(2,1)S(1)} %all-to-all-done.refs_0_.vol_ref, bf16[4,3,3,3,32,256]{5,4,3,2,1,0:T(8,128)(2,1)S(1)} %pad_maximum_fusion.1.refs_1_.refs_2_.refs_4_, ...), custom_call_target="tpu_custom_call" | custom-call | flops 4831838208 | bytes 10000000 | tf_op jit(solution)/shard_map/pallas_call | solution.py:127
  60.6 1.3 %copy-done.1 = f32[2,8,256,128]{3,2,1,0:T(8,128)} copy-done((f32[2,8,256,128]{3,2,1,0:T(8,128)}, f32[2,8,256,128]{3,2,1,0:T(8,128)S(1)}, u32[]{:S(2)}) %copy-start.1) | copy-done | bytes 2097176
  61.9 1.4 %copy-done.3 = f32[2,8,256,128]{3,2,1,0:T(8,128)} copy-done((f32[2,8,256,128]{3,2,1,0:T(8,128)}, f32[2,8,256,128]{3,2,1,0:T(8,128)S(1)}, u32[]{:S(2)}) %copy-start.3) | copy-done | bytes 2097176
  63.3 1.6 %copy-done.4 = f32[2,8,256,128]{3,2,1,0:T(8,128)S(1)} copy-done((f32[2,8,256,128]{3,2,1,0:T(8,128)S(1)}, f32[2,8,256,128]{3,2,1,0:T(8,128)}, u32[]{:S(2)}) %copy-start.4) | copy-done | bytes 2097176
  64.9 8.8 %shard_map.39 = (bf16[2,8,64,128]{3,2,1,0:T(8,128)(2,1)S(1)}, bf16[2,8,64,128]{3,2,1,0:T(8,128)(2,1)S(1)}, bf16[2,8,64,128]{3,2,1,0:T(8,128)(2,1)S(1)}, bf16[2,8,64,128]{3,2,1,0:T(8,128)(2,1)S(1)}) custom-call(f32[2,8,256,128]{3,2,1,0:T(8,128)S(1)} %copy-done.4, bf16[8,2,10,32,128]{4,3,2,1,0:T(8,128)(2,1)} %all-to-all-done.1.refs_1_, ...), custom_call_target="tpu_custom_call" | custom-call | flops 4831838208 | bytes 10000000 | tf_op jit(solution)/shard_map/pallas_call | solution.py:127
  73.7 2.9 %collective-permute-start.6 = (bf16[2,8,64,128]{3,2,1,0:T(8,128)(2,1)S(1)}, bf16[2,8,64,128]{3,2,1,0:T(8,128)(2,1)S(1)}, u32[]{:S(2)}, u32[]{:S(2)}) collective-permute-start(bf16[2,8,64,128]{3,2,1,0:T(8,128)(2,1)S(1)} %get-tuple-element.35), channel_id=1, source_target_pairs={{0,6},{1,7},{2,4},{3,5},{4,2},{5,3},{6,0},{7,1},{8,14},{9,15},{10,... | collective-permute-start | bytes 786440 | tf_op jit(solution)/shard_map/ppermute | solution.py:152
  77.3 9.1 %shard_map.41 = (bf16[2,8,64,128]{3,2,1,0:T(8,128)(2,1)S(1)}, bf16[2,8,64,128]{3,2,1,0:T(8,128)(2,1)S(1)}, bf16[2,8,64,128]{3,2,1,0:T(8,128)(2,1)S(1)}, bf16[2,8,64,128]{3,2,1,0:T(8,128)(2,1)S(1)}) custom-call(f32[2,8,256,128]{3,2,1,0:T(8,128)S(1)} %copy-done.2, bf16[8,2,10,32,128]{4,3,2,1,0:T(8,128)(2,1)} %all-to-all-done.1.refs_1_, ...), custom_call_target="tpu_custom_call" | custom-call | flops 4831838208 | bytes 10000000 | tf_op jit(solution)/shard_map/pallas_call | solution.py:127
  86.4 2.9 %collective-permute-start.12 = (bf16[2,8,64,128]{3,2,1,0:T(8,128)(2,1)S(1)}, bf16[2,8,64,128]{3,2,1,0:T(8,128)(2,1)S(1)}, u32[]{:S(2)}, u32[]{:S(2)}) collective-permute-start(bf16[2,8,64,128]{3,2,1,0:T(8,128)(2,1)S(1)} %get-tuple-element.42), channel_id=1, source_target_pairs={{0,6},{1,7},{2,4},{3,5},{4,2},{5,3},{6,0},{7,1},{8,14},{9,15},{10,... | collective-permute-start | bytes 786440 | tf_op jit(solution)/shard_map/ppermute | solution.py:152
  90.3 6.3 %collective-permute-done.12 = bf16[2,8,64,128]{3,2,1,0:T(8,128)(2,1)S(1)} collective-permute-done((bf16[2,8,64,128]{3,2,1,0:T(8,128)(2,1)S(1)}, bf16[2,8,64,128]{3,2,1,0:T(8,128)(2,1)S(1)}, u32[]{:S(2)}, u32[]{:S(2)}) %collective-permute-start.12) | collective-permute-done | bytes 262176 | tf_op jit(solution)/shard_map/ppermute | solution.py:152
  96.7 3.8 %collective-permute-done.11 = bf16[2,8,64,128]{3,2,1,0:T(8,128)(2,1)S(1)} collective-permute-done((bf16[2,8,64,128]{3,2,1,0:T(8,128)(2,1)S(1)}, bf16[2,8,64,128]{3,2,1,0:T(8,128)(2,1)S(1)}, u32[]{:S(2)}, u32[]{:S(2)}) %collective-permute-start.11) | collective-permute-done | bytes 262176 | tf_op jit(solution)/shard_map/ppermute | solution.py:152
  101.6 1.2 %collective-permute-done.13 = bf16[4,2,8,32,128]{4,3,2,1,0:T(8,128)(2,1)S(1)} collective-permute-done((bf16[4,2,8,32,128]{4,3,2,1,0:T(8,128)(2,1)S(1)}, bf16[4,2,8,32,128]{4,3,2,1,0:T(8,128)(2,1)S(1)}, u32[]{:S(2)}, u32[]{:S(2)}) %collective-permute-start.13) | collective-permute-done | bytes 524320 | tf_op jit(solution)/shard_map/ppermute | solution.py:152
  104.2 1.6 %pad_maximum_fusion = bf16[4,32,64,128]{3,2,1,0:T(8,128)(2,1)} fusion(bf16[1,32,64,128]{3,2,1,0:T(8,128)(2,1)S(1)} %get-tuple-element.46, bf16[2,32,64,128]{3,2,1,0:T(8,128)(2,1)S(1)} %bitcast.61, bf16[1,32,64,128]{3,2,1,0:T(8,128)(2,1)S(1)} %get-tuple-element.45), kind=kLoop, calls=%fused_computation.1 | loop fusion | flops 2097152 | bytes 4194304 | tf_op jit(solution)/shard_map/concatenate | solution.py:202
  (76 shorter events, 7.5 us)
Async XLA Ops:
  0.0 14.1 %collective-permute-start = (bf16[3,3,3,32,256]{4,3,2,1,0:T(8,128)(2,1)}, bf16[3,3,3,32,256]{4,3,2,1,0:T(8,128)(2,1)S(1)}, u32[]{:S(2)}, u32[]{:S(2)}) collective-permute-start(bf16[3,3,3,32,256]{4,3,2,1,0:T(8,128)(2,1)} %param.4), channel_id=1, source_target_pairs={{0,2},{1,3},{2,0},{3,1},{4,6},{5,7},{6,4},{7,5},{8,10},{9,11},{10,... | collective-permute-start | bytes 1327112 | tf_op jit(solution)/shard_map/ppermute | solution.py:152
  2.9 21.9 %collective-permute-start.1 = (bf16[3,3,3,32,256]{4,3,2,1,0:T(8,128)(2,1)}, bf16[3,3,3,32,256]{4,3,2,1,0:T(8,128)(2,1)S(1)}, u32[]{:S(2)}, u32[]{:S(2)}) collective-permute-start(bf16[3,3,3,32,256]{4,3,2,1,0:T(8,128)(2,1)} %param.4), channel_id=1, source_target_pairs={{0,4},{1,5},{2,6},{3,7},{4,0},{5,1},{6,2},{7,3},{8,12},{9,13},{10,... | collective-permute-start | bytes 1327112 | tf_op jit(solution)/shard_map/ppermute | solution.py:152
  4.5 20.7 %collective-permute-start.2 = (bf16[3,3,3,32,256]{4,3,2,1,0:T(8,128)(2,1)}, bf16[3,3,3,32,256]{4,3,2,1,0:T(8,128)(2,1)S(1)}, u32[]{:S(2)}, u32[]{:S(2)}) collective-permute-start(bf16[3,3,3,32,256]{4,3,2,1,0:T(8,128)(2,1)} %param.4), channel_id=1, source_target_pairs={{0,6},{1,7},{2,4},{3,5},{4,2},{5,3},{6,0},{7,1},{8,14},{9,15},{10,... | collective-permute-start | bytes 1327112 | tf_op jit(solution)/shard_map/ppermute | solution.py:152
  8.7 1.1 %copy-start = (bf16[8,2,10,32,128]{4,3,2,1,0:T(8,128)(2,1)}, bf16[8,2,10,32,128]{4,3,2,1,0:T(8,128)(2,1)S(1)}, u32[]{:S(2)}) copy-start(bf16[8,2,10,32,128]{4,3,2,1,0:T(8,128)(2,1)S(1)} %get-tuple-element.31) | copy-start | bytes 3932164
  9.8 16.2 %copy-start.5 = (bf16[3,3,3,32,256]{4,3,2,1,0:T(8,128)(2,1)S(1)}, bf16[3,3,3,32,256]{4,3,2,1,0:T(8,128)(2,1)}, u32[]{:S(2)}) copy-start(bf16[3,3,3,32,256]{4,3,2,1,0:T(8,128)(2,1)} %param.4) | copy-start | bytes 1327108
  9.8 28.5 %all-to-all-start = ((bf16[8,2,10,32,128]{4,3,2,1,0:T(8,128)(2,1)}), bf16[8,2,10,32,128]{4,3,2,1,0:T(8,128)(2,1)S(1)}, u32[]{:S(2)}, u32[]{:S(2)}) async-start(bf16[8,2,10,32,128]{4,3,2,1,0:T(8,128)(2,1)} %get-tuple-element.25), calls=%async_computation | async-start | bytes 2621440 | tf_op jit(solution)/shard_map/all_to_all | solution.py:160
  14.1 11.1 %copy-start.6 = (bf16[3,3,3,32,256]{4,3,2,1,0:T(8,128)(2,1)}, bf16[3,3,3,32,256]{4,3,2,1,0:T(8,128)(2,1)S(1)}, u32[]{:S(2)}) copy-start(bf16[3,3,3,32,256]{4,3,2,1,0:T(8,128)(2,1)S(1)} %collective-permute-done) | copy-start | bytes 1327108
  26.0 1.6 %copy-start.9 = (f32[256]{0:T(256)S(1)}, f32[256]{0:T(256)}, u32[]{:S(2)}) copy-start(f32[256]{0:T(256)} %param.5) | copy-start | bytes 3076
  27.5 22.8 %collective-permute-start.3 = (bf16[4,3,3,3,32,256]{5,4,3,2,1,0:T(8,128)(2,1)S(1)}, bf16[4,3,3,3,32,256]{5,4,3,2,1,0:T(8,128)(2,1)}, u32[]{:S(2)}, u32[]{:S(2)}) collective-permute-start(bf16[4,3,3,3,32,256]{5,4,3,2,1,0:T(8,128)(2,1)S(1)} %pad_maximum_fusion.1.refs_1_.refs_2_.refs_4_), channel_id=1, source_target_pairs={{0,1},{1,0},{2,3},{3,2},{4,5},{5,4},{6,7},{7,6},{8,9},{9,8},{10,11... | collective-permute-start | bytes 5308424 | tf_op jit(solution)/shard_map/ppermute | solution.py:152
  38.3 25.0 %all-to-all-start.1 = ((bf16[8,2,10,32,128]{4,3,2,1,0:T(8,128)(2,1)}), bf16[8,2,10,32,128]{4,3,2,1,0:T(8,128)(2,1)}, u32[]{:S(2)}, u32[]{:S(2)}) async-start(bf16[8,2,10,32,128]{4,3,2,1,0:T(8,128)(2,1)} %copy-done), calls=%async_computation.1 | async-start | bytes 2621440 | tf_op jit(solution)/shard_map/all_to_all | solution.py:161
  44.7 32.6 %collective-permute-start.8 = (bf16[8,1,10,32,128]{4,3,2,1,0:T(8,128)(2,1)}, bf16[8,1,10,32,128]{4,3,2,1,0:T(8,128)(2,1)}, u32[]{:S(2)}, u32[]{:S(2)}) collective-permute-start(bf16[8,1,10,32,128]{4,3,2,1,0:T(8,128)(2,1)} %get-tuple-element.37), channel_id=1, source_target_pairs={{0,8},{8,16},{16,24},{1,9},{9,17},{17,25},{2,10},{10,18},{18,26},{... | collective-permute-start | bytes 1966088 | tf_op jit(solution)/shard_map/ppermute | solution.py:196
  49.0 28.3 %collective-permute-start.9 = (bf16[8,1,10,32,128]{4,3,2,1,0:T(8,128)(2,1)}, bf16[8,1,10,32,128]{4,3,2,1,0:T(8,128)(2,1)}, u32[]{:S(2)}, u32[]{:S(2)}) collective-permute-start(bf16[8,1,10,32,128]{4,3,2,1,0:T(8,128)(2,1)} %get-tuple-element.38), channel_id=1, source_target_pairs={{8,0},{16,8},{24,16},{9,1},{17,9},{25,17},{10,2},{18,10},{26,18},{... | collective-permute-start | bytes 1966088 | tf_op jit(solution)/shard_map/ppermute | solution.py:195
  60.6 1.3 %copy-start.1 = (f32[2,8,256,128]{3,2,1,0:T(8,128)}, f32[2,8,256,128]{3,2,1,0:T(8,128)S(1)}, u32[]{:S(2)}) copy-start(f32[2,8,256,128]{3,2,1,0:T(8,128)S(1)} %get-tuple-element.36.refs_0_) | copy-start | bytes 6291460
  61.9 1.4 %copy-start.3 = (f32[2,8,256,128]{3,2,1,0:T(8,128)}, f32[2,8,256,128]{3,2,1,0:T(8,128)S(1)}, u32[]{:S(2)}) copy-start(f32[2,8,256,128]{3,2,1,0:T(8,128)S(1)} %get-tuple-element.30.refs_0_) | copy-start | bytes 6291460
  63.3 1.6 %copy-start.4 = (f32[2,8,256,128]{3,2,1,0:T(8,128)S(1)}, f32[2,8,256,128]{3,2,1,0:T(8,128)}, u32[]{:S(2)}) copy-start(f32[2,8,256,128]{3,2,1,0:T(8,128)} %copy-done.3) | copy-start | bytes 6291460
  64.9 12.4 %copy-start.2 = (f32[2,8,256,128]{3,2,1,0:T(8,128)S(1)}, f32[2,8,256,128]{3,2,1,0:T(8,128)}, u32[]{:S(2)}) copy-start(f32[2,8,256,128]{3,2,1,0:T(8,128)} %copy-done.1) | copy-start | bytes 6291460
  73.7 16.1 %collective-permute-start.6 = (bf16[2,8,64,128]{3,2,1,0:T(8,128)(2,1)S(1)}, bf16[2,8,64,128]{3,2,1,0:T(8,128)(2,1)S(1)}, u32[]{:S(2)}, u32[]{:S(2)}) collective-permute-start(bf16[2,8,64,128]{3,2,1,0:T(8,128)(2,1)S(1)} %get-tuple-element.35), channel_id=1, source_target_pairs={{0,6},{1,7},{2,4},{3,5},{4,2},{5,3},{6,0},{7,1},{8,14},{9,15},{10,... | collective-permute-start | bytes 786440 | tf_op jit(solution)/shard_map/ppermute | solution.py:152
  76.6 13.5 %collective-permute-start.5 = (bf16[2,8,64,128]{3,2,1,0:T(8,128)(2,1)S(1)}, bf16[2,8,64,128]{3,2,1,0:T(8,128)(2,1)S(1)}, u32[]{:S(2)}, u32[]{:S(2)}) collective-permute-start(bf16[2,8,64,128]{3,2,1,0:T(8,128)(2,1)S(1)} %get-tuple-element.34), channel_id=1, source_target_pairs={{0,4},{1,5},{2,6},{3,7},{4,0},{5,1},{6,2},{7,3},{8,12},{9,13},{10,... | collective-permute-start | bytes 786440 | tf_op jit(solution)/shard_map/ppermute | solution.py:152
  77.1 13.0 %collective-permute-start.4 = (bf16[2,8,64,128]{3,2,1,0:T(8,128)(2,1)S(1)}, bf16[2,8,64,128]{3,2,1,0:T(8,128)(2,1)S(1)}, u32[]{:S(2)}, u32[]{:S(2)}) collective-permute-start(bf16[2,8,64,128]{3,2,1,0:T(8,128)(2,1)S(1)} %get-tuple-element.33), channel_id=1, source_target_pairs={{0,2},{1,3},{2,0},{3,1},{4,6},{5,7},{6,4},{7,5},{8,10},{9,11},{10,... | collective-permute-start | bytes 786440 | tf_op jit(solution)/shard_map/ppermute | solution.py:152
  86.4 10.3 %collective-permute-start.12 = (bf16[2,8,64,128]{3,2,1,0:T(8,128)(2,1)S(1)}, bf16[2,8,64,128]{3,2,1,0:T(8,128)(2,1)S(1)}, u32[]{:S(2)}, u32[]{:S(2)}) collective-permute-start(bf16[2,8,64,128]{3,2,1,0:T(8,128)(2,1)S(1)} %get-tuple-element.42), channel_id=1, source_target_pairs={{0,6},{1,7},{2,4},{3,5},{4,2},{5,3},{6,0},{7,1},{8,14},{9,15},{10,... | collective-permute-start | bytes 786440 | tf_op jit(solution)/shard_map/ppermute | solution.py:152
  89.3 11.2 %collective-permute-start.11 = (bf16[2,8,64,128]{3,2,1,0:T(8,128)(2,1)S(1)}, bf16[2,8,64,128]{3,2,1,0:T(8,128)(2,1)S(1)}, u32[]{:S(2)}, u32[]{:S(2)}) collective-permute-start(bf16[2,8,64,128]{3,2,1,0:T(8,128)(2,1)S(1)} %get-tuple-element.41), channel_id=1, source_target_pairs={{0,4},{1,5},{2,6},{3,7},{4,0},{5,1},{6,2},{7,3},{8,12},{9,13},{10,... | collective-permute-start | bytes 786440 | tf_op jit(solution)/shard_map/ppermute | solution.py:152
  89.8 10.9 %collective-permute-start.10 = (bf16[2,8,64,128]{3,2,1,0:T(8,128)(2,1)S(1)}, bf16[2,8,64,128]{3,2,1,0:T(8,128)(2,1)S(1)}, u32[]{:S(2)}, u32[]{:S(2)}) collective-permute-start(bf16[2,8,64,128]{3,2,1,0:T(8,128)(2,1)S(1)} %get-tuple-element.40), channel_id=1, source_target_pairs={{0,2},{1,3},{2,0},{3,1},{4,6},{5,7},{6,4},{7,5},{8,10},{9,11},{10,... | collective-permute-start | bytes 786440 | tf_op jit(solution)/shard_map/ppermute | solution.py:152
  90.2 11.3 %collective-permute-start.7 = (bf16[4,2,8,32,128]{4,3,2,1,0:T(8,128)(2,1)S(1)}, bf16[4,2,8,32,128]{4,3,2,1,0:T(8,128)(2,1)S(1)}, u32[]{:S(2)}, u32[]{:S(2)}) collective-permute-start(bf16[4,2,8,32,128]{4,3,2,1,0:T(8,128)(2,1)S(1)} %pad_maximum_fusion.2), channel_id=1, source_target_pairs={{0,1},{1,0},{2,3},{3,2},{4,5},{5,4},{6,7},{7,6},{8,9},{9,8},{10,11... | collective-permute-start | bytes 1572872 | tf_op jit(solution)/shard_map/ppermute | solution.py:152
  100.8 2.0 %collective-permute-start.13 = (bf16[4,2,8,32,128]{4,3,2,1,0:T(8,128)(2,1)S(1)}, bf16[4,2,8,32,128]{4,3,2,1,0:T(8,128)(2,1)S(1)}, u32[]{:S(2)}, u32[]{:S(2)}) collective-permute-start(bf16[4,2,8,32,128]{4,3,2,1,0:T(8,128)(2,1)S(1)} %pad_maximum_fusion.3), channel_id=1, source_target_pairs={{0,1},{1,0},{2,3},{3,2},{4,5},{5,4},{6,7},{7,6},{8,9},{9,8},{10,11... | collective-permute-start | bytes 1572872 | tf_op jit(solution)/shard_map/ppermute | solution.py:152
  (2 other events, 1.5 us)

commit v13 on v12

--- a/solution.py
+++ b/solution.py
@@ -8,7 +8,7 @@
 from jax.sharding import PartitionSpec as P
 
 slope = 0.3
-ROWS = 2
+ROWS = 4
 
 
 def cut_kernel(parts, vol_ref, outer, inner):
@@ -65,7 +65,7 @@
     sums = [refs.pop(0) for _ in range(sums_count)]
     pieces = [refs.pop(0) for _ in range(pieces_count)]
     tap_parts = [refs.pop(0) for _ in range(tap_count)]
-    bias_ref, outs = refs[0], refs[1:]
+    bias_ref, outs, store, sems = refs[0], refs[1:-2], refs[-2], refs[-1]
     rows_in, cols = pieces[0].shape[2], pieces[0].shape[4]
     rows = rows_in - 2
     total_out = bias_ref.shape[0]
@@ -73,7 +73,19 @@
     groups, size = tap_parts[0].shape[0], tap_parts[0].shape[4]
     lane = lax.broadcasted_iota(jnp.int32, (total_out, cols), 1)
 
-    def tile(slot, row):
+    def fetch(slot):
+        return pltpu.make_async_copy(sums[0].at[slot], store.at[slot], sems.at[slot, 0])
+
+    def put(slot, step):
+        part = pl.ds(step * rows_at_once, rows_at_once)
+        return pltpu.make_async_copy(store.at[slot, part], outs[slot // 2].at[slot % 2, part], sems.at[slot, step])
+
+    if final:
+        for slot in range(len(plan)):
+            fetch(slot).start()
+
+    def tile(slot, step):
+        row = step * rows_at_once
         cells = []
         weights = []
         for a, source, plane in plan[slot]:
@@ -92,6 +104,8 @@
         total = jnp.dot(
             jnp.concatenate(weights, axis=1), jnp.concatenate(cells, axis=0), preferred_element_type=jnp.float32
         )
+        if final:
+            pl.when(step == 0)(fetch(slot).wait)
         for r in range(rows_at_once):
             part = total[:, r * cols : (r + 1) * cols].reshape(groups * tap_count, 3, size, cols)
             side = [part[:, c].reshape(total_out, cols) for c in range(3)]
@@ -99,18 +113,25 @@
             right = jnp.where(lane == cols - 1, 0.0, pltpu.roll(side[2], cols - 1, 1))
             found = side[1] + left + right
             if not final:
-                outs[slot // 2][slot % 2, row + r] = found
+                store[slot, row + r] = found
                 continue
-            shifted = found + sums[0][slot, row + r] + bias_ref[...]
+            shifted = found + store[slot, row + r] + bias_ref[...]
             done = jnp.where(shifted > 0, shifted, slope * shifted).astype(jnp.bfloat16)
             for n, out_ref in enumerate(outs):
                 out_ref[slot, row + r] = done[n * block : (n + 1) * block]
+        if not final:
+            put(slot, step).start()
 
     for slot in range(len(plan)):
 
         @pl.loop(0, rows // rows_at_once)
         def _(step):
-            tile(slot, step * rows_at_once)
+            tile(slot, step)
+
+    if not final:
+        for slot in range(len(plan)):
+            for step in range(rows // rows_at_once):
+                put(slot, step).wait()
 
 
 def convolve(plan, sums, pieces, tap_parts, bias, blocks):
@@ -120,6 +141,8 @@
     wide_bias = jnp.broadcast_to(bias[:, None], (total_out, cols))
     macs = 9 * total_out * in_chan * sum(len(terms) for terms in plan) * rows * cols
     in_vmem = pl.BlockSpec(memory_space=pltpu.VMEM)
+    in_hbm = pl.BlockSpec(memory_space=pltpu.HBM)
+    steps = rows // min(ROWS, rows)
     if blocks:
         shapes = [jax.ShapeDtypeStruct((len(plan), rows, total_out // blocks, cols), jnp.bfloat16)] * blocks
     else:
@@ -129,10 +152,14 @@
             conv_kernel, plan, min(ROWS, rows), len(sums), len(pieces), len(tap_parts), bool(blocks)
         ),
         out_shape=shapes,
-        in_specs=[in_vmem] * (len(sums) + len(pieces) + len(tap_parts) + 1),
-        out_specs=[in_vmem] * len(shapes),
+        in_specs=[in_hbm] * len(sums) + [in_vmem] * (len(pieces) + len(tap_parts) + 1),
+        out_specs=[in_vmem if blocks else in_hbm] * len(shapes),
+        scratch_shapes=[
+            pltpu.VMEM((len(plan), rows, total_out, cols), jnp.float32),
+            pltpu.SemaphoreType.DMA((len(plan), steps)),
+        ],
         cost_estimate=pl.CostEstimate(flops=2 * macs, bytes_accessed=10_000_000, transcendentals=0),
-        compiler_params=pltpu.CompilerParams(vmem_limit_bytes=12 * 2**20),
+        compiler_params=pltpu.CompilerParams(vmem_limit_bytes=16 * 2**20),
     )(*sums, *pieces, *tap_parts, wide_bias)
 
 

time: 106 us -> 106 us (level)
  no operation moved by 1% of the time
where the time goes in v13:
time: 106 us; the launch traced here: 105 us
  waiting for transfers between devices  33.1 us (31%)
  Pallas kernels  30.2 us (28%)
  starting transfers between devices  26.2 us (25%)
  local copies, waits for them, and re-layouts  12.2 us (12%)
  other arithmetic  3.31 us (3%)
    pallas_call x3, Pallas kernels, convolve(): pl.pallas_call(functools.partial(conv_kernel, plan, min(ROWS, rows), len(...  27.7 us
    ppermute x12, waiting for transfers between devices, swap(): lax.ppermute(array, axis, [(i, i ^ k) for i in range(lax.axis_size(axis))])  22.6 us
    ppermute x12, starting transfers between devices, swap(): lax.ppermute(array, axis, [(i, i ^ k) for i in range(lax.axis_size(axis))])  11.8 us
    all_to_all x1, waiting for transfers between devices, body(): outer = lax.all_to_all(outer_rows, 'filt', 0, 0)  10.5 us
    unnamed x21, local copies, waits for them, and re-layouts  9.07 us
    ppermute x1, starting transfers between devices, body(): before = lax.ppermute(last, 'slab', up)  4.33 us
    all_to_all x1, starting transfers between devices, body(): outer = lax.all_to_all(outer_rows, 'filt', 0, 0)  4.33 us
    all_to_all x1, starting transfers between devices, body(): inner = lax.all_to_all(inner_rows, 'filt', 0, 0)  4.28 us
  transfers between devices with their start and end apart: 16, of which 7 were waited for; matrix products, arithmetic and copies ran while one was open for 6% of the time, Pallas kernels for 29%

profile of v13, /device:TPU:0, one launch (start us, length us, event | category | flops | bytes accessed | tf_op | source)
XLA Modules:
  0.0 105.5 jit_solution(15693067571403643886)
XLA Ops:
  0.0 2.9 %collective-permute-start = (bf16[3,3,3,32,256]{4,3,2,1,0:T(8,128)(2,1)}, bf16[3,3,3,32,256]{4,3,2,1,0:T(8,128)(2,1)S(1)}, u32[]{:S(2)}, u32[]{:S(2)}) collective-permute-start(bf16[3,3,3,32,256]{4,3,2,1,0:T(8,128)(2,1)} %param.4), channel_id=1, source_target_pairs={{0,2},{1,3},{2,0},{3,1},{4,6},{5,7},{6,4},{7,5},{8,10},{9,11},{10,... | collective-permute-start | bytes 1327112 | tf_op jit(solution)/shard_map/ppermute | solution.py:179
  2.9 1.5 %collective-permute-start.1 = (bf16[3,3,3,32,256]{4,3,2,1,0:T(8,128)(2,1)}, bf16[3,3,3,32,256]{4,3,2,1,0:T(8,128)(2,1)S(1)}, u32[]{:S(2)}, u32[]{:S(2)}) collective-permute-start(bf16[3,3,3,32,256]{4,3,2,1,0:T(8,128)(2,1)} %param.4), channel_id=1, source_target_pairs={{0,4},{1,5},{2,6},{3,7},{4,0},{5,1},{6,2},{7,3},{8,12},{9,13},{10,... | collective-permute-start | bytes 1327112 | tf_op jit(solution)/shard_map/ppermute | solution.py:179
  4.5 2.9 %copy.38 = bf16[4,32,64,128]{3,1,2,0:T(8,128)(2,1)S(1)} copy(bf16[4,32,64,128]{3,2,1,0:T(8,128)(2,1)} %param.3) | data formatting | bytes 4194304 | tf_op args[0]
  7.4 1.3 %shard_map.37 = (bf16[8,2,10,32,128]{4,3,2,1,0:T(8,128)(2,1)}, bf16[8,2,10,32,128]{4,3,2,1,0:T(8,128)(2,1)S(1)}) custom-call(bf16[4,64,32,128]{3,2,1,0:T(8,128)(2,1)S(1)} %bitcast.59), custom_call_target="tpu_custom_call" | custom-call | tf_op jit(solution)/shard_map/pallas_call | solution.py:32
  9.8 4.3 %all-to-all-start = ((bf16[8,2,10,32,128]{4,3,2,1,0:T(8,128)(2,1)}), bf16[8,2,10,32,128]{4,3,2,1,0:T(8,128)(2,1)S(1)}, u32[]{:S(2)}, u32[]{:S(2)}) async-start(bf16[8,2,10,32,128]{4,3,2,1,0:T(8,128)(2,1)} %get-tuple-element.25), calls=%async_computation | async-start | bytes 2621440 | tf_op jit(solution)/shard_map/all_to_all | solution.py:187
  14.1 10.7 %collective-permute-done.1 = bf16[3,3,3,32,256]{4,3,2,1,0:T(8,128)(2,1)S(1)} collective-permute-done((bf16[3,3,3,32,256]{4,3,2,1,0:T(8,128)(2,1)}, bf16[3,3,3,32,256]{4,3,2,1,0:T(8,128)(2,1)S(1)}, u32[]{:S(2)}, u32[]{:S(2)}) %collective-permute-start.1) | collective-permute-done | bytes 442400 | tf_op jit(solution)/shard_map/ppermute | solution.py:179
  26.0 1.5 %pad_maximum_fusion.1.refs_1_.refs_2_.refs_4_ = bf16[4,3,3,3,32,256]{5,4,3,2,1,0:T(8,128)(2,1)S(1)} fusion(bf16[1,3,3,3,32,256]{5,4,3,2,1,0:T(8,128)(2,1)} %bitcast.65, bf16[1,3,3,3,32,256]{5,4,3,2,1,0:T(8,128)(2,1)} %bitcast.64, bf16[1,3,3,3,32,256]{5,4,3,2,1,0:T(8,128)(2,1)} %bitcast.63, bf16[1,3,3,3,32,256]{5,4,3,2,1,0:T(8,128)(2,1)S(1)} %bitcast.62), kind=kLoop, calls=%fused_computation.3 | loop fusion | flops 2654208 | bytes 3538944 | tf_op jit(solution)/shard_map/stack | solution.py:185
  27.8 10.5 %all-to-all-done.refs_0_.vol_ref = bf16[8,2,10,32,128]{4,3,2,1,0:T(8,128)(2,1)S(1)} async-done(((bf16[8,2,10,32,128]{4,3,2,1,0:T(8,128)(2,1)}), bf16[8,2,10,32,128]{4,3,2,1,0:T(8,128)(2,1)S(1)}, u32[]{:S(2)}, u32[]{:S(2)}) %all-to-all-start) | async-done | bytes 1310752 | tf_op jit(solution)/shard_map/all_to_all | solution.py:187
  38.3 4.3 %all-to-all-start.1 = ((bf16[8,2,10,32,128]{4,3,2,1,0:T(8,128)(2,1)}), bf16[8,2,10,32,128]{4,3,2,1,0:T(8,128)(2,1)}, u32[]{:S(2)}, u32[]{:S(2)}) async-start(bf16[8,2,10,32,128]{4,3,2,1,0:T(8,128)(2,1)} %copy-done), calls=%async_computation.1 | async-start | bytes 2621440 | tf_op jit(solution)/shard_map/all_to_all | solution.py:188
  43.4 1.2 %shard_map.40 = (bf16[8,1,10,32,128]{4,3,2,1,0:T(8,128)(2,1)}, bf16[8,1,10,32,128]{4,3,2,1,0:T(8,128)(2,1)}) custom-call(bf16[8,2,10,32,128]{4,3,2,1,0:T(8,128)(2,1)S(1)} %all-to-all-done.refs_0_.vol_ref), custom_call_target="tpu_custom_call" | custom-call | tf_op jit(solution)/shard_map/pallas_call | solution.py:54
  44.7 4.3 %collective-permute-start.8 = (bf16[8,1,10,32,128]{4,3,2,1,0:T(8,128)(2,1)}, bf16[8,1,10,32,128]{4,3,2,1,0:T(8,128)(2,1)}, u32[]{:S(2)}, u32[]{:S(2)}) collective-permute-start(bf16[8,1,10,32,128]{4,3,2,1,0:T(8,128)(2,1)} %get-tuple-element.37), channel_id=1, source_target_pairs={{0,8},{8,16},{16,24},{1,9},{9,17},{17,25},{2,10},{10,18},{18,26},{... | collective-permute-start | bytes 1966088 | tf_op jit(solution)/shard_map/ppermute | solution.py:223
  49.0 1.5 %collective-permute-start.9 = (bf16[8,1,10,32,128]{4,3,2,1,0:T(8,128)(2,1)}, bf16[8,1,10,32,128]{4,3,2,1,0:T(8,128)(2,1)}, u32[]{:S(2)}, u32[]{:S(2)}) collective-permute-start(bf16[8,1,10,32,128]{4,3,2,1,0:T(8,128)(2,1)} %get-tuple-element.38), channel_id=1, source_target_pairs={{8,0},{16,8},{24,16},{9,1},{17,9},{25,17},{10,2},{18,10},{26,18},{... | collective-permute-start | bytes 1966088 | tf_op jit(solution)/shard_map/ppermute | solution.py:222
  50.6 9.2 %shard_map.38 = (f32[2,8,256,128]{3,2,1,0:T(8,128)S(1)}, f32[2,8,256,128]{3,2,1,0:T(8,128)S(1)}) custom-call(bf16[8,2,10,32,128]{4,3,2,1,0:T(8,128)(2,1)S(1)} %all-to-all-done.refs_0_.vol_ref, bf16[4,3,3,3,32,256]{5,4,3,2,1,0:T(8,128)(2,1)S(1)} %pad_maximum_fusion.1.refs_1_.refs_2_.refs_4_, ...), custom_call_target="tpu_custom_call" | custom-call | flops 4831838208 | bytes 10000000 | tf_op jit(solution)/shard_map/pallas_call | solution.py:150
  59.8 1.3 %copy-done.1 = f32[2,8,256,128]{3,2,1,0:T(8,128)} copy-done((f32[2,8,256,128]{3,2,1,0:T(8,128)}, f32[2,8,256,128]{3,2,1,0:T(8,128)S(1)}, u32[]{:S(2)}) %copy-start.1) | copy-done | bytes 2097176
  61.1 1.4 %copy-done.3 = f32[2,8,256,128]{3,2,1,0:T(8,128)} copy-done((f32[2,8,256,128]{3,2,1,0:T(8,128)}, f32[2,8,256,128]{3,2,1,0:T(8,128)S(1)}, u32[]{:S(2)}) %copy-start.3) | copy-done | bytes 2097176
  62.5 1.6 %copy-done.4 = f32[2,8,256,128]{3,2,1,0:T(8,128)S(1)} copy-done((f32[2,8,256,128]{3,2,1,0:T(8,128)S(1)}, f32[2,8,256,128]{3,2,1,0:T(8,128)}, u32[]{:S(2)}) %copy-start.4) | copy-done | bytes 2097176
  64.1 9.1 %shard_map.39 = (bf16[2,8,64,128]{3,2,1,0:T(8,128)(2,1)S(1)}, bf16[2,8,64,128]{3,2,1,0:T(8,128)(2,1)S(1)}, bf16[2,8,64,128]{3,2,1,0:T(8,128)(2,1)S(1)}, bf16[2,8,64,128]{3,2,1,0:T(8,128)(2,1)S(1)}) custom-call(f32[2,8,256,128]{3,2,1,0:T(8,128)S(1)} %copy-done.4, bf16[8,2,10,32,128]{4,3,2,1,0:T(8,128)(2,1)} %all-to-all-done.1.refs_1_, ...), custom_call_target="tpu_custom_call" | custom-call | flops 4831838208 | bytes 10000000 | tf_op jit(solution)/shard_map/pallas_call | solution.py:150
  73.2 2.9 %collective-permute-start.6 = (bf16[2,8,64,128]{3,2,1,0:T(8,128)(2,1)S(1)}, bf16[2,8,64,128]{3,2,1,0:T(8,128)(2,1)S(1)}, u32[]{:S(2)}, u32[]{:S(2)}) collective-permute-start(bf16[2,8,64,128]{3,2,1,0:T(8,128)(2,1)S(1)} %get-tuple-element.35), channel_id=1, source_target_pairs={{0,6},{1,7},{2,4},{3,5},{4,2},{5,3},{6,0},{7,1},{8,14},{9,15},{10,... | collective-permute-start | bytes 786440 | tf_op jit(solution)/shard_map/ppermute | solution.py:179
  76.7 9.4 %shard_map.41 = (bf16[2,8,64,128]{3,2,1,0:T(8,128)(2,1)S(1)}, bf16[2,8,64,128]{3,2,1,0:T(8,128)(2,1)S(1)}, bf16[2,8,64,128]{3,2,1,0:T(8,128)(2,1)S(1)}, bf16[2,8,64,128]{3,2,1,0:T(8,128)(2,1)S(1)}) custom-call(f32[2,8,256,128]{3,2,1,0:T(8,128)S(1)} %copy-done.2, bf16[8,2,10,32,128]{4,3,2,1,0:T(8,128)(2,1)} %all-to-all-done.1.refs_1_, ...), custom_call_target="tpu_custom_call" | custom-call | flops 4831838208 | bytes 10000000 | tf_op jit(solution)/shard_map/pallas_call | solution.py:150
  86.2 2.9 %collective-permute-start.12 = (bf16[2,8,64,128]{3,2,1,0:T(8,128)(2,1)S(1)}, bf16[2,8,64,128]{3,2,1,0:T(8,128)(2,1)S(1)}, u32[]{:S(2)}, u32[]{:S(2)}) collective-permute-start(bf16[2,8,64,128]{3,2,1,0:T(8,128)(2,1)S(1)} %get-tuple-element.42), channel_id=1, source_target_pairs={{0,6},{1,7},{2,4},{3,5},{4,2},{5,3},{6,0},{7,1},{8,14},{9,15},{10,... | collective-permute-start | bytes 786440 | tf_op jit(solution)/shard_map/ppermute | solution.py:179
  90.1 6.3 %collective-permute-done.12 = bf16[2,8,64,128]{3,2,1,0:T(8,128)(2,1)S(1)} collective-permute-done((bf16[2,8,64,128]{3,2,1,0:T(8,128)(2,1)S(1)}, bf16[2,8,64,128]{3,2,1,0:T(8,128)(2,1)S(1)}, u32[]{:S(2)}, u32[]{:S(2)}) %collective-permute-start.12) | collective-permute-done | bytes 262176 | tf_op jit(solution)/shard_map/ppermute | solution.py:179
  96.4 3.8 %collective-permute-done.11 = bf16[2,8,64,128]{3,2,1,0:T(8,128)(2,1)S(1)} collective-permute-done((bf16[2,8,64,128]{3,2,1,0:T(8,128)(2,1)S(1)}, bf16[2,8,64,128]{3,2,1,0:T(8,128)(2,1)S(1)}, u32[]{:S(2)}, u32[]{:S(2)}) %collective-permute-start.11) | collective-permute-done | bytes 262176 | tf_op jit(solution)/shard_map/ppermute | solution.py:179
  101.4 1.2 %collective-permute-done.13 = bf16[4,2,8,32,128]{4,3,2,1,0:T(8,128)(2,1)S(1)} collective-permute-done((bf16[4,2,8,32,128]{4,3,2,1,0:T(8,128)(2,1)S(1)}, bf16[4,2,8,32,128]{4,3,2,1,0:T(8,128)(2,1)S(1)}, u32[]{:S(2)}, u32[]{:S(2)}) %collective-permute-start.13) | collective-permute-done | bytes 524320 | tf_op jit(solution)/shard_map/ppermute | solution.py:179
  103.9 1.6 %pad_maximum_fusion = bf16[4,32,64,128]{3,2,1,0:T(8,128)(2,1)} fusion(bf16[1,32,64,128]{3,2,1,0:T(8,128)(2,1)S(1)} %get-tuple-element.46, bf16[2,32,64,128]{3,2,1,0:T(8,128)(2,1)S(1)} %bitcast.61, bf16[1,32,64,128]{3,2,1,0:T(8,128)(2,1)S(1)} %get-tuple-element.45), kind=kLoop, calls=%fused_computation.1 | loop fusion | flops 2097152 | bytes 4194304 | tf_op jit(solution)/shard_map/concatenate | solution.py:229
  (76 shorter events, 7.5 us)
Async XLA Ops:
  0.0 14.1 %collective-permute-start = (bf16[3,3,3,32,256]{4,3,2,1,0:T(8,128)(2,1)}, bf16[3,3,3,32,256]{4,3,2,1,0:T(8,128)(2,1)S(1)}, u32[]{:S(2)}, u32[]{:S(2)}) collective-permute-start(bf16[3,3,3,32,256]{4,3,2,1,0:T(8,128)(2,1)} %param.4), channel_id=1, source_target_pairs={{0,2},{1,3},{2,0},{3,1},{4,6},{5,7},{6,4},{7,5},{8,10},{9,11},{10,... | collective-permute-start | bytes 1327112 | tf_op jit(solution)/shard_map/ppermute | solution.py:179
  2.9 21.9 %collective-permute-start.1 = (bf16[3,3,3,32,256]{4,3,2,1,0:T(8,128)(2,1)}, bf16[3,3,3,32,256]{4,3,2,1,0:T(8,128)(2,1)S(1)}, u32[]{:S(2)}, u32[]{:S(2)}) collective-permute-start(bf16[3,3,3,32,256]{4,3,2,1,0:T(8,128)(2,1)} %param.4), channel_id=1, source_target_pairs={{0,4},{1,5},{2,6},{3,7},{4,0},{5,1},{6,2},{7,3},{8,12},{9,13},{10,... | collective-permute-start | bytes 1327112 | tf_op jit(solution)/shard_map/ppermute | solution.py:179
  4.5 20.7 %collective-permute-start.2 = (bf16[3,3,3,32,256]{4,3,2,1,0:T(8,128)(2,1)}, bf16[3,3,3,32,256]{4,3,2,1,0:T(8,128)(2,1)S(1)}, u32[]{:S(2)}, u32[]{:S(2)}) collective-permute-start(bf16[3,3,3,32,256]{4,3,2,1,0:T(8,128)(2,1)} %param.4), channel_id=1, source_target_pairs={{0,6},{1,7},{2,4},{3,5},{4,2},{5,3},{6,0},{7,1},{8,14},{9,15},{10,... | collective-permute-start | bytes 1327112 | tf_op jit(solution)/shard_map/ppermute | solution.py:179
  8.7 1.1 %copy-start = (bf16[8,2,10,32,128]{4,3,2,1,0:T(8,128)(2,1)}, bf16[8,2,10,32,128]{4,3,2,1,0:T(8,128)(2,1)S(1)}, u32[]{:S(2)}) copy-start(bf16[8,2,10,32,128]{4,3,2,1,0:T(8,128)(2,1)S(1)} %get-tuple-element.31) | copy-start | bytes 3932164
  9.8 16.2 %copy-start.5 = (bf16[3,3,3,32,256]{4,3,2,1,0:T(8,128)(2,1)S(1)}, bf16[3,3,3,32,256]{4,3,2,1,0:T(8,128)(2,1)}, u32[]{:S(2)}) copy-start(bf16[3,3,3,32,256]{4,3,2,1,0:T(8,128)(2,1)} %param.4) | copy-start | bytes 1327108
  9.8 28.5 %all-to-all-start = ((bf16[8,2,10,32,128]{4,3,2,1,0:T(8,128)(2,1)}), bf16[8,2,10,32,128]{4,3,2,1,0:T(8,128)(2,1)S(1)}, u32[]{:S(2)}, u32[]{:S(2)}) async-start(bf16[8,2,10,32,128]{4,3,2,1,0:T(8,128)(2,1)} %get-tuple-element.25), calls=%async_computation | async-start | bytes 2621440 | tf_op jit(solution)/shard_map/all_to_all | solution.py:187
  14.1 11.1 %copy-start.6 = (bf16[3,3,3,32,256]{4,3,2,1,0:T(8,128)(2,1)}, bf16[3,3,3,32,256]{4,3,2,1,0:T(8,128)(2,1)S(1)}, u32[]{:S(2)}) copy-start(bf16[3,3,3,32,256]{4,3,2,1,0:T(8,128)(2,1)S(1)} %collective-permute-done) | copy-start | bytes 1327108
  26.0 1.6 %copy-start.9 = (f32[256]{0:T(256)S(1)}, f32[256]{0:T(256)}, u32[]{:S(2)}) copy-start(f32[256]{0:T(256)} %param.5) | copy-start | bytes 3076
  27.5 23.0 %collective-permute-start.3 = (bf16[4,3,3,3,32,256]{5,4,3,2,1,0:T(8,128)(2,1)S(1)}, bf16[4,3,3,3,32,256]{5,4,3,2,1,0:T(8,128)(2,1)}, u32[]{:S(2)}, u32[]{:S(2)}) collective-permute-start(bf16[4,3,3,3,32,256]{5,4,3,2,1,0:T(8,128)(2,1)S(1)} %pad_maximum_fusion.1.refs_1_.refs_2_.refs_4_), channel_id=1, source_target_pairs={{0,1},{1,0},{2,3},{3,2},{4,5},{5,4},{6,7},{7,6},{8,9},{9,8},{10,11... | collective-permute-start | bytes 5308424 | tf_op jit(solution)/shard_map/ppermute | solution.py:179
  38.3 24.2 %all-to-all-start.1 = ((bf16[8,2,10,32,128]{4,3,2,1,0:T(8,128)(2,1)}), bf16[8,2,10,32,128]{4,3,2,1,0:T(8,128)(2,1)}, u32[]{:S(2)}, u32[]{:S(2)}) async-start(bf16[8,2,10,32,128]{4,3,2,1,0:T(8,128)(2,1)} %copy-done), calls=%async_computation.1 | async-start | bytes 2621440 | tf_op jit(solution)/shard_map/all_to_all | solution.py:188
  44.7 32.1 %collective-permute-start.8 = (bf16[8,1,10,32,128]{4,3,2,1,0:T(8,128)(2,1)}, bf16[8,1,10,32,128]{4,3,2,1,0:T(8,128)(2,1)}, u32[]{:S(2)}, u32[]{:S(2)}) collective-permute-start(bf16[8,1,10,32,128]{4,3,2,1,0:T(8,128)(2,1)} %get-tuple-element.37), channel_id=1, source_target_pairs={{0,8},{8,16},{16,24},{1,9},{9,17},{17,25},{2,10},{10,18},{18,26},{... | collective-permute-start | bytes 1966088 | tf_op jit(solution)/shard_map/ppermute | solution.py:223
  49.0 27.8 %collective-permute-start.9 = (bf16[8,1,10,32,128]{4,3,2,1,0:T(8,128)(2,1)}, bf16[8,1,10,32,128]{4,3,2,1,0:T(8,128)(2,1)}, u32[]{:S(2)}, u32[]{:S(2)}) collective-permute-start(bf16[8,1,10,32,128]{4,3,2,1,0:T(8,128)(2,1)} %get-tuple-element.38), channel_id=1, source_target_pairs={{8,0},{16,8},{24,16},{9,1},{17,9},{25,17},{10,2},{18,10},{26,18},{... | collective-permute-start | bytes 1966088 | tf_op jit(solution)/shard_map/ppermute | solution.py:222
  59.8 1.3 %copy-start.1 = (f32[2,8,256,128]{3,2,1,0:T(8,128)}, f32[2,8,256,128]{3,2,1,0:T(8,128)S(1)}, u32[]{:S(2)}) copy-start(f32[2,8,256,128]{3,2,1,0:T(8,128)S(1)} %get-tuple-element.36.refs_0_) | copy-start | bytes 6291460
  61.1 1.4 %copy-start.3 = (f32[2,8,256,128]{3,2,1,0:T(8,128)}, f32[2,8,256,128]{3,2,1,0:T(8,128)S(1)}, u32[]{:S(2)}) copy-start(f32[2,8,256,128]{3,2,1,0:T(8,128)S(1)} %get-tuple-element.30.refs_0_) | copy-start | bytes 6291460
  62.5 1.6 %copy-start.4 = (f32[2,8,256,128]{3,2,1,0:T(8,128)S(1)}, f32[2,8,256,128]{3,2,1,0:T(8,128)}, u32[]{:S(2)}) copy-start(f32[2,8,256,128]{3,2,1,0:T(8,128)} %copy-done.3) | copy-start | bytes 6291460
  64.1 12.7 %copy-start.2 = (f32[2,8,256,128]{3,2,1,0:T(8,128)S(1)}, f32[2,8,256,128]{3,2,1,0:T(8,128)}, u32[]{:S(2)}) copy-start(f32[2,8,256,128]{3,2,1,0:T(8,128)} %copy-done.1) | copy-start | bytes 6291460
  73.2 16.4 %collective-permute-start.6 = (bf16[2,8,64,128]{3,2,1,0:T(8,128)(2,1)S(1)}, bf16[2,8,64,128]{3,2,1,0:T(8,128)(2,1)S(1)}, u32[]{:S(2)}, u32[]{:S(2)}) collective-permute-start(bf16[2,8,64,128]{3,2,1,0:T(8,128)(2,1)S(1)} %get-tuple-element.35), channel_id=1, source_target_pairs={{0,6},{1,7},{2,4},{3,5},{4,2},{5,3},{6,0},{7,1},{8,14},{9,15},{10,... | collective-permute-start | bytes 786440 | tf_op jit(solution)/shard_map/ppermute | solution.py:179
  76.0 13.8 %collective-permute-start.5 = (bf16[2,8,64,128]{3,2,1,0:T(8,128)(2,1)S(1)}, bf16[2,8,64,128]{3,2,1,0:T(8,128)(2,1)S(1)}, u32[]{:S(2)}, u32[]{:S(2)}) collective-permute-start(bf16[2,8,64,128]{3,2,1,0:T(8,128)(2,1)S(1)} %get-tuple-element.34), channel_id=1, source_target_pairs={{0,4},{1,5},{2,6},{3,7},{4,0},{5,1},{6,2},{7,3},{8,12},{9,13},{10,... | collective-permute-start | bytes 786440 | tf_op jit(solution)/shard_map/ppermute | solution.py:179
  76.6 13.3 %collective-permute-start.4 = (bf16[2,8,64,128]{3,2,1,0:T(8,128)(2,1)S(1)}, bf16[2,8,64,128]{3,2,1,0:T(8,128)(2,1)S(1)}, u32[]{:S(2)}, u32[]{:S(2)}) collective-permute-start(bf16[2,8,64,128]{3,2,1,0:T(8,128)(2,1)S(1)} %get-tuple-element.33), channel_id=1, source_target_pairs={{0,2},{1,3},{2,0},{3,1},{4,6},{5,7},{6,4},{7,5},{8,10},{9,11},{10,... | collective-permute-start | bytes 786440 | tf_op jit(solution)/shard_map/ppermute | solution.py:179
  86.2 10.3 %collective-permute-start.12 = (bf16[2,8,64,128]{3,2,1,0:T(8,128)(2,1)S(1)}, bf16[2,8,64,128]{3,2,1,0:T(8,128)(2,1)S(1)}, u32[]{:S(2)}, u32[]{:S(2)}) collective-permute-start(bf16[2,8,64,128]{3,2,1,0:T(8,128)(2,1)S(1)} %get-tuple-element.42), channel_id=1, source_target_pairs={{0,6},{1,7},{2,4},{3,5},{4,2},{5,3},{6,0},{7,1},{8,14},{9,15},{10,... | collective-permute-start | bytes 786440 | tf_op jit(solution)/shard_map/ppermute | solution.py:179
  89.0 11.2 %collective-permute-start.11 = (bf16[2,8,64,128]{3,2,1,0:T(8,128)(2,1)S(1)}, bf16[2,8,64,128]{3,2,1,0:T(8,128)(2,1)S(1)}, u32[]{:S(2)}, u32[]{:S(2)}) collective-permute-start(bf16[2,8,64,128]{3,2,1,0:T(8,128)(2,1)S(1)} %get-tuple-element.41), channel_id=1, source_target_pairs={{0,4},{1,5},{2,6},{3,7},{4,0},{5,1},{6,2},{7,3},{8,12},{9,13},{10,... | collective-permute-start | bytes 786440 | tf_op jit(solution)/shard_map/ppermute | solution.py:179
  89.6 10.9 %collective-permute-start.10 = (bf16[2,8,64,128]{3,2,1,0:T(8,128)(2,1)S(1)}, bf16[2,8,64,128]{3,2,1,0:T(8,128)(2,1)S(1)}, u32[]{:S(2)}, u32[]{:S(2)}) collective-permute-start(bf16[2,8,64,128]{3,2,1,0:T(8,128)(2,1)S(1)} %get-tuple-element.40), channel_id=1, source_target_pairs={{0,2},{1,3},{2,0},{3,1},{4,6},{5,7},{6,4},{7,5},{8,10},{9,11},{10,... | collective-permute-start | bytes 786440 | tf_op jit(solution)/shard_map/ppermute | solution.py:179
  90.0 11.3 %collective-permute-start.7 = (bf16[4,2,8,32,128]{4,3,2,1,0:T(8,128)(2,1)S(1)}, bf16[4,2,8,32,128]{4,3,2,1,0:T(8,128)(2,1)S(1)}, u32[]{:S(2)}, u32[]{:S(2)}) collective-permute-start(bf16[4,2,8,32,128]{4,3,2,1,0:T(8,128)(2,1)S(1)} %pad_maximum_fusion.2), channel_id=1, source_target_pairs={{0,1},{1,0},{2,3},{3,2},{4,5},{5,4},{6,7},{7,6},{8,9},{9,8},{10,11... | collective-permute-start | bytes 1572872 | tf_op jit(solution)/shard_map/ppermute | solution.py:179
  100.5 2.0 %collective-permute-start.13 = (bf16[4,2,8,32,128]{4,3,2,1,0:T(8,128)(2,1)S(1)}, bf16[4,2,8,32,128]{4,3,2,1,0:T(8,128)(2,1)S(1)}, u32[]{:S(2)}, u32[]{:S(2)}) collective-permute-start(bf16[4,2,8,32,128]{4,3,2,1,0:T(8,128)(2,1)S(1)} %pad_maximum_fusion.3), channel_id=1, source_target_pairs={{0,1},{1,0},{2,3},{3,2},{4,5},{5,4},{6,7},{7,6},{8,9},{9,8},{10,11... | collective-permute-start | bytes 1572872 | tf_op jit(solution)/shard_map/ppermute | solution.py:179
  (2 other events, 1.5 us)

commit v14 on v9

--- a/solution.py
+++ b/solution.py
@@ -102,10 +102,8 @@
                 out_ref[slot, row + r] = done[n * block : (n + 1) * block]
 
     for slot in range(len(plan)):
-
-        @pl.loop(0, rows // rows_at_once)
-        def _(step):
-            tile(slot, step * rows_at_once)
+        for row in range(0, rows, rows_at_once):
+            tile(slot, row)
 
 
 def convolve(plan, pieces, tap_parts, bias, blocks):
@@ -122,7 +120,7 @@
         in_specs=[in_vmem] * (len(pieces) + len(tap_parts) + 1),
         out_specs=[in_vmem] * blocks,
         cost_estimate=pl.CostEstimate(flops=2 * macs, bytes_accessed=10_000_000, transcendentals=0),
-        compiler_params=pltpu.CompilerParams(vmem_limit_bytes=20 * 2**20),
+        compiler_params=pltpu.CompilerParams(vmem_limit_bytes=16 * 2**20),
     )(*pieces, *tap_parts, wide_bias)
 
 
@@ -190,9 +188,8 @@
 
     ends = (((2, 0), *where[:2]), (*where[-2:], (3, 0)))
     outside = send_back(convolve(ends, [outer, inner, settle(before), settle(after)], tap_parts, bias, blocks))
-    whole = jnp.pad(inside, ((1, 1), (0, 0), (0, 0), (0, 0)))
-    whole = lax.dynamic_update_slice_in_dim(whole, outside[:1], 0, 0)
-    return lax.dynamic_update_slice_in_dim(whole, outside[1:], planes - 1, 0)
+    inside, outside = lax.optimization_barrier((inside, outside))
+    return jnp.concatenate([outside[:1], inside, outside[1:]])
 
 
 def solution(mesh):

time: 103 us -> 101 us (0.981)
  local copies, waits for them, and re-layouts: 9.72 us -> 7.17 us
  Pallas kernels: 23.7 us -> 21.8 us
  other arithmetic: 1.52 us -> 3.08 us
    pallas_call x2, Pallas kernels: 21.2 us -> 19.3 us  [convolve(): pl.pallas_call(functools.partial(conv_kernel, plan, min(ROWS, rows), len(...]
    concatenate x0 -> x1, other arithmetic: none -> 1.56 us  [body(): return jnp.concatenate([outside[:1], inside, outside[1:]])]
    unnamed x11 -> x9, local copies, waits for them, and re-layouts: 5.35 us -> 4.04 us
  transfers between devices with their start and end apart: 17 -> 17, of which waited for: 6 -> 6; matrix products, arithmetic and copies ran while one was open for 6% -> 6% of each run, Pallas kernels for 23% -> 22%
where the time goes in v14:
time: 101 us; the launch traced here: 100 us
  waiting for transfers between devices  37.7 us (37%)
  starting transfers between devices  29.9 us (30%)
  Pallas kernels  21.8 us (22%)
  local copies, waits for them, and re-layouts  7.17 us (7%)
  other arithmetic  3.08 us (3%)
    ppermute x13, waiting for transfers between devices, swap(): lax.ppermute(array, axis, [(i, i ^ k) for i in range(lax.axis_size(axis))])  28.4 us
    pallas_call x2, Pallas kernels, convolve(): pl.pallas_call(functools.partial(conv_kernel, plan, min(ROWS, rows), len(...  19.3 us
    ppermute x13, starting transfers between devices, swap(): lax.ppermute(array, axis, [(i, i ^ k) for i in range(lax.axis_size(axis))])  15.4 us
    all_to_all x1, waiting for transfers between devices, body(): inner = lax.all_to_all(inner_rows, 'filt', 0, 0)  9.3 us
    ppermute x1, starting transfers between devices, body(): before = lax.ppermute(last, 'slab', up)  5.41 us
    all_to_all x1, starting transfers between devices, body(): inner = lax.all_to_all(inner_rows, 'filt', 0, 0)  4.28 us
    unnamed x9, local copies, waits for them, and re-layouts  4.04 us
    all_to_all x1, starting transfers between devices, body(): outer = lax.all_to_all(outer_rows, 'filt', 0, 0)  3.57 us
  transfers between devices with their start and end apart: 17, of which 6 were waited for; matrix products, arithmetic and copies ran while one was open for 6% of the time, Pallas kernels for 22%

profile of v14, /device:TPU:0, one launch (start us, length us, event | category | flops | bytes accessed | tf_op | source)
XLA Modules:
  0.0 100.2 jit_solution(7787716002639776116)
XLA Ops:
  0.0 2.9 %collective-permute-start = (bf16[3,3,3,32,256]{4,3,2,1,0:T(8,128)(2,1)}, bf16[3,3,3,32,256]{4,3,2,1,0:T(8,128)(2,1)S(1)}, u32[]{:S(2)}, u32[]{:S(2)}) collective-permute-start(bf16[3,3,3,32,256]{4,3,2,1,0:T(8,128)(2,1)} %param.4), channel_id=1, source_target_pairs={{0,2},{1,3},{2,0},{3,1},{4,6},{5,7},{6,4},{7,5},{8,10},{9,11},{10,... | collective-permute-start | bytes 1327112 | tf_op jit(solution)/shard_map/ppermute | solution.py:140
  2.9 1.5 %collective-permute-start.1 = (bf16[3,3,3,32,256]{4,3,2,1,0:T(8,128)(2,1)}, bf16[3,3,3,32,256]{4,3,2,1,0:T(8,128)(2,1)S(1)}, u32[]{:S(2)}, u32[]{:S(2)}) collective-permute-start(bf16[3,3,3,32,256]{4,3,2,1,0:T(8,128)(2,1)} %param.4), channel_id=1, source_target_pairs={{0,4},{1,5},{2,6},{3,7},{4,0},{5,1},{6,2},{7,3},{8,12},{9,13},{10,... | collective-permute-start | bytes 1327112 | tf_op jit(solution)/shard_map/ppermute | solution.py:140
  4.5 2.9 %copy.38 = bf16[4,32,64,128]{3,1,2,0:T(8,128)(2,1)S(1)} copy(bf16[4,32,64,128]{3,2,1,0:T(8,128)(2,1)} %param.3) | data formatting | bytes 4194304 | tf_op args[0]
  7.4 1.3 %shard_map.37 = (bf16[8,2,10,32,128]{4,3,2,1,0:T(8,128)(2,1)}, bf16[8,2,10,32,128]{4,3,2,1,0:T(8,128)(2,1)S(1)}) custom-call(bf16[4,64,32,128]{3,2,1,0:T(8,128)(2,1)S(1)} %bitcast.60), custom_call_target="tpu_custom_call" | custom-call | tf_op jit(solution)/shard_map/pallas_call | solution.py:32
  9.8 3.6 %all-to-all-start = ((bf16[8,2,10,32,128]{4,3,2,1,0:T(8,128)(2,1)}), bf16[8,2,10,32,128]{4,3,2,1,0:T(8,128)(2,1)S(1)}, u32[]{:S(2)}, u32[]{:S(2)}) async-start(bf16[8,2,10,32,128]{4,3,2,1,0:T(8,128)(2,1)} %get-tuple-element.19), calls=%async_computation | async-start | bytes 2621440 | tf_op jit(solution)/shard_map/all_to_all | solution.py:153
  13.4 2.0 %collective-permute-start.2 = (bf16[3,3,3,16,256]{4,3,2,1,0:T(8,128)(2,1)S(1)}, bf16[3,3,3,16,256]{4,3,2,1,0:T(8,128)(2,1)S(1)}, u32[]{:S(2)}, u32[]{:S(2)}) collective-permute-start(bf16[3,3,3,16,256]{4,3,2,1,0:T(8,128)(2,1)S(1)} %slice.114), channel_id=1, source_target_pairs={{0,4},{1,5},{2,6},{3,7},{4,0},{5,1},{6,2},{7,3},{8,12},{9,13},{10,... | collective-permute-start | bytes 663560 | tf_op jit(solution)/shard_map/ppermute | solution.py:140
  15.4 1.5 %collective-permute-start.3 = (bf16[3,3,3,16,256]{4,3,2,1,0:T(8,128)(2,1)S(1)}, bf16[3,3,3,16,256]{4,3,2,1,0:T(8,128)(2,1)S(1)}, u32[]{:S(2)}, u32[]{:S(2)}) collective-permute-start(bf16[3,3,3,16,256]{4,3,2,1,0:T(8,128)(2,1)S(1)} %slice.115), channel_id=1, source_target_pairs={{0,2},{1,3},{2,0},{3,1},{4,6},{5,7},{6,4},{7,5},{8,10},{9,11},{10,... | collective-permute-start | bytes 663560 | tf_op jit(solution)/shard_map/ppermute | solution.py:140
  17.0 18.3 %collective-permute-done.2 = bf16[3,3,3,16,256]{4,3,2,1,0:T(8,128)(2,1)S(1)} collective-permute-done((bf16[3,3,3,16,256]{4,3,2,1,0:T(8,128)(2,1)S(1)}, bf16[3,3,3,16,256]{4,3,2,1,0:T(8,128)(2,1)S(1)}, u32[]{:S(2)}, u32[]{:S(2)}) %collective-permute-start.2) | collective-permute-done | bytes 221216 | tf_op jit(solution)/shard_map/ppermute | solution.py:140
  35.4 1.2 %pad_maximum_fusion.1.refs_2_.refs_4_ = bf16[4,3,3,3,32,256]{5,4,3,2,1,0:T(8,128)(2,1)S(1)} fusion(bf16[1,3,3,3,32,256]{5,4,3,2,1,0:T(8,128)(2,1)S(1)} %maximum_bitcast_fusion, bf16[1,3,3,3,32,256]{5,4,3,2,1,0:T(8,128)(2,1)} %bitcast.64, bf16[1,3,3,3,32,256]{5,4,3,2,1,0:T(8,128)(2,1)S(1)} %bitcast.63, bf16[1,3,3,3,32,256]{5,4,3,2,1,0:T(8,128)(2,1)S(1)} %bitcast.65), kind=kLoop, calls=%fused_computation.3 | loop fusion | flops 2654208 | bytes 3538944 | tf_op jit(solution)/shard_map/stack | solution.py:149
  36.8 4.3 %all-to-all-start.1 = ((bf16[8,2,10,32,128]{4,3,2,1,0:T(8,128)(2,1)}), bf16[8,2,10,32,128]{4,3,2,1,0:T(8,128)(2,1)}, u32[]{:S(2)}, u32[]{:S(2)}) async-start(bf16[8,2,10,32,128]{4,3,2,1,0:T(8,128)(2,1)} %copy-done), calls=%async_computation.1 | async-start | bytes 2621440 | tf_op jit(solution)/shard_map/all_to_all | solution.py:154
  42.1 1.2 %shard_map.39 = (bf16[8,1,10,32,128]{4,3,2,1,0:T(8,128)(2,1)}, bf16[8,1,10,32,128]{4,3,2,1,0:T(8,128)(2,1)}) custom-call(bf16[8,2,10,32,128]{4,3,2,1,0:T(8,128)(2,1)S(1)} %all-to-all-done.refs_0_.vol_ref), custom_call_target="tpu_custom_call" | custom-call | tf_op jit(solution)/shard_map/pallas_call | solution.py:54
  43.3 1.3 %collective-permute-start.10 = (bf16[8,1,10,32,128]{4,3,2,1,0:T(8,128)(2,1)}, bf16[8,1,10,32,128]{4,3,2,1,0:T(8,128)(2,1)}, u32[]{:S(2)}, u32[]{:S(2)}) collective-permute-start(bf16[8,1,10,32,128]{4,3,2,1,0:T(8,128)(2,1)} %get-tuple-element.26), channel_id=1, source_target_pairs={{8,0},{16,8},{24,16},{9,1},{17,9},{25,17},{10,2},{18,10},{26,18},{... | collective-permute-start | bytes 1966088 | tf_op jit(solution)/shard_map/ppermute | solution.py:186
  44.6 5.4 %collective-permute-start.9 = (bf16[8,1,10,32,128]{4,3,2,1,0:T(8,128)(2,1)}, bf16[8,1,10,32,128]{4,3,2,1,0:T(8,128)(2,1)}, u32[]{:S(2)}, u32[]{:S(2)}) collective-permute-start(bf16[8,1,10,32,128]{4,3,2,1,0:T(8,128)(2,1)} %get-tuple-element.25), channel_id=1, source_target_pairs={{0,8},{8,16},{16,24},{1,9},{9,17},{17,25},{2,10},{10,18},{18,26},{... | collective-permute-start | bytes 1966088 | tf_op jit(solution)/shard_map/ppermute | solution.py:187
  50.0 9.3 %all-to-all-done.1.refs_1_ = bf16[8,2,10,32,128]{4,3,2,1,0:T(8,128)(2,1)} async-done(((bf16[8,2,10,32,128]{4,3,2,1,0:T(8,128)(2,1)}), bf16[8,2,10,32,128]{4,3,2,1,0:T(8,128)(2,1)}, u32[]{:S(2)}, u32[]{:S(2)}) %all-to-all-start.1) | async-done | bytes 1310752 | tf_op jit(solution)/shard_map/all_to_all | solution.py:154
  59.4 9.5 %shard_map.38 = (bf16[2,8,64,128]{3,2,1,0:T(8,128)(2,1)S(1)}, bf16[2,8,64,128]{3,2,1,0:T(8,128)(2,1)S(1)}, bf16[2,8,64,128]{3,2,1,0:T(8,128)(2,1)S(1)}, bf16[2,8,64,128]{3,2,1,0:T(8,128)(2,1)S(1)}) custom-call(bf16[8,2,10,32,128]{4,3,2,1,0:T(8,128)(2,1)S(1)} %all-to-all-done.refs_0_.vol_ref, bf16[8,2,10,32,128]{4,3,2,1,0:T(8,128)(2,1)} %all-to-all-done.1.refs_1_, ...), custom_call_target="tpu_custom_call" | custom-call | flops 7247757312 | bytes 10000000 | tf_op jit(solution)/shard_map/pallas_call | solution.py:117
  69.5 1.4 %collective-permute-start.6 = (bf16[2,8,64,128]{3,2,1,0:T(8,128)(2,1)S(1)}, bf16[2,8,64,128]{3,2,1,0:T(8,128)(2,1)S(1)}, u32[]{:S(2)}, u32[]{:S(2)}) collective-permute-start(bf16[2,8,64,128]{3,2,1,0:T(8,128)(2,1)S(1)} %get-tuple-element.23), channel_id=1, source_target_pairs={{0,4},{1,5},{2,6},{3,7},{4,0},{5,1},{6,2},{7,3},{8,12},{9,13},{10,... | collective-permute-start | bytes 786440 | tf_op jit(solution)/shard_map/ppermute | solution.py:140
  70.9 1.5 %collective-permute-start.5 = (bf16[2,8,64,128]{3,2,1,0:T(8,128)(2,1)S(1)}, bf16[2,8,64,128]{3,2,1,0:T(8,128)(2,1)S(1)}, u32[]{:S(2)}, u32[]{:S(2)}) collective-permute-start(bf16[2,8,64,128]{3,2,1,0:T(8,128)(2,1)S(1)} %get-tuple-element.22), channel_id=1, source_target_pairs={{0,2},{1,3},{2,0},{3,1},{4,6},{5,7},{6,4},{7,5},{8,10},{9,11},{10,... | collective-permute-start | bytes 786440 | tf_op jit(solution)/shard_map/ppermute | solution.py:140
  72.4 9.9 %shard_map.40 = (bf16[2,8,64,128]{3,2,1,0:T(8,128)(2,1)S(1)}, bf16[2,8,64,128]{3,2,1,0:T(8,128)(2,1)S(1)}, bf16[2,8,64,128]{3,2,1,0:T(8,128)(2,1)S(1)}, bf16[2,8,64,128]{3,2,1,0:T(8,128)(2,1)S(1)}) custom-call(bf16[8,2,10,32,128]{4,3,2,1,0:T(8,128)(2,1)S(1)} %all-to-all-done.refs_0_.vol_ref, bf16[8,2,10,32,128]{4,3,2,1,0:T(8,128)(2,1)} %all-to-all-done.1.refs_1_, ...), custom_call_target="tpu_custom_call" | custom-call | flops 7247757312 | bytes 10000000 | tf_op jit(solution)/shard_map/pallas_call | solution.py:117
  83.0 1.4 %collective-permute-start.12 = (bf16[2,8,64,128]{3,2,1,0:T(8,128)(2,1)S(1)}, bf16[2,8,64,128]{3,2,1,0:T(8,128)(2,1)S(1)}, u32[]{:S(2)}, u32[]{:S(2)}) collective-permute-start(bf16[2,8,64,128]{3,2,1,0:T(8,128)(2,1)S(1)} %get-tuple-element.29), channel_id=1, source_target_pairs={{0,4},{1,5},{2,6},{3,7},{4,0},{5,1},{6,2},{7,3},{8,12},{9,13},{10,... | collective-permute-start | bytes 786440 | tf_op jit(solution)/shard_map/ppermute | solution.py:140
  84.4 1.6 %collective-permute-start.11 = (bf16[2,8,64,128]{3,2,1,0:T(8,128)(2,1)S(1)}, bf16[2,8,64,128]{3,2,1,0:T(8,128)(2,1)S(1)}, u32[]{:S(2)}, u32[]{:S(2)}) collective-permute-start(bf16[2,8,64,128]{3,2,1,0:T(8,128)(2,1)S(1)} %get-tuple-element.28), channel_id=1, source_target_pairs={{0,2},{1,3},{2,0},{3,1},{4,6},{5,7},{6,4},{7,5},{8,10},{9,11},{10,... | collective-permute-start | bytes 786440 | tf_op jit(solution)/shard_map/ppermute | solution.py:140
  86.2 6.1 %collective-permute-done.13 = bf16[2,8,64,128]{3,2,1,0:T(8,128)(2,1)S(1)} collective-permute-done((bf16[2,8,64,128]{3,2,1,0:T(8,128)(2,1)S(1)}, bf16[2,8,64,128]{3,2,1,0:T(8,128)(2,1)S(1)}, u32[]{:S(2)}, u32[]{:S(2)}) %collective-permute-start.13) | collective-permute-done | bytes 262176 | tf_op jit(solution)/shard_map/ppermute | solution.py:140
  92.4 2.7 %collective-permute-done.12 = bf16[2,8,64,128]{3,2,1,0:T(8,128)(2,1)S(1)} collective-permute-done((bf16[2,8,64,128]{3,2,1,0:T(8,128)(2,1)S(1)}, bf16[2,8,64,128]{3,2,1,0:T(8,128)(2,1)S(1)}, u32[]{:S(2)}, u32[]{:S(2)}) %collective-permute-start.12) | collective-permute-done | bytes 262176 | tf_op jit(solution)/shard_map/ppermute | solution.py:140
  96.1 1.2 %collective-permute-done.14 = bf16[4,2,8,32,128]{4,3,2,1,0:T(8,128)(2,1)S(1)} collective-permute-done((bf16[4,2,8,32,128]{4,3,2,1,0:T(8,128)(2,1)S(1)}, bf16[4,2,8,32,128]{4,3,2,1,0:T(8,128)(2,1)S(1)}, u32[]{:S(2)}, u32[]{:S(2)}) %collective-permute-start.14) | collective-permute-done | bytes 524320 | tf_op jit(solution)/shard_map/ppermute | solution.py:140
  98.6 1.6 %pad_maximum_fusion = bf16[4,32,64,128]{3,2,1,0:T(8,128)(2,1)} fusion(bf16[1,32,64,128]{3,2,1,0:T(8,128)(2,1)S(1)} %get-tuple-element.34, bf16[2,32,64,128]{3,2,1,0:T(8,128)(2,1)S(1)} %bitcast.62, bf16[1,32,64,128]{3,2,1,0:T(8,128)(2,1)S(1)} %get-tuple-element.33), kind=kLoop, calls=%fused_computation.1 | loop fusion | flops 2097152 | bytes 4194304 | tf_op jit(solution)/shard_map/concatenate | solution.py:192
  (68 shorter events, 6.2 us)
Async XLA Ops:
  0.0 13.4 %collective-permute-start = (bf16[3,3,3,32,256]{4,3,2,1,0:T(8,128)(2,1)}, bf16[3,3,3,32,256]{4,3,2,1,0:T(8,128)(2,1)S(1)}, u32[]{:S(2)}, u32[]{:S(2)}) collective-permute-start(bf16[3,3,3,32,256]{4,3,2,1,0:T(8,128)(2,1)} %param.4), channel_id=1, source_target_pairs={{0,2},{1,3},{2,0},{3,1},{4,6},{5,7},{6,4},{7,5},{8,10},{9,11},{10,... | collective-permute-start | bytes 1327112 | tf_op jit(solution)/shard_map/ppermute | solution.py:140
  2.9 12.5 %collective-permute-start.1 = (bf16[3,3,3,32,256]{4,3,2,1,0:T(8,128)(2,1)}, bf16[3,3,3,32,256]{4,3,2,1,0:T(8,128)(2,1)S(1)}, u32[]{:S(2)}, u32[]{:S(2)}) collective-permute-start(bf16[3,3,3,32,256]{4,3,2,1,0:T(8,128)(2,1)} %param.4), channel_id=1, source_target_pairs={{0,4},{1,5},{2,6},{3,7},{4,0},{5,1},{6,2},{7,3},{8,12},{9,13},{10,... | collective-permute-start | bytes 1327112 | tf_op jit(solution)/shard_map/ppermute | solution.py:140
  8.7 1.1 %copy-start = (bf16[8,2,10,32,128]{4,3,2,1,0:T(8,128)(2,1)}, bf16[8,2,10,32,128]{4,3,2,1,0:T(8,128)(2,1)S(1)}, u32[]{:S(2)}) copy-start(bf16[8,2,10,32,128]{4,3,2,1,0:T(8,128)(2,1)S(1)} %get-tuple-element.20) | copy-start | bytes 3932164
  9.8 27.0 %all-to-all-start = ((bf16[8,2,10,32,128]{4,3,2,1,0:T(8,128)(2,1)}), bf16[8,2,10,32,128]{4,3,2,1,0:T(8,128)(2,1)S(1)}, u32[]{:S(2)}, u32[]{:S(2)}) async-start(bf16[8,2,10,32,128]{4,3,2,1,0:T(8,128)(2,1)} %get-tuple-element.19), calls=%async_computation | async-start | bytes 2621440 | tf_op jit(solution)/shard_map/all_to_all | solution.py:153
  13.3 22.1 %copy-start.2 = (bf16[3,3,3,32,256]{4,3,2,1,0:T(8,128)(2,1)S(1)}, bf16[3,3,3,32,256]{4,3,2,1,0:T(8,128)(2,1)}, u32[]{:S(2)}) copy-start(bf16[3,3,3,32,256]{4,3,2,1,0:T(8,128)(2,1)} %param.4) | copy-start | bytes 1327108
  13.4 21.9 %collective-permute-start.2 = (bf16[3,3,3,16,256]{4,3,2,1,0:T(8,128)(2,1)S(1)}, bf16[3,3,3,16,256]{4,3,2,1,0:T(8,128)(2,1)S(1)}, u32[]{:S(2)}, u32[]{:S(2)}) collective-permute-start(bf16[3,3,3,16,256]{4,3,2,1,0:T(8,128)(2,1)S(1)} %slice.114), channel_id=1, source_target_pairs={{0,4},{1,5},{2,6},{3,7},{4,0},{5,1},{6,2},{7,3},{8,12},{9,13},{10,... | collective-permute-start | bytes 663560 | tf_op jit(solution)/shard_map/ppermute | solution.py:140
  15.4 20.0 %copy-start.1 = (bf16[3,3,3,32,256]{4,3,2,1,0:T(8,128)(2,1)}, bf16[3,3,3,32,256]{4,3,2,1,0:T(8,128)(2,1)S(1)}, u32[]{:S(2)}) copy-start(bf16[3,3,3,32,256]{4,3,2,1,0:T(8,128)(2,1)S(1)} %collective-permute-done.1) | copy-start | bytes 1327108
  15.4 19.9 %collective-permute-start.3 = (bf16[3,3,3,16,256]{4,3,2,1,0:T(8,128)(2,1)S(1)}, bf16[3,3,3,16,256]{4,3,2,1,0:T(8,128)(2,1)S(1)}, u32[]{:S(2)}, u32[]{:S(2)}) collective-permute-start(bf16[3,3,3,16,256]{4,3,2,1,0:T(8,128)(2,1)S(1)} %slice.115), channel_id=1, source_target_pairs={{0,2},{1,3},{2,0},{3,1},{4,6},{5,7},{6,4},{7,5},{8,10},{9,11},{10,... | collective-permute-start | bytes 663560 | tf_op jit(solution)/shard_map/ppermute | solution.py:140
  36.7 4.4 %copy-start.3 = (f32[256]{0:T(256)S(1)}, f32[256]{0:T(256)}, u32[]{:S(2)}) copy-start(f32[256]{0:T(256)} %param.5) | copy-start | bytes 3076
  36.7 22.6 %collective-permute-start.4 = (bf16[4,3,3,3,32,256]{5,4,3,2,1,0:T(8,128)(2,1)S(1)}, bf16[4,3,3,3,32,256]{5,4,3,2,1,0:T(8,128)(2,1)}, u32[]{:S(2)}, u32[]{:S(2)}) collective-permute-start(bf16[4,3,3,3,32,256]{5,4,3,2,1,0:T(8,128)(2,1)S(1)} %pad_maximum_fusion.1.refs_2_.refs_4_), channel_id=1, source_target_pairs={{0,1},{1,0},{2,3},{3,2},{4,5},{5,4},{6,7},{7,6},{8,9},{9,8},{10,11... | collective-permute-start | bytes 5308424 | tf_op jit(solution)/shard_map/ppermute | solution.py:140
  36.8 22.5 %all-to-all-start.1 = ((bf16[8,2,10,32,128]{4,3,2,1,0:T(8,128)(2,1)}), bf16[8,2,10,32,128]{4,3,2,1,0:T(8,128)(2,1)}, u32[]{:S(2)}, u32[]{:S(2)}) async-start(bf16[8,2,10,32,128]{4,3,2,1,0:T(8,128)(2,1)} %copy-done), calls=%async_computation.1 | async-start | bytes 2621440 | tf_op jit(solution)/shard_map/all_to_all | solution.py:154
  43.3 29.1 %collective-permute-start.10 = (bf16[8,1,10,32,128]{4,3,2,1,0:T(8,128)(2,1)}, bf16[8,1,10,32,128]{4,3,2,1,0:T(8,128)(2,1)}, u32[]{:S(2)}, u32[]{:S(2)}) collective-permute-start(bf16[8,1,10,32,128]{4,3,2,1,0:T(8,128)(2,1)} %get-tuple-element.26), channel_id=1, source_target_pairs={{8,0},{16,8},{24,16},{9,1},{17,9},{25,17},{10,2},{18,10},{26,18},{... | collective-permute-start | bytes 1966088 | tf_op jit(solution)/shard_map/ppermute | solution.py:186
  44.6 27.9 %collective-permute-start.9 = (bf16[8,1,10,32,128]{4,3,2,1,0:T(8,128)(2,1)}, bf16[8,1,10,32,128]{4,3,2,1,0:T(8,128)(2,1)}, u32[]{:S(2)}, u32[]{:S(2)}) collective-permute-start(bf16[8,1,10,32,128]{4,3,2,1,0:T(8,128)(2,1)} %get-tuple-element.25), channel_id=1, source_target_pairs={{0,8},{8,16},{16,24},{1,9},{9,17},{17,25},{2,10},{10,18},{18,26},{... | collective-permute-start | bytes 1966088 | tf_op jit(solution)/shard_map/ppermute | solution.py:187
  68.9 15.5 %collective-permute-start.7 = (bf16[2,8,64,128]{3,2,1,0:T(8,128)(2,1)S(1)}, bf16[2,8,64,128]{3,2,1,0:T(8,128)(2,1)S(1)}, u32[]{:S(2)}, u32[]{:S(2)}) collective-permute-start(bf16[2,8,64,128]{3,2,1,0:T(8,128)(2,1)S(1)} %get-tuple-element.24), channel_id=1, source_target_pairs={{0,6},{1,7},{2,4},{3,5},{4,2},{5,3},{6,0},{7,1},{8,14},{9,15},{10,... | collective-permute-start | bytes 786440 | tf_op jit(solution)/shard_map/ppermute | solution.py:140
  69.5 16.5 %collective-permute-start.6 = (bf16[2,8,64,128]{3,2,1,0:T(8,128)(2,1)S(1)}, bf16[2,8,64,128]{3,2,1,0:T(8,128)(2,1)S(1)}, u32[]{:S(2)}, u32[]{:S(2)}) collective-permute-start(bf16[2,8,64,128]{3,2,1,0:T(8,128)(2,1)S(1)} %get-tuple-element.23), channel_id=1, source_target_pairs={{0,4},{1,5},{2,6},{3,7},{4,0},{5,1},{6,2},{7,3},{8,12},{9,13},{10,... | collective-permute-start | bytes 786440 | tf_op jit(solution)/shard_map/ppermute | solution.py:140
  70.9 15.2 %collective-permute-start.5 = (bf16[2,8,64,128]{3,2,1,0:T(8,128)(2,1)S(1)}, bf16[2,8,64,128]{3,2,1,0:T(8,128)(2,1)S(1)}, u32[]{:S(2)}, u32[]{:S(2)}) collective-permute-start(bf16[2,8,64,128]{3,2,1,0:T(8,128)(2,1)S(1)} %get-tuple-element.22), channel_id=1, source_target_pairs={{0,2},{1,3},{2,0},{3,1},{4,6},{5,7},{6,4},{7,5},{8,10},{9,11},{10,... | collective-permute-start | bytes 786440 | tf_op jit(solution)/shard_map/ppermute | solution.py:140
  82.3 10.0 %collective-permute-start.13 = (bf16[2,8,64,128]{3,2,1,0:T(8,128)(2,1)S(1)}, bf16[2,8,64,128]{3,2,1,0:T(8,128)(2,1)S(1)}, u32[]{:S(2)}, u32[]{:S(2)}) collective-permute-start(bf16[2,8,64,128]{3,2,1,0:T(8,128)(2,1)S(1)} %get-tuple-element.30), channel_id=1, source_target_pairs={{0,6},{1,7},{2,4},{3,5},{4,2},{5,3},{6,0},{7,1},{8,14},{9,15},{10,... | collective-permute-start | bytes 786440 | tf_op jit(solution)/shard_map/ppermute | solution.py:140
  83.0 12.1 %collective-permute-start.12 = (bf16[2,8,64,128]{3,2,1,0:T(8,128)(2,1)S(1)}, bf16[2,8,64,128]{3,2,1,0:T(8,128)(2,1)S(1)}, u32[]{:S(2)}, u32[]{:S(2)}) collective-permute-start(bf16[2,8,64,128]{3,2,1,0:T(8,128)(2,1)S(1)} %get-tuple-element.29), channel_id=1, source_target_pairs={{0,4},{1,5},{2,6},{3,7},{4,0},{5,1},{6,2},{7,3},{8,12},{9,13},{10,... | collective-permute-start | bytes 786440 | tf_op jit(solution)/shard_map/ppermute | solution.py:140
  84.4 10.7 %collective-permute-start.11 = (bf16[2,8,64,128]{3,2,1,0:T(8,128)(2,1)S(1)}, bf16[2,8,64,128]{3,2,1,0:T(8,128)(2,1)S(1)}, u32[]{:S(2)}, u32[]{:S(2)}) collective-permute-start(bf16[2,8,64,128]{3,2,1,0:T(8,128)(2,1)S(1)} %get-tuple-element.28), channel_id=1, source_target_pairs={{0,2},{1,3},{2,0},{3,1},{4,6},{5,7},{6,4},{7,5},{8,10},{9,11},{10,... | collective-permute-start | bytes 786440 | tf_op jit(solution)/shard_map/ppermute | solution.py:140
  86.2 9.9 %collective-permute-start.8 = (bf16[4,2,8,32,128]{4,3,2,1,0:T(8,128)(2,1)S(1)}, bf16[4,2,8,32,128]{4,3,2,1,0:T(8,128)(2,1)S(1)}, u32[]{:S(2)}, u32[]{:S(2)}) collective-permute-start(bf16[4,2,8,32,128]{4,3,2,1,0:T(8,128)(2,1)S(1)} %pad_maximum_fusion.2), channel_id=1, source_target_pairs={{0,1},{1,0},{2,3},{3,2},{4,5},{5,4},{6,7},{7,6},{8,9},{9,8},{10,11... | collective-permute-start | bytes 1572872 | tf_op jit(solution)/shard_map/ppermute | solution.py:140
  95.3 2.0 %collective-permute-start.14 = (bf16[4,2,8,32,128]{4,3,2,1,0:T(8,128)(2,1)S(1)}, bf16[4,2,8,32,128]{4,3,2,1,0:T(8,128)(2,1)S(1)}, u32[]{:S(2)}, u32[]{:S(2)}) collective-permute-start(bf16[4,2,8,32,128]{4,3,2,1,0:T(8,128)(2,1)S(1)} %pad_maximum_fusion.3), channel_id=1, source_target_pairs={{0,1},{1,0},{2,3},{3,2},{4,5},{5,4},{6,7},{7,6},{8,9},{9,8},{10,11... | collective-permute-start | bytes 1572872 | tf_op jit(solution)/shard_map/ppermute | solution.py:140

commit v15 on v14

--- a/solution.py
+++ b/solution.py
@@ -11,7 +11,7 @@
 ROWS = 4
 
 
-def cut_kernel(parts, vol_ref, outer, inner):
+def cut_kernel(parts, vol_ref, out):
     planes, y_cells = vol_ref.shape[:2]
     rows = y_cells // parts
     for block in range(parts):
@@ -19,25 +19,19 @@
             row = block * rows + r - 1
             for plane in range(planes):
                 line = vol_ref[plane, min(max(row, 0), y_cells - 1)]
-                line = line if 0 <= row < y_cells else jnp.zeros_like(line)
-                if 0 < plane < planes - 1:
-                    inner[block, plane - 1, r] = line
-                else:
-                    outer[block, min(plane, 1), r] = line
+                out[block, plane, r] = line if 0 <= row < y_cells else jnp.zeros_like(line)
 
 
-def cut(volume, parts):
-    planes, y_cells, chan, cols = volume.shape
+def cut(planes, parts):
+    volume = planes.transpose(0, 2, 1, 3)
+    count, y_cells, chan, cols = volume.shape
     in_vmem = pl.BlockSpec(memory_space=pltpu.VMEM)
     return pl.pallas_call(
         functools.partial(cut_kernel, parts),
-        out_shape=[
-            jax.ShapeDtypeStruct((parts, count, y_cells // parts + 2, chan, cols), volume.dtype)
-            for count in (2, planes - 2)
-        ],
+        out_shape=jax.ShapeDtypeStruct((parts, count, y_cells // parts + 2, chan, cols), volume.dtype),
         in_specs=[in_vmem],
-        out_specs=[in_vmem] * 2,
-        compiler_params=pltpu.CompilerParams(vmem_limit_bytes=8 * 2**20),
+        out_specs=in_vmem,
+        compiler_params=pltpu.CompilerParams(vmem_limit_bytes=6 * 2**20),
     )(volume)
 
 
@@ -139,19 +133,21 @@
             return array
         return lax.ppermute(array, axis, [(i, i ^ k) for i in range(lax.axis_size(axis))])
 
+
+    near = [swap(kernel, k) for k in across[1 : 3 if len(across) == 4 else None]]
     if len(across) == 4:
         half = out_chan // 2
-        by_x, by_y = swap(kernel, across[1]), swap(kernel, across[2])
+        by_x, by_y = near
         far = [swap(by_x[:, :, :, :half], across[2]), swap(by_y[:, :, :, half:], across[1])]
         fetched = [kernel, by_x, by_y, jnp.concatenate(far, axis=3)]
     else:
-        fetched = [swap(kernel, k) for k in across]
+        fetched = [kernel, *near]
     same = jnp.stack(fetched)
     tap_parts = [same, swap(same, 1)]
 
-    outer_rows, inner_rows = cut(features.transpose(0, 2, 1, 3), parts)
-    outer = lax.all_to_all(outer_rows, "filt", 0, 0)
-    inner = lax.all_to_all(inner_rows, "filt", 0, 0)
+    outer = lax.all_to_all(cut(jnp.concatenate([features[:1], features[-1:]]), parts), "filt", 0, 0)
+    between = lax.optimization_barrier((features[1:-1], near))[0]
+    inner = lax.all_to_all(cut(between, parts), "filt", 0, 0)
     arrived = outer
     order = jnp.stack([me ^ k ^ c for k in across for c in range(2)])
     bias = jnp.take(bias_vector.reshape(parts, out_chan), order, axis=0).reshape(-1)

time: 101 us -> 102 us (level)
  starting transfers between devices: 29.9 us -> 31.2 us
  Pallas kernels: 21.8 us -> 22.9 us
    unnamed x9 -> x8, local copies, waits for them, and re-layouts: 4.04 us -> 0.7 us
    slice x0 -> x3, local copies, waits for them, and re-layouts: none -> 2.41 us  [the longest x1 1.27 us: body(): features[:1]]
    ppermute x13, starting transfers between devices: 15.4 us -> 16.6 us  [swap(): lax.ppermute(array, axis, [(i, i ^ k) for i in range(lax.axis_size(axis))])]
    pallas_call x1 -> x2, Pallas kernels: 1.29 us -> 2.36 us  [cut(): pl.pallas_call(functools.partial(cut_kernel, parts), out_shape=jax.ShapeD...]
  transfers between devices with their start and end apart: 17 -> 17, of which waited for: 6 -> 7; matrix products, arithmetic and copies ran while one was open for 6% -> 6% of each run, Pallas kernels for 22% -> 23%
where the time goes in v15:
time: 102 us
  waiting for transfers between devices  36.8 us (36%)
  starting transfers between devices  31.2 us (31%)
  Pallas kernels  22.9 us (22%)
  local copies, waits for them, and re-layouts  6.92 us (7%)
  other arithmetic  3.18 us (3%)
    ppermute x13, waiting for transfers between devices, swap(): lax.ppermute(array, axis, [(i, i ^ k) for i in range(lax.axis_size(axis))])  27.5 us
    pallas_call x2, Pallas kernels, convolve(): pl.pallas_call(functools.partial(conv_kernel, plan, min(ROWS, rows), len(...  19.3 us
    ppermute x13, starting transfers between devices, swap(): lax.ppermute(array, axis, [(i, i ^ k) for i in range(lax.axis_size(axis))])  16.6 us
    all_to_all x1, waiting for transfers between devices, body(): inner = lax.all_to_all(cut(between, parts), 'filt', 0, 0)  9.31 us
    ppermute x1, starting transfers between devices, body(): before = lax.ppermute(last, 'slab', up)  5.41 us
    all_to_all x1, starting transfers between devices, body(): inner = lax.all_to_all(cut(between, parts), 'filt', 0, 0)  4.4 us
    all_to_all x1, starting transfers between devices, body(): lax.all_to_all(cut(jnp.concatenate([features[:1], features[-1:]]), parts)...  3.57 us
    pallas_call x2, Pallas kernels, cut(): pl.pallas_call(functools.partial(cut_kernel, parts), out_shape=jax.ShapeD...  2.36 us
  transfers between devices with their start and end apart: 17, of which 7 were waited for; matrix products, arithmetic and copies ran while one was open for 6% of the time, Pallas kernels for 23%

profile of v15, /device:TPU:0, one launch (start us, length us, event | category | flops | bytes accessed | tf_op | source)
XLA Modules:
  0.0 101.5 jit_solution(11453816495921450641)
XLA Ops:
  0.0 2.9 %collective-permute-start = (bf16[3,3,3,32,256]{4,3,2,1,0:T(8,128)(2,1)}, bf16[3,3,3,32,256]{4,3,2,1,0:T(8,128)(2,1)S(1)}, u32[]{:S(2)}, u32[]{:S(2)}) collective-permute-start(bf16[3,3,3,32,256]{4,3,2,1,0:T(8,128)(2,1)} %param.4), channel_id=1, source_target_pairs={{0,2},{1,3},{2,0},{3,1},{4,6},{5,7},{6,4},{7,5},{8,10},{9,11},{10,... | collective-permute-start | bytes 1327112 | tf_op jit(solution)/shard_map/ppermute | solution.py:134
  2.9 1.5 %collective-permute-start.1 = (bf16[3,3,3,32,256]{4,3,2,1,0:T(8,128)(2,1)}, bf16[3,3,3,32,256]{4,3,2,1,0:T(8,128)(2,1)S(1)}, u32[]{:S(2)}, u32[]{:S(2)}) collective-permute-start(bf16[3,3,3,32,256]{4,3,2,1,0:T(8,128)(2,1)} %param.4), channel_id=1, source_target_pairs={{0,4},{1,5},{2,6},{3,7},{4,0},{5,1},{6,2},{7,3},{8,12},{9,13},{10,... | collective-permute-start | bytes 1327112 | tf_op jit(solution)/shard_map/ppermute | solution.py:134
  4.5 1.3 %fusion.1 = (bf16[1,32,64,128]{3,2,1,0:T(8,128)(2,1)S(1)}, bf16[1,32,64,128]{3,2,1,0:T(8,128)(2,1)S(1)}) fusion(bf16[4,32,64,128]{3,2,1,0:T(8,128)(2,1)} %param.3), kind=kLoop, calls=%fused_computation.45 | loop fusion | bytes 2097152 | tf_op jit(solution)/shard_map/slice | solution.py:148
  6.5 1.2 %shard_map.37 = bf16[8,2,10,32,128]{4,3,2,1,0:T(8,128)(2,1)} custom-call(bf16[2,64,32,128]{3,2,1,0:T(8,128)(2,1)S(1)} %maximum_bitcast_fusion.vol_ref), custom_call_target="tpu_custom_call" | custom-call | tf_op jit(solution)/shard_map/pallas_call | solution.py:29
  7.7 3.6 %all-to-all-start = ((bf16[8,2,10,32,128]{4,3,2,1,0:T(8,128)(2,1)}), bf16[8,2,10,32,128]{4,3,2,1,0:T(8,128)(2,1)S(1)}, u32[]{:S(2)}, u32[]{:S(2)}) async-start(bf16[8,2,10,32,128]{4,3,2,1,0:T(8,128)(2,1)} %shard_map.37), calls=%async_computation | async-start | bytes 2621440 | tf_op jit(solution)/shard_map/all_to_all | solution.py:148
  11.3 2.0 %collective-permute-done = bf16[3,3,3,32,256]{4,3,2,1,0:T(8,128)(2,1)S(1)} collective-permute-done((bf16[3,3,3,32,256]{4,3,2,1,0:T(8,128)(2,1)}, bf16[3,3,3,32,256]{4,3,2,1,0:T(8,128)(2,1)S(1)}, u32[]{:S(2)}, u32[]{:S(2)}) %collective-permute-start) | collective-permute-done | bytes 442400 | tf_op jit(solution)/shard_map/ppermute | solution.py:134
  13.3 1.8 %collective-permute-start.2 = (bf16[3,3,3,16,256]{4,3,2,1,0:T(8,128)(2,1)S(1)}, bf16[3,3,3,16,256]{4,3,2,1,0:T(8,128)(2,1)S(1)}, u32[]{:S(2)}, u32[]{:S(2)}) collective-permute-start(bf16[3,3,3,16,256]{4,3,2,1,0:T(8,128)(2,1)S(1)} %slice.126), channel_id=1, source_target_pairs={{0,4},{1,5},{2,6},{3,7},{4,0},{5,1},{6,2},{7,3},{8,12},{9,13},{10,... | collective-permute-start | bytes 663560 | tf_op jit(solution)/shard_map/ppermute | solution.py:134
  15.4 2.9 %collective-permute-start.3 = (bf16[3,3,3,16,256]{4,3,2,1,0:T(8,128)(2,1)S(1)}, bf16[3,3,3,16,256]{4,3,2,1,0:T(8,128)(2,1)S(1)}, u32[]{:S(2)}, u32[]{:S(2)}) collective-permute-start(bf16[3,3,3,16,256]{4,3,2,1,0:T(8,128)(2,1)S(1)} %slice.127), channel_id=1, source_target_pairs={{0,2},{1,3},{2,0},{3,1},{4,6},{5,7},{6,4},{7,5},{8,10},{9,11},{10,... | collective-permute-start | bytes 663560 | tf_op jit(solution)/shard_map/ppermute | solution.py:134
  18.3 15.3 %collective-permute-done.2 = bf16[3,3,3,16,256]{4,3,2,1,0:T(8,128)(2,1)S(1)} collective-permute-done((bf16[3,3,3,16,256]{4,3,2,1,0:T(8,128)(2,1)S(1)}, bf16[3,3,3,16,256]{4,3,2,1,0:T(8,128)(2,1)S(1)}, u32[]{:S(2)}, u32[]{:S(2)}) %collective-permute-start.2) | collective-permute-done | bytes 221216 | tf_op jit(solution)/shard_map/ppermute | solution.py:134
  33.6 1.2 %pad_maximum_fusion.1.refs_2_.refs_4_ = bf16[4,3,3,3,32,256]{5,4,3,2,1,0:T(8,128)(2,1)S(1)} fusion(bf16[1,3,3,3,32,256]{5,4,3,2,1,0:T(8,128)(2,1)S(1)} %maximum_bitcast_fusion.1, bf16[1,3,3,3,32,256]{5,4,3,2,1,0:T(8,128)(2,1)} %bitcast.64, bf16[1,3,3,3,32,256]{5,4,3,2,1,0:T(8,128)(2,1)S(1)} %bitcast.63, bf16[1,3,3,3,32,256]{5,4,3,2,1,0:T(8,128)(2,1)S(1)} %bitcast.65), kind=kLoop, calls=%fused_computation.2 | loop fusion | flops 2654208 | bytes 3538944 | tf_op jit(solution)/shard_map/stack | solution.py:145
  36.8 1.2 %shard_map.38 = bf16[8,2,10,32,128]{4,3,2,1,0:T(8,128)(2,1)} custom-call(bf16[2,64,32,128]{3,2,1,0:T(8,128)(2,1)S(1)} %bitcast.60), custom_call_target="tpu_custom_call" | custom-call | tf_op jit(solution)/shard_map/pallas_call | solution.py:29
  38.0 4.4 %all-to-all-start.1 = ((bf16[8,2,10,32,128]{4,3,2,1,0:T(8,128)(2,1)}), bf16[8,2,10,32,128]{4,3,2,1,0:T(8,128)(2,1)}, u32[]{:S(2)}, u32[]{:S(2)}) async-start(bf16[8,2,10,32,128]{4,3,2,1,0:T(8,128)(2,1)} %shard_map.38), calls=%async_computation.1 | async-start | bytes 2621440 | tf_op jit(solution)/shard_map/all_to_all | solution.py:150
  44.6 1.3 %collective-permute-start.10 = (bf16[8,1,10,32,128]{4,3,2,1,0:T(8,128)(2,1)}, bf16[8,1,10,32,128]{4,3,2,1,0:T(8,128)(2,1)}, u32[]{:S(2)}, u32[]{:S(2)}) collective-permute-start(bf16[8,1,10,32,128]{4,3,2,1,0:T(8,128)(2,1)} %get-tuple-element.24), channel_id=1, source_target_pairs={{8,0},{16,8},{24,16},{9,1},{17,9},{25,17},{10,2},{18,10},{26,18},{... | collective-permute-start | bytes 1966088 | tf_op jit(solution)/shard_map/ppermute | solution.py:182
  45.9 5.4 %collective-permute-start.9 = (bf16[8,1,10,32,128]{4,3,2,1,0:T(8,128)(2,1)}, bf16[8,1,10,32,128]{4,3,2,1,0:T(8,128)(2,1)}, u32[]{:S(2)}, u32[]{:S(2)}) collective-permute-start(bf16[8,1,10,32,128]{4,3,2,1,0:T(8,128)(2,1)} %get-tuple-element.23), channel_id=1, source_target_pairs={{0,8},{8,16},{16,24},{1,9},{9,17},{17,25},{2,10},{10,18},{18,26},{... | collective-permute-start | bytes 1966088 | tf_op jit(solution)/shard_map/ppermute | solution.py:183
  51.3 9.3 %all-to-all-done.1.refs_1_ = bf16[8,2,10,32,128]{4,3,2,1,0:T(8,128)(2,1)} async-done(((bf16[8,2,10,32,128]{4,3,2,1,0:T(8,128)(2,1)}), bf16[8,2,10,32,128]{4,3,2,1,0:T(8,128)(2,1)}, u32[]{:S(2)}, u32[]{:S(2)}) %all-to-all-start.1) | async-done | bytes 1310752 | tf_op jit(solution)/shard_map/all_to_all | solution.py:150
  60.7 9.5 %shard_map.39 = (bf16[2,8,64,128]{3,2,1,0:T(8,128)(2,1)S(1)}, bf16[2,8,64,128]{3,2,1,0:T(8,128)(2,1)S(1)}, bf16[2,8,64,128]{3,2,1,0:T(8,128)(2,1)S(1)}, bf16[2,8,64,128]{3,2,1,0:T(8,128)(2,1)S(1)}) custom-call(bf16[8,2,10,32,128]{4,3,2,1,0:T(8,128)(2,1)S(1)} %all-to-all-done.refs_0_.vol_ref, bf16[8,2,10,32,128]{4,3,2,1,0:T(8,128)(2,1)} %all-to-all-done.1.refs_1_, ...), custom_call_target="tpu_custom_call" | custom-call | flops 7247757312 | bytes 10000000 | tf_op jit(solution)/shard_map/pallas_call | solution.py:111
  70.9 1.4 %collective-permute-start.6 = (bf16[2,8,64,128]{3,2,1,0:T(8,128)(2,1)S(1)}, bf16[2,8,64,128]{3,2,1,0:T(8,128)(2,1)S(1)}, u32[]{:S(2)}, u32[]{:S(2)}) collective-permute-start(bf16[2,8,64,128]{3,2,1,0:T(8,128)(2,1)S(1)} %get-tuple-element.21), channel_id=1, source_target_pairs={{0,4},{1,5},{2,6},{3,7},{4,0},{5,1},{6,2},{7,3},{8,12},{9,13},{10,... | collective-permute-start | bytes 786440 | tf_op jit(solution)/shard_map/ppermute | solution.py:134
  72.2 1.5 %collective-permute-start.5 = (bf16[2,8,64,128]{3,2,1,0:T(8,128)(2,1)S(1)}, bf16[2,8,64,128]{3,2,1,0:T(8,128)(2,1)S(1)}, u32[]{:S(2)}, u32[]{:S(2)}) collective-permute-start(bf16[2,8,64,128]{3,2,1,0:T(8,128)(2,1)S(1)} %get-tuple-element.20), channel_id=1, source_target_pairs={{0,2},{1,3},{2,0},{3,1},{4,6},{5,7},{6,4},{7,5},{8,10},{9,11},{10,... | collective-permute-start | bytes 786440 | tf_op jit(solution)/shard_map/ppermute | solution.py:134
  73.8 9.9 %shard_map.41 = (bf16[2,8,64,128]{3,2,1,0:T(8,128)(2,1)S(1)}, bf16[2,8,64,128]{3,2,1,0:T(8,128)(2,1)S(1)}, bf16[2,8,64,128]{3,2,1,0:T(8,128)(2,1)S(1)}, bf16[2,8,64,128]{3,2,1,0:T(8,128)(2,1)S(1)}) custom-call(bf16[8,2,10,32,128]{4,3,2,1,0:T(8,128)(2,1)S(1)} %all-to-all-done.refs_0_.vol_ref, bf16[8,2,10,32,128]{4,3,2,1,0:T(8,128)(2,1)} %all-to-all-done.1.refs_1_, ...), custom_call_target="tpu_custom_call" | custom-call | flops 7247757312 | bytes 10000000 | tf_op jit(solution)/shard_map/pallas_call | solution.py:111
  84.3 1.4 %collective-permute-start.12 = (bf16[2,8,64,128]{3,2,1,0:T(8,128)(2,1)S(1)}, bf16[2,8,64,128]{3,2,1,0:T(8,128)(2,1)S(1)}, u32[]{:S(2)}, u32[]{:S(2)}) collective-permute-start(bf16[2,8,64,128]{3,2,1,0:T(8,128)(2,1)S(1)} %get-tuple-element.27), channel_id=1, source_target_pairs={{0,4},{1,5},{2,6},{3,7},{4,0},{5,1},{6,2},{7,3},{8,12},{9,13},{10,... | collective-permute-start | bytes 786440 | tf_op jit(solution)/shard_map/ppermute | solution.py:134
  85.7 1.6 %collective-permute-start.11 = (bf16[2,8,64,128]{3,2,1,0:T(8,128)(2,1)S(1)}, bf16[2,8,64,128]{3,2,1,0:T(8,128)(2,1)S(1)}, u32[]{:S(2)}, u32[]{:S(2)}) collective-permute-start(bf16[2,8,64,128]{3,2,1,0:T(8,128)(2,1)S(1)} %get-tuple-element.26), channel_id=1, source_target_pairs={{0,2},{1,3},{2,0},{3,1},{4,6},{5,7},{6,4},{7,5},{8,10},{9,11},{10,... | collective-permute-start | bytes 786440 | tf_op jit(solution)/shard_map/ppermute | solution.py:134
  87.6 6.1 %collective-permute-done.13 = bf16[2,8,64,128]{3,2,1,0:T(8,128)(2,1)S(1)} collective-permute-done((bf16[2,8,64,128]{3,2,1,0:T(8,128)(2,1)S(1)}, bf16[2,8,64,128]{3,2,1,0:T(8,128)(2,1)S(1)}, u32[]{:S(2)}, u32[]{:S(2)}) %collective-permute-start.13) | collective-permute-done | bytes 262176 | tf_op jit(solution)/shard_map/ppermute | solution.py:134
  93.7 2.7 %collective-permute-done.12 = bf16[2,8,64,128]{3,2,1,0:T(8,128)(2,1)S(1)} collective-permute-done((bf16[2,8,64,128]{3,2,1,0:T(8,128)(2,1)S(1)}, bf16[2,8,64,128]{3,2,1,0:T(8,128)(2,1)S(1)}, u32[]{:S(2)}, u32[]{:S(2)}) %collective-permute-start.12) | collective-permute-done | bytes 262176 | tf_op jit(solution)/shard_map/ppermute | solution.py:134
  100.0 1.6 %pad_maximum_fusion = bf16[4,32,64,128]{3,2,1,0:T(8,128)(2,1)} fusion(bf16[1,32,64,128]{3,2,1,0:T(8,128)(2,1)S(1)} %get-tuple-element.34, bf16[2,32,64,128]{3,2,1,0:T(8,128)(2,1)S(1)} %bitcast.62, bf16[1,32,64,128]{3,2,1,0:T(8,128)(2,1)S(1)} %get-tuple-element.33), kind=kLoop, calls=%fused_computation.1 | loop fusion | flops 2097152 | bytes 4194304 | tf_op jit(solution)/shard_map/concatenate | solution.py:188
  (73 shorter events, 10.1 us)
Async XLA Ops:
  0.0 13.3 %collective-permute-start = (bf16[3,3,3,32,256]{4,3,2,1,0:T(8,128)(2,1)}, bf16[3,3,3,32,256]{4,3,2,1,0:T(8,128)(2,1)S(1)}, u32[]{:S(2)}, u32[]{:S(2)}) collective-permute-start(bf16[3,3,3,32,256]{4,3,2,1,0:T(8,128)(2,1)} %param.4), channel_id=1, source_target_pairs={{0,2},{1,3},{2,0},{3,1},{4,6},{5,7},{6,4},{7,5},{8,10},{9,11},{10,... | collective-permute-start | bytes 1327112 | tf_op jit(solution)/shard_map/ppermute | solution.py:134
  2.9 12.4 %collective-permute-start.1 = (bf16[3,3,3,32,256]{4,3,2,1,0:T(8,128)(2,1)}, bf16[3,3,3,32,256]{4,3,2,1,0:T(8,128)(2,1)S(1)}, u32[]{:S(2)}, u32[]{:S(2)}) collective-permute-start(bf16[3,3,3,32,256]{4,3,2,1,0:T(8,128)(2,1)} %param.4), channel_id=1, source_target_pairs={{0,4},{1,5},{2,6},{3,7},{4,0},{5,1},{6,2},{7,3},{8,12},{9,13},{10,... | collective-permute-start | bytes 1327112 | tf_op jit(solution)/shard_map/ppermute | solution.py:134
  7.7 30.3 %all-to-all-start = ((bf16[8,2,10,32,128]{4,3,2,1,0:T(8,128)(2,1)}), bf16[8,2,10,32,128]{4,3,2,1,0:T(8,128)(2,1)S(1)}, u32[]{:S(2)}, u32[]{:S(2)}) async-start(bf16[8,2,10,32,128]{4,3,2,1,0:T(8,128)(2,1)} %shard_map.37), calls=%async_computation | async-start | bytes 2621440 | tf_op jit(solution)/shard_map/all_to_all | solution.py:148
  11.3 22.3 %copy-start.1 = (bf16[3,3,3,32,256]{4,3,2,1,0:T(8,128)(2,1)S(1)}, bf16[3,3,3,32,256]{4,3,2,1,0:T(8,128)(2,1)}, u32[]{:S(2)}) copy-start(bf16[3,3,3,32,256]{4,3,2,1,0:T(8,128)(2,1)} %param.4) | copy-start | bytes 1327108
  13.3 20.2 %collective-permute-start.2 = (bf16[3,3,3,16,256]{4,3,2,1,0:T(8,128)(2,1)S(1)}, bf16[3,3,3,16,256]{4,3,2,1,0:T(8,128)(2,1)S(1)}, u32[]{:S(2)}, u32[]{:S(2)}) collective-permute-start(bf16[3,3,3,16,256]{4,3,2,1,0:T(8,128)(2,1)S(1)} %slice.126), channel_id=1, source_target_pairs={{0,4},{1,5},{2,6},{3,7},{4,0},{5,1},{6,2},{7,3},{8,12},{9,13},{10,... | collective-permute-start | bytes 663560 | tf_op jit(solution)/shard_map/ppermute | solution.py:134
  15.4 18.2 %copy-start = (bf16[3,3,3,32,256]{4,3,2,1,0:T(8,128)(2,1)}, bf16[3,3,3,32,256]{4,3,2,1,0:T(8,128)(2,1)S(1)}, u32[]{:S(2)}) copy-start(bf16[3,3,3,32,256]{4,3,2,1,0:T(8,128)(2,1)S(1)} %collective-permute-done.1) | copy-start | bytes 1327108
  15.4 18.2 %collective-permute-start.3 = (bf16[3,3,3,16,256]{4,3,2,1,0:T(8,128)(2,1)S(1)}, bf16[3,3,3,16,256]{4,3,2,1,0:T(8,128)(2,1)S(1)}, u32[]{:S(2)}, u32[]{:S(2)}) collective-permute-start(bf16[3,3,3,16,256]{4,3,2,1,0:T(8,128)(2,1)S(1)} %slice.127), channel_id=1, source_target_pairs={{0,2},{1,3},{2,0},{3,1},{4,6},{5,7},{6,4},{7,5},{8,10},{9,11},{10,... | collective-permute-start | bytes 663560 | tf_op jit(solution)/shard_map/ppermute | solution.py:134
  34.9 1.2 %slice-start = ((bf16[4,32,64,128]{3,2,1,0:T(8,128)(2,1)}), bf16[2,32,64,128]{3,2,1,0:T(8,128)(2,1)S(1)}, s32[]{:S(2)}) async-start(bf16[4,32,64,128]{3,2,1,0:T(8,128)(2,1)} %param.3), calls=%async_computation.2 | async-start | bytes 2097152 | tf_op jit(solution)/shard_map/slice | solution.py:149
  34.9 25.7 %collective-permute-start.4 = (bf16[4,3,3,3,32,256]{5,4,3,2,1,0:T(8,128)(2,1)S(1)}, bf16[4,3,3,3,32,256]{5,4,3,2,1,0:T(8,128)(2,1)}, u32[]{:S(2)}, u32[]{:S(2)}) collective-permute-start(bf16[4,3,3,3,32,256]{5,4,3,2,1,0:T(8,128)(2,1)S(1)} %pad_maximum_fusion.1.refs_2_.refs_4_), channel_id=1, source_target_pairs={{0,1},{1,0},{2,3},{3,2},{4,5},{5,4},{6,7},{7,6},{8,9},{9,8},{10,11... | collective-permute-start | bytes 5308424 | tf_op jit(solution)/shard_map/ppermute | solution.py:134
  38.0 4.5 %copy-start.2 = (f32[256]{0:T(256)S(1)}, f32[256]{0:T(256)}, u32[]{:S(2)}) copy-start(f32[256]{0:T(256)} %param.5) | copy-start | bytes 3076
  38.0 22.6 %all-to-all-start.1 = ((bf16[8,2,10,32,128]{4,3,2,1,0:T(8,128)(2,1)}), bf16[8,2,10,32,128]{4,3,2,1,0:T(8,128)(2,1)}, u32[]{:S(2)}, u32[]{:S(2)}) async-start(bf16[8,2,10,32,128]{4,3,2,1,0:T(8,128)(2,1)} %shard_map.38), calls=%async_computation.1 | async-start | bytes 2621440 | tf_op jit(solution)/shard_map/all_to_all | solution.py:150
  44.6 29.1 %collective-permute-start.10 = (bf16[8,1,10,32,128]{4,3,2,1,0:T(8,128)(2,1)}, bf16[8,1,10,32,128]{4,3,2,1,0:T(8,128)(2,1)}, u32[]{:S(2)}, u32[]{:S(2)}) collective-permute-start(bf16[8,1,10,32,128]{4,3,2,1,0:T(8,128)(2,1)} %get-tuple-element.24), channel_id=1, source_target_pairs={{8,0},{16,8},{24,16},{9,1},{17,9},{25,17},{10,2},{18,10},{26,18},{... | collective-permute-start | bytes 1966088 | tf_op jit(solution)/shard_map/ppermute | solution.py:182
  45.9 27.9 %collective-permute-start.9 = (bf16[8,1,10,32,128]{4,3,2,1,0:T(8,128)(2,1)}, bf16[8,1,10,32,128]{4,3,2,1,0:T(8,128)(2,1)}, u32[]{:S(2)}, u32[]{:S(2)}) collective-permute-start(bf16[8,1,10,32,128]{4,3,2,1,0:T(8,128)(2,1)} %get-tuple-element.23), channel_id=1, source_target_pairs={{0,8},{8,16},{16,24},{1,9},{9,17},{17,25},{2,10},{10,18},{18,26},{... | collective-permute-start | bytes 1966088 | tf_op jit(solution)/shard_map/ppermute | solution.py:183
  70.2 15.5 %collective-permute-start.7 = (bf16[2,8,64,128]{3,2,1,0:T(8,128)(2,1)S(1)}, bf16[2,8,64,128]{3,2,1,0:T(8,128)(2,1)S(1)}, u32[]{:S(2)}, u32[]{:S(2)}) collective-permute-start(bf16[2,8,64,128]{3,2,1,0:T(8,128)(2,1)S(1)} %get-tuple-element.22), channel_id=1, source_target_pairs={{0,6},{1,7},{2,4},{3,5},{4,2},{5,3},{6,0},{7,1},{8,14},{9,15},{10,... | collective-permute-start | bytes 786440 | tf_op jit(solution)/shard_map/ppermute | solution.py:134
  70.9 16.5 %collective-permute-start.6 = (bf16[2,8,64,128]{3,2,1,0:T(8,128)(2,1)S(1)}, bf16[2,8,64,128]{3,2,1,0:T(8,128)(2,1)S(1)}, u32[]{:S(2)}, u32[]{:S(2)}) collective-permute-start(bf16[2,8,64,128]{3,2,1,0:T(8,128)(2,1)S(1)} %get-tuple-element.21), channel_id=1, source_target_pairs={{0,4},{1,5},{2,6},{3,7},{4,0},{5,1},{6,2},{7,3},{8,12},{9,13},{10,... | collective-permute-start | bytes 786440 | tf_op jit(solution)/shard_map/ppermute | solution.py:134
  72.2 15.2 %collective-permute-start.5 = (bf16[2,8,64,128]{3,2,1,0:T(8,128)(2,1)S(1)}, bf16[2,8,64,128]{3,2,1,0:T(8,128)(2,1)S(1)}, u32[]{:S(2)}, u32[]{:S(2)}) collective-permute-start(bf16[2,8,64,128]{3,2,1,0:T(8,128)(2,1)S(1)} %get-tuple-element.20), channel_id=1, source_target_pairs={{0,2},{1,3},{2,0},{3,1},{4,6},{5,7},{6,4},{7,5},{8,10},{9,11},{10,... | collective-permute-start | bytes 786440 | tf_op jit(solution)/shard_map/ppermute | solution.py:134
  83.7 10.0 %collective-permute-start.13 = (bf16[2,8,64,128]{3,2,1,0:T(8,128)(2,1)S(1)}, bf16[2,8,64,128]{3,2,1,0:T(8,128)(2,1)S(1)}, u32[]{:S(2)}, u32[]{:S(2)}) collective-permute-start(bf16[2,8,64,128]{3,2,1,0:T(8,128)(2,1)S(1)} %get-tuple-element.28), channel_id=1, source_target_pairs={{0,6},{1,7},{2,4},{3,5},{4,2},{5,3},{6,0},{7,1},{8,14},{9,15},{10,... | collective-permute-start | bytes 786440 | tf_op jit(solution)/shard_map/ppermute | solution.py:134
  84.3 12.1 %collective-permute-start.12 = (bf16[2,8,64,128]{3,2,1,0:T(8,128)(2,1)S(1)}, bf16[2,8,64,128]{3,2,1,0:T(8,128)(2,1)S(1)}, u32[]{:S(2)}, u32[]{:S(2)}) collective-permute-start(bf16[2,8,64,128]{3,2,1,0:T(8,128)(2,1)S(1)} %get-tuple-element.27), channel_id=1, source_target_pairs={{0,4},{1,5},{2,6},{3,7},{4,0},{5,1},{6,2},{7,3},{8,12},{9,13},{10,... | collective-permute-start | bytes 786440 | tf_op jit(solution)/shard_map/ppermute | solution.py:134
  85.7 10.7 %collective-permute-start.11 = (bf16[2,8,64,128]{3,2,1,0:T(8,128)(2,1)S(1)}, bf16[2,8,64,128]{3,2,1,0:T(8,128)(2,1)S(1)}, u32[]{:S(2)}, u32[]{:S(2)}) collective-permute-start(bf16[2,8,64,128]{3,2,1,0:T(8,128)(2,1)S(1)} %get-tuple-element.26), channel_id=1, source_target_pairs={{0,2},{1,3},{2,0},{3,1},{4,6},{5,7},{6,4},{7,5},{8,10},{9,11},{10,... | collective-permute-start | bytes 786440 | tf_op jit(solution)/shard_map/ppermute | solution.py:134
  87.5 9.9 %collective-permute-start.8 = (bf16[4,2,8,32,128]{4,3,2,1,0:T(8,128)(2,1)S(1)}, bf16[4,2,8,32,128]{4,3,2,1,0:T(8,128)(2,1)S(1)}, u32[]{:S(2)}, u32[]{:S(2)}) collective-permute-start(bf16[4,2,8,32,128]{4,3,2,1,0:T(8,128)(2,1)S(1)} %pad_maximum_fusion.2), channel_id=1, source_target_pairs={{0,1},{1,0},{2,3},{3,2},{4,5},{5,4},{6,7},{7,6},{8,9},{9,8},{10,11... | collective-permute-start | bytes 1572872 | tf_op jit(solution)/shard_map/ppermute | solution.py:134
  96.6 2.0 %collective-permute-start.14 = (bf16[4,2,8,32,128]{4,3,2,1,0:T(8,128)(2,1)S(1)}, bf16[4,2,8,32,128]{4,3,2,1,0:T(8,128)(2,1)S(1)}, u32[]{:S(2)}, u32[]{:S(2)}) collective-permute-start(bf16[4,2,8,32,128]{4,3,2,1,0:T(8,128)(2,1)S(1)} %pad_maximum_fusion.3), channel_id=1, source_target_pairs={{0,1},{1,0},{2,3},{3,2},{4,5},{5,4},{6,7},{7,6},{8,9},{9,8},{10,11... | collective-permute-start | bytes 1572872 | tf_op jit(solution)/shard_map/ppermute | solution.py:134

commit v16 on v15

--- a/solution.py
+++ b/solution.py
@@ -54,7 +54,7 @@
     )(volume)
 
 
-def conv_kernel(plan, rows_at_once, pieces_count, tap_count, *refs):
+def conv_kernel(plan, rows_at_once, pieces_count, tap_count, order, *refs):
     refs = list(refs)
     pieces = [refs.pop(0) for _ in range(pieces_count)]
     tap_parts = [refs.pop(0) for _ in range(tap_count)]
@@ -63,7 +63,7 @@
     rows = rows_in - 2
     total_out = bias_ref.shape[0]
     block = total_out // len(outs)
-    groups, size = tap_parts[0].shape[0], tap_parts[0].shape[4]
+    size = tap_parts[0].shape[4]
     lane = lax.broadcasted_iota(jnp.int32, (total_out, cols), 1)
 
     def tile(slot, row):
@@ -79,14 +79,14 @@
                 cells.append(jnp.concatenate(lines[b : b + rows_at_once], axis=1))
                 weights.append(
                     jnp.concatenate(
-                        [part[g, a, b].reshape(3 * size, -1) for g in range(groups) for part in tap_parts], axis=0
+                        [tap_parts[n][g, a, b].reshape(3 * size, -1) for n, g in order], axis=0
                     )
                 )
         total = jnp.dot(
             jnp.concatenate(weights, axis=1), jnp.concatenate(cells, axis=0), preferred_element_type=jnp.float32
         )
         for r in range(rows_at_once):
-            part = total[:, r * cols : (r + 1) * cols].reshape(groups * tap_count, 3, size, cols)
+            part = total[:, r * cols : (r + 1) * cols].reshape(len(order), 3, size, cols)
             side = [part[:, c].reshape(total_out, cols) for c in range(3)]
             left = jnp.where(lane == 0, 0.0, pltpu.roll(side[0], 1, 1))
             right = jnp.where(lane == cols - 1, 0.0, pltpu.roll(side[2], cols - 1, 1))
@@ -100,7 +100,7 @@
             tile(slot, row)
 
 
-def convolve(plan, pieces, tap_parts, bias, blocks):
+def convolve(plan, pieces, tap_parts, tap_order, bias, blocks):
     rows, cols = pieces[0].shape[2] - 2, pieces[0].shape[4]
     in_chan = tap_parts[0].shape[5]
     total_out = bias.shape[0]
@@ -109,7 +109,7 @@
     in_vmem = pl.BlockSpec(memory_space=pltpu.VMEM)
     shape = jax.ShapeDtypeStruct((len(plan), rows, total_out // blocks, cols), jnp.bfloat16)
     return pl.pallas_call(
-        functools.partial(conv_kernel, plan, min(ROWS, rows), len(pieces), len(tap_parts)),
+        functools.partial(conv_kernel, plan, min(ROWS, rows), len(pieces), len(tap_parts), tap_order),
         out_shape=[shape] * blocks,
         in_specs=[in_vmem] * (len(pieces) + len(tap_parts) + 1),
         out_specs=[in_vmem] * blocks,
@@ -134,20 +134,19 @@
         return lax.ppermute(array, axis, [(i, i ^ k) for i in range(lax.axis_size(axis))])
 
 
-    near = [swap(kernel, k) for k in across[1 : 3 if len(across) == 4 else None]]
-    if len(across) == 4:
-        half = out_chan // 2
-        by_x, by_y = near
-        far = [swap(by_x[:, :, :, :half], across[2]), swap(by_y[:, :, :, half:], across[1])]
-        fetched = [kernel, by_x, by_y, jnp.concatenate(far, axis=3)]
-    else:
-        fetched = [kernel, *near]
-    same = jnp.stack(fetched)
+    half = out_chan // 2
+    odd = lax.axis_index("slab") % 2
+    mine = lax.dynamic_slice_in_dim(kernel, odd * half, half, 3)
+    mine = [swap(mine, k) for k in across[1:]]
+    outer = lax.all_to_all(cut(jnp.concatenate([features[:1], features[-1:]]), parts), "filt", 0, 0)
+    between = lax.optimization_barrier((features[1:-1], mine))[0]
+    inner = lax.all_to_all(cut(between, parts), "filt", 0, 0)
+    mine = jnp.stack(mine)
+    theirs = lax.optimization_barrier((swap(mine, 1, "slab"), outer))[0]
+    rest = jnp.concatenate([jnp.where(odd == 0, mine, theirs), jnp.where(odd == 0, theirs, mine)], axis=4)
+    same = jnp.concatenate([kernel[None], rest])
     tap_parts = [same, swap(same, 1)]
-
-    outer = lax.all_to_all(cut(jnp.concatenate([features[:1], features[-1:]]), parts), "filt", 0, 0)
-    between = lax.optimization_barrier((features[1:-1], near))[0]
-    inner = lax.all_to_all(cut(between, parts), "filt", 0, 0)
+    tap_order = tuple((n, g) for g in range(len(across)) for n in range(2))
     arrived = outer
     order = jnp.stack([me ^ k ^ c for k in across for c in range(2)])
     bias = jnp.take(bias_vector.reshape(parts, out_chan), order, axis=0).reshape(-1)
@@ -157,9 +156,9 @@
         return array.transpose(1, 2, 0, 3, 4).reshape(1, -1, rows + 2, parts * chan, cols)
 
     if not aligned:
-        joined = jnp.stack(tap_parts, axis=1).transpose(2, 3, 4, 0, 1, 5, 6)
+        joined = jnp.stack([tap_parts[n][g] for n, g in tap_order]).transpose(1, 2, 3, 0, 4, 5)
         tap_parts = [joined.reshape(1, 3, 3, 3, parts * out_chan, -1)]
-        outer, inner = settle(outer), settle(inner)
+        tap_order = ((0, 0),)
 
     def send_back(results):
         count = results[0].shape[0]
@@ -175,7 +174,9 @@
     blocks = len(across)
     where = [(0, 0)] + [(1, plane) for plane in range(planes - 2)] + [(0, 1)]
     middle = tuple(tuple(where[plane - 1 : plane + 2]) for plane in range(1, planes - 1))
-    inside = send_back(convolve(middle, [outer, inner], tap_parts, bias, blocks))
+    results = convolve(middle, [outer, inner], tap_parts, tap_order, bias, blocks)
+    inside = send_back(results)
+    later_bias = lax.optimization_barrier((bias, results))[0]
     up = [(i, i + 1) for i in range(slabs - 1)]
     down = [(i + 1, i) for i in range(slabs - 1)]
     first, last = edges_of(arrived)
@@ -183,7 +184,7 @@
     before = lax.ppermute(last, "slab", up)
 
     ends = (((2, 0), *where[:2]), (*where[-2:], (3, 0)))
-    outside = send_back(convolve(ends, [outer, inner, settle(before), settle(after)], tap_parts, bias, blocks))
+    outside = send_back(convolve(ends, [outer, inner, settle(before), settle(after)], tap_parts, tap_order, later_bias, blocks))
     inside, outside = lax.optimization_barrier((inside, outside))
     return jnp.concatenate([outside[:1], inside, outside[1:]])
 

time: 102 us -> 121 us (1.19)
  waiting for transfers between devices: 36.8 us -> 58.4 us
  starting transfers between devices: 31.2 us -> 28.8 us
    ppermute x13, waiting for transfers between devices: 27.5 us -> 49.1 us  [swap(): lax.ppermute(array, axis, [(i, i ^ k) for i in range(lax.axis_size(axis))])]
    ppermute x13, starting transfers between devices: 16.6 us -> 12.7 us  [swap(): lax.ppermute(array, axis, [(i, i ^ k) for i in range(lax.axis_size(axis))])]
    all_to_all x1, starting transfers between devices: 3.57 us -> 5.17 us  [body(): lax.all_to_all(cut(jnp.concatenate([features[:1], features[-1:]]), parts)...]
  transfers between devices with their start and end apart: 17 -> 17, of which waited for: 7 -> 7; matrix products, arithmetic and copies ran while one was open for 6% -> 2% of each run, Pallas kernels for 23% -> 18%
where the time goes in v16:
time: 121 us
  waiting for transfers between devices  58.4 us (48%)
  starting transfers between devices  28.8 us (24%)
  Pallas kernels  22.9 us (19%)
  local copies, waits for them, and re-layouts  6.78 us (6%)
  other arithmetic  3.39 us (3%)
    ppermute x13, waiting for transfers between devices, swap(): lax.ppermute(array, axis, [(i, i ^ k) for i in range(lax.axis_size(axis))])  49.1 us
    pallas_call x2, Pallas kernels, convolve(): pl.pallas_call(functools.partial(conv_kernel, plan, min(ROWS, rows), len(...  19.4 us
    ppermute x13, starting transfers between devices, swap(): lax.ppermute(array, axis, [(i, i ^ k) for i in range(lax.axis_size(axis))])  12.7 us
    all_to_all x1, waiting for transfers between devices, body(): inner = lax.all_to_all(cut(between, parts), 'filt', 0, 0)  9.31 us
    ppermute x1, starting transfers between devices, body(): before = lax.ppermute(last, 'slab', up)  5.4 us
    all_to_all x1, starting transfers between devices, body(): lax.all_to_all(cut(jnp.concatenate([features[:1], features[-1:]]), parts)...  5.17 us
    all_to_all x1, starting transfers between devices, body(): inner = lax.all_to_all(cut(between, parts), 'filt', 0, 0)  4.27 us
  transfers between devices with their start and end apart: 17, of which 7 were waited for; matrix products, arithmetic and copies ran while one was open for 2% of the time, Pallas kernels for 18%

profile of v16, /device:TPU:0, one launch (start us, length us, event | category | flops | bytes accessed | tf_op | source)
XLA Modules:
  0.0 120.7 jit_solution(11503703475023503500)
XLA Ops:
  0.0 1.3 %fusion.1 = (bf16[1,32,64,128]{3,2,1,0:T(8,128)(2,1)S(1)}, bf16[1,32,64,128]{3,2,1,0:T(8,128)(2,1)S(1)}) fusion(bf16[4,32,64,128]{3,2,1,0:T(8,128)(2,1)} %param.3), kind=kLoop, calls=%fused_computation.48 | loop fusion | bytes 2097152 | tf_op jit(solution)/shard_map/slice | solution.py:141
  2.1 1.2 shard_map.37
  3.3 5.2 %all-to-all-start = ((bf16[8,2,10,32,128]{4,3,2,1,0:T(8,128)(2,1)}), bf16[8,2,10,32,128]{4,3,2,1,0:T(8,128)(2,1)S(1)}, u32[]{:S(2)}, u32[]{:S(2)}) async-start(bf16[8,2,10,32,128]{4,3,2,1,0:T(8,128)(2,1)} %shard_map.37), calls=%async_computation | async-start | bytes 2621440 | tf_op jit(solution)/shard_map/all_to_all | solution.py:141
  8.5 2.1 %collective-permute-start = (bf16[3,3,3,16,256]{4,3,2,1,0:T(8,128)(2,1)S(1)}, bf16[3,3,3,16,256]{4,3,2,1,0:T(8,128)(2,1)S(1)}, u32[]{:S(2)}, u32[]{:S(2)}) collective-permute-start(bf16[3,3,3,16,256]{4,3,2,1,0:T(8,128)(2,1)S(1)} %constant_dynamic-slice_fusion), channel_id=1, source_target_pairs={{0,2},{1,3},{2,0},{3,1},{4,6},{5,7},{6,4},{7,5},{8,10},{9,11},{10,... | collective-permute-start | bytes 663560 | tf_op jit(solution)/shard_map/ppermute | solution.py:134
  10.5 1.5 %collective-permute-start.1 = (bf16[3,3,3,16,256]{4,3,2,1,0:T(8,128)(2,1)S(1)}, bf16[3,3,3,16,256]{4,3,2,1,0:T(8,128)(2,1)S(1)}, u32[]{:S(2)}, u32[]{:S(2)}) collective-permute-start(bf16[3,3,3,16,256]{4,3,2,1,0:T(8,128)(2,1)S(1)} %constant_dynamic-slice_fusion), channel_id=1, source_target_pairs={{0,4},{1,5},{2,6},{3,7},{4,0},{5,1},{6,2},{7,3},{8,12},{9,13},{10,... | collective-permute-start | bytes 663560 | tf_op jit(solution)/shard_map/ppermute | solution.py:134
  12.1 18.9 %collective-permute-done = bf16[3,3,3,16,256]{4,3,2,1,0:T(8,128)(2,1)S(1)} collective-permute-done((bf16[3,3,3,16,256]{4,3,2,1,0:T(8,128)(2,1)S(1)}, bf16[3,3,3,16,256]{4,3,2,1,0:T(8,128)(2,1)S(1)}, u32[]{:S(2)}, u32[]{:S(2)}) %collective-permute-start) | collective-permute-done | bytes 221216 | tf_op jit(solution)/shard_map/ppermute | solution.py:134
  31.0 5.2 %collective-permute-done.2 = bf16[3,3,3,16,256]{4,3,2,1,0:T(8,128)(2,1)S(1)} collective-permute-done((bf16[3,3,3,16,256]{4,3,2,1,0:T(8,128)(2,1)S(1)}, bf16[3,3,3,16,256]{4,3,2,1,0:T(8,128)(2,1)S(1)}, u32[]{:S(2)}, u32[]{:S(2)}) %collective-permute-start.2) | collective-permute-done | bytes 221216 | tf_op jit(solution)/shard_map/ppermute | solution.py:134
  36.3 1.6 %collective-permute-start.3 = (bf16[3,3,3,3,16,256]{5,4,3,2,1,0:T(8,128)(2,1)S(1)}, bf16[3,3,3,3,16,256]{5,4,3,2,1,0:T(8,128)(2,1)}, u32[]{:S(2)}, u32[]{:S(2)}) collective-permute-start(bf16[3,3,3,3,16,256]{5,4,3,2,1,0:T(8,128)(2,1)S(1)} %pad_maximum_fusion.1), channel_id=1, source_target_pairs={{0,8},{8,0},{16,24},{24,16},{1,9},{9,1},{17,25},{25,17},{2,10},{10... | collective-permute-start | bytes 1990664 | tf_op jit(solution)/shard_map/ppermute | solution.py:134
  37.9 15.0 %collective-permute-done.3 = bf16[3,3,3,3,16,256]{5,4,3,2,1,0:T(8,128)(2,1)} collective-permute-done((bf16[3,3,3,3,16,256]{5,4,3,2,1,0:T(8,128)(2,1)S(1)}, bf16[3,3,3,3,16,256]{5,4,3,2,1,0:T(8,128)(2,1)}, u32[]{:S(2)}, u32[]{:S(2)}) %collective-permute-start.3) | collective-permute-done | bytes 663584 | tf_op jit(solution)/shard_map/ppermute | solution.py:134
  52.9 1.2 broadcast_select_fusion.1
  56.0 1.2 shard_map.38
  57.2 4.3 %all-to-all-start.1 = ((bf16[8,2,10,32,128]{4,3,2,1,0:T(8,128)(2,1)}), bf16[8,2,10,32,128]{4,3,2,1,0:T(8,128)(2,1)}, u32[]{:S(2)}, u32[]{:S(2)}) async-start(bf16[8,2,10,32,128]{4,3,2,1,0:T(8,128)(2,1)} %shard_map.38), calls=%async_computation.1 | async-start | bytes 2621440 | tf_op jit(solution)/shard_map/all_to_all | solution.py:143
  63.7 1.3 %collective-permute-start.10 = (bf16[8,1,10,32,128]{4,3,2,1,0:T(8,128)(2,1)}, bf16[8,1,10,32,128]{4,3,2,1,0:T(8,128)(2,1)}, u32[]{:S(2)}, u32[]{:S(2)}) collective-permute-start(bf16[8,1,10,32,128]{4,3,2,1,0:T(8,128)(2,1)} %get-tuple-element.27), channel_id=1, source_target_pairs={{8,0},{16,8},{24,16},{9,1},{17,9},{25,17},{10,2},{18,10},{26,18},{... | collective-permute-start | bytes 1966088 | tf_op jit(solution)/shard_map/ppermute | solution.py:183
  65.0 5.4 %collective-permute-start.9 = (bf16[8,1,10,32,128]{4,3,2,1,0:T(8,128)(2,1)}, bf16[8,1,10,32,128]{4,3,2,1,0:T(8,128)(2,1)}, u32[]{:S(2)}, u32[]{:S(2)}) collective-permute-start(bf16[8,1,10,32,128]{4,3,2,1,0:T(8,128)(2,1)} %get-tuple-element.26), channel_id=1, source_target_pairs={{0,8},{8,16},{16,24},{1,9},{9,17},{17,25},{2,10},{10,18},{18,26},{... | collective-permute-start | bytes 1966088 | tf_op jit(solution)/shard_map/ppermute | solution.py:184
  70.4 9.3 %all-to-all-done.1.refs_1_ = bf16[8,2,10,32,128]{4,3,2,1,0:T(8,128)(2,1)} async-done(((bf16[8,2,10,32,128]{4,3,2,1,0:T(8,128)(2,1)}), bf16[8,2,10,32,128]{4,3,2,1,0:T(8,128)(2,1)}, u32[]{:S(2)}, u32[]{:S(2)}) %all-to-all-start.1) | async-done | bytes 1310752 | tf_op jit(solution)/shard_map/all_to_all | solution.py:143
  79.8 9.5 %shard_map.39 = (bf16[2,8,64,128]{3,2,1,0:T(8,128)(2,1)S(1)}, bf16[2,8,64,128]{3,2,1,0:T(8,128)(2,1)S(1)}, bf16[2,8,64,128]{3,2,1,0:T(8,128)(2,1)S(1)}, bf16[2,8,64,128]{3,2,1,0:T(8,128)(2,1)S(1)}) custom-call(bf16[8,2,10,32,128]{4,3,2,1,0:T(8,128)(2,1)S(1)} %all-to-all-done.refs_0_.vol_ref, bf16[8,2,10,32,128]{4,3,2,1,0:T(8,128)(2,1)} %all-to-all-done.1.refs_1_, ...), custom_call_target="tpu_custom_call" | custom-call | flops 7247757312 | bytes 10000000 | tf_op jit(solution)/shard_map/pallas_call | solution.py:111
  89.9 1.4 %collective-permute-start.6 = (bf16[2,8,64,128]{3,2,1,0:T(8,128)(2,1)S(1)}, bf16[2,8,64,128]{3,2,1,0:T(8,128)(2,1)S(1)}, u32[]{:S(2)}, u32[]{:S(2)}) collective-permute-start(bf16[2,8,64,128]{3,2,1,0:T(8,128)(2,1)S(1)} %get-tuple-element.24), channel_id=1, source_target_pairs={{0,4},{1,5},{2,6},{3,7},{4,0},{5,1},{6,2},{7,3},{8,12},{9,13},{10,... | collective-permute-start | bytes 786440 | tf_op jit(solution)/shard_map/ppermute | solution.py:134
  91.3 1.5 %collective-permute-start.5 = (bf16[2,8,64,128]{3,2,1,0:T(8,128)(2,1)S(1)}, bf16[2,8,64,128]{3,2,1,0:T(8,128)(2,1)S(1)}, u32[]{:S(2)}, u32[]{:S(2)}) collective-permute-start(bf16[2,8,64,128]{3,2,1,0:T(8,128)(2,1)S(1)} %get-tuple-element.23), channel_id=1, source_target_pairs={{0,2},{1,3},{2,0},{3,1},{4,6},{5,7},{6,4},{7,5},{8,10},{9,11},{10,... | collective-permute-start | bytes 786440 | tf_op jit(solution)/shard_map/ppermute | solution.py:134
  92.9 9.9 %shard_map.41 = (bf16[2,8,64,128]{3,2,1,0:T(8,128)(2,1)S(1)}, bf16[2,8,64,128]{3,2,1,0:T(8,128)(2,1)S(1)}, bf16[2,8,64,128]{3,2,1,0:T(8,128)(2,1)S(1)}, bf16[2,8,64,128]{3,2,1,0:T(8,128)(2,1)S(1)}) custom-call(bf16[8,2,10,32,128]{4,3,2,1,0:T(8,128)(2,1)S(1)} %all-to-all-done.refs_0_.vol_ref, bf16[8,2,10,32,128]{4,3,2,1,0:T(8,128)(2,1)} %all-to-all-done.1.refs_1_, ...), custom_call_target="tpu_custom_call" | custom-call | flops 7247757312 | bytes 10000000 | tf_op jit(solution)/shard_map/pallas_call | solution.py:111
  103.5 1.4 %collective-permute-start.12 = (bf16[2,8,64,128]{3,2,1,0:T(8,128)(2,1)S(1)}, bf16[2,8,64,128]{3,2,1,0:T(8,128)(2,1)S(1)}, u32[]{:S(2)}, u32[]{:S(2)}) collective-permute-start(bf16[2,8,64,128]{3,2,1,0:T(8,128)(2,1)S(1)} %get-tuple-element.31), channel_id=1, source_target_pairs={{0,4},{1,5},{2,6},{3,7},{4,0},{5,1},{6,2},{7,3},{8,12},{9,13},{10,... | collective-permute-start | bytes 786440 | tf_op jit(solution)/shard_map/ppermute | solution.py:134
  104.9 1.6 %collective-permute-start.11 = (bf16[2,8,64,128]{3,2,1,0:T(8,128)(2,1)S(1)}, bf16[2,8,64,128]{3,2,1,0:T(8,128)(2,1)S(1)}, u32[]{:S(2)}, u32[]{:S(2)}) collective-permute-start(bf16[2,8,64,128]{3,2,1,0:T(8,128)(2,1)S(1)} %get-tuple-element.30), channel_id=1, source_target_pairs={{0,2},{1,3},{2,0},{3,1},{4,6},{5,7},{6,4},{7,5},{8,10},{9,11},{10,... | collective-permute-start | bytes 786440 | tf_op jit(solution)/shard_map/ppermute | solution.py:134
  106.7 6.1 %collective-permute-done.13 = bf16[2,8,64,128]{3,2,1,0:T(8,128)(2,1)S(1)} collective-permute-done((bf16[2,8,64,128]{3,2,1,0:T(8,128)(2,1)S(1)}, bf16[2,8,64,128]{3,2,1,0:T(8,128)(2,1)S(1)}, u32[]{:S(2)}, u32[]{:S(2)}) %collective-permute-start.13) | collective-permute-done | bytes 262176 | tf_op jit(solution)/shard_map/ppermute | solution.py:134
  112.9 2.7 %collective-permute-done.12 = bf16[2,8,64,128]{3,2,1,0:T(8,128)(2,1)S(1)} collective-permute-done((bf16[2,8,64,128]{3,2,1,0:T(8,128)(2,1)S(1)}, bf16[2,8,64,128]{3,2,1,0:T(8,128)(2,1)S(1)}, u32[]{:S(2)}, u32[]{:S(2)}) %collective-permute-start.12) | collective-permute-done | bytes 262176 | tf_op jit(solution)/shard_map/ppermute | solution.py:134
  119.1 1.6 %pad_maximum_fusion = bf16[4,32,64,128]{3,2,1,0:T(8,128)(2,1)} fusion(bf16[1,32,64,128]{3,2,1,0:T(8,128)(2,1)S(1)} %get-tuple-element.40, bf16[2,32,64,128]{3,2,1,0:T(8,128)(2,1)S(1)} %bitcast.61, bf16[1,32,64,128]{3,2,1,0:T(8,128)(2,1)S(1)} %get-tuple-element.39), kind=kLoop, calls=%fused_computation.1 | loop fusion | flops 2097152 | bytes 4194304 | tf_op jit(solution)/shard_map/concatenate | solution.py:189
  (72 shorter events, 10.1 us)
Async XLA Ops:
  2.1 6.4 %copy-start = (bf16[3,3,3,32,256]{4,3,2,1,0:T(8,128)(2,1)S(1)}, bf16[3,3,3,32,256]{4,3,2,1,0:T(8,128)(2,1)}, u32[]{:S(2)}) copy-start(bf16[3,3,3,32,256]{4,3,2,1,0:T(8,128)(2,1)} %param.4) | copy-start | bytes 1327108
  3.3 49.6 %all-to-all-start = ((bf16[8,2,10,32,128]{4,3,2,1,0:T(8,128)(2,1)}), bf16[8,2,10,32,128]{4,3,2,1,0:T(8,128)(2,1)S(1)}, u32[]{:S(2)}, u32[]{:S(2)}) async-start(bf16[8,2,10,32,128]{4,3,2,1,0:T(8,128)(2,1)} %shard_map.37), calls=%async_computation | async-start | bytes 2621440 | tf_op jit(solution)/shard_map/all_to_all | solution.py:141
  8.5 22.5 %collective-permute-start = (bf16[3,3,3,16,256]{4,3,2,1,0:T(8,128)(2,1)S(1)}, bf16[3,3,3,16,256]{4,3,2,1,0:T(8,128)(2,1)S(1)}, u32[]{:S(2)}, u32[]{:S(2)}) collective-permute-start(bf16[3,3,3,16,256]{4,3,2,1,0:T(8,128)(2,1)S(1)} %constant_dynamic-slice_fusion), channel_id=1, source_target_pairs={{0,2},{1,3},{2,0},{3,1},{4,6},{5,7},{6,4},{7,5},{8,10},{9,11},{10,... | collective-permute-start | bytes 663560 | tf_op jit(solution)/shard_map/ppermute | solution.py:134
  10.5 20.5 %collective-permute-start.1 = (bf16[3,3,3,16,256]{4,3,2,1,0:T(8,128)(2,1)S(1)}, bf16[3,3,3,16,256]{4,3,2,1,0:T(8,128)(2,1)S(1)}, u32[]{:S(2)}, u32[]{:S(2)}) collective-permute-start(bf16[3,3,3,16,256]{4,3,2,1,0:T(8,128)(2,1)S(1)} %constant_dynamic-slice_fusion), channel_id=1, source_target_pairs={{0,4},{1,5},{2,6},{3,7},{4,0},{5,1},{6,2},{7,3},{8,12},{9,13},{10,... | collective-permute-start | bytes 663560 | tf_op jit(solution)/shard_map/ppermute | solution.py:134
  12.0 24.2 %collective-permute-start.2 = (bf16[3,3,3,16,256]{4,3,2,1,0:T(8,128)(2,1)S(1)}, bf16[3,3,3,16,256]{4,3,2,1,0:T(8,128)(2,1)S(1)}, u32[]{:S(2)}, u32[]{:S(2)}) collective-permute-start(bf16[3,3,3,16,256]{4,3,2,1,0:T(8,128)(2,1)S(1)} %constant_dynamic-slice_fusion), channel_id=1, source_target_pairs={{0,6},{1,7},{2,4},{3,5},{4,2},{5,3},{6,0},{7,1},{8,14},{9,15},{10,... | collective-permute-start | bytes 663560 | tf_op jit(solution)/shard_map/ppermute | solution.py:134
  36.3 16.6 %collective-permute-start.3 = (bf16[3,3,3,3,16,256]{5,4,3,2,1,0:T(8,128)(2,1)S(1)}, bf16[3,3,3,3,16,256]{5,4,3,2,1,0:T(8,128)(2,1)}, u32[]{:S(2)}, u32[]{:S(2)}) collective-permute-start(bf16[3,3,3,3,16,256]{5,4,3,2,1,0:T(8,128)(2,1)S(1)} %pad_maximum_fusion.1), channel_id=1, source_target_pairs={{0,8},{8,0},{16,24},{24,16},{1,9},{9,1},{17,25},{25,17},{2,10},{10... | collective-permute-start | bytes 1990664 | tf_op jit(solution)/shard_map/ppermute | solution.py:134
  54.1 1.2 %slice-start = ((bf16[4,32,64,128]{3,2,1,0:T(8,128)(2,1)}), bf16[2,32,64,128]{3,2,1,0:T(8,128)(2,1)S(1)}, s32[]{:S(2)}) async-start(bf16[4,32,64,128]{3,2,1,0:T(8,128)(2,1)} %param.3), calls=%async_computation.2 | async-start | bytes 2097152 | tf_op jit(solution)/shard_map/slice | solution.py:142
  54.3 25.4 %collective-permute-start.4 = (bf16[4,3,3,3,32,256]{5,4,3,2,1,0:T(8,128)(2,1)S(1)}, bf16[4,3,3,3,32,256]{5,4,3,2,1,0:T(8,128)(2,1)}, u32[]{:S(2)}, u32[]{:S(2)}) collective-permute-start(bf16[4,3,3,3,32,256]{5,4,3,2,1,0:T(8,128)(2,1)S(1)} %maximum_maximum_fusion.refs_2_.refs_4_), channel_id=1, source_target_pairs={{0,1},{1,0},{2,3},{3,2},{4,5},{5,4},{6,7},{7,6},{8,9},{9,8},{10,11... | collective-permute-start | bytes 5308424 | tf_op jit(solution)/shard_map/ppermute | solution.py:134
  56.0 5.5 %copy-start.1 = (f32[256]{0:T(256)S(1)}, f32[256]{0:T(256)}, u32[]{:S(2)}) copy-start(f32[256]{0:T(256)} %param.5) | copy-start | bytes 3076
  57.2 22.5 %all-to-all-start.1 = ((bf16[8,2,10,32,128]{4,3,2,1,0:T(8,128)(2,1)}), bf16[8,2,10,32,128]{4,3,2,1,0:T(8,128)(2,1)}, u32[]{:S(2)}, u32[]{:S(2)}) async-start(bf16[8,2,10,32,128]{4,3,2,1,0:T(8,128)(2,1)} %shard_map.38), calls=%async_computation.1 | async-start | bytes 2621440 | tf_op jit(solution)/shard_map/all_to_all | solution.py:143
  63.7 29.1 %collective-permute-start.10 = (bf16[8,1,10,32,128]{4,3,2,1,0:T(8,128)(2,1)}, bf16[8,1,10,32,128]{4,3,2,1,0:T(8,128)(2,1)}, u32[]{:S(2)}, u32[]{:S(2)}) collective-permute-start(bf16[8,1,10,32,128]{4,3,2,1,0:T(8,128)(2,1)} %get-tuple-element.27), channel_id=1, source_target_pairs={{8,0},{16,8},{24,16},{9,1},{17,9},{25,17},{10,2},{18,10},{26,18},{... | collective-permute-start | bytes 1966088 | tf_op jit(solution)/shard_map/ppermute | solution.py:183
  65.0 27.9 %collective-permute-start.9 = (bf16[8,1,10,32,128]{4,3,2,1,0:T(8,128)(2,1)}, bf16[8,1,10,32,128]{4,3,2,1,0:T(8,128)(2,1)}, u32[]{:S(2)}, u32[]{:S(2)}) collective-permute-start(bf16[8,1,10,32,128]{4,3,2,1,0:T(8,128)(2,1)} %get-tuple-element.26), channel_id=1, source_target_pairs={{0,8},{8,16},{16,24},{1,9},{9,17},{17,25},{2,10},{10,18},{18,26},{... | collective-permute-start | bytes 1966088 | tf_op jit(solution)/shard_map/ppermute | solution.py:184
  89.3 15.6 %collective-permute-start.7 = (bf16[2,8,64,128]{3,2,1,0:T(8,128)(2,1)S(1)}, bf16[2,8,64,128]{3,2,1,0:T(8,128)(2,1)S(1)}, u32[]{:S(2)}, u32[]{:S(2)}) collective-permute-start(bf16[2,8,64,128]{3,2,1,0:T(8,128)(2,1)S(1)} %get-tuple-element.25), channel_id=1, source_target_pairs={{0,6},{1,7},{2,4},{3,5},{4,2},{5,3},{6,0},{7,1},{8,14},{9,15},{10,... | collective-permute-start | bytes 786440 | tf_op jit(solution)/shard_map/ppermute | solution.py:134
  89.9 16.6 %collective-permute-start.6 = (bf16[2,8,64,128]{3,2,1,0:T(8,128)(2,1)S(1)}, bf16[2,8,64,128]{3,2,1,0:T(8,128)(2,1)S(1)}, u32[]{:S(2)}, u32[]{:S(2)}) collective-permute-start(bf16[2,8,64,128]{3,2,1,0:T(8,128)(2,1)S(1)} %get-tuple-element.24), channel_id=1, source_target_pairs={{0,4},{1,5},{2,6},{3,7},{4,0},{5,1},{6,2},{7,3},{8,12},{9,13},{10,... | collective-permute-start | bytes 786440 | tf_op jit(solution)/shard_map/ppermute | solution.py:134
  91.3 15.3 %collective-permute-start.5 = (bf16[2,8,64,128]{3,2,1,0:T(8,128)(2,1)S(1)}, bf16[2,8,64,128]{3,2,1,0:T(8,128)(2,1)S(1)}, u32[]{:S(2)}, u32[]{:S(2)}) collective-permute-start(bf16[2,8,64,128]{3,2,1,0:T(8,128)(2,1)S(1)} %get-tuple-element.23), channel_id=1, source_target_pairs={{0,2},{1,3},{2,0},{3,1},{4,6},{5,7},{6,4},{7,5},{8,10},{9,11},{10,... | collective-permute-start | bytes 786440 | tf_op jit(solution)/shard_map/ppermute | solution.py:134
  102.8 10.0 %collective-permute-start.13 = (bf16[2,8,64,128]{3,2,1,0:T(8,128)(2,1)S(1)}, bf16[2,8,64,128]{3,2,1,0:T(8,128)(2,1)S(1)}, u32[]{:S(2)}, u32[]{:S(2)}) collective-permute-start(bf16[2,8,64,128]{3,2,1,0:T(8,128)(2,1)S(1)} %get-tuple-element.32), channel_id=1, source_target_pairs={{0,6},{1,7},{2,4},{3,5},{4,2},{5,3},{6,0},{7,1},{8,14},{9,15},{10,... | collective-permute-start | bytes 786440 | tf_op jit(solution)/shard_map/ppermute | solution.py:134
  103.5 12.1 %collective-permute-start.12 = (bf16[2,8,64,128]{3,2,1,0:T(8,128)(2,1)S(1)}, bf16[2,8,64,128]{3,2,1,0:T(8,128)(2,1)S(1)}, u32[]{:S(2)}, u32[]{:S(2)}) collective-permute-start(bf16[2,8,64,128]{3,2,1,0:T(8,128)(2,1)S(1)} %get-tuple-element.31), channel_id=1, source_target_pairs={{0,4},{1,5},{2,6},{3,7},{4,0},{5,1},{6,2},{7,3},{8,12},{9,13},{10,... | collective-permute-start | bytes 786440 | tf_op jit(solution)/shard_map/ppermute | solution.py:134
  104.9 10.7 %collective-permute-start.11 = (bf16[2,8,64,128]{3,2,1,0:T(8,128)(2,1)S(1)}, bf16[2,8,64,128]{3,2,1,0:T(8,128)(2,1)S(1)}, u32[]{:S(2)}, u32[]{:S(2)}) collective-permute-start(bf16[2,8,64,128]{3,2,1,0:T(8,128)(2,1)S(1)} %get-tuple-element.30), channel_id=1, source_target_pairs={{0,2},{1,3},{2,0},{3,1},{4,6},{5,7},{6,4},{7,5},{8,10},{9,11},{10,... | collective-permute-start | bytes 786440 | tf_op jit(solution)/shard_map/ppermute | solution.py:134
  106.7 9.9 %collective-permute-start.8 = (bf16[4,2,8,32,128]{4,3,2,1,0:T(8,128)(2,1)S(1)}, bf16[4,2,8,32,128]{4,3,2,1,0:T(8,128)(2,1)S(1)}, u32[]{:S(2)}, u32[]{:S(2)}) collective-permute-start(bf16[4,2,8,32,128]{4,3,2,1,0:T(8,128)(2,1)S(1)} %pad_maximum_fusion.2), channel_id=1, source_target_pairs={{0,1},{1,0},{2,3},{3,2},{4,5},{5,4},{6,7},{7,6},{8,9},{9,8},{10,11... | collective-permute-start | bytes 1572872 | tf_op jit(solution)/shard_map/ppermute | solution.py:134
  115.8 2.0 %collective-permute-start.14 = (bf16[4,2,8,32,128]{4,3,2,1,0:T(8,128)(2,1)S(1)}, bf16[4,2,8,32,128]{4,3,2,1,0:T(8,128)(2,1)S(1)}, u32[]{:S(2)}, u32[]{:S(2)}) collective-permute-start(bf16[4,2,8,32,128]{4,3,2,1,0:T(8,128)(2,1)S(1)} %pad_maximum_fusion.3), channel_id=1, source_target_pairs={{0,1},{1,0},{2,3},{3,2},{4,5},{5,4},{6,7},{7,6},{8,9},{9,8},{10,11... | collective-permute-start | bytes 1572872 | tf_op jit(solution)/shard_map/ppermute | solution.py:134

commit v17 on v16

--- a/solution.py
+++ b/solution.py
@@ -54,8 +54,9 @@
     )(volume)
 
 
-def conv_kernel(plan, rows_at_once, pieces_count, tap_count, order, *refs):
+def conv_kernel(plan, rows_at_once, sums_count, pieces_count, tap_count, order, final, *refs):
     refs = list(refs)
+    sums = [refs.pop(0) for _ in range(sums_count)]
     pieces = [refs.pop(0) for _ in range(pieces_count)]
     tap_parts = [refs.pop(0) for _ in range(tap_count)]
     bias_ref, outs = refs[0], refs[1:]
@@ -69,7 +70,7 @@
     def tile(slot, row):
         cells = []
         weights = []
-        for a, (source, plane) in enumerate(plan[slot]):
+        for a, source, plane in plan[slot]:
             piece = pieces[source]
             lines = [
                 jnp.concatenate([piece[s, plane, row + r] for s in range(piece.shape[0])], axis=0)
@@ -90,7 +91,13 @@
             side = [part[:, c].reshape(total_out, cols) for c in range(3)]
             left = jnp.where(lane == 0, 0.0, pltpu.roll(side[0], 1, 1))
             right = jnp.where(lane == cols - 1, 0.0, pltpu.roll(side[2], cols - 1, 1))
-            shifted = side[1] + left + right + bias_ref[...]
+            found = side[1] + left + right
+            if sums:
+                found = found + sums[0][slot, row + r]
+            if not final:
+                outs[0][slot, row + r] = found
+                continue
+            shifted = found + bias_ref[...]
             done = jnp.where(shifted > 0, shifted, slope * shifted).astype(jnp.bfloat16)
             for n, out_ref in enumerate(outs):
                 out_ref[slot, row + r] = done[n * block : (n + 1) * block]
@@ -100,22 +107,27 @@
             tile(slot, row)
 
 
-def convolve(plan, pieces, tap_parts, tap_order, bias, blocks):
+def convolve(plan, sums, pieces, tap_parts, tap_order, bias, blocks):
     rows, cols = pieces[0].shape[2] - 2, pieces[0].shape[4]
     in_chan = tap_parts[0].shape[5]
     total_out = bias.shape[0]
     wide_bias = jnp.broadcast_to(bias[:, None], (total_out, cols))
-    macs = 27 * total_out * in_chan * len(plan) * rows * cols
+    macs = 9 * total_out * in_chan * sum(len(terms) for terms in plan) * rows * cols
     in_vmem = pl.BlockSpec(memory_space=pltpu.VMEM)
-    shape = jax.ShapeDtypeStruct((len(plan), rows, total_out // blocks, cols), jnp.bfloat16)
+    if blocks:
+        shapes = [jax.ShapeDtypeStruct((len(plan), rows, total_out // blocks, cols), jnp.bfloat16)] * blocks
+    else:
+        shapes = [jax.ShapeDtypeStruct((len(plan), rows, total_out, cols), jnp.float32)]
     return pl.pallas_call(
-        functools.partial(conv_kernel, plan, min(ROWS, rows), len(pieces), len(tap_parts), tap_order),
-        out_shape=[shape] * blocks,
-        in_specs=[in_vmem] * (len(pieces) + len(tap_parts) + 1),
-        out_specs=[in_vmem] * blocks,
+        functools.partial(
+            conv_kernel, plan, min(ROWS, rows), len(sums), len(pieces), len(tap_parts), tap_order, bool(blocks)
+        ),
+        out_shape=shapes,
+        in_specs=[in_vmem] * (len(sums) + len(pieces) + len(tap_parts) + 1),
+        out_specs=[in_vmem] * len(shapes),
         cost_estimate=pl.CostEstimate(flops=2 * macs, bytes_accessed=10_000_000, transcendentals=0),
         compiler_params=pltpu.CompilerParams(vmem_limit_bytes=16 * 2**20),
-    )(*pieces, *tap_parts, wide_bias)
+    )(*sums, *pieces, *tap_parts, wide_bias)
 
 
 def body(features, kernel, bias_vector):
@@ -134,19 +146,21 @@
         return lax.ppermute(array, axis, [(i, i ^ k) for i in range(lax.axis_size(axis))])
 
 
-    half = out_chan // 2
-    odd = lax.axis_index("slab") % 2
-    mine = lax.dynamic_slice_in_dim(kernel, odd * half, half, 3)
-    mine = [swap(mine, k) for k in across[1:]]
+    near = [swap(kernel, k) for k in across[1 : 3 if len(across) == 4 else None]]
     outer = lax.all_to_all(cut(jnp.concatenate([features[:1], features[-1:]]), parts), "filt", 0, 0)
-    between = lax.optimization_barrier((features[1:-1], mine))[0]
-    inner = lax.all_to_all(cut(between, parts), "filt", 0, 0)
-    mine = jnp.stack(mine)
-    theirs = lax.optimization_barrier((swap(mine, 1, "slab"), outer))[0]
-    rest = jnp.concatenate([jnp.where(odd == 0, mine, theirs), jnp.where(odd == 0, theirs, mine)], axis=4)
-    same = jnp.concatenate([kernel[None], rest])
+    between = lax.optimization_barrier((features[1:-1], near))[0]
+    inner_rows = cut(between, parts)
+    inner = lax.all_to_all(inner_rows, "filt", 0, 0)
+    same = jnp.stack([kernel, *near])
     tap_parts = [same, swap(same, 1)]
-    tap_order = tuple((n, g) for g in range(len(across)) for n in range(2))
+    tap_order = tuple((n, g) for g in range(len(near) + 1) for n in range(2))
+    if len(across) == 4:
+        half = out_chan // 2
+        by_x, by_y = lax.optimization_barrier((near, inner_rows))[0]
+        far = [swap(by_x[:, :, :, :half], across[2]), swap(by_y[:, :, :, half:], across[1])]
+        far = jnp.concatenate(far, axis=3)[None]
+        tap_parts += [far, swap(far, 1)]
+        tap_order += ((2, 0), (3, 0))
     arrived = outer
     order = jnp.stack([me ^ k ^ c for k in across for c in range(2)])
     bias = jnp.take(bias_vector.reshape(parts, out_chan), order, axis=0).reshape(-1)
@@ -173,8 +187,16 @@
 
     blocks = len(across)
     where = [(0, 0)] + [(1, plane) for plane in range(planes - 2)] + [(0, 1)]
-    middle = tuple(tuple(where[plane - 1 : plane + 2]) for plane in range(1, planes - 1))
-    results = convolve(middle, [outer, inner], tap_parts, tap_order, bias, blocks)
+
+    def terms(plane, taps):
+        return tuple((a, *where[plane + a - 1]) for a in taps)
+
+    inside_planes = range(1, planes - 1)
+    begun = tuple(terms(plane, [a for a in range(3) if plane + a - 1 in (0, planes - 1)]) for plane in inside_planes)
+    rest = tuple(terms(plane, [a for a in range(3) if 0 < plane + a - 1 < planes - 1]) for plane in inside_planes)
+    rest = tuple(tuple((a, n - 1, p) for a, n, p in found) for found in rest)
+    early = convolve(begun, [], [outer], tap_parts, tap_order, bias, 0)
+    results = convolve(rest, early, [inner], tap_parts, tap_order, bias, blocks)
     inside = send_back(results)
     later_bias = lax.optimization_barrier((bias, results))[0]
     up = [(i, i + 1) for i in range(slabs - 1)]
@@ -183,8 +205,8 @@
     after = lax.ppermute(first, "slab", down)
     before = lax.ppermute(last, "slab", up)
 
-    ends = (((2, 0), *where[:2]), (*where[-2:], (3, 0)))
-    outside = send_back(convolve(ends, [outer, inner, settle(before), settle(after)], tap_parts, tap_order, later_bias, blocks))
+    ends = ((0, 2, 0), *terms(0, [1, 2])), (*terms(planes - 1, [0, 1]), (2, 3, 0))
+    outside = send_back(convolve(ends, [], [outer, inner, settle(before), settle(after)], tap_parts, tap_order, later_bias, blocks))
     inside, outside = lax.optimization_barrier((inside, outside))
     return jnp.concatenate([outside[:1], inside, outside[1:]])
 

time: 121 us -> 123 us (1.017)
  local copies, waits for them, and re-layouts: 6.78 us -> 14.1 us
  waiting for transfers between devices: 58.4 us -> 51.2 us
  Pallas kernels: 22.9 us -> 24.2 us
    all_to_all x1, waiting for transfers between devices: 9.31 us -> 0.01 us  [body(): inner = lax.all_to_all(inner_rows, 'filt', 0, 0)]
    unnamed x6 -> x16, local copies, waits for them, and re-layouts: 0.7 us -> 6.38 us
    ppermute x13 -> x14, waiting for transfers between devices: 49.1 us -> 51.1 us  [swap(): lax.ppermute(array, axis, [(i, i ^ k) for i in range(lax.axis_size(axis))])]
    ppermute x13 -> x14, starting transfers between devices: 12.7 us -> 14.3 us  [swap(): lax.ppermute(array, axis, [(i, i ^ k) for i in range(lax.axis_size(axis))])]
    slice x2 -> x4, local copies, waits for them, and re-layouts: 0.92 us -> 2.54 us  [the longest x2 1.14 us: body(): between = lax.optimization_barrier((features[1:-1], near))[0]]
    pallas_call x2 -> x3, Pallas kernels: 19.4 us -> 20.7 us  [convolve(): pl.pallas_call(functools.partial(conv_kernel, plan, min(ROWS, rows), len(...]
  transfers between devices with their start and end apart: 17 -> 18, of which waited for: 7 -> 6; matrix products, arithmetic and copies ran while one was open for 2% -> 4% of each run, Pallas kernels for 18% -> 19%
where the time goes in v17:
time: 123 us
  waiting for transfers between devices  51.2 us (42%)
  starting transfers between devices  29.8 us (24%)
  Pallas kernels  24.2 us (20%)
  local copies, waits for them, and re-layouts  14.1 us (11%)
  other arithmetic  3.09 us (3%)
    ppermute x14, waiting for transfers between devices, swap(): lax.ppermute(array, axis, [(i, i ^ k) for i in range(lax.axis_size(axis))])  51.1 us
    pallas_call x3, Pallas kernels, convolve(): pl.pallas_call(functools.partial(conv_kernel, plan, min(ROWS, rows), len(...  20.7 us
    ppermute x14, starting transfers between devices, swap(): lax.ppermute(array, axis, [(i, i ^ k) for i in range(lax.axis_size(axis))])  14.3 us
    unnamed x16, local copies, waits for them, and re-layouts  6.38 us
    all_to_all x1, starting transfers between devices, body(): lax.all_to_all(cut(jnp.concatenate([features[:1], features[-1:]]), parts)...  5.3 us
    all_to_all x1, starting transfers between devices, body(): inner = lax.all_to_all(inner_rows, 'filt', 0, 0)  4.41 us
    ppermute x1, starting transfers between devices, body(): before = lax.ppermute(last, 'slab', up)  4.32 us
  transfers between devices with their start and end apart: 18, of which 6 were waited for; matrix products, arithmetic and copies ran while one was open for 4% of the time, Pallas kernels for 19%

profile of v17, /device:TPU:0, one launch (start us, length us, event | category | flops | bytes accessed | tf_op | source)
XLA Modules:
  0.0 122.8 jit_solution(16401465735842864190)
XLA Ops:
  0.0 1.3 %fusion.1 = (bf16[1,32,64,128]{3,2,1,0:T(8,128)(2,1)S(1)}, bf16[1,32,64,128]{3,2,1,0:T(8,128)(2,1)S(1)}) fusion(bf16[4,32,64,128]{3,2,1,0:T(8,128)(2,1)} %param.3), kind=kLoop, calls=%fused_computation.45 | loop fusion | bytes 2097152 | tf_op jit(solution)/shard_map/slice | solution.py:150
  3.3 5.3 %all-to-all-start = ((bf16[8,2,10,32,128]{4,3,2,1,0:T(8,128)(2,1)}), bf16[8,2,10,32,128]{4,3,2,1,0:T(8,128)(2,1)S(1)}, u32[]{:S(2)}, u32[]{:S(2)}) async-start(bf16[8,2,10,32,128]{4,3,2,1,0:T(8,128)(2,1)} %shard_map.37), calls=%async_computation | async-start | bytes 2621440 | tf_op jit(solution)/shard_map/all_to_all | solution.py:150
  8.6 2.0 %collective-permute-start = (bf16[3,3,3,32,256]{4,3,2,1,0:T(8,128)(2,1)S(1)}, bf16[3,3,3,32,256]{4,3,2,1,0:T(8,128)(2,1)S(1)}, u32[]{:S(2)}, u32[]{:S(2)}) collective-permute-start(bf16[3,3,3,32,256]{4,3,2,1,0:T(8,128)(2,1)S(1)} %copy-done.5), channel_id=1, source_target_pairs={{0,2},{1,3},{2,0},{3,1},{4,6},{5,7},{6,4},{7,5},{8,10},{9,11},{10,... | collective-permute-start | bytes 1327112 | tf_op jit(solution)/shard_map/ppermute | solution.py:146
  10.6 1.5 %collective-permute-start.1 = (bf16[3,3,3,32,256]{4,3,2,1,0:T(8,128)(2,1)S(1)}, bf16[3,3,3,32,256]{4,3,2,1,0:T(8,128)(2,1)S(1)}, u32[]{:S(2)}, u32[]{:S(2)}) collective-permute-start(bf16[3,3,3,32,256]{4,3,2,1,0:T(8,128)(2,1)S(1)} %copy-done.5), channel_id=1, source_target_pairs={{0,4},{1,5},{2,6},{3,7},{4,0},{5,1},{6,2},{7,3},{8,12},{9,13},{10,... | collective-permute-start | bytes 1327112 | tf_op jit(solution)/shard_map/ppermute | solution.py:146
  12.0 23.3 %collective-permute-done = bf16[3,3,3,32,256]{4,3,2,1,0:T(8,128)(2,1)S(1)} collective-permute-done((bf16[3,3,3,32,256]{4,3,2,1,0:T(8,128)(2,1)S(1)}, bf16[3,3,3,32,256]{4,3,2,1,0:T(8,128)(2,1)S(1)}, u32[]{:S(2)}, u32[]{:S(2)}) %collective-permute-start) | collective-permute-done | bytes 442400 | tf_op jit(solution)/shard_map/ppermute | solution.py:146
  39.7 4.4 %all-to-all-start.1 = ((bf16[8,2,10,32,128]{4,3,2,1,0:T(8,128)(2,1)}), bf16[8,2,10,32,128]{4,3,2,1,0:T(8,128)(2,1)}, u32[]{:S(2)}, u32[]{:S(2)}) async-start(bf16[8,2,10,32,128]{4,3,2,1,0:T(8,128)(2,1)} %shard_map.38), calls=%async_computation.1 | async-start | bytes 2621440 | tf_op jit(solution)/shard_map/all_to_all | solution.py:153
  44.9 1.9 %collective-permute-start.3 = (bf16[3,3,3,16,256]{4,3,2,1,0:T(8,128)(2,1)}, bf16[3,3,3,16,256]{4,3,2,1,0:T(8,128)(2,1)S(1)}, u32[]{:S(2)}, u32[]{:S(2)}) collective-permute-start(bf16[3,3,3,16,256]{4,3,2,1,0:T(8,128)(2,1)} %slice.96), channel_id=1, source_target_pairs={{0,4},{1,5},{2,6},{3,7},{4,0},{5,1},{6,2},{7,3},{8,12},{9,13},{10,... | collective-permute-start | bytes 663560 | tf_op jit(solution)/shard_map/ppermute | solution.py:146
  47.5 1.5 %collective-permute-start.4 = (bf16[3,3,3,16,256]{4,3,2,1,0:T(8,128)(2,1)}, bf16[3,3,3,16,256]{4,3,2,1,0:T(8,128)(2,1)S(1)}, u32[]{:S(2)}, u32[]{:S(2)}) collective-permute-start(bf16[3,3,3,16,256]{4,3,2,1,0:T(8,128)(2,1)} %slice.97), channel_id=1, source_target_pairs={{0,2},{1,3},{2,0},{3,1},{4,6},{5,7},{6,4},{7,5},{8,10},{9,11},{10,... | collective-permute-start | bytes 663560 | tf_op jit(solution)/shard_map/ppermute | solution.py:146
  49.7 16.3 %collective-permute-done.3 = bf16[3,3,3,16,256]{4,3,2,1,0:T(8,128)(2,1)S(1)} collective-permute-done((bf16[3,3,3,16,256]{4,3,2,1,0:T(8,128)(2,1)}, bf16[3,3,3,16,256]{4,3,2,1,0:T(8,128)(2,1)S(1)}, u32[]{:S(2)}, u32[]{:S(2)}) %collective-permute-start.3) | collective-permute-done | bytes 221216 | tf_op jit(solution)/shard_map/ppermute | solution.py:146
  66.4 1.2 shard_map.41
  67.6 4.3 %collective-permute-start.10 = (bf16[8,1,10,32,128]{4,3,2,1,0:T(8,128)(2,1)}, bf16[8,1,10,32,128]{4,3,2,1,0:T(8,128)(2,1)}, u32[]{:S(2)}, u32[]{:S(2)}) collective-permute-start(bf16[8,1,10,32,128]{4,3,2,1,0:T(8,128)(2,1)} %get-tuple-element.28), channel_id=1, source_target_pairs={{0,8},{8,16},{16,24},{1,9},{9,17},{17,25},{2,10},{10,18},{18,26},{... | collective-permute-start | bytes 1966088 | tf_op jit(solution)/shard_map/ppermute | solution.py:206
  71.9 1.5 %collective-permute-start.11 = (bf16[8,1,10,32,128]{4,3,2,1,0:T(8,128)(2,1)}, bf16[8,1,10,32,128]{4,3,2,1,0:T(8,128)(2,1)}, u32[]{:S(2)}, u32[]{:S(2)}) collective-permute-start(bf16[8,1,10,32,128]{4,3,2,1,0:T(8,128)(2,1)} %get-tuple-element.29), channel_id=1, source_target_pairs={{8,0},{16,8},{24,16},{9,1},{17,9},{25,17},{10,2},{18,10},{26,18},{... | collective-permute-start | bytes 1966088 | tf_op jit(solution)/shard_map/ppermute | solution.py:205
  75.2 4.1 %shard_map.39.refs_0_ = f32[2,8,256,128]{3,2,1,0:T(8,128)S(1)} custom-call(bf16[8,2,10,32,128]{4,3,2,1,0:T(8,128)(2,1)S(1)} %all-to-all-done.refs_0_.vol_ref, bf16[3,3,3,3,32,256]{5,4,3,2,1,0:T(8,128)(2,1)S(1)} %pad_maximum_fusion.1.refs_1_.refs_2_.refs_4_, bf16[3,3,3,3,32,256]{5,4,3,2,1,0:T(8,128)(2,1)} %collective-permute-done.2.refs_2_.refs_3_.refs_5_, ...), custom_call_target="tpu_custom_call" | custom-call | flops 2415919104 | bytes 10000000 | tf_op jit(solution)/shard_map/pallas_call | solution.py:121
  79.3 1.3 %copy-done.3 = f32[2,8,256,128]{3,2,1,0:T(8,128)} copy-done((f32[2,8,256,128]{3,2,1,0:T(8,128)}, f32[2,8,256,128]{3,2,1,0:T(8,128)S(1)}, u32[]{:S(2)}) %copy-start.3) | copy-done | bytes 2097176
  81.6 1.6 %copy-done.4 = f32[2,8,256,128]{3,2,1,0:T(8,128)S(1)} copy-done((f32[2,8,256,128]{3,2,1,0:T(8,128)S(1)}, f32[2,8,256,128]{3,2,1,0:T(8,128)}, u32[]{:S(2)}) %copy-start.4) | copy-done | bytes 2097176
  83.2 6.9 %shard_map.40 = (bf16[2,8,64,128]{3,2,1,0:T(8,128)(2,1)S(1)}, bf16[2,8,64,128]{3,2,1,0:T(8,128)(2,1)S(1)}, bf16[2,8,64,128]{3,2,1,0:T(8,128)(2,1)S(1)}, bf16[2,8,64,128]{3,2,1,0:T(8,128)(2,1)S(1)}) custom-call(f32[2,8,256,128]{3,2,1,0:T(8,128)S(1)} %copy-done.4, bf16[8,2,10,32,128]{4,3,2,1,0:T(8,128)(2,1)} %all-to-all-done.1.refs_1_, ...), custom_call_target="tpu_custom_call" | custom-call | flops 4831838208 | bytes 10000000 | tf_op jit(solution)/shard_map/pallas_call | solution.py:121
  90.1 1.5 %collective-permute-start.8 = (bf16[2,8,64,128]{3,2,1,0:T(8,128)(2,1)S(1)}, bf16[2,8,64,128]{3,2,1,0:T(8,128)(2,1)S(1)}, u32[]{:S(2)}, u32[]{:S(2)}) collective-permute-start(bf16[2,8,64,128]{3,2,1,0:T(8,128)(2,1)S(1)} %get-tuple-element.27), channel_id=1, source_target_pairs={{0,6},{1,7},{2,4},{3,5},{4,2},{5,3},{6,0},{7,1},{8,14},{9,15},{10,... | collective-permute-start | bytes 786440 | tf_op jit(solution)/shard_map/ppermute | solution.py:146
  91.7 1.4 %collective-permute-start.7 = (bf16[2,8,64,128]{3,2,1,0:T(8,128)(2,1)S(1)}, bf16[2,8,64,128]{3,2,1,0:T(8,128)(2,1)S(1)}, u32[]{:S(2)}, u32[]{:S(2)}) collective-permute-start(bf16[2,8,64,128]{3,2,1,0:T(8,128)(2,1)S(1)} %get-tuple-element.26), channel_id=1, source_target_pairs={{0,4},{1,5},{2,6},{3,7},{4,0},{5,1},{6,2},{7,3},{8,12},{9,13},{10,... | collective-permute-start | bytes 786440 | tf_op jit(solution)/shard_map/ppermute | solution.py:146
  93.8 9.7 %shard_map.42 = (bf16[2,8,64,128]{3,2,1,0:T(8,128)(2,1)S(1)}, bf16[2,8,64,128]{3,2,1,0:T(8,128)(2,1)S(1)}, bf16[2,8,64,128]{3,2,1,0:T(8,128)(2,1)S(1)}, bf16[2,8,64,128]{3,2,1,0:T(8,128)(2,1)S(1)}) custom-call(bf16[8,2,10,32,128]{4,3,2,1,0:T(8,128)(2,1)S(1)} %all-to-all-done.refs_0_.vol_ref, bf16[8,2,10,32,128]{4,3,2,1,0:T(8,128)(2,1)} %all-to-all-done.1.refs_1_, ...), custom_call_target="tpu_custom_call" | custom-call | flops 7247757312 | bytes 10000000 | tf_op jit(solution)/shard_map/pallas_call | solution.py:121
  103.5 1.5 %collective-permute-start.14 = (bf16[2,8,64,128]{3,2,1,0:T(8,128)(2,1)S(1)}, bf16[2,8,64,128]{3,2,1,0:T(8,128)(2,1)S(1)}, u32[]{:S(2)}, u32[]{:S(2)}) collective-permute-start(bf16[2,8,64,128]{3,2,1,0:T(8,128)(2,1)S(1)} %get-tuple-element.34), channel_id=1, source_target_pairs={{0,6},{1,7},{2,4},{3,5},{4,2},{5,3},{6,0},{7,1},{8,14},{9,15},{10,... | collective-permute-start | bytes 786440 | tf_op jit(solution)/shard_map/ppermute | solution.py:146
  105.1 1.4 %collective-permute-start.13 = (bf16[2,8,64,128]{3,2,1,0:T(8,128)(2,1)S(1)}, bf16[2,8,64,128]{3,2,1,0:T(8,128)(2,1)S(1)}, u32[]{:S(2)}, u32[]{:S(2)}) collective-permute-start(bf16[2,8,64,128]{3,2,1,0:T(8,128)(2,1)S(1)} %get-tuple-element.33), channel_id=1, source_target_pairs={{0,4},{1,5},{2,6},{3,7},{4,0},{5,1},{6,2},{7,3},{8,12},{9,13},{10,... | collective-permute-start | bytes 786440 | tf_op jit(solution)/shard_map/ppermute | solution.py:146
  107.5 6.3 %collective-permute-done.14 = bf16[2,8,64,128]{3,2,1,0:T(8,128)(2,1)S(1)} collective-permute-done((bf16[2,8,64,128]{3,2,1,0:T(8,128)(2,1)S(1)}, bf16[2,8,64,128]{3,2,1,0:T(8,128)(2,1)S(1)}, u32[]{:S(2)}, u32[]{:S(2)}) %collective-permute-start.14) | collective-permute-done | bytes 262176 | tf_op jit(solution)/shard_map/ppermute | solution.py:146
  113.8 3.9 %collective-permute-done.13 = bf16[2,8,64,128]{3,2,1,0:T(8,128)(2,1)S(1)} collective-permute-done((bf16[2,8,64,128]{3,2,1,0:T(8,128)(2,1)S(1)}, bf16[2,8,64,128]{3,2,1,0:T(8,128)(2,1)S(1)}, u32[]{:S(2)}, u32[]{:S(2)}) %collective-permute-start.13) | collective-permute-done | bytes 262176 | tf_op jit(solution)/shard_map/ppermute | solution.py:146
  121.3 1.6 %pad_maximum_fusion = bf16[4,32,64,128]{3,2,1,0:T(8,128)(2,1)} fusion(bf16[1,32,64,128]{3,2,1,0:T(8,128)(2,1)S(1)} %get-tuple-element.40, bf16[2,32,64,128]{3,2,1,0:T(8,128)(2,1)S(1)} %bitcast.62, bf16[1,32,64,128]{3,2,1,0:T(8,128)(2,1)S(1)} %get-tuple-element.39), kind=kLoop, calls=%fused_computation.1 | loop fusion | flops 2097152 | bytes 4194304 | tf_op jit(solution)/shard_map/concatenate | solution.py:211
  (85 shorter events, 16.6 us)
Async XLA Ops:
  3.3 5.3 %copy-start.5 = (bf16[3,3,3,32,256]{4,3,2,1,0:T(8,128)(2,1)S(1)}, bf16[3,3,3,32,256]{4,3,2,1,0:T(8,128)(2,1)}, u32[]{:S(2)}) copy-start(bf16[3,3,3,32,256]{4,3,2,1,0:T(8,128)(2,1)} %param.4) | copy-start | bytes 1327108
  3.3 36.4 %all-to-all-start = ((bf16[8,2,10,32,128]{4,3,2,1,0:T(8,128)(2,1)}), bf16[8,2,10,32,128]{4,3,2,1,0:T(8,128)(2,1)S(1)}, u32[]{:S(2)}, u32[]{:S(2)}) async-start(bf16[8,2,10,32,128]{4,3,2,1,0:T(8,128)(2,1)} %shard_map.37), calls=%async_computation | async-start | bytes 2621440 | tf_op jit(solution)/shard_map/all_to_all | solution.py:150
  8.6 26.8 %collective-permute-start = (bf16[3,3,3,32,256]{4,3,2,1,0:T(8,128)(2,1)S(1)}, bf16[3,3,3,32,256]{4,3,2,1,0:T(8,128)(2,1)S(1)}, u32[]{:S(2)}, u32[]{:S(2)}) collective-permute-start(bf16[3,3,3,32,256]{4,3,2,1,0:T(8,128)(2,1)S(1)} %copy-done.5), channel_id=1, source_target_pairs={{0,2},{1,3},{2,0},{3,1},{4,6},{5,7},{6,4},{7,5},{8,10},{9,11},{10,... | collective-permute-start | bytes 1327112 | tf_op jit(solution)/shard_map/ppermute | solution.py:146
  10.6 24.8 %collective-permute-start.1 = (bf16[3,3,3,32,256]{4,3,2,1,0:T(8,128)(2,1)S(1)}, bf16[3,3,3,32,256]{4,3,2,1,0:T(8,128)(2,1)S(1)}, u32[]{:S(2)}, u32[]{:S(2)}) collective-permute-start(bf16[3,3,3,32,256]{4,3,2,1,0:T(8,128)(2,1)S(1)} %copy-done.5), channel_id=1, source_target_pairs={{0,4},{1,5},{2,6},{3,7},{4,0},{5,1},{6,2},{7,3},{8,12},{9,13},{10,... | collective-permute-start | bytes 1327112 | tf_op jit(solution)/shard_map/ppermute | solution.py:146
  36.6 1.2 %slice-start = ((bf16[4,32,64,128]{3,2,1,0:T(8,128)(2,1)}), bf16[2,32,64,128]{3,2,1,0:T(8,128)(2,1)S(1)}, s32[]{:S(2)}) async-start(bf16[4,32,64,128]{3,2,1,0:T(8,128)(2,1)} %param.3), calls=%async_computation.2 | async-start | bytes 2097152 | tf_op jit(solution)/shard_map/slice | solution.py:151
  36.6 37.5 %collective-permute-start.2 = (bf16[3,3,3,3,32,256]{5,4,3,2,1,0:T(8,128)(2,1)S(1)}, bf16[3,3,3,3,32,256]{5,4,3,2,1,0:T(8,128)(2,1)}, u32[]{:S(2)}, u32[]{:S(2)}) collective-permute-start(bf16[3,3,3,3,32,256]{5,4,3,2,1,0:T(8,128)(2,1)S(1)} %pad_maximum_fusion.1.refs_1_.refs_2_.refs_4_), channel_id=1, source_target_pairs={{0,1},{1,0},{2,3},{3,2},{4,5},{5,4},{6,7},{7,6},{8,9},{9,8},{10,11... | collective-permute-start | bytes 3981320 | tf_op jit(solution)/shard_map/ppermute | solution.py:146
  39.7 9.3 %copy-start.6 = (f32[256]{0:T(256)S(1)}, f32[256]{0:T(256)}, u32[]{:S(2)}) copy-start(f32[256]{0:T(256)} %param.5) | copy-start | bytes 3076
  39.7 41.0 %all-to-all-start.1 = ((bf16[8,2,10,32,128]{4,3,2,1,0:T(8,128)(2,1)}), bf16[8,2,10,32,128]{4,3,2,1,0:T(8,128)(2,1)}, u32[]{:S(2)}, u32[]{:S(2)}) async-start(bf16[8,2,10,32,128]{4,3,2,1,0:T(8,128)(2,1)} %shard_map.38), calls=%async_computation.1 | async-start | bytes 2621440 | tf_op jit(solution)/shard_map/all_to_all | solution.py:153
  44.9 21.1 %collective-permute-start.3 = (bf16[3,3,3,16,256]{4,3,2,1,0:T(8,128)(2,1)}, bf16[3,3,3,16,256]{4,3,2,1,0:T(8,128)(2,1)S(1)}, u32[]{:S(2)}, u32[]{:S(2)}) collective-permute-start(bf16[3,3,3,16,256]{4,3,2,1,0:T(8,128)(2,1)} %slice.96), channel_id=1, source_target_pairs={{0,4},{1,5},{2,6},{3,7},{4,0},{5,1},{6,2},{7,3},{8,12},{9,13},{10,... | collective-permute-start | bytes 663560 | tf_op jit(solution)/shard_map/ppermute | solution.py:146
  47.5 18.6 %collective-permute-start.4 = (bf16[3,3,3,16,256]{4,3,2,1,0:T(8,128)(2,1)}, bf16[3,3,3,16,256]{4,3,2,1,0:T(8,128)(2,1)S(1)}, u32[]{:S(2)}, u32[]{:S(2)}) collective-permute-start(bf16[3,3,3,16,256]{4,3,2,1,0:T(8,128)(2,1)} %slice.97), channel_id=1, source_target_pairs={{0,2},{1,3},{2,0},{3,1},{4,6},{5,7},{6,4},{7,5},{8,10},{9,11},{10,... | collective-permute-start | bytes 663560 | tf_op jit(solution)/shard_map/ppermute | solution.py:146
  66.1 7.2 %collective-permute-start.5 = (bf16[1,3,3,3,32,256]{5,4,3,2,1,0:T(8,128)(2,1)S(1)}, bf16[1,3,3,3,32,256]{5,4,3,2,1,0:T(8,128)(2,1)S(1)}, u32[]{:S(2)}, u32[]{:S(2)}) collective-permute-start(bf16[1,3,3,3,32,256]{5,4,3,2,1,0:T(8,128)(2,1)S(1)} %maximum_bitcast_fusion.1.refs_3_.refs_4_.refs_6_), channel_id=1, source_target_pairs={{0,1},{1,0},{2,3},{3,2},{4,5},{5,4},{6,7},{7,6},{8,9},{9,8},{10,11... | collective-permute-start | bytes 1327112 | tf_op jit(solution)/shard_map/ppermute | solution.py:146
  67.6 26.2 %collective-permute-start.10 = (bf16[8,1,10,32,128]{4,3,2,1,0:T(8,128)(2,1)}, bf16[8,1,10,32,128]{4,3,2,1,0:T(8,128)(2,1)}, u32[]{:S(2)}, u32[]{:S(2)}) collective-permute-start(bf16[8,1,10,32,128]{4,3,2,1,0:T(8,128)(2,1)} %get-tuple-element.28), channel_id=1, source_target_pairs={{0,8},{8,16},{16,24},{1,9},{9,17},{17,25},{2,10},{10,18},{18,26},{... | collective-permute-start | bytes 1966088 | tf_op jit(solution)/shard_map/ppermute | solution.py:206
  71.9 21.8 %collective-permute-start.11 = (bf16[8,1,10,32,128]{4,3,2,1,0:T(8,128)(2,1)}, bf16[8,1,10,32,128]{4,3,2,1,0:T(8,128)(2,1)}, u32[]{:S(2)}, u32[]{:S(2)}) collective-permute-start(bf16[8,1,10,32,128]{4,3,2,1,0:T(8,128)(2,1)} %get-tuple-element.29), channel_id=1, source_target_pairs={{8,0},{16,8},{24,16},{9,1},{17,9},{25,17},{10,2},{18,10},{26,18},{... | collective-permute-start | bytes 1966088 | tf_op jit(solution)/shard_map/ppermute | solution.py:205
  74.2 1.0 copy-start.1
  79.3 1.3 %copy-start.3 = (f32[2,8,256,128]{3,2,1,0:T(8,128)}, f32[2,8,256,128]{3,2,1,0:T(8,128)S(1)}, u32[]{:S(2)}) copy-start(f32[2,8,256,128]{3,2,1,0:T(8,128)S(1)} %shard_map.39.refs_0_) | copy-start | bytes 6291460
  81.6 1.6 %copy-start.4 = (f32[2,8,256,128]{3,2,1,0:T(8,128)S(1)}, f32[2,8,256,128]{3,2,1,0:T(8,128)}, u32[]{:S(2)}) copy-start(f32[2,8,256,128]{3,2,1,0:T(8,128)} %copy-done.3) | copy-start | bytes 6291460
  90.1 16.4 %collective-permute-start.8 = (bf16[2,8,64,128]{3,2,1,0:T(8,128)(2,1)S(1)}, bf16[2,8,64,128]{3,2,1,0:T(8,128)(2,1)S(1)}, u32[]{:S(2)}, u32[]{:S(2)}) collective-permute-start(bf16[2,8,64,128]{3,2,1,0:T(8,128)(2,1)S(1)} %get-tuple-element.27), channel_id=1, source_target_pairs={{0,6},{1,7},{2,4},{3,5},{4,2},{5,3},{6,0},{7,1},{8,14},{9,15},{10,... | collective-permute-start | bytes 786440 | tf_op jit(solution)/shard_map/ppermute | solution.py:146
  91.7 15.6 %collective-permute-start.7 = (bf16[2,8,64,128]{3,2,1,0:T(8,128)(2,1)S(1)}, bf16[2,8,64,128]{3,2,1,0:T(8,128)(2,1)S(1)}, u32[]{:S(2)}, u32[]{:S(2)}) collective-permute-start(bf16[2,8,64,128]{3,2,1,0:T(8,128)(2,1)S(1)} %get-tuple-element.26), channel_id=1, source_target_pairs={{0,4},{1,5},{2,6},{3,7},{4,0},{5,1},{6,2},{7,3},{8,12},{9,13},{10,... | collective-permute-start | bytes 786440 | tf_op jit(solution)/shard_map/ppermute | solution.py:146
  93.1 14.2 %collective-permute-start.6 = (bf16[2,8,64,128]{3,2,1,0:T(8,128)(2,1)S(1)}, bf16[2,8,64,128]{3,2,1,0:T(8,128)(2,1)S(1)}, u32[]{:S(2)}, u32[]{:S(2)}) collective-permute-start(bf16[2,8,64,128]{3,2,1,0:T(8,128)(2,1)S(1)} %get-tuple-element.25), channel_id=1, source_target_pairs={{0,2},{1,3},{2,0},{3,1},{4,6},{5,7},{6,4},{7,5},{8,10},{9,11},{10,... | collective-permute-start | bytes 786440 | tf_op jit(solution)/shard_map/ppermute | solution.py:146
  103.5 10.2 %collective-permute-start.14 = (bf16[2,8,64,128]{3,2,1,0:T(8,128)(2,1)S(1)}, bf16[2,8,64,128]{3,2,1,0:T(8,128)(2,1)S(1)}, u32[]{:S(2)}, u32[]{:S(2)}) collective-permute-start(bf16[2,8,64,128]{3,2,1,0:T(8,128)(2,1)S(1)} %get-tuple-element.34), channel_id=1, source_target_pairs={{0,6},{1,7},{2,4},{3,5},{4,2},{5,3},{6,0},{7,1},{8,14},{9,15},{10,... | collective-permute-start | bytes 786440 | tf_op jit(solution)/shard_map/ppermute | solution.py:146
  105.1 12.6 %collective-permute-start.13 = (bf16[2,8,64,128]{3,2,1,0:T(8,128)(2,1)S(1)}, bf16[2,8,64,128]{3,2,1,0:T(8,128)(2,1)S(1)}, u32[]{:S(2)}, u32[]{:S(2)}) collective-permute-start(bf16[2,8,64,128]{3,2,1,0:T(8,128)(2,1)S(1)} %get-tuple-element.33), channel_id=1, source_target_pairs={{0,4},{1,5},{2,6},{3,7},{4,0},{5,1},{6,2},{7,3},{8,12},{9,13},{10,... | collective-permute-start | bytes 786440 | tf_op jit(solution)/shard_map/ppermute | solution.py:146
  106.5 11.2 %collective-permute-start.12 = (bf16[2,8,64,128]{3,2,1,0:T(8,128)(2,1)S(1)}, bf16[2,8,64,128]{3,2,1,0:T(8,128)(2,1)S(1)}, u32[]{:S(2)}, u32[]{:S(2)}) collective-permute-start(bf16[2,8,64,128]{3,2,1,0:T(8,128)(2,1)S(1)} %get-tuple-element.32), channel_id=1, source_target_pairs={{0,2},{1,3},{2,0},{3,1},{4,6},{5,7},{6,4},{7,5},{8,10},{9,11},{10,... | collective-permute-start | bytes 786440 | tf_op jit(solution)/shard_map/ppermute | solution.py:146
  107.4 11.3 %collective-permute-start.9 = (bf16[4,2,8,32,128]{4,3,2,1,0:T(8,128)(2,1)S(1)}, bf16[4,2,8,32,128]{4,3,2,1,0:T(8,128)(2,1)S(1)}, u32[]{:S(2)}, u32[]{:S(2)}) collective-permute-start(bf16[4,2,8,32,128]{4,3,2,1,0:T(8,128)(2,1)S(1)} %pad_maximum_fusion.2), channel_id=1, source_target_pairs={{0,1},{1,0},{2,3},{3,2},{4,5},{5,4},{6,7},{7,6},{8,9},{9,8},{10,11... | collective-permute-start | bytes 1572872 | tf_op jit(solution)/shard_map/ppermute | solution.py:146
  117.9 2.0 %collective-permute-start.15 = (bf16[4,2,8,32,128]{4,3,2,1,0:T(8,128)(2,1)S(1)}, bf16[4,2,8,32,128]{4,3,2,1,0:T(8,128)(2,1)S(1)}, u32[]{:S(2)}, u32[]{:S(2)}) collective-permute-start(bf16[4,2,8,32,128]{4,3,2,1,0:T(8,128)(2,1)S(1)} %pad_maximum_fusion.3), channel_id=1, source_target_pairs={{0,1},{1,0},{2,3},{3,2},{4,5},{5,4},{6,7},{7,6},{8,9},{9,8},{10,11... | collective-permute-start | bytes 1572872 | tf_op jit(solution)/shard_map/ppermute | solution.py:146
  (2 other events, 1.8 us)

commit v18 on v17

--- a/solution.py
+++ b/solution.py
@@ -146,21 +146,14 @@
         return lax.ppermute(array, axis, [(i, i ^ k) for i in range(lax.axis_size(axis))])
 
 
-    near = [swap(kernel, k) for k in across[1 : 3 if len(across) == 4 else None]]
-    outer = lax.all_to_all(cut(jnp.concatenate([features[:1], features[-1:]]), parts), "filt", 0, 0)
-    between = lax.optimization_barrier((features[1:-1], near))[0]
-    inner_rows = cut(between, parts)
-    inner = lax.all_to_all(inner_rows, "filt", 0, 0)
-    same = jnp.stack([kernel, *near])
+    outer_rows = cut(jnp.concatenate([features[:1], features[-1:]]), parts)
+    fetched = [swap(kernel, k) for k in across]
+    fetched = lax.optimization_barrier((fetched, outer_rows))[0]
+    same = jnp.stack(fetched)
     tap_parts = [same, swap(same, 1)]
-    tap_order = tuple((n, g) for g in range(len(near) + 1) for n in range(2))
-    if len(across) == 4:
-        half = out_chan // 2
-        by_x, by_y = lax.optimization_barrier((near, inner_rows))[0]
-        far = [swap(by_x[:, :, :, :half], across[2]), swap(by_y[:, :, :, half:], across[1])]
-        far = jnp.concatenate(far, axis=3)[None]
-        tap_parts += [far, swap(far, 1)]
-        tap_order += ((2, 0), (3, 0))
+    tap_order = tuple((n, g) for g in range(len(across)) for n in range(2))
+    outer = lax.all_to_all(outer_rows, "filt", 0, 0)
+    inner = lax.all_to_all(cut(features[1:-1], parts), "filt", 0, 0)
     arrived = outer
     order = jnp.stack([me ^ k ^ c for k in across for c in range(2)])
     bias = jnp.take(bias_vector.reshape(parts, out_chan), order, axis=0).reshape(-1)
@@ -198,7 +191,6 @@
     early = convolve(begun, [], [outer], tap_parts, tap_order, bias, 0)
     results = convolve(rest, early, [inner], tap_parts, tap_order, bias, blocks)
     inside = send_back(results)
-    later_bias = lax.optimization_barrier((bias, results))[0]
     up = [(i, i + 1) for i in range(slabs - 1)]
     down = [(i + 1, i) for i in range(slabs - 1)]
     first, last = edges_of(arrived)
@@ -206,7 +198,7 @@
     before = lax.ppermute(last, "slab", up)
 
     ends = ((0, 2, 0), *terms(0, [1, 2])), (*terms(planes - 1, [0, 1]), (2, 3, 0))
-    outside = send_back(convolve(ends, [], [outer, inner, settle(before), settle(after)], tap_parts, tap_order, later_bias, blocks))
+    outside = send_back(convolve(ends, [], [outer, inner, settle(before), settle(after)], tap_parts, tap_order, bias, blocks))
     inside, outside = lax.optimization_barrier((inside, outside))
     return jnp.concatenate([outside[:1], inside, outside[1:]])
 

time: 123 us -> 101 us (0.82)
  waiting for transfers between devices: 51.2 us -> 35.5 us
  local copies, waits for them, and re-layouts: 14.1 us -> 10.6 us
  starting transfers between devices: 29.8 us -> 26.3 us
    ppermute x14 -> x12, waiting for transfers between devices: 51.1 us -> 23.2 us  [swap(): lax.ppermute(array, axis, [(i, i ^ k) for i in range(lax.axis_size(axis))])]
    all_to_all x2, waiting for transfers between devices: 0.01 us -> 12.3 us  [the longest x1 7.74 us: body(): outer = lax.all_to_all(outer_rows, 'filt', 0, 0)]
    ppermute x14 -> x12, starting transfers between devices: 14.3 us -> 11.9 us  [swap(): lax.ppermute(array, axis, [(i, i ^ k) for i in range(lax.axis_size(axis))])]
    slice x5 -> x3, local copies, waits for them, and re-layouts: 3.81 us -> 2.41 us  [the longest x1 1.27 us: body(): outer_rows = cut(jnp.concatenate([features[:1], features[-1:]]), parts)]
    unnamed x16 -> x17, local copies, waits for them, and re-layouts: 6.38 us -> 5.04 us
  transfers between devices with their start and end apart: 18 -> 16, of which waited for: 6 -> 8; matrix products, arithmetic and copies ran while one was open for 4% -> 6% of each run, Pallas kernels for 19% -> 24%
where the time goes in v18:
time: 101 us
  waiting for transfers between devices  35.5 us (35%)
  starting transfers between devices  26.3 us (26%)
  Pallas kernels  24.7 us (24%)
  local copies, waits for them, and re-layouts  10.6 us (10%)
  other arithmetic  3.4 us (3%)
    ppermute x12, waiting for transfers between devices, swap(): lax.ppermute(array, axis, [(i, i ^ k) for i in range(lax.axis_size(axis))])  23.2 us
    pallas_call x3, Pallas kernels, convolve(): pl.pallas_call(functools.partial(conv_kernel, plan, min(ROWS, rows), len(...  21.1 us
    ppermute x12, starting transfers between devices, swap(): lax.ppermute(array, axis, [(i, i ^ k) for i in range(lax.axis_size(axis))])  11.9 us
    all_to_all x1, waiting for transfers between devices, body(): outer = lax.all_to_all(outer_rows, 'filt', 0, 0)  7.74 us
    unnamed x17, local copies, waits for them, and re-layouts  5.04 us
    all_to_all x1, waiting for transfers between devices, body(): inner = lax.all_to_all(cut(features[1:-1], parts), 'filt', 0, 0)  4.54 us
    ppermute x1, starting transfers between devices, body(): before = lax.ppermute(last, 'slab', up)  4.34 us
    all_to_all x1, starting transfers between devices, body(): outer = lax.all_to_all(outer_rows, 'filt', 0, 0)  4.33 us
  transfers between devices with their start and end apart: 16, of which 8 were waited for; matrix products, arithmetic and copies ran while one was open for 6% of the time, Pallas kernels for 24%

profile of v18, /device:TPU:0, one launch (start us, length us, event | category | flops | bytes accessed | tf_op | source)
XLA Modules:
  0.0 100.8 jit_solution(11197071210089581277)
XLA Ops:
  0.0 2.9 %collective-permute-start = (bf16[3,3,3,32,256]{4,3,2,1,0:T(8,128)(2,1)}, bf16[3,3,3,32,256]{4,3,2,1,0:T(8,128)(2,1)S(1)}, u32[]{:S(2)}, u32[]{:S(2)}) collective-permute-start(bf16[3,3,3,32,256]{4,3,2,1,0:T(8,128)(2,1)} %param.4), channel_id=1, source_target_pairs={{0,2},{1,3},{2,0},{3,1},{4,6},{5,7},{6,4},{7,5},{8,10},{9,11},{10,... | collective-permute-start | bytes 1327112 | tf_op jit(solution)/shard_map/ppermute | solution.py:146
  2.9 1.5 %collective-permute-start.1 = (bf16[3,3,3,32,256]{4,3,2,1,0:T(8,128)(2,1)}, bf16[3,3,3,32,256]{4,3,2,1,0:T(8,128)(2,1)S(1)}, u32[]{:S(2)}, u32[]{:S(2)}) collective-permute-start(bf16[3,3,3,32,256]{4,3,2,1,0:T(8,128)(2,1)} %param.4), channel_id=1, source_target_pairs={{0,4},{1,5},{2,6},{3,7},{4,0},{5,1},{6,2},{7,3},{8,12},{9,13},{10,... | collective-permute-start | bytes 1327112 | tf_op jit(solution)/shard_map/ppermute | solution.py:146
  4.5 1.3 %fusion.1 = (bf16[1,32,64,128]{3,2,1,0:T(8,128)(2,1)S(1)}, bf16[1,32,64,128]{3,2,1,0:T(8,128)(2,1)S(1)}) fusion(bf16[4,32,64,128]{3,2,1,0:T(8,128)(2,1)} %param.3), kind=kLoop, calls=%fused_computation.45 | loop fusion | bytes 2097152 | tf_op jit(solution)/shard_map/slice | solution.py:149
  7.7 4.3 %all-to-all-start = ((bf16[8,2,10,32,128]{4,3,2,1,0:T(8,128)(2,1)}), bf16[8,2,10,32,128]{4,3,2,1,0:T(8,128)(2,1)S(1)}, u32[]{:S(2)}, u32[]{:S(2)}) async-start(bf16[8,2,10,32,128]{4,3,2,1,0:T(8,128)(2,1)} %shard_map.37), calls=%async_computation | async-start | bytes 2621440 | tf_op jit(solution)/shard_map/all_to_all | solution.py:155
  12.0 2.1 %collective-permute-done = bf16[3,3,3,32,256]{4,3,2,1,0:T(8,128)(2,1)S(1)} collective-permute-done((bf16[3,3,3,32,256]{4,3,2,1,0:T(8,128)(2,1)}, bf16[3,3,3,32,256]{4,3,2,1,0:T(8,128)(2,1)S(1)}, u32[]{:S(2)}, u32[]{:S(2)}) %collective-permute-start) | collective-permute-done | bytes 442400 | tf_op jit(solution)/shard_map/ppermute | solution.py:146
  14.1 10.7 %collective-permute-done.1 = bf16[3,3,3,32,256]{4,3,2,1,0:T(8,128)(2,1)S(1)} collective-permute-done((bf16[3,3,3,32,256]{4,3,2,1,0:T(8,128)(2,1)}, bf16[3,3,3,32,256]{4,3,2,1,0:T(8,128)(2,1)S(1)}, u32[]{:S(2)}, u32[]{:S(2)}) %collective-permute-start.1) | collective-permute-done | bytes 442400 | tf_op jit(solution)/shard_map/ppermute | solution.py:146
  26.0 1.5 %pad_maximum_fusion.1.refs_1_.refs_2_.refs_4_ = bf16[4,3,3,3,32,256]{5,4,3,2,1,0:T(8,128)(2,1)S(1)} fusion(bf16[1,3,3,3,32,256]{5,4,3,2,1,0:T(8,128)(2,1)} %bitcast.67, bf16[1,3,3,3,32,256]{5,4,3,2,1,0:T(8,128)(2,1)} %bitcast.66, bf16[1,3,3,3,32,256]{5,4,3,2,1,0:T(8,128)(2,1)} %bitcast.65, bf16[1,3,3,3,32,256]{5,4,3,2,1,0:T(8,128)(2,1)S(1)} %bitcast.64), kind=kLoop, calls=%fused_computation.2 | loop fusion | flops 2654208 | bytes 3538944 | tf_op jit(solution)/shard_map/stack | solution.py:152
  30.6 7.7 %all-to-all-done.refs_0_.vol_ref = bf16[8,2,10,32,128]{4,3,2,1,0:T(8,128)(2,1)S(1)} async-done(((bf16[8,2,10,32,128]{4,3,2,1,0:T(8,128)(2,1)}), bf16[8,2,10,32,128]{4,3,2,1,0:T(8,128)(2,1)S(1)}, u32[]{:S(2)}, u32[]{:S(2)}) %all-to-all-start) | async-done | bytes 1310752 | tf_op jit(solution)/shard_map/all_to_all | solution.py:155
  38.3 4.3 %all-to-all-start.1 = ((bf16[8,2,10,32,128]{4,3,2,1,0:T(8,128)(2,1)}), bf16[8,2,10,32,128]{4,3,2,1,0:T(8,128)(2,1)}, u32[]{:S(2)}, u32[]{:S(2)}) async-start(bf16[8,2,10,32,128]{4,3,2,1,0:T(8,128)(2,1)} %shard_map.39), calls=%async_computation.1 | async-start | bytes 2621440 | tf_op jit(solution)/shard_map/all_to_all | solution.py:156
  44.8 4.3 %collective-permute-start.8 = (bf16[8,1,10,32,128]{4,3,2,1,0:T(8,128)(2,1)}, bf16[8,1,10,32,128]{4,3,2,1,0:T(8,128)(2,1)}, u32[]{:S(2)}, u32[]{:S(2)}) collective-permute-start(bf16[8,1,10,32,128]{4,3,2,1,0:T(8,128)(2,1)} %get-tuple-element.29), channel_id=1, source_target_pairs={{0,8},{8,16},{16,24},{1,9},{9,17},{17,25},{2,10},{10,18},{18,26},{... | collective-permute-start | bytes 1966088 | tf_op jit(solution)/shard_map/ppermute | solution.py:198
  49.1 1.5 %collective-permute-start.9 = (bf16[8,1,10,32,128]{4,3,2,1,0:T(8,128)(2,1)}, bf16[8,1,10,32,128]{4,3,2,1,0:T(8,128)(2,1)}, u32[]{:S(2)}, u32[]{:S(2)}) collective-permute-start(bf16[8,1,10,32,128]{4,3,2,1,0:T(8,128)(2,1)} %get-tuple-element.30), channel_id=1, source_target_pairs={{8,0},{16,8},{24,16},{9,1},{17,9},{25,17},{10,2},{18,10},{26,18},{... | collective-permute-start | bytes 1966088 | tf_op jit(solution)/shard_map/ppermute | solution.py:197
  50.7 4.2 %shard_map.38.refs_0_ = f32[2,8,256,128]{3,2,1,0:T(8,128)S(1)} custom-call(bf16[8,2,10,32,128]{4,3,2,1,0:T(8,128)(2,1)S(1)} %all-to-all-done.refs_0_.vol_ref, bf16[4,3,3,3,32,256]{5,4,3,2,1,0:T(8,128)(2,1)S(1)} %pad_maximum_fusion.1.refs_1_.refs_2_.refs_4_, bf16[4,3,3,3,32,256]{5,4,3,2,1,0:T(8,128)(2,1)} %collective-permute-done.3.refs_2_.refs_3_.refs_5_, ...), custom_call_target="tpu_custom_call" | custom-call | flops 2415919104 | bytes 10000000 | tf_op jit(solution)/shard_map/pallas_call | solution.py:121
  55.0 1.3 %copy-done = f32[2,8,256,128]{3,2,1,0:T(8,128)} copy-done((f32[2,8,256,128]{3,2,1,0:T(8,128)}, f32[2,8,256,128]{3,2,1,0:T(8,128)S(1)}, u32[]{:S(2)}) %copy-start) | copy-done | bytes 2097176
  56.3 4.5 %all-to-all-done.1.refs_1_ = bf16[8,2,10,32,128]{4,3,2,1,0:T(8,128)(2,1)} async-done(((bf16[8,2,10,32,128]{4,3,2,1,0:T(8,128)(2,1)}), bf16[8,2,10,32,128]{4,3,2,1,0:T(8,128)(2,1)}, u32[]{:S(2)}, u32[]{:S(2)}) %all-to-all-start.1) | async-done | bytes 1310752 | tf_op jit(solution)/shard_map/all_to_all | solution.py:156
  60.8 1.6 %copy-done.1 = f32[2,8,256,128]{3,2,1,0:T(8,128)S(1)} copy-done((f32[2,8,256,128]{3,2,1,0:T(8,128)S(1)}, f32[2,8,256,128]{3,2,1,0:T(8,128)}, u32[]{:S(2)}) %copy-start.1) | copy-done | bytes 2097176
  62.4 7.0 %shard_map.40 = (bf16[2,8,64,128]{3,2,1,0:T(8,128)(2,1)S(1)}, bf16[2,8,64,128]{3,2,1,0:T(8,128)(2,1)S(1)}, bf16[2,8,64,128]{3,2,1,0:T(8,128)(2,1)S(1)}, bf16[2,8,64,128]{3,2,1,0:T(8,128)(2,1)S(1)}) custom-call(f32[2,8,256,128]{3,2,1,0:T(8,128)S(1)} %copy-done.1, bf16[8,2,10,32,128]{4,3,2,1,0:T(8,128)(2,1)} %all-to-all-done.1.refs_1_, ...), custom_call_target="tpu_custom_call" | custom-call | flops 4831838208 | bytes 10000000 | tf_op jit(solution)/shard_map/pallas_call | solution.py:121
  70.1 1.4 %collective-permute-start.5 = (bf16[2,8,64,128]{3,2,1,0:T(8,128)(2,1)S(1)}, bf16[2,8,64,128]{3,2,1,0:T(8,128)(2,1)S(1)}, u32[]{:S(2)}, u32[]{:S(2)}) collective-permute-start(bf16[2,8,64,128]{3,2,1,0:T(8,128)(2,1)S(1)} %get-tuple-element.27), channel_id=1, source_target_pairs={{0,4},{1,5},{2,6},{3,7},{4,0},{5,1},{6,2},{7,3},{8,12},{9,13},{10,... | collective-permute-start | bytes 786440 | tf_op jit(solution)/shard_map/ppermute | solution.py:146
  71.5 1.5 %collective-permute-start.4 = (bf16[2,8,64,128]{3,2,1,0:T(8,128)(2,1)S(1)}, bf16[2,8,64,128]{3,2,1,0:T(8,128)(2,1)S(1)}, u32[]{:S(2)}, u32[]{:S(2)}) collective-permute-start(bf16[2,8,64,128]{3,2,1,0:T(8,128)(2,1)S(1)} %get-tuple-element.26), channel_id=1, source_target_pairs={{0,2},{1,3},{2,0},{3,1},{4,6},{5,7},{6,4},{7,5},{8,10},{9,11},{10,... | collective-permute-start | bytes 786440 | tf_op jit(solution)/shard_map/ppermute | solution.py:146
  73.0 9.9 %shard_map.42 = (bf16[2,8,64,128]{3,2,1,0:T(8,128)(2,1)S(1)}, bf16[2,8,64,128]{3,2,1,0:T(8,128)(2,1)S(1)}, bf16[2,8,64,128]{3,2,1,0:T(8,128)(2,1)S(1)}, bf16[2,8,64,128]{3,2,1,0:T(8,128)(2,1)S(1)}) custom-call(bf16[8,2,10,32,128]{4,3,2,1,0:T(8,128)(2,1)S(1)} %all-to-all-done.refs_0_.vol_ref, bf16[8,2,10,32,128]{4,3,2,1,0:T(8,128)(2,1)} %all-to-all-done.1.refs_1_, ...), custom_call_target="tpu_custom_call" | custom-call | flops 7247757312 | bytes 10000000 | tf_op jit(solution)/shard_map/pallas_call | solution.py:121
  83.6 1.4 %collective-permute-start.11 = (bf16[2,8,64,128]{3,2,1,0:T(8,128)(2,1)S(1)}, bf16[2,8,64,128]{3,2,1,0:T(8,128)(2,1)S(1)}, u32[]{:S(2)}, u32[]{:S(2)}) collective-permute-start(bf16[2,8,64,128]{3,2,1,0:T(8,128)(2,1)S(1)} %get-tuple-element.33), channel_id=1, source_target_pairs={{0,4},{1,5},{2,6},{3,7},{4,0},{5,1},{6,2},{7,3},{8,12},{9,13},{10,... | collective-permute-start | bytes 786440 | tf_op jit(solution)/shard_map/ppermute | solution.py:146
  85.0 1.6 %collective-permute-start.10 = (bf16[2,8,64,128]{3,2,1,0:T(8,128)(2,1)S(1)}, bf16[2,8,64,128]{3,2,1,0:T(8,128)(2,1)S(1)}, u32[]{:S(2)}, u32[]{:S(2)}) collective-permute-start(bf16[2,8,64,128]{3,2,1,0:T(8,128)(2,1)S(1)} %get-tuple-element.32), channel_id=1, source_target_pairs={{0,2},{1,3},{2,0},{3,1},{4,6},{5,7},{6,4},{7,5},{8,10},{9,11},{10,... | collective-permute-start | bytes 786440 | tf_op jit(solution)/shard_map/ppermute | solution.py:146
  86.8 6.1 %collective-permute-done.12 = bf16[2,8,64,128]{3,2,1,0:T(8,128)(2,1)S(1)} collective-permute-done((bf16[2,8,64,128]{3,2,1,0:T(8,128)(2,1)S(1)}, bf16[2,8,64,128]{3,2,1,0:T(8,128)(2,1)S(1)}, u32[]{:S(2)}, u32[]{:S(2)}) %collective-permute-start.12) | collective-permute-done | bytes 262176 | tf_op jit(solution)/shard_map/ppermute | solution.py:146
  93.0 2.7 %collective-permute-done.11 = bf16[2,8,64,128]{3,2,1,0:T(8,128)(2,1)S(1)} collective-permute-done((bf16[2,8,64,128]{3,2,1,0:T(8,128)(2,1)S(1)}, bf16[2,8,64,128]{3,2,1,0:T(8,128)(2,1)S(1)}, u32[]{:S(2)}, u32[]{:S(2)}) %collective-permute-start.11) | collective-permute-done | bytes 262176 | tf_op jit(solution)/shard_map/ppermute | solution.py:146
  99.2 1.6 %pad_maximum_fusion = bf16[4,32,64,128]{3,2,1,0:T(8,128)(2,1)} fusion(bf16[1,32,64,128]{3,2,1,0:T(8,128)(2,1)S(1)} %get-tuple-element.40, bf16[2,32,64,128]{3,2,1,0:T(8,128)(2,1)S(1)} %bitcast.63, bf16[1,32,64,128]{3,2,1,0:T(8,128)(2,1)S(1)} %get-tuple-element.39), kind=kLoop, calls=%fused_computation.1 | loop fusion | flops 2097152 | bytes 4194304 | tf_op jit(solution)/shard_map/concatenate | solution.py:203
  (77 shorter events, 13.3 us)
Async XLA Ops:
  0.0 14.1 %collective-permute-start = (bf16[3,3,3,32,256]{4,3,2,1,0:T(8,128)(2,1)}, bf16[3,3,3,32,256]{4,3,2,1,0:T(8,128)(2,1)S(1)}, u32[]{:S(2)}, u32[]{:S(2)}) collective-permute-start(bf16[3,3,3,32,256]{4,3,2,1,0:T(8,128)(2,1)} %param.4), channel_id=1, source_target_pairs={{0,2},{1,3},{2,0},{3,1},{4,6},{5,7},{6,4},{7,5},{8,10},{9,11},{10,... | collective-permute-start | bytes 1327112 | tf_op jit(solution)/shard_map/ppermute | solution.py:146
  2.9 21.9 %collective-permute-start.1 = (bf16[3,3,3,32,256]{4,3,2,1,0:T(8,128)(2,1)}, bf16[3,3,3,32,256]{4,3,2,1,0:T(8,128)(2,1)S(1)}, u32[]{:S(2)}, u32[]{:S(2)}) collective-permute-start(bf16[3,3,3,32,256]{4,3,2,1,0:T(8,128)(2,1)} %param.4), channel_id=1, source_target_pairs={{0,4},{1,5},{2,6},{3,7},{4,0},{5,1},{6,2},{7,3},{8,12},{9,13},{10,... | collective-permute-start | bytes 1327112 | tf_op jit(solution)/shard_map/ppermute | solution.py:146
  4.5 20.7 %collective-permute-start.2 = (bf16[3,3,3,32,256]{4,3,2,1,0:T(8,128)(2,1)}, bf16[3,3,3,32,256]{4,3,2,1,0:T(8,128)(2,1)S(1)}, u32[]{:S(2)}, u32[]{:S(2)}) collective-permute-start(bf16[3,3,3,32,256]{4,3,2,1,0:T(8,128)(2,1)} %param.4), channel_id=1, source_target_pairs={{0,6},{1,7},{2,4},{3,5},{4,2},{5,3},{6,0},{7,1},{8,14},{9,15},{10,... | collective-permute-start | bytes 1327112 | tf_op jit(solution)/shard_map/ppermute | solution.py:146
  7.7 18.2 %copy-start.2 = (bf16[3,3,3,32,256]{4,3,2,1,0:T(8,128)(2,1)S(1)}, bf16[3,3,3,32,256]{4,3,2,1,0:T(8,128)(2,1)}, u32[]{:S(2)}) copy-start(bf16[3,3,3,32,256]{4,3,2,1,0:T(8,128)(2,1)} %param.4) | copy-start | bytes 1327108
  7.7 30.6 %all-to-all-start = ((bf16[8,2,10,32,128]{4,3,2,1,0:T(8,128)(2,1)}), bf16[8,2,10,32,128]{4,3,2,1,0:T(8,128)(2,1)S(1)}, u32[]{:S(2)}, u32[]{:S(2)}) async-start(bf16[8,2,10,32,128]{4,3,2,1,0:T(8,128)(2,1)} %shard_map.37), calls=%async_computation | async-start | bytes 2621440 | tf_op jit(solution)/shard_map/all_to_all | solution.py:155
  14.1 11.1 %copy-start.3 = (bf16[3,3,3,32,256]{4,3,2,1,0:T(8,128)(2,1)}, bf16[3,3,3,32,256]{4,3,2,1,0:T(8,128)(2,1)S(1)}, u32[]{:S(2)}) copy-start(bf16[3,3,3,32,256]{4,3,2,1,0:T(8,128)(2,1)S(1)} %collective-permute-done) | copy-start | bytes 1327108
  24.8 0.8 copy-start.4
  25.2 0.8 copy-start.5
  27.5 1.2 %slice-start = ((bf16[4,32,64,128]{3,2,1,0:T(8,128)(2,1)}), bf16[2,32,64,128]{3,2,1,0:T(8,128)(2,1)S(1)}, s32[]{:S(2)}) async-start(bf16[4,32,64,128]{3,2,1,0:T(8,128)(2,1)} %param.3), calls=%async_computation.2 | async-start | bytes 2097152 | tf_op jit(solution)/shard_map/slice | solution.py:156
  27.5 23.1 %collective-permute-start.3 = (bf16[4,3,3,3,32,256]{5,4,3,2,1,0:T(8,128)(2,1)S(1)}, bf16[4,3,3,3,32,256]{5,4,3,2,1,0:T(8,128)(2,1)}, u32[]{:S(2)}, u32[]{:S(2)}) collective-permute-start(bf16[4,3,3,3,32,256]{5,4,3,2,1,0:T(8,128)(2,1)S(1)} %pad_maximum_fusion.1.refs_1_.refs_2_.refs_4_), channel_id=1, source_target_pairs={{0,1},{1,0},{2,3},{3,2},{4,5},{5,4},{6,7},{7,6},{8,9},{9,8},{10,11... | collective-permute-start | bytes 5308424 | tf_op jit(solution)/shard_map/ppermute | solution.py:146
  30.6 12.1 %copy-start.6 = (f32[256]{0:T(256)S(1)}, f32[256]{0:T(256)}, u32[]{:S(2)}) copy-start(f32[256]{0:T(256)} %param.5) | copy-start | bytes 3076
  38.3 22.5 %all-to-all-start.1 = ((bf16[8,2,10,32,128]{4,3,2,1,0:T(8,128)(2,1)}), bf16[8,2,10,32,128]{4,3,2,1,0:T(8,128)(2,1)}, u32[]{:S(2)}, u32[]{:S(2)}) async-start(bf16[8,2,10,32,128]{4,3,2,1,0:T(8,128)(2,1)} %shard_map.39), calls=%async_computation.1 | async-start | bytes 2621440 | tf_op jit(solution)/shard_map/all_to_all | solution.py:156
  44.8 28.2 %collective-permute-start.8 = (bf16[8,1,10,32,128]{4,3,2,1,0:T(8,128)(2,1)}, bf16[8,1,10,32,128]{4,3,2,1,0:T(8,128)(2,1)}, u32[]{:S(2)}, u32[]{:S(2)}) collective-permute-start(bf16[8,1,10,32,128]{4,3,2,1,0:T(8,128)(2,1)} %get-tuple-element.29), channel_id=1, source_target_pairs={{0,8},{8,16},{16,24},{1,9},{9,17},{17,25},{2,10},{10,18},{18,26},{... | collective-permute-start | bytes 1966088 | tf_op jit(solution)/shard_map/ppermute | solution.py:198
  49.1 23.9 %collective-permute-start.9 = (bf16[8,1,10,32,128]{4,3,2,1,0:T(8,128)(2,1)}, bf16[8,1,10,32,128]{4,3,2,1,0:T(8,128)(2,1)}, u32[]{:S(2)}, u32[]{:S(2)}) collective-permute-start(bf16[8,1,10,32,128]{4,3,2,1,0:T(8,128)(2,1)} %get-tuple-element.30), channel_id=1, source_target_pairs={{8,0},{16,8},{24,16},{9,1},{17,9},{25,17},{10,2},{18,10},{26,18},{... | collective-permute-start | bytes 1966088 | tf_op jit(solution)/shard_map/ppermute | solution.py:197
  55.0 1.3 %copy-start = (f32[2,8,256,128]{3,2,1,0:T(8,128)}, f32[2,8,256,128]{3,2,1,0:T(8,128)S(1)}, u32[]{:S(2)}) copy-start(f32[2,8,256,128]{3,2,1,0:T(8,128)S(1)} %shard_map.38.refs_0_) | copy-start | bytes 6291460
  60.8 1.6 %copy-start.1 = (f32[2,8,256,128]{3,2,1,0:T(8,128)S(1)}, f32[2,8,256,128]{3,2,1,0:T(8,128)}, u32[]{:S(2)}) copy-start(f32[2,8,256,128]{3,2,1,0:T(8,128)} %copy-done) | copy-start | bytes 6291460
  69.5 15.5 %collective-permute-start.6 = (bf16[2,8,64,128]{3,2,1,0:T(8,128)(2,1)S(1)}, bf16[2,8,64,128]{3,2,1,0:T(8,128)(2,1)S(1)}, u32[]{:S(2)}, u32[]{:S(2)}) collective-permute-start(bf16[2,8,64,128]{3,2,1,0:T(8,128)(2,1)S(1)} %get-tuple-element.28), channel_id=1, source_target_pairs={{0,6},{1,7},{2,4},{3,5},{4,2},{5,3},{6,0},{7,1},{8,14},{9,15},{10,... | collective-permute-start | bytes 786440 | tf_op jit(solution)/shard_map/ppermute | solution.py:146
  70.1 16.5 %collective-permute-start.5 = (bf16[2,8,64,128]{3,2,1,0:T(8,128)(2,1)S(1)}, bf16[2,8,64,128]{3,2,1,0:T(8,128)(2,1)S(1)}, u32[]{:S(2)}, u32[]{:S(2)}) collective-permute-start(bf16[2,8,64,128]{3,2,1,0:T(8,128)(2,1)S(1)} %get-tuple-element.27), channel_id=1, source_target_pairs={{0,4},{1,5},{2,6},{3,7},{4,0},{5,1},{6,2},{7,3},{8,12},{9,13},{10,... | collective-permute-start | bytes 786440 | tf_op jit(solution)/shard_map/ppermute | solution.py:146
  71.5 15.2 %collective-permute-start.4 = (bf16[2,8,64,128]{3,2,1,0:T(8,128)(2,1)S(1)}, bf16[2,8,64,128]{3,2,1,0:T(8,128)(2,1)S(1)}, u32[]{:S(2)}, u32[]{:S(2)}) collective-permute-start(bf16[2,8,64,128]{3,2,1,0:T(8,128)(2,1)S(1)} %get-tuple-element.26), channel_id=1, source_target_pairs={{0,2},{1,3},{2,0},{3,1},{4,6},{5,7},{6,4},{7,5},{8,10},{9,11},{10,... | collective-permute-start | bytes 786440 | tf_op jit(solution)/shard_map/ppermute | solution.py:146
  82.9 10.0 %collective-permute-start.12 = (bf16[2,8,64,128]{3,2,1,0:T(8,128)(2,1)S(1)}, bf16[2,8,64,128]{3,2,1,0:T(8,128)(2,1)S(1)}, u32[]{:S(2)}, u32[]{:S(2)}) collective-permute-start(bf16[2,8,64,128]{3,2,1,0:T(8,128)(2,1)S(1)} %get-tuple-element.34), channel_id=1, source_target_pairs={{0,6},{1,7},{2,4},{3,5},{4,2},{5,3},{6,0},{7,1},{8,14},{9,15},{10,... | collective-permute-start | bytes 786440 | tf_op jit(solution)/shard_map/ppermute | solution.py:146
  83.6 12.1 %collective-permute-start.11 = (bf16[2,8,64,128]{3,2,1,0:T(8,128)(2,1)S(1)}, bf16[2,8,64,128]{3,2,1,0:T(8,128)(2,1)S(1)}, u32[]{:S(2)}, u32[]{:S(2)}) collective-permute-start(bf16[2,8,64,128]{3,2,1,0:T(8,128)(2,1)S(1)} %get-tuple-element.33), channel_id=1, source_target_pairs={{0,4},{1,5},{2,6},{3,7},{4,0},{5,1},{6,2},{7,3},{8,12},{9,13},{10,... | collective-permute-start | bytes 786440 | tf_op jit(solution)/shard_map/ppermute | solution.py:146
  85.0 10.7 %collective-permute-start.10 = (bf16[2,8,64,128]{3,2,1,0:T(8,128)(2,1)S(1)}, bf16[2,8,64,128]{3,2,1,0:T(8,128)(2,1)S(1)}, u32[]{:S(2)}, u32[]{:S(2)}) collective-permute-start(bf16[2,8,64,128]{3,2,1,0:T(8,128)(2,1)S(1)} %get-tuple-element.32), channel_id=1, source_target_pairs={{0,2},{1,3},{2,0},{3,1},{4,6},{5,7},{6,4},{7,5},{8,10},{9,11},{10,... | collective-permute-start | bytes 786440 | tf_op jit(solution)/shard_map/ppermute | solution.py:146
  86.8 9.9 %collective-permute-start.7 = (bf16[4,2,8,32,128]{4,3,2,1,0:T(8,128)(2,1)S(1)}, bf16[4,2,8,32,128]{4,3,2,1,0:T(8,128)(2,1)S(1)}, u32[]{:S(2)}, u32[]{:S(2)}) collective-permute-start(bf16[4,2,8,32,128]{4,3,2,1,0:T(8,128)(2,1)S(1)} %pad_maximum_fusion.2), channel_id=1, source_target_pairs={{0,1},{1,0},{2,3},{3,2},{4,5},{5,4},{6,7},{7,6},{8,9},{9,8},{10,11... | collective-permute-start | bytes 1572872 | tf_op jit(solution)/shard_map/ppermute | solution.py:146
  95.9 2.0 %collective-permute-start.13 = (bf16[4,2,8,32,128]{4,3,2,1,0:T(8,128)(2,1)S(1)}, bf16[4,2,8,32,128]{4,3,2,1,0:T(8,128)(2,1)S(1)}, u32[]{:S(2)}, u32[]{:S(2)}) collective-permute-start(bf16[4,2,8,32,128]{4,3,2,1,0:T(8,128)(2,1)S(1)} %pad_maximum_fusion.3), channel_id=1, source_target_pairs={{0,1},{1,0},{2,3},{3,2},{4,5},{5,4},{6,7},{7,6},{8,9},{9,8},{10,11... | collective-permute-start | bytes 1572872 | tf_op jit(solution)/shard_map/ppermute | solution.py:146

commit v19 on v15

--- a/solution.py
+++ b/solution.py
@@ -135,19 +135,18 @@
 
 
     near = [swap(kernel, k) for k in across[1 : 3 if len(across) == 4 else None]]
+    outer_rows = cut(jnp.concatenate([features[:1], features[-1:]]), parts)
+    inner_rows = cut(features[1:-1], parts)
     if len(across) == 4:
         half = out_chan // 2
         by_x, by_y = near
         far = [swap(by_x[:, :, :, :half], across[2]), swap(by_y[:, :, :, half:], across[1])]
-        fetched = [kernel, by_x, by_y, jnp.concatenate(far, axis=3)]
-    else:
-        fetched = [kernel, *near]
-    same = jnp.stack(fetched)
+        far = lax.optimization_barrier((far, inner_rows))[0]
+        near = [by_x, by_y, jnp.concatenate(far, axis=3)]
+    same = jnp.stack([kernel, *near])
     tap_parts = [same, swap(same, 1)]
-
-    outer = lax.all_to_all(cut(jnp.concatenate([features[:1], features[-1:]]), parts), "filt", 0, 0)
-    between = lax.optimization_barrier((features[1:-1], near))[0]
-    inner = lax.all_to_all(cut(between, parts), "filt", 0, 0)
+    outer = lax.all_to_all(outer_rows, "filt", 0, 0)
+    inner = lax.all_to_all(inner_rows, "filt", 0, 0)
     arrived = outer
     order = jnp.stack([me ^ k ^ c for k in across for c in range(2)])
     bias = jnp.take(bias_vector.reshape(parts, out_chan), order, axis=0).reshape(-1)

time: 102 us -> 97.7 us (0.958)
  waiting for transfers between devices: 36.8 us -> 34.9 us
  local copies, waits for them, and re-layouts: 6.92 us -> 5.8 us
    ppermute x13, waiting for transfers between devices: 27.5 us -> 25.6 us  [swap(): lax.ppermute(array, axis, [(i, i ^ k) for i in range(lax.axis_size(axis))])]
    slice x3, local copies, waits for them, and re-layouts: 2.41 us -> 1.28 us  [the longest x1 1.27 us: body(): outer_rows = cut(jnp.concatenate([features[:1], features[-1:]]), parts)]
  transfers between devices with their start and end apart: 17 -> 17, of which waited for: 7 -> 7; matrix products, arithmetic and copies ran while one was open for 6% -> 5% of each run, Pallas kernels for 23% -> 23%
where the time goes in v19:
time: 97.7 us; the launch traced here: 97.4 us
  waiting for transfers between devices  34.9 us (36%)
  starting transfers between devices  31.1 us (32%)
  Pallas kernels  22.9 us (23%)
  local copies, waits for them, and re-layouts  5.8 us (6%)
  other arithmetic  2.17 us (2%)
    ppermute x13, waiting for transfers between devices, swap(): lax.ppermute(array, axis, [(i, i ^ k) for i in range(lax.axis_size(axis))])  25.6 us
    pallas_call x2, Pallas kernels, convolve(): pl.pallas_call(functools.partial(conv_kernel, plan, min(ROWS, rows), len(...  19.3 us
    ppermute x13, starting transfers between devices, swap(): lax.ppermute(array, axis, [(i, i ^ k) for i in range(lax.axis_size(axis))])  16.6 us
    all_to_all x1, waiting for transfers between devices, body(): inner = lax.all_to_all(inner_rows, 'filt', 0, 0)  9.32 us
    ppermute x1, starting transfers between devices, body(): before = lax.ppermute(last, 'slab', up)  5.41 us
    all_to_all x1, starting transfers between devices, body(): inner = lax.all_to_all(inner_rows, 'filt', 0, 0)  4.29 us
    all_to_all x1, starting transfers between devices, body(): outer = lax.all_to_all(outer_rows, 'filt', 0, 0)  3.57 us
    pallas_call x2, Pallas kernels, cut(): pl.pallas_call(functools.partial(cut_kernel, parts), out_shape=jax.ShapeD...  2.35 us
  transfers between devices with their start and end apart: 17, of which 7 were waited for; matrix products, arithmetic and copies ran while one was open for 5% of the time, Pallas kernels for 23%

profile of v19, /device:TPU:0, one launch (start us, length us, event | category | flops | bytes accessed | tf_op | source)
XLA Modules:
  0.0 97.4 jit_solution(10058553466883355348)
XLA Ops:
  0.0 2.9 %collective-permute-start = (bf16[3,3,3,32,256]{4,3,2,1,0:T(8,128)(2,1)}, bf16[3,3,3,32,256]{4,3,2,1,0:T(8,128)(2,1)S(1)}, u32[]{:S(2)}, u32[]{:S(2)}) collective-permute-start(bf16[3,3,3,32,256]{4,3,2,1,0:T(8,128)(2,1)} %param.4), channel_id=1, source_target_pairs={{0,2},{1,3},{2,0},{3,1},{4,6},{5,7},{6,4},{7,5},{8,10},{9,11},{10,... | collective-permute-start | bytes 1327112 | tf_op jit(solution)/shard_map/ppermute | solution.py:134
  2.9 1.5 %collective-permute-start.1 = (bf16[3,3,3,32,256]{4,3,2,1,0:T(8,128)(2,1)}, bf16[3,3,3,32,256]{4,3,2,1,0:T(8,128)(2,1)S(1)}, u32[]{:S(2)}, u32[]{:S(2)}) collective-permute-start(bf16[3,3,3,32,256]{4,3,2,1,0:T(8,128)(2,1)} %param.4), channel_id=1, source_target_pairs={{0,4},{1,5},{2,6},{3,7},{4,0},{5,1},{6,2},{7,3},{8,12},{9,13},{10,... | collective-permute-start | bytes 1327112 | tf_op jit(solution)/shard_map/ppermute | solution.py:134
  4.5 1.3 %fusion.1 = (bf16[1,32,64,128]{3,2,1,0:T(8,128)(2,1)S(1)}, bf16[1,32,64,128]{3,2,1,0:T(8,128)(2,1)S(1)}) fusion(bf16[4,32,64,128]{3,2,1,0:T(8,128)(2,1)} %param.3), kind=kLoop, calls=%fused_computation.46 | loop fusion | bytes 2097152 | tf_op jit(solution)/shard_map/slice | solution.py:138
  6.5 1.2 %shard_map.37 = bf16[8,2,10,32,128]{4,3,2,1,0:T(8,128)(2,1)} custom-call(bf16[2,64,32,128]{3,2,1,0:T(8,128)(2,1)S(1)} %maximum_bitcast_fusion.vol_ref), custom_call_target="tpu_custom_call" | custom-call | tf_op jit(solution)/shard_map/pallas_call | solution.py:29
  7.7 3.6 %all-to-all-start = ((bf16[8,2,10,32,128]{4,3,2,1,0:T(8,128)(2,1)}), bf16[8,2,10,32,128]{4,3,2,1,0:T(8,128)(2,1)S(1)}, u32[]{:S(2)}, u32[]{:S(2)}) async-start(bf16[8,2,10,32,128]{4,3,2,1,0:T(8,128)(2,1)} %shard_map.37), calls=%async_computation | async-start | bytes 2621440 | tf_op jit(solution)/shard_map/all_to_all | solution.py:148
  11.3 2.0 %collective-permute-done = bf16[3,3,3,32,256]{4,3,2,1,0:T(8,128)(2,1)S(1)} collective-permute-done((bf16[3,3,3,32,256]{4,3,2,1,0:T(8,128)(2,1)}, bf16[3,3,3,32,256]{4,3,2,1,0:T(8,128)(2,1)S(1)}, u32[]{:S(2)}, u32[]{:S(2)}) %collective-permute-start) | collective-permute-done | bytes 442400 | tf_op jit(solution)/shard_map/ppermute | solution.py:134
  13.3 1.8 %collective-permute-start.2 = (bf16[3,3,3,16,256]{4,3,2,1,0:T(8,128)(2,1)S(1)}, bf16[3,3,3,16,256]{4,3,2,1,0:T(8,128)(2,1)S(1)}, u32[]{:S(2)}, u32[]{:S(2)}) collective-permute-start(bf16[3,3,3,16,256]{4,3,2,1,0:T(8,128)(2,1)S(1)} %slice.126), channel_id=1, source_target_pairs={{0,4},{1,5},{2,6},{3,7},{4,0},{5,1},{6,2},{7,3},{8,12},{9,13},{10,... | collective-permute-start | bytes 663560 | tf_op jit(solution)/shard_map/ppermute | solution.py:134
  15.4 2.9 %collective-permute-start.3 = (bf16[3,3,3,16,256]{4,3,2,1,0:T(8,128)(2,1)S(1)}, bf16[3,3,3,16,256]{4,3,2,1,0:T(8,128)(2,1)S(1)}, u32[]{:S(2)}, u32[]{:S(2)}) collective-permute-start(bf16[3,3,3,16,256]{4,3,2,1,0:T(8,128)(2,1)S(1)} %slice.127), channel_id=1, source_target_pairs={{0,2},{1,3},{2,0},{3,1},{4,6},{5,7},{6,4},{7,5},{8,10},{9,11},{10,... | collective-permute-start | bytes 663560 | tf_op jit(solution)/shard_map/ppermute | solution.py:134
  19.0 1.2 %shard_map.38 = bf16[8,2,10,32,128]{4,3,2,1,0:T(8,128)(2,1)} custom-call(bf16[2,64,32,128]{3,2,1,0:T(8,128)(2,1)S(1)} %bitcast.62), custom_call_target="tpu_custom_call" | custom-call | tf_op jit(solution)/shard_map/pallas_call | solution.py:29
  20.2 13.4 %collective-permute-done.2 = bf16[3,3,3,16,256]{4,3,2,1,0:T(8,128)(2,1)S(1)} collective-permute-done((bf16[3,3,3,16,256]{4,3,2,1,0:T(8,128)(2,1)S(1)}, bf16[3,3,3,16,256]{4,3,2,1,0:T(8,128)(2,1)S(1)}, u32[]{:S(2)}, u32[]{:S(2)}) %collective-permute-start.2) | collective-permute-done | bytes 221216 | tf_op jit(solution)/shard_map/ppermute | solution.py:134
  34.0 4.3 %all-to-all-start.1 = ((bf16[8,2,10,32,128]{4,3,2,1,0:T(8,128)(2,1)}), bf16[8,2,10,32,128]{4,3,2,1,0:T(8,128)(2,1)}, u32[]{:S(2)}, u32[]{:S(2)}) async-start(bf16[8,2,10,32,128]{4,3,2,1,0:T(8,128)(2,1)} %shard_map.38), calls=%async_computation.1 | async-start | bytes 2621440 | tf_op jit(solution)/shard_map/all_to_all | solution.py:149
  40.5 1.3 %collective-permute-start.10 = (bf16[8,1,10,32,128]{4,3,2,1,0:T(8,128)(2,1)}, bf16[8,1,10,32,128]{4,3,2,1,0:T(8,128)(2,1)}, u32[]{:S(2)}, u32[]{:S(2)}) collective-permute-start(bf16[8,1,10,32,128]{4,3,2,1,0:T(8,128)(2,1)} %get-tuple-element.26), channel_id=1, source_target_pairs={{8,0},{16,8},{24,16},{9,1},{17,9},{25,17},{10,2},{18,10},{26,18},{... | collective-permute-start | bytes 1966088 | tf_op jit(solution)/shard_map/ppermute | solution.py:181
  41.8 5.4 %collective-permute-start.9 = (bf16[8,1,10,32,128]{4,3,2,1,0:T(8,128)(2,1)}, bf16[8,1,10,32,128]{4,3,2,1,0:T(8,128)(2,1)}, u32[]{:S(2)}, u32[]{:S(2)}) collective-permute-start(bf16[8,1,10,32,128]{4,3,2,1,0:T(8,128)(2,1)} %get-tuple-element.25), channel_id=1, source_target_pairs={{0,8},{8,16},{16,24},{1,9},{9,17},{17,25},{2,10},{10,18},{18,26},{... | collective-permute-start | bytes 1966088 | tf_op jit(solution)/shard_map/ppermute | solution.py:182
  47.2 9.3 %all-to-all-done.1.refs_1_ = bf16[8,2,10,32,128]{4,3,2,1,0:T(8,128)(2,1)} async-done(((bf16[8,2,10,32,128]{4,3,2,1,0:T(8,128)(2,1)}), bf16[8,2,10,32,128]{4,3,2,1,0:T(8,128)(2,1)}, u32[]{:S(2)}, u32[]{:S(2)}) %all-to-all-start.1) | async-done | bytes 1310752 | tf_op jit(solution)/shard_map/all_to_all | solution.py:149
  56.6 9.5 %shard_map.39 = (bf16[2,8,64,128]{3,2,1,0:T(8,128)(2,1)S(1)}, bf16[2,8,64,128]{3,2,1,0:T(8,128)(2,1)S(1)}, bf16[2,8,64,128]{3,2,1,0:T(8,128)(2,1)S(1)}, bf16[2,8,64,128]{3,2,1,0:T(8,128)(2,1)S(1)}) custom-call(bf16[8,2,10,32,128]{4,3,2,1,0:T(8,128)(2,1)S(1)} %all-to-all-done.refs_0_.vol_ref, bf16[8,2,10,32,128]{4,3,2,1,0:T(8,128)(2,1)} %all-to-all-done.1.refs_1_, ...), custom_call_target="tpu_custom_call" | custom-call | flops 7247757312 | bytes 10000000 | tf_op jit(solution)/shard_map/pallas_call | solution.py:111
  66.7 1.4 %collective-permute-start.6 = (bf16[2,8,64,128]{3,2,1,0:T(8,128)(2,1)S(1)}, bf16[2,8,64,128]{3,2,1,0:T(8,128)(2,1)S(1)}, u32[]{:S(2)}, u32[]{:S(2)}) collective-permute-start(bf16[2,8,64,128]{3,2,1,0:T(8,128)(2,1)S(1)} %get-tuple-element.23), channel_id=1, source_target_pairs={{0,4},{1,5},{2,6},{3,7},{4,0},{5,1},{6,2},{7,3},{8,12},{9,13},{10,... | collective-permute-start | bytes 786440 | tf_op jit(solution)/shard_map/ppermute | solution.py:134
  68.1 1.5 %collective-permute-start.5 = (bf16[2,8,64,128]{3,2,1,0:T(8,128)(2,1)S(1)}, bf16[2,8,64,128]{3,2,1,0:T(8,128)(2,1)S(1)}, u32[]{:S(2)}, u32[]{:S(2)}) collective-permute-start(bf16[2,8,64,128]{3,2,1,0:T(8,128)(2,1)S(1)} %get-tuple-element.22), channel_id=1, source_target_pairs={{0,2},{1,3},{2,0},{3,1},{4,6},{5,7},{6,4},{7,5},{8,10},{9,11},{10,... | collective-permute-start | bytes 786440 | tf_op jit(solution)/shard_map/ppermute | solution.py:134
  69.6 9.9 %shard_map.41 = (bf16[2,8,64,128]{3,2,1,0:T(8,128)(2,1)S(1)}, bf16[2,8,64,128]{3,2,1,0:T(8,128)(2,1)S(1)}, bf16[2,8,64,128]{3,2,1,0:T(8,128)(2,1)S(1)}, bf16[2,8,64,128]{3,2,1,0:T(8,128)(2,1)S(1)}) custom-call(bf16[8,2,10,32,128]{4,3,2,1,0:T(8,128)(2,1)S(1)} %all-to-all-done.refs_0_.vol_ref, bf16[8,2,10,32,128]{4,3,2,1,0:T(8,128)(2,1)} %all-to-all-done.1.refs_1_, ...), custom_call_target="tpu_custom_call" | custom-call | flops 7247757312 | bytes 10000000 | tf_op jit(solution)/shard_map/pallas_call | solution.py:111
  80.2 1.4 %collective-permute-start.12 = (bf16[2,8,64,128]{3,2,1,0:T(8,128)(2,1)S(1)}, bf16[2,8,64,128]{3,2,1,0:T(8,128)(2,1)S(1)}, u32[]{:S(2)}, u32[]{:S(2)}) collective-permute-start(bf16[2,8,64,128]{3,2,1,0:T(8,128)(2,1)S(1)} %get-tuple-element.29), channel_id=1, source_target_pairs={{0,4},{1,5},{2,6},{3,7},{4,0},{5,1},{6,2},{7,3},{8,12},{9,13},{10,... | collective-permute-start | bytes 786440 | tf_op jit(solution)/shard_map/ppermute | solution.py:134
  81.6 1.6 %collective-permute-start.11 = (bf16[2,8,64,128]{3,2,1,0:T(8,128)(2,1)S(1)}, bf16[2,8,64,128]{3,2,1,0:T(8,128)(2,1)S(1)}, u32[]{:S(2)}, u32[]{:S(2)}) collective-permute-start(bf16[2,8,64,128]{3,2,1,0:T(8,128)(2,1)S(1)} %get-tuple-element.28), channel_id=1, source_target_pairs={{0,2},{1,3},{2,0},{3,1},{4,6},{5,7},{6,4},{7,5},{8,10},{9,11},{10,... | collective-permute-start | bytes 786440 | tf_op jit(solution)/shard_map/ppermute | solution.py:134
  83.5 6.1 %collective-permute-done.13 = bf16[2,8,64,128]{3,2,1,0:T(8,128)(2,1)S(1)} collective-permute-done((bf16[2,8,64,128]{3,2,1,0:T(8,128)(2,1)S(1)}, bf16[2,8,64,128]{3,2,1,0:T(8,128)(2,1)S(1)}, u32[]{:S(2)}, u32[]{:S(2)}) %collective-permute-start.13) | collective-permute-done | bytes 262176 | tf_op jit(solution)/shard_map/ppermute | solution.py:134
  89.6 2.7 %collective-permute-done.12 = bf16[2,8,64,128]{3,2,1,0:T(8,128)(2,1)S(1)} collective-permute-done((bf16[2,8,64,128]{3,2,1,0:T(8,128)(2,1)S(1)}, bf16[2,8,64,128]{3,2,1,0:T(8,128)(2,1)S(1)}, u32[]{:S(2)}, u32[]{:S(2)}) %collective-permute-start.12) | collective-permute-done | bytes 262176 | tf_op jit(solution)/shard_map/ppermute | solution.py:134
  93.3 1.2 %collective-permute-done.14 = bf16[4,2,8,32,128]{4,3,2,1,0:T(8,128)(2,1)S(1)} collective-permute-done((bf16[4,2,8,32,128]{4,3,2,1,0:T(8,128)(2,1)S(1)}, bf16[4,2,8,32,128]{4,3,2,1,0:T(8,128)(2,1)S(1)}, u32[]{:S(2)}, u32[]{:S(2)}) %collective-permute-start.14) | collective-permute-done | bytes 524320 | tf_op jit(solution)/shard_map/ppermute | solution.py:134
  95.8 1.6 %pad_maximum_fusion = bf16[4,32,64,128]{3,2,1,0:T(8,128)(2,1)} fusion(bf16[1,32,64,128]{3,2,1,0:T(8,128)(2,1)S(1)} %get-tuple-element.36, bf16[2,32,64,128]{3,2,1,0:T(8,128)(2,1)S(1)} %bitcast.64, bf16[1,32,64,128]{3,2,1,0:T(8,128)(2,1)S(1)} %get-tuple-element.35), kind=kLoop, calls=%fused_computation.1 | loop fusion | flops 2097152 | bytes 4194304 | tf_op jit(solution)/shard_map/concatenate | solution.py:187
  (75 shorter events, 8.1 us)
Async XLA Ops:
  0.0 13.3 %collective-permute-start = (bf16[3,3,3,32,256]{4,3,2,1,0:T(8,128)(2,1)}, bf16[3,3,3,32,256]{4,3,2,1,0:T(8,128)(2,1)S(1)}, u32[]{:S(2)}, u32[]{:S(2)}) collective-permute-start(bf16[3,3,3,32,256]{4,3,2,1,0:T(8,128)(2,1)} %param.4), channel_id=1, source_target_pairs={{0,2},{1,3},{2,0},{3,1},{4,6},{5,7},{6,4},{7,5},{8,10},{9,11},{10,... | collective-permute-start | bytes 1327112 | tf_op jit(solution)/shard_map/ppermute | solution.py:134
  2.9 12.4 %collective-permute-start.1 = (bf16[3,3,3,32,256]{4,3,2,1,0:T(8,128)(2,1)}, bf16[3,3,3,32,256]{4,3,2,1,0:T(8,128)(2,1)S(1)}, u32[]{:S(2)}, u32[]{:S(2)}) collective-permute-start(bf16[3,3,3,32,256]{4,3,2,1,0:T(8,128)(2,1)} %param.4), channel_id=1, source_target_pairs={{0,4},{1,5},{2,6},{3,7},{4,0},{5,1},{6,2},{7,3},{8,12},{9,13},{10,... | collective-permute-start | bytes 1327112 | tf_op jit(solution)/shard_map/ppermute | solution.py:134
  7.7 26.3 %all-to-all-start = ((bf16[8,2,10,32,128]{4,3,2,1,0:T(8,128)(2,1)}), bf16[8,2,10,32,128]{4,3,2,1,0:T(8,128)(2,1)S(1)}, u32[]{:S(2)}, u32[]{:S(2)}) async-start(bf16[8,2,10,32,128]{4,3,2,1,0:T(8,128)(2,1)} %shard_map.37), calls=%async_computation | async-start | bytes 2621440 | tf_op jit(solution)/shard_map/all_to_all | solution.py:148
  11.3 7.0 %slice-start = ((bf16[4,32,64,128]{3,2,1,0:T(8,128)(2,1)}), bf16[2,32,64,128]{3,2,1,0:T(8,128)(2,1)S(1)}, s32[]{:S(2)}) async-start(bf16[4,32,64,128]{3,2,1,0:T(8,128)(2,1)} %param.3), calls=%async_computation.2 | async-start | bytes 2097152 | tf_op jit(solution)/shard_map/slice | solution.py:139
  13.3 20.2 %collective-permute-start.2 = (bf16[3,3,3,16,256]{4,3,2,1,0:T(8,128)(2,1)S(1)}, bf16[3,3,3,16,256]{4,3,2,1,0:T(8,128)(2,1)S(1)}, u32[]{:S(2)}, u32[]{:S(2)}) collective-permute-start(bf16[3,3,3,16,256]{4,3,2,1,0:T(8,128)(2,1)S(1)} %slice.126), channel_id=1, source_target_pairs={{0,4},{1,5},{2,6},{3,7},{4,0},{5,1},{6,2},{7,3},{8,12},{9,13},{10,... | collective-permute-start | bytes 663560 | tf_op jit(solution)/shard_map/ppermute | solution.py:134
  15.4 3.6 %copy-start = (bf16[3,3,3,32,256]{4,3,2,1,0:T(8,128)(2,1)}, bf16[3,3,3,32,256]{4,3,2,1,0:T(8,128)(2,1)S(1)}, u32[]{:S(2)}) copy-start(bf16[3,3,3,32,256]{4,3,2,1,0:T(8,128)(2,1)S(1)} %collective-permute-done.1) | copy-start | bytes 1327108
  15.4 18.2 %collective-permute-start.3 = (bf16[3,3,3,16,256]{4,3,2,1,0:T(8,128)(2,1)S(1)}, bf16[3,3,3,16,256]{4,3,2,1,0:T(8,128)(2,1)S(1)}, u32[]{:S(2)}, u32[]{:S(2)}) collective-permute-start(bf16[3,3,3,16,256]{4,3,2,1,0:T(8,128)(2,1)S(1)} %slice.127), channel_id=1, source_target_pairs={{0,2},{1,3},{2,0},{3,1},{4,6},{5,7},{6,4},{7,5},{8,10},{9,11},{10,... | collective-permute-start | bytes 663560 | tf_op jit(solution)/shard_map/ppermute | solution.py:134
  19.0 14.6 %copy-start.2 = (bf16[3,3,3,32,256]{4,3,2,1,0:T(8,128)(2,1)S(1)}, bf16[3,3,3,32,256]{4,3,2,1,0:T(8,128)(2,1)}, u32[]{:S(2)}) copy-start(bf16[3,3,3,32,256]{4,3,2,1,0:T(8,128)(2,1)} %param.4) | copy-start | bytes 1327108
  19.0 14.6 %copy-start.1 = (bf16[3,3,3,32,256]{4,3,2,1,0:T(8,128)(2,1)S(1)}, bf16[3,3,3,32,256]{4,3,2,1,0:T(8,128)(2,1)}, u32[]{:S(2)}) copy-start(bf16[3,3,3,32,256]{4,3,2,1,0:T(8,128)(2,1)} %copy-done) | copy-start | bytes 1327108
  33.9 4.4 %copy-start.3 = (f32[256]{0:T(256)S(1)}, f32[256]{0:T(256)}, u32[]{:S(2)}) copy-start(f32[256]{0:T(256)} %param.5) | copy-start | bytes 3076
  33.9 22.6 %collective-permute-start.4 = (bf16[4,3,3,3,32,256]{5,4,3,2,1,0:T(8,128)(2,1)S(1)}, bf16[4,3,3,3,32,256]{5,4,3,2,1,0:T(8,128)(2,1)}, u32[]{:S(2)}, u32[]{:S(2)}) collective-permute-start(bf16[4,3,3,3,32,256]{5,4,3,2,1,0:T(8,128)(2,1)S(1)} %pad_maximum_fusion.1.refs_2_.refs_4_), channel_id=1, source_target_pairs={{0,1},{1,0},{2,3},{3,2},{4,5},{5,4},{6,7},{7,6},{8,9},{9,8},{10,11... | collective-permute-start | bytes 5308424 | tf_op jit(solution)/shard_map/ppermute | solution.py:134
  34.0 22.5 %all-to-all-start.1 = ((bf16[8,2,10,32,128]{4,3,2,1,0:T(8,128)(2,1)}), bf16[8,2,10,32,128]{4,3,2,1,0:T(8,128)(2,1)}, u32[]{:S(2)}, u32[]{:S(2)}) async-start(bf16[8,2,10,32,128]{4,3,2,1,0:T(8,128)(2,1)} %shard_map.38), calls=%async_computation.1 | async-start | bytes 2621440 | tf_op jit(solution)/shard_map/all_to_all | solution.py:149
  40.5 29.2 %collective-permute-start.10 = (bf16[8,1,10,32,128]{4,3,2,1,0:T(8,128)(2,1)}, bf16[8,1,10,32,128]{4,3,2,1,0:T(8,128)(2,1)}, u32[]{:S(2)}, u32[]{:S(2)}) collective-permute-start(bf16[8,1,10,32,128]{4,3,2,1,0:T(8,128)(2,1)} %get-tuple-element.26), channel_id=1, source_target_pairs={{8,0},{16,8},{24,16},{9,1},{17,9},{25,17},{10,2},{18,10},{26,18},{... | collective-permute-start | bytes 1966088 | tf_op jit(solution)/shard_map/ppermute | solution.py:181
  41.8 27.9 %collective-permute-start.9 = (bf16[8,1,10,32,128]{4,3,2,1,0:T(8,128)(2,1)}, bf16[8,1,10,32,128]{4,3,2,1,0:T(8,128)(2,1)}, u32[]{:S(2)}, u32[]{:S(2)}) collective-permute-start(bf16[8,1,10,32,128]{4,3,2,1,0:T(8,128)(2,1)} %get-tuple-element.25), channel_id=1, source_target_pairs={{0,8},{8,16},{16,24},{1,9},{9,17},{17,25},{2,10},{10,18},{18,26},{... | collective-permute-start | bytes 1966088 | tf_op jit(solution)/shard_map/ppermute | solution.py:182
  66.1 15.5 %collective-permute-start.7 = (bf16[2,8,64,128]{3,2,1,0:T(8,128)(2,1)S(1)}, bf16[2,8,64,128]{3,2,1,0:T(8,128)(2,1)S(1)}, u32[]{:S(2)}, u32[]{:S(2)}) collective-permute-start(bf16[2,8,64,128]{3,2,1,0:T(8,128)(2,1)S(1)} %get-tuple-element.24), channel_id=1, source_target_pairs={{0,6},{1,7},{2,4},{3,5},{4,2},{5,3},{6,0},{7,1},{8,14},{9,15},{10,... | collective-permute-start | bytes 786440 | tf_op jit(solution)/shard_map/ppermute | solution.py:134
  66.7 16.5 %collective-permute-start.6 = (bf16[2,8,64,128]{3,2,1,0:T(8,128)(2,1)S(1)}, bf16[2,8,64,128]{3,2,1,0:T(8,128)(2,1)S(1)}, u32[]{:S(2)}, u32[]{:S(2)}) collective-permute-start(bf16[2,8,64,128]{3,2,1,0:T(8,128)(2,1)S(1)} %get-tuple-element.23), channel_id=1, source_target_pairs={{0,4},{1,5},{2,6},{3,7},{4,0},{5,1},{6,2},{7,3},{8,12},{9,13},{10,... | collective-permute-start | bytes 786440 | tf_op jit(solution)/shard_map/ppermute | solution.py:134
  68.1 15.2 %collective-permute-start.5 = (bf16[2,8,64,128]{3,2,1,0:T(8,128)(2,1)S(1)}, bf16[2,8,64,128]{3,2,1,0:T(8,128)(2,1)S(1)}, u32[]{:S(2)}, u32[]{:S(2)}) collective-permute-start(bf16[2,8,64,128]{3,2,1,0:T(8,128)(2,1)S(1)} %get-tuple-element.22), channel_id=1, source_target_pairs={{0,2},{1,3},{2,0},{3,1},{4,6},{5,7},{6,4},{7,5},{8,10},{9,11},{10,... | collective-permute-start | bytes 786440 | tf_op jit(solution)/shard_map/ppermute | solution.py:134
  79.5 10.0 %collective-permute-start.13 = (bf16[2,8,64,128]{3,2,1,0:T(8,128)(2,1)S(1)}, bf16[2,8,64,128]{3,2,1,0:T(8,128)(2,1)S(1)}, u32[]{:S(2)}, u32[]{:S(2)}) collective-permute-start(bf16[2,8,64,128]{3,2,1,0:T(8,128)(2,1)S(1)} %get-tuple-element.30), channel_id=1, source_target_pairs={{0,6},{1,7},{2,4},{3,5},{4,2},{5,3},{6,0},{7,1},{8,14},{9,15},{10,... | collective-permute-start | bytes 786440 | tf_op jit(solution)/shard_map/ppermute | solution.py:134
  80.2 12.1 %collective-permute-start.12 = (bf16[2,8,64,128]{3,2,1,0:T(8,128)(2,1)S(1)}, bf16[2,8,64,128]{3,2,1,0:T(8,128)(2,1)S(1)}, u32[]{:S(2)}, u32[]{:S(2)}) collective-permute-start(bf16[2,8,64,128]{3,2,1,0:T(8,128)(2,1)S(1)} %get-tuple-element.29), channel_id=1, source_target_pairs={{0,4},{1,5},{2,6},{3,7},{4,0},{5,1},{6,2},{7,3},{8,12},{9,13},{10,... | collective-permute-start | bytes 786440 | tf_op jit(solution)/shard_map/ppermute | solution.py:134
  81.6 10.7 %collective-permute-start.11 = (bf16[2,8,64,128]{3,2,1,0:T(8,128)(2,1)S(1)}, bf16[2,8,64,128]{3,2,1,0:T(8,128)(2,1)S(1)}, u32[]{:S(2)}, u32[]{:S(2)}) collective-permute-start(bf16[2,8,64,128]{3,2,1,0:T(8,128)(2,1)S(1)} %get-tuple-element.28), channel_id=1, source_target_pairs={{0,2},{1,3},{2,0},{3,1},{4,6},{5,7},{6,4},{7,5},{8,10},{9,11},{10,... | collective-permute-start | bytes 786440 | tf_op jit(solution)/shard_map/ppermute | solution.py:134
  83.4 9.9 %collective-permute-start.8 = (bf16[4,2,8,32,128]{4,3,2,1,0:T(8,128)(2,1)S(1)}, bf16[4,2,8,32,128]{4,3,2,1,0:T(8,128)(2,1)S(1)}, u32[]{:S(2)}, u32[]{:S(2)}) collective-permute-start(bf16[4,2,8,32,128]{4,3,2,1,0:T(8,128)(2,1)S(1)} %pad_maximum_fusion.2), channel_id=1, source_target_pairs={{0,1},{1,0},{2,3},{3,2},{4,5},{5,4},{6,7},{7,6},{8,9},{9,8},{10,11... | collective-permute-start | bytes 1572872 | tf_op jit(solution)/shard_map/ppermute | solution.py:134
  92.5 2.0 %collective-permute-start.14 = (bf16[4,2,8,32,128]{4,3,2,1,0:T(8,128)(2,1)S(1)}, bf16[4,2,8,32,128]{4,3,2,1,0:T(8,128)(2,1)S(1)}, u32[]{:S(2)}, u32[]{:S(2)}) collective-permute-start(bf16[4,2,8,32,128]{4,3,2,1,0:T(8,128)(2,1)S(1)} %pad_maximum_fusion.3), channel_id=1, source_target_pairs={{0,1},{1,0},{2,3},{3,2},{4,5},{5,4},{6,7},{7,6},{8,9},{9,8},{10,11... | collective-permute-start | bytes 1572872 | tf_op jit(solution)/shard_map/ppermute | solution.py:134

commit v20 on v19

--- a/solution.py
+++ b/solution.py
@@ -8,7 +8,7 @@
 from jax.sharding import PartitionSpec as P
 
 slope = 0.3
-ROWS = 4
+ROWS = 8
 
 
 def cut_kernel(parts, vol_ref, out):

time: 97.7 us -> 97.7 us (level)
  no operation moved by 1% of the time
where the time goes in v20:
time: 97.7 us; the launch traced here: 97.4 us
  waiting for transfers between devices  34.9 us (36%)
  starting transfers between devices  31.1 us (32%)
  Pallas kernels  22.9 us (23%)
  local copies, waits for them, and re-layouts  5.8 us (6%)
  other arithmetic  2.17 us (2%)
    ppermute x13, waiting for transfers between devices, swap(): lax.ppermute(array, axis, [(i, i ^ k) for i in range(lax.axis_size(axis))])  25.6 us
    pallas_call x2, Pallas kernels, convolve(): pl.pallas_call(functools.partial(conv_kernel, plan, min(ROWS, rows), len(...  19.4 us
    ppermute x13, starting transfers between devices, swap(): lax.ppermute(array, axis, [(i, i ^ k) for i in range(lax.axis_size(axis))])  16.6 us
    all_to_all x1, waiting for transfers between devices, body(): inner = lax.all_to_all(inner_rows, 'filt', 0, 0)  9.32 us
    ppermute x1, starting transfers between devices, body(): before = lax.ppermute(last, 'slab', up)  5.41 us
    all_to_all x1, starting transfers between devices, body(): inner = lax.all_to_all(inner_rows, 'filt', 0, 0)  4.29 us
    all_to_all x1, starting transfers between devices, body(): outer = lax.all_to_all(outer_rows, 'filt', 0, 0)  3.57 us
    pallas_call x2, Pallas kernels, cut(): pl.pallas_call(functools.partial(cut_kernel, parts), out_shape=jax.ShapeD...  2.35 us
  transfers between devices with their start and end apart: 17, of which 7 were waited for; matrix products, arithmetic and copies ran while one was open for 5% of the time, Pallas kernels for 23%

profile of v20, /device:TPU:0, one launch (start us, length us, event | category | flops | bytes accessed | tf_op | source)
XLA Modules:
  0.0 97.4 jit_solution(17475840893257479172)
XLA Ops:
  0.0 2.9 %collective-permute-start = (bf16[3,3,3,32,256]{4,3,2,1,0:T(8,128)(2,1)}, bf16[3,3,3,32,256]{4,3,2,1,0:T(8,128)(2,1)S(1)}, u32[]{:S(2)}, u32[]{:S(2)}) collective-permute-start(bf16[3,3,3,32,256]{4,3,2,1,0:T(8,128)(2,1)} %param.4), channel_id=1, source_target_pairs={{0,2},{1,3},{2,0},{3,1},{4,6},{5,7},{6,4},{7,5},{8,10},{9,11},{10,... | collective-permute-start | bytes 1327112 | tf_op jit(solution)/shard_map/ppermute | solution.py:134
  2.9 1.5 %collective-permute-start.1 = (bf16[3,3,3,32,256]{4,3,2,1,0:T(8,128)(2,1)}, bf16[3,3,3,32,256]{4,3,2,1,0:T(8,128)(2,1)S(1)}, u32[]{:S(2)}, u32[]{:S(2)}) collective-permute-start(bf16[3,3,3,32,256]{4,3,2,1,0:T(8,128)(2,1)} %param.4), channel_id=1, source_target_pairs={{0,4},{1,5},{2,6},{3,7},{4,0},{5,1},{6,2},{7,3},{8,12},{9,13},{10,... | collective-permute-start | bytes 1327112 | tf_op jit(solution)/shard_map/ppermute | solution.py:134
  4.5 1.3 %fusion.1 = (bf16[1,32,64,128]{3,2,1,0:T(8,128)(2,1)S(1)}, bf16[1,32,64,128]{3,2,1,0:T(8,128)(2,1)S(1)}) fusion(bf16[4,32,64,128]{3,2,1,0:T(8,128)(2,1)} %param.3), kind=kLoop, calls=%fused_computation.46 | loop fusion | bytes 2097152 | tf_op jit(solution)/shard_map/slice | solution.py:138
  6.5 1.2 %shard_map.37 = bf16[8,2,10,32,128]{4,3,2,1,0:T(8,128)(2,1)} custom-call(bf16[2,64,32,128]{3,2,1,0:T(8,128)(2,1)S(1)} %maximum_bitcast_fusion.vol_ref), custom_call_target="tpu_custom_call" | custom-call | tf_op jit(solution)/shard_map/pallas_call | solution.py:29
  7.7 3.6 %all-to-all-start = ((bf16[8,2,10,32,128]{4,3,2,1,0:T(8,128)(2,1)}), bf16[8,2,10,32,128]{4,3,2,1,0:T(8,128)(2,1)S(1)}, u32[]{:S(2)}, u32[]{:S(2)}) async-start(bf16[8,2,10,32,128]{4,3,2,1,0:T(8,128)(2,1)} %shard_map.37), calls=%async_computation | async-start | bytes 2621440 | tf_op jit(solution)/shard_map/all_to_all | solution.py:148
  11.3 2.0 %collective-permute-done = bf16[3,3,3,32,256]{4,3,2,1,0:T(8,128)(2,1)S(1)} collective-permute-done((bf16[3,3,3,32,256]{4,3,2,1,0:T(8,128)(2,1)}, bf16[3,3,3,32,256]{4,3,2,1,0:T(8,128)(2,1)S(1)}, u32[]{:S(2)}, u32[]{:S(2)}) %collective-permute-start) | collective-permute-done | bytes 442400 | tf_op jit(solution)/shard_map/ppermute | solution.py:134
  13.3 1.8 %collective-permute-start.2 = (bf16[3,3,3,16,256]{4,3,2,1,0:T(8,128)(2,1)S(1)}, bf16[3,3,3,16,256]{4,3,2,1,0:T(8,128)(2,1)S(1)}, u32[]{:S(2)}, u32[]{:S(2)}) collective-permute-start(bf16[3,3,3,16,256]{4,3,2,1,0:T(8,128)(2,1)S(1)} %slice.126), channel_id=1, source_target_pairs={{0,4},{1,5},{2,6},{3,7},{4,0},{5,1},{6,2},{7,3},{8,12},{9,13},{10,... | collective-permute-start | bytes 663560 | tf_op jit(solution)/shard_map/ppermute | solution.py:134
  15.4 2.9 %collective-permute-start.3 = (bf16[3,3,3,16,256]{4,3,2,1,0:T(8,128)(2,1)S(1)}, bf16[3,3,3,16,256]{4,3,2,1,0:T(8,128)(2,1)S(1)}, u32[]{:S(2)}, u32[]{:S(2)}) collective-permute-start(bf16[3,3,3,16,256]{4,3,2,1,0:T(8,128)(2,1)S(1)} %slice.127), channel_id=1, source_target_pairs={{0,2},{1,3},{2,0},{3,1},{4,6},{5,7},{6,4},{7,5},{8,10},{9,11},{10,... | collective-permute-start | bytes 663560 | tf_op jit(solution)/shard_map/ppermute | solution.py:134
  19.0 1.2 %shard_map.38 = bf16[8,2,10,32,128]{4,3,2,1,0:T(8,128)(2,1)} custom-call(bf16[2,64,32,128]{3,2,1,0:T(8,128)(2,1)S(1)} %bitcast.62), custom_call_target="tpu_custom_call" | custom-call | tf_op jit(solution)/shard_map/pallas_call | solution.py:29
  20.2 13.4 %collective-permute-done.2 = bf16[3,3,3,16,256]{4,3,2,1,0:T(8,128)(2,1)S(1)} collective-permute-done((bf16[3,3,3,16,256]{4,3,2,1,0:T(8,128)(2,1)S(1)}, bf16[3,3,3,16,256]{4,3,2,1,0:T(8,128)(2,1)S(1)}, u32[]{:S(2)}, u32[]{:S(2)}) %collective-permute-start.2) | collective-permute-done | bytes 221216 | tf_op jit(solution)/shard_map/ppermute | solution.py:134
  34.0 4.3 %all-to-all-start.1 = ((bf16[8,2,10,32,128]{4,3,2,1,0:T(8,128)(2,1)}), bf16[8,2,10,32,128]{4,3,2,1,0:T(8,128)(2,1)}, u32[]{:S(2)}, u32[]{:S(2)}) async-start(bf16[8,2,10,32,128]{4,3,2,1,0:T(8,128)(2,1)} %shard_map.38), calls=%async_computation.1 | async-start | bytes 2621440 | tf_op jit(solution)/shard_map/all_to_all | solution.py:149
  40.5 1.3 %collective-permute-start.10 = (bf16[8,1,10,32,128]{4,3,2,1,0:T(8,128)(2,1)}, bf16[8,1,10,32,128]{4,3,2,1,0:T(8,128)(2,1)}, u32[]{:S(2)}, u32[]{:S(2)}) collective-permute-start(bf16[8,1,10,32,128]{4,3,2,1,0:T(8,128)(2,1)} %get-tuple-element.26), channel_id=1, source_target_pairs={{8,0},{16,8},{24,16},{9,1},{17,9},{25,17},{10,2},{18,10},{26,18},{... | collective-permute-start | bytes 1966088 | tf_op jit(solution)/shard_map/ppermute | solution.py:181
  41.8 5.4 %collective-permute-start.9 = (bf16[8,1,10,32,128]{4,3,2,1,0:T(8,128)(2,1)}, bf16[8,1,10,32,128]{4,3,2,1,0:T(8,128)(2,1)}, u32[]{:S(2)}, u32[]{:S(2)}) collective-permute-start(bf16[8,1,10,32,128]{4,3,2,1,0:T(8,128)(2,1)} %get-tuple-element.25), channel_id=1, source_target_pairs={{0,8},{8,16},{16,24},{1,9},{9,17},{17,25},{2,10},{10,18},{18,26},{... | collective-permute-start | bytes 1966088 | tf_op jit(solution)/shard_map/ppermute | solution.py:182
  47.2 9.3 %all-to-all-done.1.refs_1_ = bf16[8,2,10,32,128]{4,3,2,1,0:T(8,128)(2,1)} async-done(((bf16[8,2,10,32,128]{4,3,2,1,0:T(8,128)(2,1)}), bf16[8,2,10,32,128]{4,3,2,1,0:T(8,128)(2,1)}, u32[]{:S(2)}, u32[]{:S(2)}) %all-to-all-start.1) | async-done | bytes 1310752 | tf_op jit(solution)/shard_map/all_to_all | solution.py:149
  56.6 9.5 %shard_map.39 = (bf16[2,8,64,128]{3,2,1,0:T(8,128)(2,1)S(1)}, bf16[2,8,64,128]{3,2,1,0:T(8,128)(2,1)S(1)}, bf16[2,8,64,128]{3,2,1,0:T(8,128)(2,1)S(1)}, bf16[2,8,64,128]{3,2,1,0:T(8,128)(2,1)S(1)}) custom-call(bf16[8,2,10,32,128]{4,3,2,1,0:T(8,128)(2,1)S(1)} %all-to-all-done.refs_0_.vol_ref, bf16[8,2,10,32,128]{4,3,2,1,0:T(8,128)(2,1)} %all-to-all-done.1.refs_1_, ...), custom_call_target="tpu_custom_call" | custom-call | flops 7247757312 | bytes 10000000 | tf_op jit(solution)/shard_map/pallas_call | solution.py:111
  66.7 1.4 %collective-permute-start.6 = (bf16[2,8,64,128]{3,2,1,0:T(8,128)(2,1)S(1)}, bf16[2,8,64,128]{3,2,1,0:T(8,128)(2,1)S(1)}, u32[]{:S(2)}, u32[]{:S(2)}) collective-permute-start(bf16[2,8,64,128]{3,2,1,0:T(8,128)(2,1)S(1)} %get-tuple-element.23), channel_id=1, source_target_pairs={{0,4},{1,5},{2,6},{3,7},{4,0},{5,1},{6,2},{7,3},{8,12},{9,13},{10,... | collective-permute-start | bytes 786440 | tf_op jit(solution)/shard_map/ppermute | solution.py:134
  68.1 1.5 %collective-permute-start.5 = (bf16[2,8,64,128]{3,2,1,0:T(8,128)(2,1)S(1)}, bf16[2,8,64,128]{3,2,1,0:T(8,128)(2,1)S(1)}, u32[]{:S(2)}, u32[]{:S(2)}) collective-permute-start(bf16[2,8,64,128]{3,2,1,0:T(8,128)(2,1)S(1)} %get-tuple-element.22), channel_id=1, source_target_pairs={{0,2},{1,3},{2,0},{3,1},{4,6},{5,7},{6,4},{7,5},{8,10},{9,11},{10,... | collective-permute-start | bytes 786440 | tf_op jit(solution)/shard_map/ppermute | solution.py:134
  69.6 9.9 %shard_map.41 = (bf16[2,8,64,128]{3,2,1,0:T(8,128)(2,1)S(1)}, bf16[2,8,64,128]{3,2,1,0:T(8,128)(2,1)S(1)}, bf16[2,8,64,128]{3,2,1,0:T(8,128)(2,1)S(1)}, bf16[2,8,64,128]{3,2,1,0:T(8,128)(2,1)S(1)}) custom-call(bf16[8,2,10,32,128]{4,3,2,1,0:T(8,128)(2,1)S(1)} %all-to-all-done.refs_0_.vol_ref, bf16[8,2,10,32,128]{4,3,2,1,0:T(8,128)(2,1)} %all-to-all-done.1.refs_1_, ...), custom_call_target="tpu_custom_call" | custom-call | flops 7247757312 | bytes 10000000 | tf_op jit(solution)/shard_map/pallas_call | solution.py:111
  80.2 1.4 %collective-permute-start.12 = (bf16[2,8,64,128]{3,2,1,0:T(8,128)(2,1)S(1)}, bf16[2,8,64,128]{3,2,1,0:T(8,128)(2,1)S(1)}, u32[]{:S(2)}, u32[]{:S(2)}) collective-permute-start(bf16[2,8,64,128]{3,2,1,0:T(8,128)(2,1)S(1)} %get-tuple-element.29), channel_id=1, source_target_pairs={{0,4},{1,5},{2,6},{3,7},{4,0},{5,1},{6,2},{7,3},{8,12},{9,13},{10,... | collective-permute-start | bytes 786440 | tf_op jit(solution)/shard_map/ppermute | solution.py:134
  81.6 1.6 %collective-permute-start.11 = (bf16[2,8,64,128]{3,2,1,0:T(8,128)(2,1)S(1)}, bf16[2,8,64,128]{3,2,1,0:T(8,128)(2,1)S(1)}, u32[]{:S(2)}, u32[]{:S(2)}) collective-permute-start(bf16[2,8,64,128]{3,2,1,0:T(8,128)(2,1)S(1)} %get-tuple-element.28), channel_id=1, source_target_pairs={{0,2},{1,3},{2,0},{3,1},{4,6},{5,7},{6,4},{7,5},{8,10},{9,11},{10,... | collective-permute-start | bytes 786440 | tf_op jit(solution)/shard_map/ppermute | solution.py:134
  83.5 6.1 %collective-permute-done.13 = bf16[2,8,64,128]{3,2,1,0:T(8,128)(2,1)S(1)} collective-permute-done((bf16[2,8,64,128]{3,2,1,0:T(8,128)(2,1)S(1)}, bf16[2,8,64,128]{3,2,1,0:T(8,128)(2,1)S(1)}, u32[]{:S(2)}, u32[]{:S(2)}) %collective-permute-start.13) | collective-permute-done | bytes 262176 | tf_op jit(solution)/shard_map/ppermute | solution.py:134
  89.6 2.7 %collective-permute-done.12 = bf16[2,8,64,128]{3,2,1,0:T(8,128)(2,1)S(1)} collective-permute-done((bf16[2,8,64,128]{3,2,1,0:T(8,128)(2,1)S(1)}, bf16[2,8,64,128]{3,2,1,0:T(8,128)(2,1)S(1)}, u32[]{:S(2)}, u32[]{:S(2)}) %collective-permute-start.12) | collective-permute-done | bytes 262176 | tf_op jit(solution)/shard_map/ppermute | solution.py:134
  93.3 1.2 %collective-permute-done.14 = bf16[4,2,8,32,128]{4,3,2,1,0:T(8,128)(2,1)S(1)} collective-permute-done((bf16[4,2,8,32,128]{4,3,2,1,0:T(8,128)(2,1)S(1)}, bf16[4,2,8,32,128]{4,3,2,1,0:T(8,128)(2,1)S(1)}, u32[]{:S(2)}, u32[]{:S(2)}) %collective-permute-start.14) | collective-permute-done | bytes 524320 | tf_op jit(solution)/shard_map/ppermute | solution.py:134
  95.8 1.6 %pad_maximum_fusion = bf16[4,32,64,128]{3,2,1,0:T(8,128)(2,1)} fusion(bf16[1,32,64,128]{3,2,1,0:T(8,128)(2,1)S(1)} %get-tuple-element.36, bf16[2,32,64,128]{3,2,1,0:T(8,128)(2,1)S(1)} %bitcast.64, bf16[1,32,64,128]{3,2,1,0:T(8,128)(2,1)S(1)} %get-tuple-element.35), kind=kLoop, calls=%fused_computation.1 | loop fusion | flops 2097152 | bytes 4194304 | tf_op jit(solution)/shard_map/concatenate | solution.py:187
  (75 shorter events, 8.1 us)
Async XLA Ops:
  0.0 13.3 %collective-permute-start = (bf16[3,3,3,32,256]{4,3,2,1,0:T(8,128)(2,1)}, bf16[3,3,3,32,256]{4,3,2,1,0:T(8,128)(2,1)S(1)}, u32[]{:S(2)}, u32[]{:S(2)}) collective-permute-start(bf16[3,3,3,32,256]{4,3,2,1,0:T(8,128)(2,1)} %param.4), channel_id=1, source_target_pairs={{0,2},{1,3},{2,0},{3,1},{4,6},{5,7},{6,4},{7,5},{8,10},{9,11},{10,... | collective-permute-start | bytes 1327112 | tf_op jit(solution)/shard_map/ppermute | solution.py:134
  2.9 12.4 %collective-permute-start.1 = (bf16[3,3,3,32,256]{4,3,2,1,0:T(8,128)(2,1)}, bf16[3,3,3,32,256]{4,3,2,1,0:T(8,128)(2,1)S(1)}, u32[]{:S(2)}, u32[]{:S(2)}) collective-permute-start(bf16[3,3,3,32,256]{4,3,2,1,0:T(8,128)(2,1)} %param.4), channel_id=1, source_target_pairs={{0,4},{1,5},{2,6},{3,7},{4,0},{5,1},{6,2},{7,3},{8,12},{9,13},{10,... | collective-permute-start | bytes 1327112 | tf_op jit(solution)/shard_map/ppermute | solution.py:134
  7.7 26.3 %all-to-all-start = ((bf16[8,2,10,32,128]{4,3,2,1,0:T(8,128)(2,1)}), bf16[8,2,10,32,128]{4,3,2,1,0:T(8,128)(2,1)S(1)}, u32[]{:S(2)}, u32[]{:S(2)}) async-start(bf16[8,2,10,32,128]{4,3,2,1,0:T(8,128)(2,1)} %shard_map.37), calls=%async_computation | async-start | bytes 2621440 | tf_op jit(solution)/shard_map/all_to_all | solution.py:148
  11.3 7.0 %slice-start = ((bf16[4,32,64,128]{3,2,1,0:T(8,128)(2,1)}), bf16[2,32,64,128]{3,2,1,0:T(8,128)(2,1)S(1)}, s32[]{:S(2)}) async-start(bf16[4,32,64,128]{3,2,1,0:T(8,128)(2,1)} %param.3), calls=%async_computation.2 | async-start | bytes 2097152 | tf_op jit(solution)/shard_map/slice | solution.py:139
  13.3 20.2 %collective-permute-start.2 = (bf16[3,3,3,16,256]{4,3,2,1,0:T(8,128)(2,1)S(1)}, bf16[3,3,3,16,256]{4,3,2,1,0:T(8,128)(2,1)S(1)}, u32[]{:S(2)}, u32[]{:S(2)}) collective-permute-start(bf16[3,3,3,16,256]{4,3,2,1,0:T(8,128)(2,1)S(1)} %slice.126), channel_id=1, source_target_pairs={{0,4},{1,5},{2,6},{3,7},{4,0},{5,1},{6,2},{7,3},{8,12},{9,13},{10,... | collective-permute-start | bytes 663560 | tf_op jit(solution)/shard_map/ppermute | solution.py:134
  15.4 3.6 %copy-start = (bf16[3,3,3,32,256]{4,3,2,1,0:T(8,128)(2,1)}, bf16[3,3,3,32,256]{4,3,2,1,0:T(8,128)(2,1)S(1)}, u32[]{:S(2)}) copy-start(bf16[3,3,3,32,256]{4,3,2,1,0:T(8,128)(2,1)S(1)} %collective-permute-done.1) | copy-start | bytes 1327108
  15.4 18.2 %collective-permute-start.3 = (bf16[3,3,3,16,256]{4,3,2,1,0:T(8,128)(2,1)S(1)}, bf16[3,3,3,16,256]{4,3,2,1,0:T(8,128)(2,1)S(1)}, u32[]{:S(2)}, u32[]{:S(2)}) collective-permute-start(bf16[3,3,3,16,256]{4,3,2,1,0:T(8,128)(2,1)S(1)} %slice.127), channel_id=1, source_target_pairs={{0,2},{1,3},{2,0},{3,1},{4,6},{5,7},{6,4},{7,5},{8,10},{9,11},{10,... | collective-permute-start | bytes 663560 | tf_op jit(solution)/shard_map/ppermute | solution.py:134
  19.0 14.6 %copy-start.2 = (bf16[3,3,3,32,256]{4,3,2,1,0:T(8,128)(2,1)S(1)}, bf16[3,3,3,32,256]{4,3,2,1,0:T(8,128)(2,1)}, u32[]{:S(2)}) copy-start(bf16[3,3,3,32,256]{4,3,2,1,0:T(8,128)(2,1)} %param.4) | copy-start | bytes 1327108
  19.0 14.6 %copy-start.1 = (bf16[3,3,3,32,256]{4,3,2,1,0:T(8,128)(2,1)S(1)}, bf16[3,3,3,32,256]{4,3,2,1,0:T(8,128)(2,1)}, u32[]{:S(2)}) copy-start(bf16[3,3,3,32,256]{4,3,2,1,0:T(8,128)(2,1)} %copy-done) | copy-start | bytes 1327108
  33.9 4.4 %copy-start.3 = (f32[256]{0:T(256)S(1)}, f32[256]{0:T(256)}, u32[]{:S(2)}) copy-start(f32[256]{0:T(256)} %param.5) | copy-start | bytes 3076
  33.9 22.6 %collective-permute-start.4 = (bf16[4,3,3,3,32,256]{5,4,3,2,1,0:T(8,128)(2,1)S(1)}, bf16[4,3,3,3,32,256]{5,4,3,2,1,0:T(8,128)(2,1)}, u32[]{:S(2)}, u32[]{:S(2)}) collective-permute-start(bf16[4,3,3,3,32,256]{5,4,3,2,1,0:T(8,128)(2,1)S(1)} %pad_maximum_fusion.1.refs_2_.refs_4_), channel_id=1, source_target_pairs={{0,1},{1,0},{2,3},{3,2},{4,5},{5,4},{6,7},{7,6},{8,9},{9,8},{10,11... | collective-permute-start | bytes 5308424 | tf_op jit(solution)/shard_map/ppermute | solution.py:134
  34.0 22.5 %all-to-all-start.1 = ((bf16[8,2,10,32,128]{4,3,2,1,0:T(8,128)(2,1)}), bf16[8,2,10,32,128]{4,3,2,1,0:T(8,128)(2,1)}, u32[]{:S(2)}, u32[]{:S(2)}) async-start(bf16[8,2,10,32,128]{4,3,2,1,0:T(8,128)(2,1)} %shard_map.38), calls=%async_computation.1 | async-start | bytes 2621440 | tf_op jit(solution)/shard_map/all_to_all | solution.py:149
  40.5 29.2 %collective-permute-start.10 = (bf16[8,1,10,32,128]{4,3,2,1,0:T(8,128)(2,1)}, bf16[8,1,10,32,128]{4,3,2,1,0:T(8,128)(2,1)}, u32[]{:S(2)}, u32[]{:S(2)}) collective-permute-start(bf16[8,1,10,32,128]{4,3,2,1,0:T(8,128)(2,1)} %get-tuple-element.26), channel_id=1, source_target_pairs={{8,0},{16,8},{24,16},{9,1},{17,9},{25,17},{10,2},{18,10},{26,18},{... | collective-permute-start | bytes 1966088 | tf_op jit(solution)/shard_map/ppermute | solution.py:181
  41.8 27.9 %collective-permute-start.9 = (bf16[8,1,10,32,128]{4,3,2,1,0:T(8,128)(2,1)}, bf16[8,1,10,32,128]{4,3,2,1,0:T(8,128)(2,1)}, u32[]{:S(2)}, u32[]{:S(2)}) collective-permute-start(bf16[8,1,10,32,128]{4,3,2,1,0:T(8,128)(2,1)} %get-tuple-element.25), channel_id=1, source_target_pairs={{0,8},{8,16},{16,24},{1,9},{9,17},{17,25},{2,10},{10,18},{18,26},{... | collective-permute-start | bytes 1966088 | tf_op jit(solution)/shard_map/ppermute | solution.py:182
  66.1 15.5 %collective-permute-start.7 = (bf16[2,8,64,128]{3,2,1,0:T(8,128)(2,1)S(1)}, bf16[2,8,64,128]{3,2,1,0:T(8,128)(2,1)S(1)}, u32[]{:S(2)}, u32[]{:S(2)}) collective-permute-start(bf16[2,8,64,128]{3,2,1,0:T(8,128)(2,1)S(1)} %get-tuple-element.24), channel_id=1, source_target_pairs={{0,6},{1,7},{2,4},{3,5},{4,2},{5,3},{6,0},{7,1},{8,14},{9,15},{10,... | collective-permute-start | bytes 786440 | tf_op jit(solution)/shard_map/ppermute | solution.py:134
  66.7 16.5 %collective-permute-start.6 = (bf16[2,8,64,128]{3,2,1,0:T(8,128)(2,1)S(1)}, bf16[2,8,64,128]{3,2,1,0:T(8,128)(2,1)S(1)}, u32[]{:S(2)}, u32[]{:S(2)}) collective-permute-start(bf16[2,8,64,128]{3,2,1,0:T(8,128)(2,1)S(1)} %get-tuple-element.23), channel_id=1, source_target_pairs={{0,4},{1,5},{2,6},{3,7},{4,0},{5,1},{6,2},{7,3},{8,12},{9,13},{10,... | collective-permute-start | bytes 786440 | tf_op jit(solution)/shard_map/ppermute | solution.py:134
  68.1 15.2 %collective-permute-start.5 = (bf16[2,8,64,128]{3,2,1,0:T(8,128)(2,1)S(1)}, bf16[2,8,64,128]{3,2,1,0:T(8,128)(2,1)S(1)}, u32[]{:S(2)}, u32[]{:S(2)}) collective-permute-start(bf16[2,8,64,128]{3,2,1,0:T(8,128)(2,1)S(1)} %get-tuple-element.22), channel_id=1, source_target_pairs={{0,2},{1,3},{2,0},{3,1},{4,6},{5,7},{6,4},{7,5},{8,10},{9,11},{10,... | collective-permute-start | bytes 786440 | tf_op jit(solution)/shard_map/ppermute | solution.py:134
  79.6 10.0 %collective-permute-start.13 = (bf16[2,8,64,128]{3,2,1,0:T(8,128)(2,1)S(1)}, bf16[2,8,64,128]{3,2,1,0:T(8,128)(2,1)S(1)}, u32[]{:S(2)}, u32[]{:S(2)}) collective-permute-start(bf16[2,8,64,128]{3,2,1,0:T(8,128)(2,1)S(1)} %get-tuple-element.30), channel_id=1, source_target_pairs={{0,6},{1,7},{2,4},{3,5},{4,2},{5,3},{6,0},{7,1},{8,14},{9,15},{10,... | collective-permute-start | bytes 786440 | tf_op jit(solution)/shard_map/ppermute | solution.py:134
  80.2 12.1 %collective-permute-start.12 = (bf16[2,8,64,128]{3,2,1,0:T(8,128)(2,1)S(1)}, bf16[2,8,64,128]{3,2,1,0:T(8,128)(2,1)S(1)}, u32[]{:S(2)}, u32[]{:S(2)}) collective-permute-start(bf16[2,8,64,128]{3,2,1,0:T(8,128)(2,1)S(1)} %get-tuple-element.29), channel_id=1, source_target_pairs={{0,4},{1,5},{2,6},{3,7},{4,0},{5,1},{6,2},{7,3},{8,12},{9,13},{10,... | collective-permute-start | bytes 786440 | tf_op jit(solution)/shard_map/ppermute | solution.py:134
  81.6 10.7 %collective-permute-start.11 = (bf16[2,8,64,128]{3,2,1,0:T(8,128)(2,1)S(1)}, bf16[2,8,64,128]{3,2,1,0:T(8,128)(2,1)S(1)}, u32[]{:S(2)}, u32[]{:S(2)}) collective-permute-start(bf16[2,8,64,128]{3,2,1,0:T(8,128)(2,1)S(1)} %get-tuple-element.28), channel_id=1, source_target_pairs={{0,2},{1,3},{2,0},{3,1},{4,6},{5,7},{6,4},{7,5},{8,10},{9,11},{10,... | collective-permute-start | bytes 786440 | tf_op jit(solution)/shard_map/ppermute | solution.py:134
  83.4 9.9 %collective-permute-start.8 = (bf16[4,2,8,32,128]{4,3,2,1,0:T(8,128)(2,1)S(1)}, bf16[4,2,8,32,128]{4,3,2,1,0:T(8,128)(2,1)S(1)}, u32[]{:S(2)}, u32[]{:S(2)}) collective-permute-start(bf16[4,2,8,32,128]{4,3,2,1,0:T(8,128)(2,1)S(1)} %pad_maximum_fusion.2), channel_id=1, source_target_pairs={{0,1},{1,0},{2,3},{3,2},{4,5},{5,4},{6,7},{7,6},{8,9},{9,8},{10,11... | collective-permute-start | bytes 1572872 | tf_op jit(solution)/shard_map/ppermute | solution.py:134
  92.5 2.0 %collective-permute-start.14 = (bf16[4,2,8,32,128]{4,3,2,1,0:T(8,128)(2,1)S(1)}, bf16[4,2,8,32,128]{4,3,2,1,0:T(8,128)(2,1)S(1)}, u32[]{:S(2)}, u32[]{:S(2)}) collective-permute-start(bf16[4,2,8,32,128]{4,3,2,1,0:T(8,128)(2,1)S(1)} %pad_maximum_fusion.3), channel_id=1, source_target_pairs={{0,1},{1,0},{2,3},{3,2},{4,5},{5,4},{6,7},{7,6},{8,9},{9,8},{10,11... | collective-permute-start | bytes 1572872 | tf_op jit(solution)/shard_map/ppermute | solution.py:134

commit v21 on v18

--- a/solution.py
+++ b/solution.py
@@ -146,14 +146,20 @@
         return lax.ppermute(array, axis, [(i, i ^ k) for i in range(lax.axis_size(axis))])
 
 
+    near = [swap(kernel, k) for k in across[1 : 3 if len(across) == 4 else None]]
     outer_rows = cut(jnp.concatenate([features[:1], features[-1:]]), parts)
-    fetched = [swap(kernel, k) for k in across]
-    fetched = lax.optimization_barrier((fetched, outer_rows))[0]
-    same = jnp.stack(fetched)
+    inner_rows = cut(features[1:-1], parts)
+    if len(across) == 4:
+        half = out_chan // 2
+        by_x, by_y = lax.optimization_barrier((near, outer_rows))[0]
+        far = [swap(by_x[:, :, :, :half], across[2]), swap(by_y[:, :, :, half:], across[1])]
+        far = lax.optimization_barrier((far, inner_rows))[0]
+        near = [by_x, by_y, jnp.concatenate(far, axis=3)]
+    same = jnp.stack([kernel, *near])
     tap_parts = [same, swap(same, 1)]
     tap_order = tuple((n, g) for g in range(len(across)) for n in range(2))
     outer = lax.all_to_all(outer_rows, "filt", 0, 0)
-    inner = lax.all_to_all(cut(features[1:-1], parts), "filt", 0, 0)
+    inner = lax.all_to_all(inner_rows, "filt", 0, 0)
     arrived = outer
     order = jnp.stack([me ^ k ^ c for k in across for c in range(2)])
     bias = jnp.take(bias_vector.reshape(parts, out_chan), order, axis=0).reshape(-1)

time: 101 us -> 103 us (1.020)
  starting transfers between devices: 26.3 us -> 28.6 us
    all_to_all x1, waiting for transfers between devices: 7.74 us -> 14.5 us  [body(): outer = lax.all_to_all(outer_rows, 'filt', 0, 0)]
    ppermute x12 -> x13, waiting for transfers between devices: 23.2 us -> 17.3 us  [swap(): lax.ppermute(array, axis, [(i, i ^ k) for i in range(lax.axis_size(axis))])]
    ppermute x12 -> x13, starting transfers between devices: 11.9 us -> 14.1 us  [swap(): lax.ppermute(array, axis, [(i, i ^ k) for i in range(lax.axis_size(axis))])]
    ppermute x1, starting transfers between devices: 4.34 us -> 5.42 us  [body(): before = lax.ppermute(last, 'slab', up)]
    unnamed x17 -> x15, local copies, waits for them, and re-layouts: 5.04 us -> 4.29 us
  transfers between devices with their start and end apart: 16 -> 17, of which waited for: 8 -> 8; matrix products, arithmetic and copies ran while one was open for 6% -> 7% of each run, Pallas kernels for 24% -> 24%
where the time goes in v21:
time: 103 us; the launch traced here: 102 us
  waiting for transfers between devices  35.5 us (34%)
  starting transfers between devices  28.6 us (28%)
  Pallas kernels  24.7 us (24%)
  local copies, waits for them, and re-layouts  10.1 us (10%)
  other arithmetic  3.1 us (3%)
    pallas_call x3, Pallas kernels, convolve(): pl.pallas_call(functools.partial(conv_kernel, plan, min(ROWS, rows), len(...  21.1 us
    ppermute x13, waiting for transfers between devices, swap(): lax.ppermute(array, axis, [(i, i ^ k) for i in range(lax.axis_size(axis))])  17.3 us
    all_to_all x1, waiting for transfers between devices, body(): outer = lax.all_to_all(outer_rows, 'filt', 0, 0)  14.5 us
    ppermute x13, starting transfers between devices, swap(): lax.ppermute(array, axis, [(i, i ^ k) for i in range(lax.axis_size(axis))])  14.1 us
    ppermute x1, starting transfers between devices, body(): before = lax.ppermute(last, 'slab', up)  5.42 us
    unnamed x15, local copies, waits for them, and re-layouts  4.29 us
    all_to_all x1, starting transfers between devices, body(): inner = lax.all_to_all(inner_rows, 'filt', 0, 0)  4.27 us
    all_to_all x1, waiting for transfers between devices, body(): inner = lax.all_to_all(inner_rows, 'filt', 0, 0)  3.65 us
  transfers between devices with their start and end apart: 17, of which 8 were waited for; matrix products, arithmetic and copies ran while one was open for 7% of the time, Pallas kernels for 24%

profile of v21, /device:TPU:0, one launch (start us, length us, event | category | flops | bytes accessed | tf_op | source)
XLA Modules:
  0.0 102.5 jit_solution(18410080335529716859)
XLA Ops:
  0.0 2.9 %collective-permute-start = (bf16[3,3,3,32,256]{4,3,2,1,0:T(8,128)(2,1)}, bf16[3,3,3,32,256]{4,3,2,1,0:T(8,128)(2,1)S(1)}, u32[]{:S(2)}, u32[]{:S(2)}) collective-permute-start(bf16[3,3,3,32,256]{4,3,2,1,0:T(8,128)(2,1)} %param.4), channel_id=1, source_target_pairs={{0,2},{1,3},{2,0},{3,1},{4,6},{5,7},{6,4},{7,5},{8,10},{9,11},{10,... | collective-permute-start | bytes 1327112 | tf_op jit(solution)/shard_map/ppermute | solution.py:146
  2.9 1.5 %collective-permute-start.1 = (bf16[3,3,3,32,256]{4,3,2,1,0:T(8,128)(2,1)}, bf16[3,3,3,32,256]{4,3,2,1,0:T(8,128)(2,1)S(1)}, u32[]{:S(2)}, u32[]{:S(2)}) collective-permute-start(bf16[3,3,3,32,256]{4,3,2,1,0:T(8,128)(2,1)} %param.4), channel_id=1, source_target_pairs={{0,4},{1,5},{2,6},{3,7},{4,0},{5,1},{6,2},{7,3},{8,12},{9,13},{10,... | collective-permute-start | bytes 1327112 | tf_op jit(solution)/shard_map/ppermute | solution.py:146
  4.5 1.3 %fusion.1 = (bf16[1,32,64,128]{3,2,1,0:T(8,128)(2,1)S(1)}, bf16[1,32,64,128]{3,2,1,0:T(8,128)(2,1)S(1)}) fusion(bf16[4,32,64,128]{3,2,1,0:T(8,128)(2,1)} %param.3), kind=kLoop, calls=%fused_computation.46 | loop fusion | bytes 2097152 | tf_op jit(solution)/shard_map/slice | solution.py:150
  7.7 5.6 %collective-permute-done = bf16[3,3,3,32,256]{4,3,2,1,0:T(8,128)(2,1)S(1)} collective-permute-done((bf16[3,3,3,32,256]{4,3,2,1,0:T(8,128)(2,1)}, bf16[3,3,3,32,256]{4,3,2,1,0:T(8,128)(2,1)S(1)}, u32[]{:S(2)}, u32[]{:S(2)}) %collective-permute-start) | collective-permute-done | bytes 442400 | tf_op jit(solution)/shard_map/ppermute | solution.py:146
  13.3 1.5 %collective-permute-done.1 = bf16[3,3,3,32,256]{4,3,2,1,0:T(8,128)(2,1)S(1)} collective-permute-done((bf16[3,3,3,32,256]{4,3,2,1,0:T(8,128)(2,1)}, bf16[3,3,3,32,256]{4,3,2,1,0:T(8,128)(2,1)S(1)}, u32[]{:S(2)}, u32[]{:S(2)}) %collective-permute-start.1) | collective-permute-done | bytes 442400 | tf_op jit(solution)/shard_map/ppermute | solution.py:146
  15.5 1.5 %collective-permute-start.2 = (bf16[3,3,3,16,256]{4,3,2,1,0:T(8,128)(2,1)}, bf16[3,3,3,16,256]{4,3,2,1,0:T(8,128)(2,1)S(1)}, u32[]{:S(2)}, u32[]{:S(2)}) collective-permute-start(bf16[3,3,3,16,256]{4,3,2,1,0:T(8,128)(2,1)} %slice.95), channel_id=1, source_target_pairs={{0,4},{1,5},{2,6},{3,7},{4,0},{5,1},{6,2},{7,3},{8,12},{9,13},{10,... | collective-permute-start | bytes 663560 | tf_op jit(solution)/shard_map/ppermute | solution.py:146
  18.3 3.6 %all-to-all-start = ((bf16[8,2,10,32,128]{4,3,2,1,0:T(8,128)(2,1)}), bf16[8,2,10,32,128]{4,3,2,1,0:T(8,128)(2,1)S(1)}, u32[]{:S(2)}, u32[]{:S(2)}) async-start(bf16[8,2,10,32,128]{4,3,2,1,0:T(8,128)(2,1)} %shard_map.37), calls=%async_computation | async-start | bytes 2621440 | tf_op jit(solution)/shard_map/all_to_all | solution.py:161
  25.5 14.5 %all-to-all-done.refs_0_.vol_ref = bf16[8,2,10,32,128]{4,3,2,1,0:T(8,128)(2,1)S(1)} async-done(((bf16[8,2,10,32,128]{4,3,2,1,0:T(8,128)(2,1)}), bf16[8,2,10,32,128]{4,3,2,1,0:T(8,128)(2,1)S(1)}, u32[]{:S(2)}, u32[]{:S(2)}) %all-to-all-start) | async-done | bytes 1310752 | tf_op jit(solution)/shard_map/all_to_all | solution.py:161
  40.0 4.3 %all-to-all-start.1 = ((bf16[8,2,10,32,128]{4,3,2,1,0:T(8,128)(2,1)}), bf16[8,2,10,32,128]{4,3,2,1,0:T(8,128)(2,1)}, u32[]{:S(2)}, u32[]{:S(2)}) async-start(bf16[8,2,10,32,128]{4,3,2,1,0:T(8,128)(2,1)} %shard_map.38), calls=%async_computation.1 | async-start | bytes 2621440 | tf_op jit(solution)/shard_map/all_to_all | solution.py:162
  46.5 1.3 %collective-permute-start.10 = (bf16[8,1,10,32,128]{4,3,2,1,0:T(8,128)(2,1)}, bf16[8,1,10,32,128]{4,3,2,1,0:T(8,128)(2,1)}, u32[]{:S(2)}, u32[]{:S(2)}) collective-permute-start(bf16[8,1,10,32,128]{4,3,2,1,0:T(8,128)(2,1)} %get-tuple-element.30), channel_id=1, source_target_pairs={{8,0},{16,8},{24,16},{9,1},{17,9},{25,17},{10,2},{18,10},{26,18},{... | collective-permute-start | bytes 1966088 | tf_op jit(solution)/shard_map/ppermute | solution.py:203
  47.8 5.4 %collective-permute-start.9 = (bf16[8,1,10,32,128]{4,3,2,1,0:T(8,128)(2,1)}, bf16[8,1,10,32,128]{4,3,2,1,0:T(8,128)(2,1)}, u32[]{:S(2)}, u32[]{:S(2)}) collective-permute-start(bf16[8,1,10,32,128]{4,3,2,1,0:T(8,128)(2,1)} %get-tuple-element.29), channel_id=1, source_target_pairs={{0,8},{8,16},{16,24},{1,9},{9,17},{17,25},{2,10},{10,18},{18,26},{... | collective-permute-start | bytes 1966088 | tf_op jit(solution)/shard_map/ppermute | solution.py:204
  53.3 4.2 %shard_map.39.refs_0_ = f32[2,8,256,128]{3,2,1,0:T(8,128)S(1)} custom-call(bf16[8,2,10,32,128]{4,3,2,1,0:T(8,128)(2,1)S(1)} %all-to-all-done.refs_0_.vol_ref, bf16[4,3,3,3,32,256]{5,4,3,2,1,0:T(8,128)(2,1)S(1)} %pad_maximum_fusion.1.refs_1_.refs_2_.refs_4_, bf16[4,3,3,3,32,256]{5,4,3,2,1,0:T(8,128)(2,1)} %collective-permute-done.4.refs_2_.refs_3_.refs_5_, ...), custom_call_target="tpu_custom_call" | custom-call | flops 2415919104 | bytes 10000000 | tf_op jit(solution)/shard_map/pallas_call | solution.py:121
  57.5 1.3 %copy-done = f32[2,8,256,128]{3,2,1,0:T(8,128)} copy-done((f32[2,8,256,128]{3,2,1,0:T(8,128)}, f32[2,8,256,128]{3,2,1,0:T(8,128)S(1)}, u32[]{:S(2)}) %copy-start) | copy-done | bytes 2097176
  58.9 3.7 %all-to-all-done.1.refs_1_ = bf16[8,2,10,32,128]{4,3,2,1,0:T(8,128)(2,1)} async-done(((bf16[8,2,10,32,128]{4,3,2,1,0:T(8,128)(2,1)}), bf16[8,2,10,32,128]{4,3,2,1,0:T(8,128)(2,1)}, u32[]{:S(2)}, u32[]{:S(2)}) %all-to-all-start.1) | async-done | bytes 1310752 | tf_op jit(solution)/shard_map/all_to_all | solution.py:162
  62.5 1.6 %copy-done.1 = f32[2,8,256,128]{3,2,1,0:T(8,128)S(1)} copy-done((f32[2,8,256,128]{3,2,1,0:T(8,128)S(1)}, f32[2,8,256,128]{3,2,1,0:T(8,128)}, u32[]{:S(2)}) %copy-start.1) | copy-done | bytes 2097176
  64.1 7.0 %shard_map.40 = (bf16[2,8,64,128]{3,2,1,0:T(8,128)(2,1)S(1)}, bf16[2,8,64,128]{3,2,1,0:T(8,128)(2,1)S(1)}, bf16[2,8,64,128]{3,2,1,0:T(8,128)(2,1)S(1)}, bf16[2,8,64,128]{3,2,1,0:T(8,128)(2,1)S(1)}) custom-call(f32[2,8,256,128]{3,2,1,0:T(8,128)S(1)} %copy-done.1, bf16[8,2,10,32,128]{4,3,2,1,0:T(8,128)(2,1)} %all-to-all-done.1.refs_1_, ...), custom_call_target="tpu_custom_call" | custom-call | flops 4831838208 | bytes 10000000 | tf_op jit(solution)/shard_map/pallas_call | solution.py:121
  71.8 1.4 %collective-permute-start.6 = (bf16[2,8,64,128]{3,2,1,0:T(8,128)(2,1)S(1)}, bf16[2,8,64,128]{3,2,1,0:T(8,128)(2,1)S(1)}, u32[]{:S(2)}, u32[]{:S(2)}) collective-permute-start(bf16[2,8,64,128]{3,2,1,0:T(8,128)(2,1)S(1)} %get-tuple-element.27), channel_id=1, source_target_pairs={{0,4},{1,5},{2,6},{3,7},{4,0},{5,1},{6,2},{7,3},{8,12},{9,13},{10,... | collective-permute-start | bytes 786440 | tf_op jit(solution)/shard_map/ppermute | solution.py:146
  73.2 1.5 %collective-permute-start.5 = (bf16[2,8,64,128]{3,2,1,0:T(8,128)(2,1)S(1)}, bf16[2,8,64,128]{3,2,1,0:T(8,128)(2,1)S(1)}, u32[]{:S(2)}, u32[]{:S(2)}) collective-permute-start(bf16[2,8,64,128]{3,2,1,0:T(8,128)(2,1)S(1)} %get-tuple-element.26), channel_id=1, source_target_pairs={{0,2},{1,3},{2,0},{3,1},{4,6},{5,7},{6,4},{7,5},{8,10},{9,11},{10,... | collective-permute-start | bytes 786440 | tf_op jit(solution)/shard_map/ppermute | solution.py:146
  74.7 9.9 %shard_map.42 = (bf16[2,8,64,128]{3,2,1,0:T(8,128)(2,1)S(1)}, bf16[2,8,64,128]{3,2,1,0:T(8,128)(2,1)S(1)}, bf16[2,8,64,128]{3,2,1,0:T(8,128)(2,1)S(1)}, bf16[2,8,64,128]{3,2,1,0:T(8,128)(2,1)S(1)}) custom-call(bf16[8,2,10,32,128]{4,3,2,1,0:T(8,128)(2,1)S(1)} %all-to-all-done.refs_0_.vol_ref, bf16[8,2,10,32,128]{4,3,2,1,0:T(8,128)(2,1)} %all-to-all-done.1.refs_1_, ...), custom_call_target="tpu_custom_call" | custom-call | flops 7247757312 | bytes 10000000 | tf_op jit(solution)/shard_map/pallas_call | solution.py:121
  85.3 1.4 %collective-permute-start.12 = (bf16[2,8,64,128]{3,2,1,0:T(8,128)(2,1)S(1)}, bf16[2,8,64,128]{3,2,1,0:T(8,128)(2,1)S(1)}, u32[]{:S(2)}, u32[]{:S(2)}) collective-permute-start(bf16[2,8,64,128]{3,2,1,0:T(8,128)(2,1)S(1)} %get-tuple-element.33), channel_id=1, source_target_pairs={{0,4},{1,5},{2,6},{3,7},{4,0},{5,1},{6,2},{7,3},{8,12},{9,13},{10,... | collective-permute-start | bytes 786440 | tf_op jit(solution)/shard_map/ppermute | solution.py:146
  86.7 1.6 %collective-permute-start.11 = (bf16[2,8,64,128]{3,2,1,0:T(8,128)(2,1)S(1)}, bf16[2,8,64,128]{3,2,1,0:T(8,128)(2,1)S(1)}, u32[]{:S(2)}, u32[]{:S(2)}) collective-permute-start(bf16[2,8,64,128]{3,2,1,0:T(8,128)(2,1)S(1)} %get-tuple-element.32), channel_id=1, source_target_pairs={{0,2},{1,3},{2,0},{3,1},{4,6},{5,7},{6,4},{7,5},{8,10},{9,11},{10,... | collective-permute-start | bytes 786440 | tf_op jit(solution)/shard_map/ppermute | solution.py:146
  88.5 6.1 %collective-permute-done.13 = bf16[2,8,64,128]{3,2,1,0:T(8,128)(2,1)S(1)} collective-permute-done((bf16[2,8,64,128]{3,2,1,0:T(8,128)(2,1)S(1)}, bf16[2,8,64,128]{3,2,1,0:T(8,128)(2,1)S(1)}, u32[]{:S(2)}, u32[]{:S(2)}) %collective-permute-start.13) | collective-permute-done | bytes 262176 | tf_op jit(solution)/shard_map/ppermute | solution.py:146
  94.7 2.7 %collective-permute-done.12 = bf16[2,8,64,128]{3,2,1,0:T(8,128)(2,1)S(1)} collective-permute-done((bf16[2,8,64,128]{3,2,1,0:T(8,128)(2,1)S(1)}, bf16[2,8,64,128]{3,2,1,0:T(8,128)(2,1)S(1)}, u32[]{:S(2)}, u32[]{:S(2)}) %collective-permute-start.12) | collective-permute-done | bytes 262176 | tf_op jit(solution)/shard_map/ppermute | solution.py:146
  100.9 1.6 %pad_maximum_fusion = bf16[4,32,64,128]{3,2,1,0:T(8,128)(2,1)} fusion(bf16[1,32,64,128]{3,2,1,0:T(8,128)(2,1)S(1)} %get-tuple-element.40, bf16[2,32,64,128]{3,2,1,0:T(8,128)(2,1)S(1)} %bitcast.64, bf16[1,32,64,128]{3,2,1,0:T(8,128)(2,1)S(1)} %get-tuple-element.39), kind=kLoop, calls=%fused_computation.1 | loop fusion | flops 2097152 | bytes 4194304 | tf_op jit(solution)/shard_map/concatenate | solution.py:209
  (80 shorter events, 14.6 us)
Async XLA Ops:
  0.0 13.3 %collective-permute-start = (bf16[3,3,3,32,256]{4,3,2,1,0:T(8,128)(2,1)}, bf16[3,3,3,32,256]{4,3,2,1,0:T(8,128)(2,1)S(1)}, u32[]{:S(2)}, u32[]{:S(2)}) collective-permute-start(bf16[3,3,3,32,256]{4,3,2,1,0:T(8,128)(2,1)} %param.4), channel_id=1, source_target_pairs={{0,2},{1,3},{2,0},{3,1},{4,6},{5,7},{6,4},{7,5},{8,10},{9,11},{10,... | collective-permute-start | bytes 1327112 | tf_op jit(solution)/shard_map/ppermute | solution.py:146
  2.9 11.8 %collective-permute-start.1 = (bf16[3,3,3,32,256]{4,3,2,1,0:T(8,128)(2,1)}, bf16[3,3,3,32,256]{4,3,2,1,0:T(8,128)(2,1)S(1)}, u32[]{:S(2)}, u32[]{:S(2)}) collective-permute-start(bf16[3,3,3,32,256]{4,3,2,1,0:T(8,128)(2,1)} %param.4), channel_id=1, source_target_pairs={{0,4},{1,5},{2,6},{3,7},{4,0},{5,1},{6,2},{7,3},{8,12},{9,13},{10,... | collective-permute-start | bytes 1327112 | tf_op jit(solution)/shard_map/ppermute | solution.py:146
  14.8 7.1 %copy-start.2 = (bf16[3,3,3,32,256]{4,3,2,1,0:T(8,128)(2,1)}, bf16[3,3,3,32,256]{4,3,2,1,0:T(8,128)(2,1)S(1)}, u32[]{:S(2)}) copy-start(bf16[3,3,3,32,256]{4,3,2,1,0:T(8,128)(2,1)S(1)} %collective-permute-done.1) | copy-start | bytes 1327108
  15.5 8.3 %collective-permute-start.2 = (bf16[3,3,3,16,256]{4,3,2,1,0:T(8,128)(2,1)}, bf16[3,3,3,16,256]{4,3,2,1,0:T(8,128)(2,1)S(1)}, u32[]{:S(2)}, u32[]{:S(2)}) collective-permute-start(bf16[3,3,3,16,256]{4,3,2,1,0:T(8,128)(2,1)} %slice.95), channel_id=1, source_target_pairs={{0,4},{1,5},{2,6},{3,7},{4,0},{5,1},{6,2},{7,3},{8,12},{9,13},{10,... | collective-permute-start | bytes 663560 | tf_op jit(solution)/shard_map/ppermute | solution.py:146
  17.7 4.1 %slice-start = ((bf16[4,32,64,128]{3,2,1,0:T(8,128)(2,1)}), bf16[2,32,64,128]{3,2,1,0:T(8,128)(2,1)S(1)}, s32[]{:S(2)}) async-start(bf16[4,32,64,128]{3,2,1,0:T(8,128)(2,1)} %param.3), calls=%async_computation.2 | async-start | bytes 2097152 | tf_op jit(solution)/shard_map/slice | solution.py:151
  17.7 6.2 %collective-permute-start.3 = (bf16[3,3,3,16,256]{4,3,2,1,0:T(8,128)(2,1)}, bf16[3,3,3,16,256]{4,3,2,1,0:T(8,128)(2,1)}, u32[]{:S(2)}, u32[]{:S(2)}) collective-permute-start(bf16[3,3,3,16,256]{4,3,2,1,0:T(8,128)(2,1)} %slice.96), channel_id=1, source_target_pairs={{0,2},{1,3},{2,0},{3,1},{4,6},{5,7},{6,4},{7,5},{8,10},{9,11},{10,... | collective-permute-start | bytes 663560 | tf_op jit(solution)/shard_map/ppermute | solution.py:146
  18.3 21.7 %all-to-all-start = ((bf16[8,2,10,32,128]{4,3,2,1,0:T(8,128)(2,1)}), bf16[8,2,10,32,128]{4,3,2,1,0:T(8,128)(2,1)S(1)}, u32[]{:S(2)}, u32[]{:S(2)}) async-start(bf16[8,2,10,32,128]{4,3,2,1,0:T(8,128)(2,1)} %shard_map.37), calls=%async_computation | async-start | bytes 2621440 | tf_op jit(solution)/shard_map/all_to_all | solution.py:161
  22.6 2.4 %copy-start.3 = (bf16[3,3,3,32,256]{4,3,2,1,0:T(8,128)(2,1)S(1)}, bf16[3,3,3,32,256]{4,3,2,1,0:T(8,128)(2,1)}, u32[]{:S(2)}) copy-start(bf16[3,3,3,32,256]{4,3,2,1,0:T(8,128)(2,1)} %copy-done.2) | copy-start | bytes 1327108
  22.6 2.4 %copy-start.4 = (bf16[3,3,3,32,256]{4,3,2,1,0:T(8,128)(2,1)S(1)}, bf16[3,3,3,32,256]{4,3,2,1,0:T(8,128)(2,1)}, u32[]{:S(2)}) copy-start(bf16[3,3,3,32,256]{4,3,2,1,0:T(8,128)(2,1)} %param.4) | copy-start | bytes 1327108
  25.2 19.1 %copy-start.5 = (f32[256]{0:T(256)S(1)}, f32[256]{0:T(256)}, u32[]{:S(2)}) copy-start(f32[256]{0:T(256)} %param.5) | copy-start | bytes 3076
  25.2 28.0 %collective-permute-start.4 = (bf16[4,3,3,3,32,256]{5,4,3,2,1,0:T(8,128)(2,1)S(1)}, bf16[4,3,3,3,32,256]{5,4,3,2,1,0:T(8,128)(2,1)}, u32[]{:S(2)}, u32[]{:S(2)}) collective-permute-start(bf16[4,3,3,3,32,256]{5,4,3,2,1,0:T(8,128)(2,1)S(1)} %pad_maximum_fusion.1.refs_1_.refs_2_.refs_4_), channel_id=1, source_target_pairs={{0,1},{1,0},{2,3},{3,2},{4,5},{5,4},{6,7},{7,6},{8,9},{9,8},{10,11... | collective-permute-start | bytes 5308424 | tf_op jit(solution)/shard_map/ppermute | solution.py:146
  40.0 22.5 %all-to-all-start.1 = ((bf16[8,2,10,32,128]{4,3,2,1,0:T(8,128)(2,1)}), bf16[8,2,10,32,128]{4,3,2,1,0:T(8,128)(2,1)}, u32[]{:S(2)}, u32[]{:S(2)}) async-start(bf16[8,2,10,32,128]{4,3,2,1,0:T(8,128)(2,1)} %shard_map.38), calls=%async_computation.1 | async-start | bytes 2621440 | tf_op jit(solution)/shard_map/all_to_all | solution.py:162
  46.5 28.2 %collective-permute-start.10 = (bf16[8,1,10,32,128]{4,3,2,1,0:T(8,128)(2,1)}, bf16[8,1,10,32,128]{4,3,2,1,0:T(8,128)(2,1)}, u32[]{:S(2)}, u32[]{:S(2)}) collective-permute-start(bf16[8,1,10,32,128]{4,3,2,1,0:T(8,128)(2,1)} %get-tuple-element.30), channel_id=1, source_target_pairs={{8,0},{16,8},{24,16},{9,1},{17,9},{25,17},{10,2},{18,10},{26,18},{... | collective-permute-start | bytes 1966088 | tf_op jit(solution)/shard_map/ppermute | solution.py:203
  47.8 26.9 %collective-permute-start.9 = (bf16[8,1,10,32,128]{4,3,2,1,0:T(8,128)(2,1)}, bf16[8,1,10,32,128]{4,3,2,1,0:T(8,128)(2,1)}, u32[]{:S(2)}, u32[]{:S(2)}) collective-permute-start(bf16[8,1,10,32,128]{4,3,2,1,0:T(8,128)(2,1)} %get-tuple-element.29), channel_id=1, source_target_pairs={{0,8},{8,16},{16,24},{1,9},{9,17},{17,25},{2,10},{10,18},{18,26},{... | collective-permute-start | bytes 1966088 | tf_op jit(solution)/shard_map/ppermute | solution.py:204
  57.5 1.3 %copy-start = (f32[2,8,256,128]{3,2,1,0:T(8,128)}, f32[2,8,256,128]{3,2,1,0:T(8,128)S(1)}, u32[]{:S(2)}) copy-start(f32[2,8,256,128]{3,2,1,0:T(8,128)S(1)} %shard_map.39.refs_0_) | copy-start | bytes 6291460
  62.5 1.6 %copy-start.1 = (f32[2,8,256,128]{3,2,1,0:T(8,128)S(1)}, f32[2,8,256,128]{3,2,1,0:T(8,128)}, u32[]{:S(2)}) copy-start(f32[2,8,256,128]{3,2,1,0:T(8,128)} %copy-done) | copy-start | bytes 6291460
  71.2 15.5 %collective-permute-start.7 = (bf16[2,8,64,128]{3,2,1,0:T(8,128)(2,1)S(1)}, bf16[2,8,64,128]{3,2,1,0:T(8,128)(2,1)S(1)}, u32[]{:S(2)}, u32[]{:S(2)}) collective-permute-start(bf16[2,8,64,128]{3,2,1,0:T(8,128)(2,1)S(1)} %get-tuple-element.28), channel_id=1, source_target_pairs={{0,6},{1,7},{2,4},{3,5},{4,2},{5,3},{6,0},{7,1},{8,14},{9,15},{10,... | collective-permute-start | bytes 786440 | tf_op jit(solution)/shard_map/ppermute | solution.py:146
  71.8 16.5 %collective-permute-start.6 = (bf16[2,8,64,128]{3,2,1,0:T(8,128)(2,1)S(1)}, bf16[2,8,64,128]{3,2,1,0:T(8,128)(2,1)S(1)}, u32[]{:S(2)}, u32[]{:S(2)}) collective-permute-start(bf16[2,8,64,128]{3,2,1,0:T(8,128)(2,1)S(1)} %get-tuple-element.27), channel_id=1, source_target_pairs={{0,4},{1,5},{2,6},{3,7},{4,0},{5,1},{6,2},{7,3},{8,12},{9,13},{10,... | collective-permute-start | bytes 786440 | tf_op jit(solution)/shard_map/ppermute | solution.py:146
  73.2 15.2 %collective-permute-start.5 = (bf16[2,8,64,128]{3,2,1,0:T(8,128)(2,1)S(1)}, bf16[2,8,64,128]{3,2,1,0:T(8,128)(2,1)S(1)}, u32[]{:S(2)}, u32[]{:S(2)}) collective-permute-start(bf16[2,8,64,128]{3,2,1,0:T(8,128)(2,1)S(1)} %get-tuple-element.26), channel_id=1, source_target_pairs={{0,2},{1,3},{2,0},{3,1},{4,6},{5,7},{6,4},{7,5},{8,10},{9,11},{10,... | collective-permute-start | bytes 786440 | tf_op jit(solution)/shard_map/ppermute | solution.py:146
  84.6 10.0 %collective-permute-start.13 = (bf16[2,8,64,128]{3,2,1,0:T(8,128)(2,1)S(1)}, bf16[2,8,64,128]{3,2,1,0:T(8,128)(2,1)S(1)}, u32[]{:S(2)}, u32[]{:S(2)}) collective-permute-start(bf16[2,8,64,128]{3,2,1,0:T(8,128)(2,1)S(1)} %get-tuple-element.34), channel_id=1, source_target_pairs={{0,6},{1,7},{2,4},{3,5},{4,2},{5,3},{6,0},{7,1},{8,14},{9,15},{10,... | collective-permute-start | bytes 786440 | tf_op jit(solution)/shard_map/ppermute | solution.py:146
  85.3 12.1 %collective-permute-start.12 = (bf16[2,8,64,128]{3,2,1,0:T(8,128)(2,1)S(1)}, bf16[2,8,64,128]{3,2,1,0:T(8,128)(2,1)S(1)}, u32[]{:S(2)}, u32[]{:S(2)}) collective-permute-start(bf16[2,8,64,128]{3,2,1,0:T(8,128)(2,1)S(1)} %get-tuple-element.33), channel_id=1, source_target_pairs={{0,4},{1,5},{2,6},{3,7},{4,0},{5,1},{6,2},{7,3},{8,12},{9,13},{10,... | collective-permute-start | bytes 786440 | tf_op jit(solution)/shard_map/ppermute | solution.py:146
  86.7 10.7 %collective-permute-start.11 = (bf16[2,8,64,128]{3,2,1,0:T(8,128)(2,1)S(1)}, bf16[2,8,64,128]{3,2,1,0:T(8,128)(2,1)S(1)}, u32[]{:S(2)}, u32[]{:S(2)}) collective-permute-start(bf16[2,8,64,128]{3,2,1,0:T(8,128)(2,1)S(1)} %get-tuple-element.32), channel_id=1, source_target_pairs={{0,2},{1,3},{2,0},{3,1},{4,6},{5,7},{6,4},{7,5},{8,10},{9,11},{10,... | collective-permute-start | bytes 786440 | tf_op jit(solution)/shard_map/ppermute | solution.py:146
  88.5 9.9 %collective-permute-start.8 = (bf16[4,2,8,32,128]{4,3,2,1,0:T(8,128)(2,1)S(1)}, bf16[4,2,8,32,128]{4,3,2,1,0:T(8,128)(2,1)S(1)}, u32[]{:S(2)}, u32[]{:S(2)}) collective-permute-start(bf16[4,2,8,32,128]{4,3,2,1,0:T(8,128)(2,1)S(1)} %pad_maximum_fusion.2), channel_id=1, source_target_pairs={{0,1},{1,0},{2,3},{3,2},{4,5},{5,4},{6,7},{7,6},{8,9},{9,8},{10,11... | collective-permute-start | bytes 1572872 | tf_op jit(solution)/shard_map/ppermute | solution.py:146
  97.5 2.0 %collective-permute-start.14 = (bf16[4,2,8,32,128]{4,3,2,1,0:T(8,128)(2,1)S(1)}, bf16[4,2,8,32,128]{4,3,2,1,0:T(8,128)(2,1)S(1)}, u32[]{:S(2)}, u32[]{:S(2)}) collective-permute-start(bf16[4,2,8,32,128]{4,3,2,1,0:T(8,128)(2,1)S(1)} %pad_maximum_fusion.3), channel_id=1, source_target_pairs={{0,1},{1,0},{2,3},{3,2},{4,5},{5,4},{6,7},{7,6},{8,9},{9,8},{10,11... | collective-permute-start | bytes 1572872 | tf_op jit(solution)/shard_map/ppermute | solution.py:146
